TPU v7x, 32 devices: a whole 2x2x4 slice. The times are simulated.
32 devices in a mesh: groups: 2 (over x), req: 16 (over z, y, core).
Axes of the slice: x: 2, y: 2, z: 4, core: 2. Of those that a mesh axis runs over, the one named last changes fastest.
Arguments:
- queries: bfloat16 [2, 2048, 512], P(None, ('groups', 'req')), parts along dimension 1, may hold values from -40 to 40
- new_kv: bfloat16 [2, 2048, 128], P(None, ('groups', 'req')), parts along dimension 1, may hold values from -4 to 4
- cache: bfloat16 [2, 2048, 128, 128], P(None, ('groups', 'req')), parts along dimension 1, may hold values from -4 to 4
- lengths: int32 [2, 256], P(None, 'groups'), parts along dimension 1, may hold values from 2 to 128
- residual: bfloat16 [2, 256, 2880], P(None, ('groups', 'req')), parts along dimension 1, may hold values from -30 to 30
- o_proj: bfloat16 [4096, 2880], P('req'), may hold values from -1 to 1
- router: bfloat16 [2880, 16], replicated, may hold values from -0.109375 to 0.109375
- w_gate: bfloat16 [64, 2880, 360], P('req'), may hold values from -0.109375 to 0.109375
- w_up: bfloat16 [64, 2880, 360], P('req'), may hold values from -0.109375 to 0.109375
- w_down: bfloat16 [64, 360, 2880], P('req'), may hold values from -0.15625 to 0.15625
- routes: int32 [2, 256, 4], P(None, ('groups', 'req')), parts along dimension 1, may hold values from 0 to 15, all different within a row; in each aligned block of 8 rows (0 to 7, 8 to 15, ..., all dimensions but the last counted through in order) at most 4 rows name the same one
Outputs:
- attended: bfloat16 [2, 256, 2880], P(None, ('groups', 'req')), parts along dimension 1
- layer_out: bfloat16 [2, 256, 2880], P(None, ('groups', 'req')), parts along dimension 1
There are 2 independent parts, one for each index of `groups`. A program takes and returns all parts, laid end to end along the dimension named above; an argument that names none is the same for every part. Nothing has to cross between parts.
Inputs may be any that keep to these rules, and one draw needn't show every extreme that they name: `routes`: each row names 4 different experts; of the 8 rows of one device of one micro-batch at most 4 name any one expert, and in every draw some expert is named by exactly 4 rows of some device.
All inputs are finite; a program needn't handle non-finite values.
Results may differ from a plain program's by a relative error of at most 0.0075.
Values may be sent and summed in bfloat16 or wider, within the bound.
No kernel may reach another device: no remote copies, remote signals or barrier semaphores. Data moves between devices by JAX's collectives and lax.ppermute only.
A program may use at most 128 MiB of HBM per device.

v0:
```python
import math

import jax
import jax.numpy as jnp
from jax import lax
from jax.sharding import PartitionSpec as P

D = 2880
HD = 64
KVH = 8
QPK = 8
WIN = 128
EXPERTS = 16
SPLIT = 4
TOPK = 4
MB = 2
REQ_DEV = 8
FFS = 360
CAP = 4


def from_partner(value, axis, stride):
    mask = 2**stride
    pairs = [(source, source ^ mask) for source in range(lax.axis_size(axis))]
    return lax.ppermute(value, axis, pairs)


def attention_rows(query_rows, new_pair, cache_rows, live_count):
    row_total = query_rows.shape[0]
    query_heads = query_rows.reshape(row_total, QPK, HD)
    factor = 1.0 / math.sqrt(HD)
    scores = (
        jnp.einsum(
            "rqd,rpd->rqp", query_heads, cache_rows[:, :, :HD], preferred_element_type=jnp.float32
        )
        * factor
    )
    own_score = (
        jnp.einsum("rqd,rd->rq", query_heads, new_pair[:, :HD], preferred_element_type=jnp.float32)
        * factor
    )
    live = jnp.arange(WIN)[None, None, :] < live_count[:, None, None]
    masked = jnp.where(live, scores, -jnp.inf)
    top_score = jnp.maximum(jnp.max(masked, axis=2), own_score)
    weight_cached = jnp.exp(masked - top_score[:, :, None])
    weight_own = jnp.exp(own_score - top_score)
    total = jnp.sum(weight_cached, axis=2) + weight_own
    prob_cached = (weight_cached / total[:, :, None]).astype(jnp.bfloat16)
    prob_own = (weight_own / total).astype(jnp.bfloat16)
    mixed = jnp.einsum(
        "rqp,rpd->rqd", prob_cached, cache_rows[:, :, HD:], preferred_element_type=jnp.float32
    )
    mixed = (
        mixed
        + prob_own.astype(jnp.float32)[:, :, None]
        * new_pair[:, HD:].astype(jnp.float32)[:, None, :]
    )
    return mixed.astype(jnp.bfloat16)


def bit_value(device_index, bit_number):
    return device_index // (1 << bit_number) % 2


def expert_grouped(buffer, w_gate, w_up, w_down, device_count, device_index):
    batch_width = buffer.shape[0]
    spread = max(1, device_count // EXPERTS)
    experts_local = max(1, EXPERTS // device_count)
    quarters_local = SPLIT // spread
    piece_rows = CAP // spread
    sent = buffer.reshape(batch_width, EXPERTS * spread, piece_rows, D)
    arrived = lax.all_to_all(sent, "req", split_axis=1, concat_axis=2, tiled=True)
    spread_levels = spread.bit_length() - 1
    for section_bit in range(spread_levels):
        upper = bit_value(device_index, section_bit) == 1
        received = from_partner(arrived, "req", section_bit)
        arrived = jnp.where(
            upper,
            jnp.concatenate([received, arrived], axis=2),
            jnp.concatenate([arrived, received], axis=2),
        )
    gate_local = w_gate.reshape(experts_local, quarters_local, D, FFS)
    up_local = w_up.reshape(experts_local, quarters_local, D, FFS)
    down_local = w_down.reshape(experts_local, quarters_local, FFS, D)
    gate_hidden = jnp.einsum(
        "merd,eqdf->meqrf", arrived, gate_local, preferred_element_type=jnp.float32
    )
    up_hidden = jnp.einsum(
        "merd,eqdf->meqrf", arrived, up_local, preferred_element_type=jnp.float32
    )
    active = ((up_hidden + 1.0) * gate_hidden * jax.nn.sigmoid(1.702 * gate_hidden)).astype(
        jnp.bfloat16
    )
    partial_out = jnp.einsum(
        "meqrf,eqfd->merd", active, down_local, preferred_element_type=jnp.float32
    )
    for section_bit in reversed(range(spread_levels)):
        upper = bit_value(device_index, section_bit) == 1
        halves = partial_out.reshape(batch_width, experts_local, 2, partial_out.shape[2] // 2, D)
        keep_part = jnp.where(upper, halves[:, :, 1], halves[:, :, 0])
        send_part = jnp.where(upper, halves[:, :, 0], halves[:, :, 1])
        received = from_partner(send_part.astype(jnp.bfloat16), "req", section_bit).astype(
            send_part.dtype
        )
        partial_out = keep_part + received
    came_back = lax.all_to_all(
        partial_out.astype(jnp.bfloat16), "req", split_axis=2, concat_axis=1, tiled=True
    ).astype(partial_out.dtype)
    return came_back.reshape(batch_width, EXPERTS * CAP, D)


def shards(queries, new_kv, cache, lengths, residual, o_proj, router, w_gate, w_up, w_down, routes):
    device_count = lax.axis_size("req")
    device_index = lax.axis_index("req")
    group_size = device_count // KVH
    group_bits = group_size.bit_length() - 1
    local_rows = queries.shape[1]
    request_count = local_rows * group_size
    block_index = device_index % group_size
    local_lengths = lax.dynamic_slice_in_dim(lengths, block_index * local_rows, local_rows, 1)

    def process_batches(first_batch, batch_width):
        query_part = queries[first_batch : first_batch + batch_width].reshape(
            batch_width * local_rows, QPK * HD
        )
        pair_part = new_kv[first_batch : first_batch + batch_width].reshape(
            batch_width * local_rows, 2 * HD
        )
        cache_part = cache[first_batch : first_batch + batch_width].reshape(
            batch_width * local_rows, WIN, 2 * HD
        )
        live_part = local_lengths[first_batch : first_batch + batch_width].reshape(
            batch_width * local_rows
        )
        mixed = attention_rows(query_part, pair_part, cache_part, live_part)
        held = mixed.reshape(batch_width, local_rows, group_size, QPK // group_size * HD)
        for section_bit in range(group_bits):
            upper = bit_value(device_index, section_bit) == 1
            paired = held.reshape(batch_width, held.shape[1], held.shape[2] // 2, 2, held.shape[3])
            keep_part = jnp.where(upper, paired[:, :, :, 1], paired[:, :, :, 0])
            send_part = jnp.where(upper, paired[:, :, :, 0], paired[:, :, :, 1])
            received = from_partner(send_part, "req", section_bit)
            held = jnp.where(
                upper,
                jnp.concatenate([received, keep_part], axis=1),
                jnp.concatenate([keep_part, received], axis=1),
            )
        head_rows = held.reshape(batch_width, request_count, held.shape[3]).transpose(1, 0, 2)
        summed = lax.psum_scatter(
            jnp.einsum("rmk,kd->rmd", head_rows, o_proj, preferred_element_type=jnp.float32),
            "req",
            scatter_dimension=0,
            tiled=True,
        )
        attended_wide = residual[first_batch : first_batch + batch_width].astype(
            jnp.float32
        ) + summed.transpose(1, 0, 2)
        attended = attended_wide.astype(jnp.bfloat16)
        attended_wide = attended.astype(jnp.float32)
        normed = (
            attended_wide
            * lax.rsqrt(jnp.mean(attended_wide * attended_wide, axis=2, keepdims=True) + 1e-05)
        ).astype(jnp.bfloat16)
        logits = jnp.einsum("mrd,de->mre", normed, router, preferred_element_type=jnp.float32)
        route_ids = routes[first_batch : first_batch + batch_width]
        chosen = jnp.take_along_axis(logits, route_ids, axis=2)
        gates = 1.0 / jnp.sum(jnp.exp(chosen[:, :, None, :] - chosen[:, :, :, None]), axis=3)
        one_hot = (
            route_ids.reshape(batch_width, REQ_DEV * TOPK)[:, :, None]
            == jnp.arange(EXPERTS, dtype=jnp.int32)[None, None, :]
        ).astype(jnp.int32)
        earlier = jnp.cumsum(one_hot, axis=1) - one_hot
        ranks = jnp.sum(earlier * one_hot, axis=2).reshape(batch_width, REQ_DEV, TOPK)
        batch_offset = (jnp.arange(batch_width, dtype=jnp.int32) * (EXPERTS * CAP))[:, None, None]
        flat_index = batch_offset + route_ids * CAP + ranks
        repeated = jnp.repeat(normed.reshape(batch_width * REQ_DEV, D), TOPK, axis=0)
        buffer = (
            jnp.zeros((batch_width * EXPERTS * CAP, D), jnp.bfloat16)
            .at[flat_index.reshape(-1)]
            .set(repeated)
        )
        buffer = buffer.reshape(batch_width, EXPERTS, CAP, D)
        returned = expert_grouped(buffer, w_gate, w_up, w_down, device_count, device_index)
        picked = jnp.take(returned.reshape(batch_width * EXPERTS * CAP, D), flat_index, axis=0)
        mixture = jnp.sum(gates[:, :, :, None] * picked, axis=2)
        layer = (attended_wide + mixture).astype(jnp.bfloat16)
        return (attended, layer)

    results = [process_batches(batch_index, 1) for batch_index in range(MB)]
    attended_all = jnp.concatenate([result[0] for result in results], axis=0)
    layer_all = jnp.concatenate([result[1] for result in results], axis=0)
    return (attended_all, layer_all)


def solution(mesh):
    placed = (
        P(None, ("groups", "req"), None),
        P(None, ("groups", "req"), None),
        P(None, ("groups", "req"), None, None),
        P(None, "groups"),
        P(None, ("groups", "req"), None),
        P("req", None),
        P(),
        P("req", None, None),
        P("req", None, None),
        P("req", None, None),
        P(None, ("groups", "req"), None),
    )
    return jax.shard_map(
        shards,
        mesh=mesh,
        in_specs=placed,
        out_specs=(P(None, ("groups", "req"), None), P(None, ("groups", "req"), None)),
        check_vma=False,
    )
```

profile of v0, /device:TPU:0, one launch (start us, length us, event | category | flops | bytes accessed | tf_op | source)
XLA Modules:
  0.0 243.5 jit_solution(3754402669353376935)
XLA Ops:
  7.2 4.8 %fusion.88 = (bf16[1,64,128,128]{3,2,1,0:T(8,128)(2,1)}, bf16[1,64,128,128]{3,2,1,0:T(8,128)(2,1)}) fusion(bf16[2,64,128,128]{3,2,1,0:T(8,128)(2,1)} %param.17), kind=kLoop, calls=%fused_computation.172 | loop fusion | bytes 8388608 | tf_op jit(solution)/shard_map/slice | solution.py:129
  12.1 4.1 %copy.162 = bf16[1,64,128,128]{2,3,1,0:T(8,128)(2,1)} copy(bf16[1,64,128,128]{3,2,1,0:T(8,128)(2,1)} %get-tuple-element.19) | data formatting | bytes 4194304
  16.2 0.1 reshape_reshape.16
  16.6 0.2 fusion.68
  16.8 1.8 fusion.93
  18.7 0.2 fusion.33
  19.0 0.7 fusion.13
  19.7 0.2 reshape_reshape.17
  20.0 0.5 collective-permute-start.1
  20.5 4.1 %copy.159 = bf16[1,64,128,128]{2,3,1,0:T(8,128)(2,1)} copy(bf16[1,64,128,128]{3,2,1,0:T(8,128)(2,1)} %get-tuple-element.18) | data formatting | bytes 4194304
  24.6 0.1 reshape_reshape.14
  24.7 0.2 fusion.70
  24.9 1.8 fusion.94
  26.7 0.2 fusion.32
  27.0 0.7 fusion.12
  27.7 0.2 reshape_reshape.15
  28.0 0.1 collective-permute-start
  28.7 0.5 convolution_bitcast_fusion
  29.3 3.1 %copy.132 = f32[128,1,2880]{2,1,0:T(1,128)} copy(f32[128,1,2880]{0,2,1:T(8,128)S(1)} %convolution_bitcast_fusion) | data formatting | bytes 2949120 | tf_op jit(solution)/shard_map/rmk,kd->rmd/dot_general | solution.py:150
  32.3 0.5 convolution_bitcast_fusion.1
  32.9 3.1 %copy.128 = f32[128,1,2880]{2,1,0:T(1,128)} copy(f32[128,1,2880]{0,2,1:T(8,128)S(1)} %convolution_bitcast_fusion.1) | data formatting | bytes 2949120 | tf_op jit(solution)/shard_map/rmk,kd->rmd/dot_general | solution.py:150
  36.0 0.2 select_reduce_fusion.1
  36.4 0.2 select_reduce_fusion
  38.0 0.6 dynamic-slice
  39.3 102.8 %all-reduce.5.cloned.1.call-done = (f32[128,1,2880]{2,1,0:T(1,128)}, f32[128,1,2880]{2,1,0:T(1,128)}) async-done(((f32[128,1,2880]{2,1,0:T(1,128)}, f32[128,1,2880]{2,1,0:T(1,128)}), (f32[128,1,2880]{2,1,0:T(1,128)}, f32[128,1,2880]{2,1,0:T(1,128)})) %all-reduce.5.cloned.1.call-update) | async-done | bytes 2949136
  142.1 0.9 constant_dynamic-slice_fusion.1
  143.0 0.9 constant_dynamic-slice_fusion
  143.9 0.2 fusion.46
  144.3 1.0 scatter_custom_fusion.1
  145.3 0.8 reshape.675
  146.1 4.2 %all-to-all-start.2 = ((bf16[1,16,4,2880]{3,2,0,1:T(4,128)(2,1)}), bf16[1,16,4,2880]{3,2,0,1:T(4,128)(2,1)S(1)}, u32[]{:S(2)}, u32[]{:S(2)}) async-start(bf16[1,16,4,2880]{3,2,0,1:T(4,128)(2,1)} %reshape.675), calls=%async_computation.2 | async-start | bytes 753664 | tf_op jit(solution)/shard_map/all_to_all | solution.py:72
  150.3 0.1 fusion.97
  150.5 0.1 fusion.95
  150.6 0.7 gather_fusion
  151.5 0.7 gather_fusion.2
  152.6 1.0 scatter_custom_fusion
  153.6 0.8 reshape.668
  154.6 0.7 pad_maximum_fusion
  155.2 7.0 %all-to-all-done.2 = bf16[1,16,4,2880]{3,2,0,1:T(4,128)(2,1)S(1)} async-done(((bf16[1,16,4,2880]{3,2,0,1:T(4,128)(2,1)}), bf16[1,16,4,2880]{3,2,0,1:T(4,128)(2,1)S(1)}, u32[]{:S(2)}, u32[]{:S(2)}) %all-to-all-start.2) | async-done | bytes 368672 | tf_op jit(solution)/shard_map/all_to_all | solution.py:72
  162.2 3.7 %all-to-all-start = ((bf16[1,16,4,2880]{3,2,0,1:T(4,128)(2,1)}), bf16[1,16,4,2880]{3,2,0,1:T(4,128)(2,1)S(1)}, u32[]{:S(2)}, u32[]{:S(2)}) async-start(bf16[1,16,4,2880]{3,2,0,1:T(4,128)(2,1)} %reshape.668), calls=%async_computation | async-start | bytes 753664 | tf_op jit(solution)/shard_map/all_to_all | solution.py:72
  165.9 0.2 reshape.787
  166.1 6.1 %fusion.98 = f32[64,4,360]{2,0,1:T(8,128)S(1)} fusion(bf16[64,2880,1]{1,0,2:T(8,128)(2,1)S(1)} %reshape.787, bf16[4,2880,360]{1,2,0:T(8,128)(2,1)} %param.22), kind=kOutput, calls=%fused_computation.184 | convolution fusion | flops 530841600 | bytes 9031680 | tf_op jit(solution)/shard_map/merd,eqdf->meqrf/dot_general | solution.py:85
  172.2 9.9 %fusion.2 = bf16[1,1,64,2880]{3,2,0,1:T(8,128)(2,1)S(1)} fusion(bf16[4,360,2880]{2,1,0:T(8,128)(2,1)} %param.24, f32[64,4,360]{2,0,1:T(8,128)S(1)} %fusion.98, bf16[64,2880,1]{1,0,2:T(8,128)(2,1)S(1)} %reshape.787, bf16[4,2880,360]{1,2,0:T(8,128)(2,1)} %param.23), kind=kOutput, calls=%fused_computation.12 | convolution fusion | flops 1062604800 | bytes 17694720 | tf_op jit(solution)/shard_map/meqrf,eqfd->merd/dot_general | solution.py:94
  182.1 0.6 copy.185
  182.7 0.5 broadcast.520
  183.2 3.0 %reduce.8 = bf16[64,2880]{1,0:T(8,128)(2,1)S(1)} reduce(bf16[64,1,1,2880]{3,2,1,0:T(2,128)(2,1)S(1)} %bitcast.159, bf16[]{:T(256)} %broadcast.520), dimensions={1,2}, to_apply=%bitcast.153.reduce_sub_computation | reduce | bytes 737282
  186.2 1.1 reshape.797
  187.4 5.8 %all-to-all-start.3 = ((bf16[16,2,5760]{2,1,0:T(2,128)(2,1)}), bf16[16,2,5760]{2,1,0:T(2,128)(2,1)S(1)}, u32[]{:S(2)}, u32[]{:S(2)}) async-start(bf16[16,2,5760]{2,1,0:T(2,128)(2,1)} %reshape.797), calls=%async_computation.3 | async-start | bytes 737280 | tf_op jit(solution)/shard_map/all_to_all | solution.py:106
  193.2 0.2 reshape.785
  193.3 6.1 %fusion.96 = f32[64,4,360]{2,0,1:T(8,128)S(1)} fusion(bf16[64,2880,1]{1,0,2:T(8,128)(2,1)S(1)} %reshape.785, bf16[4,2880,360]{1,2,0:T(8,128)(2,1)} %param.22), kind=kOutput, calls=%fused_computation.182 | convolution fusion | flops 530841600 | bytes 9031680 | tf_op jit(solution)/shard_map/merd,eqdf->meqrf/dot_general | solution.py:85
  199.4 9.9 %fusion.3 = bf16[1,1,64,2880]{3,2,0,1:T(8,128)(2,1)S(1)} fusion(bf16[4,360,2880]{2,1,0:T(8,128)(2,1)} %param.24, f32[64,4,360]{2,0,1:T(8,128)S(1)} %fusion.96, bf16[64,2880,1]{1,0,2:T(8,128)(2,1)S(1)} %reshape.785, bf16[4,2880,360]{1,2,0:T(8,128)(2,1)} %param.23), kind=kOutput, calls=%fused_computation.13 | convolution fusion | flops 1062604800 | bytes 17694720 | tf_op jit(solution)/shard_map/meqrf,eqfd->merd/dot_general | solution.py:94
  209.4 0.6 copy.186
  209.9 3.0 %reduce.9 = bf16[64,2880]{1,0:T(8,128)(2,1)S(1)} reduce(bf16[64,1,1,2880]{3,2,1,0:T(2,128)(2,1)S(1)} %bitcast.160, bf16[]{:T(256)} %broadcast.520), dimensions={1,2}, to_apply=%bitcast.154.reduce_sub_computation | reduce | bytes 737282
  212.9 1.1 reshape.799
  214.1 6.0 %all-to-all-start.1 = ((bf16[16,2,5760]{2,1,0:T(2,128)(2,1)}), bf16[16,2,5760]{2,1,0:T(2,128)(2,1)}, u32[]{:S(2)}, u32[]{:S(2)}) async-start(bf16[16,2,5760]{2,1,0:T(2,128)(2,1)} %reshape.799), calls=%async_computation.1 | async-start | bytes 737280 | tf_op jit(solution)/shard_map/all_to_all | solution.py:106
  220.1 0.6 reshape.798
  220.8 0.7 gather_fusion.3
  221.6 0.3 fusion.30
  222.0 10.0 %all-to-all-done.1 = bf16[16,2,5760]{2,1,0:T(2,128)(2,1)} async-done(((bf16[16,2,5760]{2,1,0:T(2,128)(2,1)}), bf16[16,2,5760]{2,1,0:T(2,128)(2,1)}, u32[]{:S(2)}, u32[]{:S(2)}) %all-to-all-start.1) | async-done | bytes 368672 | tf_op jit(solution)/shard_map/all_to_all | solution.py:106
  232.0 2.8 %reshape.800 = bf16[64,1,1,2880]{3,2,1,0:T(2,128)(2,1)S(1)} reshape(bf16[16,2,5760]{2,1,0:T(2,128)(2,1)} %all-to-all-done.1) | data formatting | bytes 737280
  234.9 0.7 gather_fusion.1
  235.6 0.1 reshape.770
  235.7 0.3 fusion.31
  236.0 0.7 pad_maximum_fusion.1
  (98 shorter events, 4.0 us)
Async XLA Ops:
  7.2 21.5 %copy-start = (bf16[256,2880]{0,1:T(8,128)(2,1)S(1)}, bf16[256,2880]{0,1:T(8,128)(2,1)}, u32[]{:S(2)}) copy-start(bf16[256,2880]{0,1:T(8,128)(2,1)} %param.20) | copy-start | bytes 4423684
  7.2 134.9 %all-reduce.5.cloned.1.call-start = ((), (), s32[]{:S(2)}) async-start(), calls=%async_computation.4 | async-start | bytes 6029312
  12.1 4.1 %copy-start.4 = (bf16[2,64,512]{2,1,0:T(8,128)(2,1)S(1)}, bf16[2,64,512]{2,1,0:T(8,128)(2,1)}, u32[]{:S(2)}) copy-start(bf16[2,64,512]{2,1,0:T(8,128)(2,1)} %param.15) | copy-start | bytes 393220
  12.1 4.3 %copy-start.8 = (s32[2,128]{1,0:T(2,128)S(1)}, s32[2,128]{1,0:T(2,128)}, u32[]{:S(2)}) copy-start(s32[2,128]{1,0:T(2,128)} %param.18) | copy-start | bytes 3076
  12.1 4.4 %copy-start.7 = (bf16[2,64,128]{2,1,0:T(8,128)(2,1)S(1)}, bf16[2,64,128]{2,1,0:T(8,128)(2,1)}, u32[]{:S(2)}) copy-start(bf16[2,64,128]{2,1,0:T(8,128)(2,1)} %param.16) | copy-start | bytes 98308
  16.4 2.6 %copy-start.1 = (bf16[1,64,128,128]{2,3,1,0:T(8,128)(2,1)S(1)}, bf16[1,64,128,128]{2,3,1,0:T(8,128)(2,1)}, u32[]{:S(2)}) copy-start(bf16[1,64,128,128]{2,3,1,0:T(8,128)(2,1)} %copy.162) | copy-start | bytes 6291460
  20.0 8.7 %collective-permute-start.1 = (bf16[1,64,1,256]{3,1,2,0:T(8,128)(2,1)S(1)}, bf16[1,64,1,256]{3,1,2,0:T(8,128)(2,1)S(1)}, u32[]{:S(2)}, u32[]{:S(2)}) collective-permute-start(bf16[1,64,1,256]{3,1,2,0:T(8,128)(2,1)S(1)} %get-tuple-element.24), channel_id=1, source_target_pairs={{0,1},{1,0},{2,3},{3,2},{4,5},{5,4},{6,7},{7,6},{8,9},{9,8},{10,11... | collective-permute-start | bytes 98312 | tf_op jit(solution)/shard_map/ppermute | solution.py:25
  24.7 2.3 copy-start.2
  26.7 1.4 copy-start.6
  28.0 4.3 %collective-permute-start = (bf16[1,64,1,256]{3,1,2,0:T(8,128)(2,1)S(1)}, bf16[1,64,1,256]{3,1,2,0:T(8,128)(2,1)S(1)}, u32[]{:S(2)}, u32[]{:S(2)}) collective-permute-start(bf16[1,64,1,256]{3,1,2,0:T(8,128)(2,1)S(1)} %get-tuple-element.20), channel_id=1, source_target_pairs={{0,1},{1,0},{2,3},{3,2},{4,5},{5,4},{6,7},{7,6},{8,9},{9,8},{10,11... | collective-permute-start | bytes 98312 | tf_op jit(solution)/shard_map/ppermute | solution.py:25
  36.0 2.0 copy-start.9
  36.0 107.9 %copy-start.5 = (bf16[2,8,2880]{2,1,0:T(8,128)(2,1)S(1)}, bf16[2,8,2880]{2,1,0:T(8,128)(2,1)}, u32[]{:S(2)}) copy-start(bf16[2,8,2880]{2,1,0:T(8,128)(2,1)} %param.19) | copy-start | bytes 276484
  36.0 114.3 %copy-start.3 = (bf16[2880,16]{0,1:T(8,128)(2,1)S(1)}, bf16[2880,16]{0,1:T(8,128)(2,1)}, u32[]{:S(2)}) copy-start(bf16[2880,16]{0,1:T(8,128)(2,1)} %param.21) | copy-start | bytes 276484
  146.1 16.1 %all-to-all-start.2 = ((bf16[1,16,4,2880]{3,2,0,1:T(4,128)(2,1)}), bf16[1,16,4,2880]{3,2,0,1:T(4,128)(2,1)S(1)}, u32[]{:S(2)}, u32[]{:S(2)}) async-start(bf16[1,16,4,2880]{3,2,0,1:T(4,128)(2,1)} %reshape.675), calls=%async_computation.2 | async-start | bytes 753664 | tf_op jit(solution)/shard_map/all_to_all | solution.py:72
  162.2 25.2 %all-to-all-start = ((bf16[1,16,4,2880]{3,2,0,1:T(4,128)(2,1)}), bf16[1,16,4,2880]{3,2,0,1:T(4,128)(2,1)S(1)}, u32[]{:S(2)}, u32[]{:S(2)}) async-start(bf16[1,16,4,2880]{3,2,0,1:T(4,128)(2,1)} %reshape.668), calls=%async_computation | async-start | bytes 753664 | tf_op jit(solution)/shard_map/all_to_all | solution.py:72
  187.4 26.7 %all-to-all-start.3 = ((bf16[16,2,5760]{2,1,0:T(2,128)(2,1)}), bf16[16,2,5760]{2,1,0:T(2,128)(2,1)S(1)}, u32[]{:S(2)}, u32[]{:S(2)}) async-start(bf16[16,2,5760]{2,1,0:T(2,128)(2,1)} %reshape.797), calls=%async_computation.3 | async-start | bytes 737280 | tf_op jit(solution)/shard_map/all_to_all | solution.py:106
  214.1 17.9 %all-to-all-start.1 = ((bf16[16,2,5760]{2,1,0:T(2,128)(2,1)}), bf16[16,2,5760]{2,1,0:T(2,128)(2,1)}, u32[]{:S(2)}, u32[]{:S(2)}) async-start(bf16[16,2,5760]{2,1,0:T(2,128)(2,1)} %reshape.799), calls=%async_computation.1 | async-start | bytes 737280 | tf_op jit(solution)/shard_map/all_to_all | solution.py:106
Sparse Core Ops, SparseCore 0:
  36.1 105.8 all-reduce.4
where the time goes:
time: 244 us
  waiting for transfers between devices  120 us (49%)
  local copies, waits for them, and re-layouts  39.3 us (16%)
  matrix products  38.8 us (16%)
  starting transfers between devices  20.4 us (8%)
  between operations  15.3 us (6%)
  other arithmetic  9.88 us (4%)
    unnamed x2, waiting for transfers between devices  103 us
    dot_general x2, matrix products, expert_grouped(): jnp.einsum('meqrf,eqfd->merd', active, down_local, preferred_element_type...  19.8 us
    unnamed x30, local copies, waits for them, and re-layouts  16.8 us
    dot_general x2, matrix products, expert_grouped(): jnp.einsum('merd,eqdf->meqrf', arrived, gate_local, preferred_element_typ...  12.1 us
    all_to_all x2, starting transfers between devices, expert_grouped(): lax.all_to_all(partial_out.astype(jnp.bfloat16), 'req', split_axis=2, con...  11.8 us
    all_to_all x2, waiting for transfers between devices, expert_grouped(): lax.all_to_all(partial_out.astype(jnp.bfloat16), 'req', split_axis=2, con...  10 us
    all_to_all x2, starting transfers between devices, expert_grouped(): lax.all_to_all(sent, 'req', split_axis=1, concat_axis=2, tiled=True)  7.88 us
    all_to_all x2, waiting for transfers between devices, expert_grouped(): lax.all_to_all(sent, 'req', split_axis=1, concat_axis=2, tiled=True)  6.99 us
  transfers between devices with their start and end apart: 7, of which 3 were waited for; matrix products, arithmetic and copies ran while one was open for 26% of the time, Pallas kernels for 0%

commit v1 on v0

v1 whole, which is shorter than its diff:
```python
import math

import jax
import jax.numpy as jnp
from jax import lax
from jax.sharding import PartitionSpec as P

HD = 64
KVH = 8
QPK = 8
EXPERTS = 16
SPLIT = 4
REQ_DEV = 8


def plan(device_count):
    bits = device_count.bit_length() - 1
    stages = [(0, 1)] if bits else []
    bit = 1
    while bit < bits:
        width = min(2, bits - bit)
        stages.append((bit, width))
        bit += width
    masks = [0]
    for bit, width in stages:
        masks = [mask | (r << bit) for mask in masks for r in range(1 << width)]
    return stages, masks


def from_mask(value, mask):
    pairs = [(source, source ^ mask) for source in range(lax.axis_size("req"))]
    return lax.ppermute(value, "req", pairs)


def scatter_sum(parts, stages):
    for bit, width in stages:
        parts = parts.reshape((1 << width, -1) + parts.shape[1:])
        total = parts[0].astype(jnp.float32)
        for r in range(1, 1 << width):
            total = total + from_mask(parts[r].astype(jnp.bfloat16), r << bit).astype(jnp.float32)
        parts = total
    return parts[0]


def gather_rows(rows, stages):
    held = rows[None]
    for bit, width in reversed(stages):
        held = jnp.concatenate(
            [held] + [from_mask(held, r << bit) for r in range(1, 1 << width)], axis=0
        )
    return held


def attention_rows(query_rows, new_pair, cache_rows, live_count):
    row_total = query_rows.shape[0]
    window = cache_rows.shape[1]
    query_heads = query_rows.reshape(row_total, QPK, HD)
    factor = 1.0 / math.sqrt(HD)
    scores = (
        jnp.einsum(
            "rqd,rpd->rqp", query_heads, cache_rows[:, :, :HD], preferred_element_type=jnp.float32
        )
        * factor
    )
    own_score = (
        jnp.einsum("rqd,rd->rq", query_heads, new_pair[:, :HD], preferred_element_type=jnp.float32)
        * factor
    )
    live = jnp.arange(window)[None, None, :] < live_count[:, None, None]
    masked = jnp.where(live, scores, -jnp.inf)
    top_score = jnp.maximum(jnp.max(masked, axis=2), own_score)
    weight_cached = jnp.exp(masked - top_score[:, :, None])
    weight_own = jnp.exp(own_score - top_score)
    total = jnp.sum(weight_cached, axis=2) + weight_own
    prob_cached = (weight_cached / total[:, :, None]).astype(jnp.bfloat16)
    prob_own = (weight_own / total).astype(jnp.bfloat16)
    mixed = jnp.einsum(
        "rqp,rpd->rqd", prob_cached, cache_rows[:, :, HD:], preferred_element_type=jnp.float32
    )
    mixed = (
        mixed
        + prob_own.astype(jnp.float32)[:, :, None]
        * new_pair[:, HD:].astype(jnp.float32)[:, None, :]
    )
    return mixed.astype(jnp.bfloat16).reshape(row_total, QPK * HD)


def trade_heads(mixed, group_size, device_index):
    batch, rows, width = mixed.shape
    mine = device_index % group_size
    by_member = mixed.reshape(batch, rows, group_size, width // group_size)
    held = []
    for r in range(group_size):
        part = lax.dynamic_index_in_dim(by_member, mine ^ r, 2, keepdims=False)
        held.append(part if r == 0 else from_mask(part, r))
    held = jnp.stack(held)
    held = jnp.take(held, mine ^ jnp.arange(group_size), axis=0)
    return held.transpose(0, 2, 1, 3).reshape(group_size * rows, batch, width // group_size)


def shards(queries, new_kv, cache, lengths, residual, o_proj, router, w_gate, w_up, w_down, routes):
    device_count = lax.axis_size("req")
    device_index = lax.axis_index("req")
    stages, masks = plan(device_count)
    group_size = max(1, device_count // KVH)
    batch, local_rows = queries.shape[:2]
    width = residual.shape[2]
    block_rows = batch * REQ_DEV
    block_index = device_index % group_size
    local_lengths = lax.dynamic_slice_in_dim(lengths, block_index * local_rows, local_rows, 1)

    mixed = attention_rows(
        queries.reshape((-1,) + queries.shape[2:]),
        new_kv.reshape((-1,) + new_kv.shape[2:]),
        cache.reshape((-1,) + cache.shape[2:]),
        local_lengths.reshape(-1),
    ).reshape(batch, local_rows, QPK * HD)
    heads = trade_heads(mixed, group_size, device_index)
    heads = heads.reshape(device_count, REQ_DEV, batch, -1).transpose(0, 2, 1, 3)
    heads = jnp.take(heads, device_index ^ jnp.array(masks, jnp.int32), axis=0)
    parts = jnp.dot(
        heads.reshape(device_count * block_rows, -1), o_proj, preferred_element_type=jnp.float32
    ).reshape(device_count, block_rows, width)
    summed = scatter_sum(parts, stages)

    attended = (residual.reshape(block_rows, width).astype(jnp.float32) + summed).astype(
        jnp.bfloat16
    )
    attended_wide = attended.astype(jnp.float32)
    normed = (
        attended_wide
        * lax.rsqrt(jnp.mean(attended_wide * attended_wide, axis=1, keepdims=True) + 1e-05)
    ).astype(jnp.bfloat16)
    logits = jnp.dot(normed, router, preferred_element_type=jnp.float32)
    chosen_one = routes.reshape(block_rows, -1)[:, :, None] == jnp.arange(EXPERTS)[None, None, :]
    chosen = jnp.sum(jnp.where(chosen_one, logits[:, None, :], 0.0), axis=2)
    gates = 1.0 / jnp.sum(jnp.exp(chosen[:, None, :] - chosen[:, :, None]), axis=2)
    dense = jnp.sum(jnp.where(chosen_one, gates[:, :, None], 0.0), axis=1)
    high = lax.reduce_precision(dense, 8, 7)
    payload = jnp.concatenate(
        [normed, high.astype(jnp.bfloat16), (dense - high).astype(jnp.bfloat16)], axis=1
    )

    gathered = gather_rows(payload, stages).reshape(device_count * block_rows, -1)
    rows_in = gathered[:, :width]
    tail = gathered[:, width:].astype(jnp.float32)
    all_gates = tail[:, :EXPERTS] + tail[:, EXPERTS:]
    local_entries = w_gate.shape[0]
    partial = 0.0
    for entry in range(local_entries):
        expert = (device_index * local_entries + entry) // SPLIT
        gate_hidden = jnp.dot(rows_in, w_gate[entry], preferred_element_type=jnp.float32)
        up_hidden = jnp.dot(rows_in, w_up[entry], preferred_element_type=jnp.float32)
        active = ((up_hidden + 1.0) * gate_hidden * jax.nn.sigmoid(1.702 * gate_hidden)).astype(
            jnp.bfloat16
        )
        out = jnp.dot(active, w_down[entry], preferred_element_type=jnp.float32)
        partial = partial + out * lax.dynamic_slice_in_dim(all_gates, expert, 1, 1)
    mixture = scatter_sum(partial.reshape(device_count, block_rows, width), stages)
    layer = (attended_wide + mixture).astype(jnp.bfloat16)
    return attended.reshape(residual.shape), layer.reshape(residual.shape)


def solution(mesh):
    placed = (
        P(None, ("groups", "req"), None),
        P(None, ("groups", "req"), None),
        P(None, ("groups", "req"), None, None),
        P(None, "groups"),
        P(None, ("groups", "req"), None),
        P("req", None),
        P(),
        P("req", None, None),
        P("req", None, None),
        P("req", None, None),
        P(None, ("groups", "req"), None),
    )
    return jax.shard_map(
        shards,
        mesh=mesh,
        in_specs=placed,
        out_specs=(P(None, ("groups", "req"), None), P(None, ("groups", "req"), None)),
        check_vma=False,
    )
```

time: 244 us -> 133 us (0.55)
  waiting for transfers between devices: 120 us -> 40.2 us
  local copies, waits for them, and re-layouts: 39.3 us -> 20.9 us
  between operations: 15.3 us -> 1.09 us
  matrix products: 38.8 us -> 45.9 us
  other arithmetic: 9.88 us -> 5.18 us
    unnamed x2 -> x0, waiting for transfers between devices: 103 us -> none
    ppermute x2 -> x16, waiting for transfers between devices: 0.01 us -> 40.2 us  [from_mask(): return lax.ppermute(value, 'req', pairs)]
    all_to_all x4 -> x0, starting transfers between devices: 19.7 us -> none  [the longest x2 11.8 us: expert_grouped(): lax.all_to_all(partial_out.astype(jnp.bfloat16), 'req', split_axis=2, con...]
    ppermute x2 -> x16, starting transfers between devices: 0.65 us -> 18.8 us  [from_mask(): return lax.ppermute(value, 'req', pairs)]
    all_to_all x4 -> x0, waiting for transfers between devices: 17 us -> none  [the longest x2 10 us: expert_grouped(): lax.all_to_all(partial_out.astype(jnp.bfloat16), 'req', split_axis=2, con...]
    dot_general x8 -> x10, matrix products: 33.3 us -> 40.5 us  [the longest x4 29.5 us: shards(): out = jnp.dot(active, w_down[entry], preferred_element_type=jnp.float32)]
    dot_general x2 -> x1, local copies, waits for them, and re-layouts: 6.17 us -> 0.05 us  [attention_rows(): jnp.einsum('rqd,rd->rq', query_heads, new_pair[:, :HD], preferred_element...]
    unnamed x30 -> x26, local copies, waits for them, and re-layouts: 16.8 us -> 10.8 us
  transfers between devices with their start and end apart: 7 -> 16, of which waited for: 3 -> 15; matrix products, arithmetic and copies ran while one was open for 26% -> 3% of each run, Pallas kernels for 0% -> 0%
where the time goes in v1:
time: 133 us; the launch traced here: 132 us
  matrix products  45.9 us (35%)
  waiting for transfers between devices  40.2 us (30%)
  local copies, waits for them, and re-layouts  20.9 us (16%)
  starting transfers between devices  18.8 us (14%)
  other arithmetic  5.18 us (4%)
    ppermute x16, waiting for transfers between devices, from_mask(): return lax.ppermute(value, 'req', pairs)  40.2 us
    dot_general x4, matrix products, shards(): out = jnp.dot(active, w_down[entry], preferred_element_type=jnp.float32)  29.5 us
    ppermute x16, starting transfers between devices, from_mask(): return lax.ppermute(value, 'req', pairs)  18.8 us
    unnamed x26, local copies, waits for them, and re-layouts  10.8 us
    dot_general x4, matrix products, shards(): jnp.dot(rows_in, w_gate[entry], preferred_element_type=jnp.float32)  10.2 us
    slice x8, local copies, waits for them, and re-layouts, scatter_sum(): parts[r].astype(jnp.bfloat16)  3.95 us
    dot_general x1, matrix products, attention_rows(): jnp.einsum('rqp,rpd->rqd', prob_cached, cache_rows[:, :, HD:], preferred_...  2.87 us
    another operation x2, other arithmetic  2.66 us
  transfers between devices with their start and end apart: 16, of which 15 were waited for; matrix products, arithmetic and copies ran while one was open for 3% of the time, Pallas kernels for 0%

profile of v1, /device:TPU:0, one launch (start us, length us, event | category | flops | bytes accessed | tf_op | source)
XLA Modules:
  0.0 132.1 jit_solution(7700039222546100357)
XLA Ops:
  0.7 0.9 constant_dynamic-slice_fusion.2
  1.7 6.4 %copy.48 = bf16[2,64,128,128]{2,3,1,0:T(8,128)(2,1)} copy(bf16[2,64,128,128]{3,2,1,0:T(8,128)(2,1)} %param.14) | data formatting | bytes 8388608 | tf_op args[2]
  8.1 0.2 reshape_reshape.8
  8.3 2.3 %fusion.183 = (f32[128,8]{1,0:T(8,128)S(1)}, f32[128,8,128]{2,1,0:T(8,128)S(1)}) fusion(bf16[128,8,64]{2,1,0:T(8,128)(2,1)S(1)} %reshape_reshape.8, bf16[128,128,128]{1,2,0:T(8,128)(2,1)} %bitcast.148, pred[128,128]{1,0:T(8,128)(4,1)S(1)} %iota_compare_fusion), kind=kOutput, calls=%fused_computation.199 | convolution fusion | flops 17169408 | bytes 2772992 | tf_op jit(solution)/shard_map/rqd,rpd->rqp/dot_general | solution.py:60
  10.8 0.3 fusion.162
  11.3 0.4 fusion.107
  12.0 2.9 %fusion.48 = bf16[128,8,64]{2,1,0:T(8,128)(2,1)S(1)} fusion(bf16[128,128,128]{1,2,0:T(8,128)(2,1)} %bitcast.149, f32[128,8,128]{2,1,0:T(8,128)S(1)} %get-tuple-element.41, f32[128,64]{1,0:T(8,128)S(1)} %get-tuple-element.35, f32[128,8]{1,0:T(8,128)S(1)} %copy.53, f32[128,8]{1,0:T(8,128)S(1)} %copy.52, f32[128,8]{1,0:T(8,128)S(1)} %copy.50), kind=kOutput, calls=%fused_computation.52 | convolution fusion | flops 17367040 | bytes 2797568 | tf_op jit(solution)/shard_map/rqp,rpd->rqd/dot_general | solution.py:77
  14.8 0.2 reshape_reshape_reshape.3
  15.1 0.3 constant_dynamic-slice_fusion.1
  15.4 0.5 collective-permute-start
  16.2 0.6 collective-permute-done
  16.8 0.6 gather_fusion
  17.5 0.6 gather_fusion.1
  18.2 0.6 fusion.184
  18.8 1.6 %copy-done.2 = f32[256,2880]{0,1:T(8,128)} copy-done((f32[256,2880]{0,1:T(8,128)}, f32[256,2880]{0,1:T(8,128)S(1)}, u32[]{:S(2)}) %copy-start.2) | copy-done | bytes 2949144
  20.5 1.2 copy.57
  21.6 0.4 collective-permute-start.1
  22.1 0.5 copy.56
  22.6 1.6 %collective-permute-done.1 = bf16[8,16,2880]{2,1,0:T(8,128)(2,1)} collective-permute-done((bf16[8,16,2880]{2,1,0:T(8,128)(2,1)}, bf16[8,16,2880]{2,1,0:T(8,128)(2,1)}, u32[]{:S(2)}, u32[]{:S(2)}) %collective-permute-start.1) | collective-permute-done | bytes 737312 | tf_op jit(solution)/shard_map/ppermute | solution.py:32
  24.2 1.3 fusion.180
  25.6 2.9 %collective-permute-start.2 = (bf16[2,16,2880]{2,1,0:T(8,128)(2,1)S(1)}, bf16[2,16,2880]{2,1,0:T(8,128)(2,1)S(1)}, u32[]{:S(2)}, u32[]{:S(2)}) collective-permute-start(bf16[2,16,2880]{2,1,0:T(8,128)(2,1)S(1)} %get-tuple-element.19), channel_id=1, source_target_pairs={{0,2},{1,3},{2,0},{3,1},{4,6},{5,7},{6,4},{7,5},{8,10},{9,11},{10,... | collective-permute-start | bytes 552968 | tf_op jit(solution)/shard_map/ppermute | solution.py:32
  28.5 1.6 %collective-permute-start.3 = (bf16[2,16,2880]{2,1,0:T(8,128)(2,1)S(1)}, bf16[2,16,2880]{2,1,0:T(8,128)(2,1)S(1)}, u32[]{:S(2)}, u32[]{:S(2)}) collective-permute-start(bf16[2,16,2880]{2,1,0:T(8,128)(2,1)S(1)} %get-tuple-element.21), channel_id=1, source_target_pairs={{0,4},{1,5},{2,6},{3,7},{4,0},{5,1},{6,2},{7,3},{8,12},{9,13},{10,... | collective-permute-start | bytes 552968 | tf_op jit(solution)/shard_map/ppermute | solution.py:32
  30.1 3.5 %collective-permute-done.2 = bf16[2,16,2880]{2,1,0:T(8,128)(2,1)S(1)} collective-permute-done((bf16[2,16,2880]{2,1,0:T(8,128)(2,1)S(1)}, bf16[2,16,2880]{2,1,0:T(8,128)(2,1)S(1)}, u32[]{:S(2)}, u32[]{:S(2)}) %collective-permute-start.2) | collective-permute-done | bytes 184352 | tf_op jit(solution)/shard_map/ppermute | solution.py:32
  33.5 2.6 %collective-permute-done.3 = bf16[2,16,2880]{2,1,0:T(8,128)(2,1)S(1)} collective-permute-done((bf16[2,16,2880]{2,1,0:T(8,128)(2,1)S(1)}, bf16[2,16,2880]{2,1,0:T(8,128)(2,1)S(1)}, u32[]{:S(2)}, u32[]{:S(2)}) %collective-permute-start.3) | collective-permute-done | bytes 184352 | tf_op jit(solution)/shard_map/ppermute | solution.py:32
  36.1 2.7 %collective-permute-done.4 = bf16[2,16,2880]{2,1,0:T(8,128)(2,1)S(1)} collective-permute-done((bf16[2,16,2880]{2,1,0:T(8,128)(2,1)S(1)}, bf16[2,16,2880]{2,1,0:T(8,128)(2,1)S(1)}, u32[]{:S(2)}, u32[]{:S(2)}) %collective-permute-start.4) | collective-permute-done | bytes 184352 | tf_op jit(solution)/shard_map/ppermute | solution.py:32
  38.9 2.8 %collective-permute-start.5 = (bf16[1,16,2880]{2,1,0:T(8,128)(2,1)S(1)}, bf16[1,16,2880]{2,1,0:T(8,128)(2,1)S(1)}, u32[]{:S(2)}, u32[]{:S(2)}) collective-permute-start(bf16[1,16,2880]{2,1,0:T(8,128)(2,1)S(1)} %slice.352), channel_id=1, source_target_pairs={{0,8},{1,9},{2,10},{3,11},{4,12},{5,13},{6,14},{7,15},{8,0},{9,1},... | collective-permute-start | bytes 276488 | tf_op jit(solution)/shard_map/ppermute | solution.py:32
  41.8 4.0 %collective-permute-done.5 = bf16[1,16,2880]{2,1,0:T(8,128)(2,1)S(1)} collective-permute-done((bf16[1,16,2880]{2,1,0:T(8,128)(2,1)S(1)}, bf16[1,16,2880]{2,1,0:T(8,128)(2,1)S(1)}, u32[]{:S(2)}, u32[]{:S(2)}) %collective-permute-start.5) | collective-permute-done | bytes 92192 | tf_op jit(solution)/shard_map/ppermute | solution.py:32
  46.3 0.2 select_reduce_fusion.1
  46.7 1.5 %collective-permute-start.6 = (bf16[1,16,2912]{2,1,0:T(8,128)(2,1)S(1)}, bf16[1,16,2912]{2,1,0:T(8,128)(2,1)S(1)}, u32[]{:S(2)}, u32[]{:S(2)}) collective-permute-start(bf16[1,16,2912]{2,1,0:T(8,128)(2,1)S(1)} %bitcast.152), channel_id=1, source_target_pairs={{0,8},{1,9},{2,10},{3,11},{4,12},{5,13},{6,14},{7,15},{8,0},{9,1},... | collective-permute-start | bytes 279560 | tf_op jit(solution)/shard_map/ppermute | solution.py:32
  48.2 0.7 constant_dynamic-update-slice_fusion.4
  48.8 4.4 %collective-permute-done.6 = bf16[1,16,2912]{2,1,0:T(8,128)(2,1)S(1)} collective-permute-done((bf16[1,16,2912]{2,1,0:T(8,128)(2,1)S(1)}, bf16[1,16,2912]{2,1,0:T(8,128)(2,1)S(1)}, u32[]{:S(2)}, u32[]{:S(2)}) %collective-permute-start.6) | collective-permute-done | bytes 93216 | tf_op jit(solution)/shard_map/ppermute | solution.py:32
  53.3 1.4 %collective-permute-start.8 = (bf16[2,16,2912]{2,1,0:T(8,128)(2,1)S(1)}, bf16[2,16,2912]{2,1,0:T(8,128)(2,1)S(1)}, u32[]{:S(2)}, u32[]{:S(2)}) collective-permute-start(bf16[2,16,2912]{2,1,0:T(8,128)(2,1)S(1)} %pad_maximum_fusion), channel_id=1, source_target_pairs={{0,4},{1,5},{2,6},{3,7},{4,0},{5,1},{6,2},{7,3},{8,12},{9,13},{10,... | collective-permute-start | bytes 559112 | tf_op jit(solution)/shard_map/ppermute | solution.py:32
  54.8 2.0 %collective-permute-start.9 = (bf16[2,16,2912]{2,1,0:T(8,128)(2,1)S(1)}, bf16[2,16,2912]{2,1,0:T(8,128)(2,1)S(1)}, u32[]{:S(2)}, u32[]{:S(2)}) collective-permute-start(bf16[2,16,2912]{2,1,0:T(8,128)(2,1)S(1)} %pad_maximum_fusion), channel_id=1, source_target_pairs={{0,6},{1,7},{2,4},{3,5},{4,2},{5,3},{6,0},{7,1},{8,14},{9,15},{10,... | collective-permute-start | bytes 559112 | tf_op jit(solution)/shard_map/ppermute | solution.py:32
  56.8 0.6 constant_dynamic-update-slice_fusion.3
  57.5 2.6 %collective-permute-done.7 = bf16[2,16,2912]{2,1,0:T(8,128)(2,1)S(1)} collective-permute-done((bf16[2,16,2912]{2,1,0:T(8,128)(2,1)S(1)}, bf16[2,16,2912]{2,1,0:T(8,128)(2,1)S(1)}, u32[]{:S(2)}, u32[]{:S(2)}) %collective-permute-start.7) | collective-permute-done | bytes 186400 | tf_op jit(solution)/shard_map/ppermute | solution.py:32
  60.1 0.7 constant_dynamic-update-slice_fusion.2
  60.8 0.7 constant_dynamic-update-slice_fusion.1
  61.5 0.9 collective-permute-done.9
  62.4 0.7 constant_dynamic-update-slice_fusion
  63.1 2.4 %collective-permute-done.10 = bf16[8,16,2912]{2,1,0:T(8,128)(2,1)S(1)} collective-permute-done((bf16[8,16,2912]{2,1,0:T(8,128)(2,1)}, bf16[8,16,2912]{2,1,0:T(8,128)(2,1)S(1)}, u32[]{:S(2)}, u32[]{:S(2)}) %collective-permute-start.10) | collective-permute-done | bytes 745504 | tf_op jit(solution)/shard_map/ppermute | solution.py:32
  65.7 3.1 %fusion.19 = f32[256,360]{0,1:T(8,128)} fusion(bf16[4,2880,360]{1,2,0:T(8,128)(2,1)} %param.19, bf16[256,2912]{1,0:T(8,128)(2,1)S(1)} %bitcast.161), kind=kOutput, calls=%fused_computation.25 | convolution fusion | flops 530841600 | bytes 3979264 | tf_op jit(solution)/shard_map/dot_general | solution.py:152
  68.8 2.4 %fusion.14 = f32[256,360]{0,1:T(8,128)S(1)} fusion(bf16[4,2880,360]{1,2,0:T(8,128)(2,1)} %param.19, bf16[256,2912]{1,0:T(8,128)(2,1)S(1)} %bitcast.162), kind=kOutput, calls=%fused_computation.20 | convolution fusion | flops 530841600 | bytes 3979264 | tf_op jit(solution)/shard_map/dot_general | solution.py:152
  71.2 2.4 %fusion.9 = f32[256,360]{0,1:T(8,128)S(1)} fusion(bf16[4,2880,360]{1,2,0:T(8,128)(2,1)} %param.19, bf16[256,2912]{1,0:T(8,128)(2,1)S(1)} %bitcast.163), kind=kOutput, calls=%fused_computation.15 | convolution fusion | flops 530841600 | bytes 3979264 | tf_op jit(solution)/shard_map/dot_general | solution.py:152
  73.6 2.4 %fusion.4 = f32[256,360]{0,1:T(8,128)S(1)} fusion(bf16[4,2880,360]{1,2,0:T(8,128)(2,1)} %param.19, bf16[256,2912]{1,0:T(8,128)(2,1)S(1)} %bitcast.164), kind=kOutput, calls=%fused_computation.10 | convolution fusion | flops 530841600 | bytes 3979264 | tf_op jit(solution)/shard_map/dot_general | solution.py:152
  76.1 0.4 dynamic-slice_reduce_fusion
  76.5 6.8 %convolution_multiply_fusion.3 = f32[256,2880]{0,1:T(8,128)} fusion(bf16[4,360,2880]{2,1,0:T(8,128)(2,1)} %param.21, f32[256]{0:T(256)S(1)} %get-tuple-element.5, f32[256,360]{0,1:T(8,128)} %fusion.19, bf16[4,2880,360]{1,2,0:T(8,128)(2,1)} %param.20, bf16[256,2912]{1,0:T(8,128)(2,1)S(1)} %bitcast.165), kind=kOutput, calls=%fused_computation.8 | convolution fusion | flops 1063157760 | bytes 9049088 | tf_op jit(solution)/shard_map/dot_general | solution.py:157
  83.2 7.7 %fusion.2 = f32[256,2880]{0,1:T(8,128)} fusion(f32[256,2880]{0,1:T(8,128)} %convolution_multiply_fusion.3, bf16[4,360,2880]{2,1,0:T(8,128)(2,1)} %param.21, f32[256]{0:T(256)S(1)} %get-tuple-element.4, f32[256,360]{0,1:T(8,128)S(1)} %fusion.14, bf16[4,2880,360]{1,2,0:T(8,128)(2,1)} %param.20, bf16[256,2912]{1,0:T(8,128)(2,1)S(1)} %bitcast.166), kind=kOutput, calls=%fused_computation.7 | convolution fusion | flops 1063895040 | bytes 11998208 | tf_op jit(solution)/shard_map/dot_general | solution.py:157
  90.9 7.5 %fusion.1 = f32[256,2880]{0,1:T(8,128)} fusion(f32[256,2880]{0,1:T(8,128)} %fusion.2, bf16[4,360,2880]{2,1,0:T(8,128)(2,1)} %param.21, f32[256]{0:T(256)S(1)} %get-tuple-element.3, f32[256,360]{0,1:T(8,128)S(1)} %fusion.9, bf16[4,2880,360]{1,2,0:T(8,128)(2,1)} %param.20, bf16[256,2912]{1,0:T(8,128)(2,1)S(1)} %bitcast.167), kind=kOutput, calls=%fused_computation.5 | convolution fusion | flops 1063895040 | bytes 11998208 | tf_op jit(solution)/shard_map/dot_general | solution.py:157
  98.5 7.5 %fusion = f32[256,2880]{0,1:T(8,128)} fusion(f32[256,2880]{0,1:T(8,128)} %fusion.1, bf16[4,360,2880]{2,1,0:T(8,128)(2,1)} %param.21, f32[256]{0:T(256)S(1)} %get-tuple-element.2, f32[256,360]{0,1:T(8,128)S(1)} %fusion.4, bf16[4,2880,360]{1,2,0:T(8,128)(2,1)} %param.20, bf16[256,2912]{1,0:T(8,128)(2,1)S(1)} %bitcast.168), kind=kOutput, calls=%fused_computation.3 | convolution fusion | flops 1063895040 | bytes 11998208 | tf_op jit(solution)/shard_map/dot_general | solution.py:157
  106.0 1.4 %slice.349 = bf16[128,2880]{0,1:T(8,128)(2,1)S(1)} slice(f32[256,2880]{0,1:T(8,128)} %fusion), slice={[128:256], [0:2880]} | slice | bytes 1474560 | tf_op jit(solution)/shard_map/slice | solution.py:40
  107.4 1.2 copy.60
  108.7 0.4 slice-done.1
  109.1 0.5 copy.59
  109.5 1.6 %collective-permute-done.11 = bf16[8,16,2880]{2,1,0:T(8,128)(2,1)} collective-permute-done((bf16[8,16,2880]{2,1,0:T(8,128)(2,1)}, bf16[8,16,2880]{2,1,0:T(8,128)(2,1)}, u32[]{:S(2)}, u32[]{:S(2)}) %collective-permute-start.11) | collective-permute-done | bytes 737312 | tf_op jit(solution)/shard_map/ppermute | solution.py:32
  111.2 1.4 %fusion.178 = (bf16[8,16,2880]{2,1,0:T(8,128)(2,1)S(1)}, f32[8,16,2880]{2,1,0:T(8,128)S(1)}) fusion(f32[8,16,2880]{2,1,0:T(8,128)S(1)} %bitcast.151, bf16[8,16,2880]{2,1,0:T(8,128)(2,1)} %collective-permute-done.11), kind=kLoop, calls=%fused_computation.195 | loop fusion | flops 1105920 | bytes 4423680 | tf_op jit(solution)/shard_map/convert.4
  112.6 0.4 collective-permute-start.12
  113.0 1.1 collective-permute-start.13
  114.2 2.0 %collective-permute-start.14 = (bf16[2,16,2880]{2,1,0:T(8,128)(2,1)S(1)}, bf16[2,16,2880]{2,1,0:T(8,128)(2,1)S(1)}, u32[]{:S(2)}, u32[]{:S(2)}) collective-permute-start(bf16[2,16,2880]{2,1,0:T(8,128)(2,1)S(1)} %get-tuple-element.17), channel_id=1, source_target_pairs={{0,6},{1,7},{2,4},{3,5},{4,2},{5,3},{6,0},{7,1},{8,14},{9,15},{10,... | collective-permute-start | bytes 552968 | tf_op jit(solution)/shard_map/ppermute | solution.py:32
  116.2 3.3 %collective-permute-done.12 = bf16[2,16,2880]{2,1,0:T(8,128)(2,1)S(1)} collective-permute-done((bf16[2,16,2880]{2,1,0:T(8,128)(2,1)S(1)}, bf16[2,16,2880]{2,1,0:T(8,128)(2,1)S(1)}, u32[]{:S(2)}, u32[]{:S(2)}) %collective-permute-start.12) | collective-permute-done | bytes 184352 | tf_op jit(solution)/shard_map/ppermute | solution.py:32
  119.4 1.2 collective-permute-done.13
  120.7 4.0 %collective-permute-done.14 = bf16[2,16,2880]{2,1,0:T(8,128)(2,1)S(1)} collective-permute-done((bf16[2,16,2880]{2,1,0:T(8,128)(2,1)S(1)}, bf16[2,16,2880]{2,1,0:T(8,128)(2,1)S(1)}, u32[]{:S(2)}, u32[]{:S(2)}) %collective-permute-start.14) | collective-permute-done | bytes 184352 | tf_op jit(solution)/shard_map/ppermute | solution.py:32
  124.8 1.9 %collective-permute-start.15 = (bf16[1,16,2880]{2,1,0:T(8,128)(2,1)S(1)}, bf16[1,16,2880]{2,1,0:T(8,128)(2,1)S(1)}, u32[]{:S(2)}, u32[]{:S(2)}) collective-permute-start(bf16[1,16,2880]{2,1,0:T(8,128)(2,1)S(1)} %slice.351), channel_id=1, source_target_pairs={{0,8},{1,9},{2,10},{3,11},{4,12},{5,13},{6,14},{7,15},{8,0},{9,1},... | collective-permute-start | bytes 276488 | tf_op jit(solution)/shard_map/ppermute | solution.py:32
  126.7 4.6 %collective-permute-done.15 = bf16[1,16,2880]{2,1,0:T(8,128)(2,1)S(1)} collective-permute-done((bf16[1,16,2880]{2,1,0:T(8,128)(2,1)S(1)}, bf16[1,16,2880]{2,1,0:T(8,128)(2,1)S(1)}, u32[]{:S(2)}, u32[]{:S(2)}) %collective-permute-start.15) | collective-permute-done | bytes 92192 | tf_op jit(solution)/shard_map/ppermute | solution.py:32
  131.4 0.7 fusion.153
  (72 shorter events, 3.0 us)
Async XLA Ops:
  0.6 17.5 %copy-start = (bf16[256,2880]{0,1:T(8,128)(2,1)S(1)}, bf16[256,2880]{0,1:T(8,128)(2,1)}, u32[]{:S(2)}) copy-start(bf16[256,2880]{0,1:T(8,128)(2,1)} %param.17) | copy-start | bytes 4423684
  1.7 6.4 %copy-start.4 = (bf16[2,64,512]{2,1,0:T(8,128)(2,1)S(1)}, bf16[2,64,512]{2,1,0:T(8,128)(2,1)}, u32[]{:S(2)}) copy-start(bf16[2,64,512]{2,1,0:T(8,128)(2,1)} %param.12) | copy-start | bytes 393220
  8.1 2.6 %copy-start.5 = (bf16[2,64,128]{2,1,0:T(8,128)(2,1)S(1)}, bf16[2,64,128]{2,1,0:T(8,128)(2,1)}, u32[]{:S(2)}) copy-start(bf16[2,64,128]{2,1,0:T(8,128)(2,1)} %param.13) | copy-start | bytes 98308
  11.9 4.0 %copy-start.8 = (s32[16]{0:T(128)S(1)}, s32[16]{0:T(128)}, u32[]{:S(2)}) copy-start(s32[16]{0:T(128)} %constant.114.clone) | copy-start | bytes 196
  15.4 1.4 %collective-permute-start = (bf16[2,64,256]{2,1,0:T(8,128)(2,1)S(1)}, bf16[2,64,256]{2,1,0:T(8,128)(2,1)S(1)}, u32[]{:S(2)}, u32[]{:S(2)}) collective-permute-start(bf16[2,64,256]{2,1,0:T(8,128)(2,1)S(1)} %bitcast.158), channel_id=1, source_target_pairs={{0,1},{1,0},{2,3},{3,2},{4,5},{5,4},{6,7},{7,6},{8,9},{9,8},{10,11... | collective-permute-start | bytes 196616 | tf_op jit(solution)/shard_map/ppermute | solution.py:32
  18.8 1.6 %copy-start.2 = (f32[256,2880]{0,1:T(8,128)}, f32[256,2880]{0,1:T(8,128)S(1)}, u32[]{:S(2)}) copy-start(f32[256,2880]{0,1:T(8,128)S(1)} %fusion.184) | copy-start | bytes 8847364
  20.5 1.6 %slice-start = ((f32[256,2880]{0,1:T(8,128)}), f32[128,2880]{0,1:T(8,128)S(1)}, s32[]{:S(2)}) async-start(f32[256,2880]{0,1:T(8,128)} %copy-done.2), calls=%async_computation | async-start | bytes 2949120 | tf_op jit(solution)/shard_map/slice | solution.py:38
  21.6 2.6 %collective-permute-start.1 = (bf16[8,16,2880]{2,1,0:T(8,128)(2,1)}, bf16[8,16,2880]{2,1,0:T(8,128)(2,1)}, u32[]{:S(2)}, u32[]{:S(2)}) collective-permute-start(bf16[8,16,2880]{2,1,0:T(8,128)(2,1)} %bitcast.11), channel_id=1, source_target_pairs={{0,1},{1,0},{2,3},{3,2},{4,5},{5,4},{6,7},{7,6},{8,9},{9,8},{10,11... | collective-permute-start | bytes 2211848 | tf_op jit(solution)/shard_map/ppermute | solution.py:32
  25.5 16.3 %copy-start.7 = (s32[2,8,4]{1,2,0:T(4,128)S(1)}, s32[2,8,4]{1,2,0:T(4,128)}, u32[]{:S(2)}) copy-start(s32[2,8,4]{1,2,0:T(4,128)} %param.22) | copy-start | bytes 772
  25.5 20.4 %copy-start.3 = (bf16[2,8,2880]{2,1,0:T(8,128)(2,1)S(1)}, bf16[2,8,2880]{2,1,0:T(8,128)(2,1)}, u32[]{:S(2)}) copy-start(bf16[2,8,2880]{2,1,0:T(8,128)(2,1)} %param.16) | copy-start | bytes 276484
  25.5 20.6 %copy-start.6 = (bf16[2880,16]{0,1:T(8,128)(2,1)S(1)}, bf16[2880,16]{0,1:T(8,128)(2,1)}, u32[]{:S(2)}) copy-start(bf16[2880,16]{0,1:T(8,128)(2,1)} %param.18) | copy-start | bytes 276484
  25.6 8.0 %collective-permute-start.2 = (bf16[2,16,2880]{2,1,0:T(8,128)(2,1)S(1)}, bf16[2,16,2880]{2,1,0:T(8,128)(2,1)S(1)}, u32[]{:S(2)}, u32[]{:S(2)}) collective-permute-start(bf16[2,16,2880]{2,1,0:T(8,128)(2,1)S(1)} %get-tuple-element.19), channel_id=1, source_target_pairs={{0,2},{1,3},{2,0},{3,1},{4,6},{5,7},{6,4},{7,5},{8,10},{9,11},{10,... | collective-permute-start | bytes 552968 | tf_op jit(solution)/shard_map/ppermute | solution.py:32
  28.5 7.6 %collective-permute-start.3 = (bf16[2,16,2880]{2,1,0:T(8,128)(2,1)S(1)}, bf16[2,16,2880]{2,1,0:T(8,128)(2,1)S(1)}, u32[]{:S(2)}, u32[]{:S(2)}) collective-permute-start(bf16[2,16,2880]{2,1,0:T(8,128)(2,1)S(1)} %get-tuple-element.21), channel_id=1, source_target_pairs={{0,4},{1,5},{2,6},{3,7},{4,0},{5,1},{6,2},{7,3},{8,12},{9,13},{10,... | collective-permute-start | bytes 552968 | tf_op jit(solution)/shard_map/ppermute | solution.py:32
  30.1 8.8 %collective-permute-start.4 = (bf16[2,16,2880]{2,1,0:T(8,128)(2,1)S(1)}, bf16[2,16,2880]{2,1,0:T(8,128)(2,1)S(1)}, u32[]{:S(2)}, u32[]{:S(2)}) collective-permute-start(bf16[2,16,2880]{2,1,0:T(8,128)(2,1)S(1)} %get-tuple-element.20), channel_id=1, source_target_pairs={{0,6},{1,7},{2,4},{3,5},{4,2},{5,3},{6,0},{7,1},{8,14},{9,15},{10,... | collective-permute-start | bytes 552968 | tf_op jit(solution)/shard_map/ppermute | solution.py:32
  38.9 6.9 %collective-permute-start.5 = (bf16[1,16,2880]{2,1,0:T(8,128)(2,1)S(1)}, bf16[1,16,2880]{2,1,0:T(8,128)(2,1)S(1)}, u32[]{:S(2)}, u32[]{:S(2)}) collective-permute-start(bf16[1,16,2880]{2,1,0:T(8,128)(2,1)S(1)} %slice.352), channel_id=1, source_target_pairs={{0,8},{1,9},{2,10},{3,11},{4,12},{5,13},{6,14},{7,15},{8,0},{9,1},... | collective-permute-start | bytes 276488 | tf_op jit(solution)/shard_map/ppermute | solution.py:32
  46.7 6.5 %collective-permute-start.6 = (bf16[1,16,2912]{2,1,0:T(8,128)(2,1)S(1)}, bf16[1,16,2912]{2,1,0:T(8,128)(2,1)S(1)}, u32[]{:S(2)}, u32[]{:S(2)}) collective-permute-start(bf16[1,16,2912]{2,1,0:T(8,128)(2,1)S(1)} %bitcast.152), channel_id=1, source_target_pairs={{0,8},{1,9},{2,10},{3,11},{4,12},{5,13},{6,14},{7,15},{8,0},{9,1},... | collective-permute-start | bytes 279560 | tf_op jit(solution)/shard_map/ppermute | solution.py:32
  53.2 6.8 %collective-permute-start.7 = (bf16[2,16,2912]{2,1,0:T(8,128)(2,1)S(1)}, bf16[2,16,2912]{2,1,0:T(8,128)(2,1)S(1)}, u32[]{:S(2)}, u32[]{:S(2)}) collective-permute-start(bf16[2,16,2912]{2,1,0:T(8,128)(2,1)S(1)} %pad_maximum_fusion), channel_id=1, source_target_pairs={{0,2},{1,3},{2,0},{3,1},{4,6},{5,7},{6,4},{7,5},{8,10},{9,11},{10,... | collective-permute-start | bytes 559112 | tf_op jit(solution)/shard_map/ppermute | solution.py:32
  53.3 7.5 %collective-permute-start.8 = (bf16[2,16,2912]{2,1,0:T(8,128)(2,1)S(1)}, bf16[2,16,2912]{2,1,0:T(8,128)(2,1)S(1)}, u32[]{:S(2)}, u32[]{:S(2)}) collective-permute-start(bf16[2,16,2912]{2,1,0:T(8,128)(2,1)S(1)} %pad_maximum_fusion), channel_id=1, source_target_pairs={{0,4},{1,5},{2,6},{3,7},{4,0},{5,1},{6,2},{7,3},{8,12},{9,13},{10,... | collective-permute-start | bytes 559112 | tf_op jit(solution)/shard_map/ppermute | solution.py:32
  54.8 7.6 %collective-permute-start.9 = (bf16[2,16,2912]{2,1,0:T(8,128)(2,1)S(1)}, bf16[2,16,2912]{2,1,0:T(8,128)(2,1)S(1)}, u32[]{:S(2)}, u32[]{:S(2)}) collective-permute-start(bf16[2,16,2912]{2,1,0:T(8,128)(2,1)S(1)} %pad_maximum_fusion), channel_id=1, source_target_pairs={{0,6},{1,7},{2,4},{3,5},{4,2},{5,3},{6,0},{7,1},{8,14},{9,15},{10,... | collective-permute-start | bytes 559112 | tf_op jit(solution)/shard_map/ppermute | solution.py:32
  63.1 2.4 %collective-permute-start.10 = (bf16[8,16,2912]{2,1,0:T(8,128)(2,1)}, bf16[8,16,2912]{2,1,0:T(8,128)(2,1)S(1)}, u32[]{:S(2)}, u32[]{:S(2)}) collective-permute-start(bf16[8,16,2912]{2,1,0:T(8,128)(2,1)} %get-tuple-element.22), channel_id=1, source_target_pairs={{0,1},{1,0},{2,3},{3,2},{4,5},{5,4},{6,7},{7,6},{8,9},{9,8},{10,11... | collective-permute-start | bytes 2236424 | tf_op jit(solution)/shard_map/ppermute | solution.py:32
  107.4 1.6 %slice-start.1 = ((f32[256,2880]{0,1:T(8,128)}), f32[128,2880]{0,1:T(8,128)S(1)}, s32[]{:S(2)}) async-start(f32[256,2880]{0,1:T(8,128)} %fusion), calls=%async_computation.1 | async-start | bytes 2949120 | tf_op jit(solution)/shard_map/slice | solution.py:38
  108.6 2.6 %collective-permute-start.11 = (bf16[8,16,2880]{2,1,0:T(8,128)(2,1)}, bf16[8,16,2880]{2,1,0:T(8,128)(2,1)}, u32[]{:S(2)}, u32[]{:S(2)}) collective-permute-start(bf16[8,16,2880]{2,1,0:T(8,128)(2,1)} %bitcast.30), channel_id=1, source_target_pairs={{0,1},{1,0},{2,3},{3,2},{4,5},{5,4},{6,7},{7,6},{8,9},{9,8},{10,11... | collective-permute-start | bytes 2211848 | tf_op jit(solution)/shard_map/ppermute | solution.py:32
  111.2 20.9 %copy-start.1 = (bf16[256,2880]{0,1:T(8,128)(2,1)S(1)}, bf16[256,2880]{0,1:T(8,128)(2,1)}, u32[]{:S(2)}) copy-start(bf16[256,2880]{0,1:T(8,128)(2,1)} %param.17) | copy-start | bytes 4423684
  112.6 6.8 %collective-permute-start.12 = (bf16[2,16,2880]{2,1,0:T(8,128)(2,1)S(1)}, bf16[2,16,2880]{2,1,0:T(8,128)(2,1)S(1)}, u32[]{:S(2)}, u32[]{:S(2)}) collective-permute-start(bf16[2,16,2880]{2,1,0:T(8,128)(2,1)S(1)} %get-tuple-element.16), channel_id=1, source_target_pairs={{0,2},{1,3},{2,0},{3,1},{4,6},{5,7},{6,4},{7,5},{8,10},{9,11},{10,... | collective-permute-start | bytes 552968 | tf_op jit(solution)/shard_map/ppermute | solution.py:32
  113.0 7.6 %collective-permute-start.13 = (bf16[2,16,2880]{2,1,0:T(8,128)(2,1)S(1)}, bf16[2,16,2880]{2,1,0:T(8,128)(2,1)S(1)}, u32[]{:S(2)}, u32[]{:S(2)}) collective-permute-start(bf16[2,16,2880]{2,1,0:T(8,128)(2,1)S(1)} %get-tuple-element.18), channel_id=1, source_target_pairs={{0,4},{1,5},{2,6},{3,7},{4,0},{5,1},{6,2},{7,3},{8,12},{9,13},{10,... | collective-permute-start | bytes 552968 | tf_op jit(solution)/shard_map/ppermute | solution.py:32
  114.2 10.5 %collective-permute-start.14 = (bf16[2,16,2880]{2,1,0:T(8,128)(2,1)S(1)}, bf16[2,16,2880]{2,1,0:T(8,128)(2,1)S(1)}, u32[]{:S(2)}, u32[]{:S(2)}) collective-permute-start(bf16[2,16,2880]{2,1,0:T(8,128)(2,1)S(1)} %get-tuple-element.17), channel_id=1, source_target_pairs={{0,6},{1,7},{2,4},{3,5},{4,2},{5,3},{6,0},{7,1},{8,14},{9,15},{10,... | collective-permute-start | bytes 552968 | tf_op jit(solution)/shard_map/ppermute | solution.py:32
  124.8 6.6 %collective-permute-start.15 = (bf16[1,16,2880]{2,1,0:T(8,128)(2,1)S(1)}, bf16[1,16,2880]{2,1,0:T(8,128)(2,1)S(1)}, u32[]{:S(2)}, u32[]{:S(2)}) collective-permute-start(bf16[1,16,2880]{2,1,0:T(8,128)(2,1)S(1)} %slice.351), channel_id=1, source_target_pairs={{0,8},{1,9},{2,10},{3,11},{4,12},{5,13},{6,14},{7,15},{8,0},{9,1},... | collective-permute-start | bytes 276488 | tf_op jit(solution)/shard_map/ppermute | solution.py:32

commit v2 on v1

v2 whole, which is shorter than its diff:
```python
import functools
import math

import jax
import jax.numpy as jnp
from jax import lax
from jax.experimental import pallas as pl
from jax.experimental.pallas import tpu as pltpu
from jax.sharding import PartitionSpec as P

HD = 64
KVH = 8
QPK = 8
EXPERTS = 16
SPLIT = 4
REQ_DEV = 8
CHUNK = 128
ROWS_LAST = (((1,), (1,)), ((), ()))


def plan(device_count):
    bits = device_count.bit_length() - 1
    stages = [(0, 1)] if bits else []
    bit = 1
    while bit < bits:
        width = min(2, bits - bit)
        stages.append((bit, width))
        bit += width
    masks = [0]
    for bit, width in stages:
        masks = [mask | (r << bit) for mask in masks for r in range(1 << width)]
    return stages, masks


def from_mask(value, mask):
    pairs = [(source, source ^ mask) for source in range(lax.axis_size("req"))]
    return lax.ppermute(value, "req", pairs)


def scatter_sum(keep, send, stages):
    block_rows, width = keep.shape[0], keep.shape[1]
    total = keep.astype(jnp.float32) + from_mask(send, 1).astype(jnp.float32)
    for bit, bits in stages[1:]:
        size = total.shape[0] >> bits
        pieces = [total[r * size : (r + 1) * size] for r in range(1 << bits)]
        total = pieces[0]
        for r in range(1, 1 << bits):
            moved = from_mask(pieces[r].astype(jnp.bfloat16), r << bit)
            total = total + moved.astype(jnp.float32)
    return total


def gather_rows(rows, stages):
    pieces = [rows]
    for bit, bits in reversed(stages):
        if bit:
            held = jnp.concatenate(pieces, axis=0) if len(pieces) > 1 else pieces[0]
            pieces = [held] + [from_mask(held, r << bit) for r in range(1, 1 << bits)]
        else:
            pieces = pieces + [from_mask(piece, 1) for piece in pieces]
    return pieces


def attention_kernel(
    group, blocks, lengths, place, q_ref, kv_ref, cache_ref, *refs
):
    outs = refs[:group]
    query, scores, mixed = refs[group:]
    rows, window, pair = cache_ref.shape
    batch, block = pl.program_id(0), pl.program_id(1)
    low = lax.broadcasted_iota(jnp.int32, (rows, pair), 1) < HD
    for h in range(QPK):
        tile = q_ref[:, (h // 2) * pair : (h // 2 + 1) * pair].astype(jnp.float32)
        tile = tile * (1.0 / math.sqrt(HD))
        if h % 2:
            tile = pltpu.roll(tile, HD, 1)
        query[pl.ds(h, rows, stride=QPK), :] = jnp.where(low, tile, 0.0)
    fresh = kv_ref[...].astype(jnp.float32)
    fresh = jnp.broadcast_to(fresh[:, None, :], (rows, QPK, pair)).reshape(rows * QPK, pair)
    own = jnp.sum(query[...] * fresh, axis=1, keepdims=True)
    position = lax.broadcasted_iota(jnp.int32, (QPK, window), 1)
    first = place[0] * (rows * blocks) + block * rows
    for r in range(rows):
        part = slice(r * QPK, (r + 1) * QPK)
        found = lax.dot_general(
            query[part, :].astype(jnp.bfloat16),
            cache_ref[r],
            ROWS_LAST,
            preferred_element_type=jnp.float32,
        )
        scores[part, :] = jnp.where(position < lengths[batch, first + r], found, -jnp.inf)
    top = jnp.maximum(jnp.max(scores[...], axis=1, keepdims=True), own)
    weight = jnp.exp(scores[...] - top)
    weight_own = jnp.exp(own - top)
    total = jnp.sum(weight, axis=1, keepdims=True) + weight_own
    scores[...] = weight / total
    prob_own = (weight_own / total).astype(jnp.bfloat16).astype(jnp.float32)
    for r in range(rows):
        part = slice(r * QPK, (r + 1) * QPK)
        mixed[part, :] = jnp.dot(
            scores[part, :].astype(jnp.bfloat16), cache_ref[r], preferred_element_type=jnp.float32
        )
    mixed[...] = mixed[...] + prob_own * fresh
    heads = QPK // group
    for r in range(group):
        start = (place[0] ^ r) * heads
        for j in range(0, heads, 2):
            left = pltpu.roll(mixed[pl.ds(start + j, rows, stride=QPK), :], HD, 1)
            if heads == 1:
                outs[r][...] = left[:, :HD].astype(jnp.bfloat16)
            else:
                right = mixed[pl.ds(start + j + 1, rows, stride=QPK), :]
                outs[r][:, j * HD : (j + 2) * HD] = jnp.where(low, left, right).astype(
                    jnp.bfloat16
                )


def attention(lengths, place, queries, new_kv, cache, group, block=32):
    batch, rows, window, pair = cache.shape
    block = min(block, rows)
    width = QPK // group * HD
    return pl.pallas_call(
        functools.partial(attention_kernel, group, rows // block),
        out_shape=[jax.ShapeDtypeStruct((batch, rows, width), jnp.bfloat16)] * group,
        grid_spec=pltpu.PrefetchScalarGridSpec(
            num_scalar_prefetch=2,
            grid=(batch, rows // block),
            in_specs=[
                pl.BlockSpec((None, block, QPK * HD), lambda m, i, *_: (m, i, 0)),
                pl.BlockSpec((None, block, pair), lambda m, i, *_: (m, i, 0)),
                pl.BlockSpec((None, block, window, pair), lambda m, i, *_: (m, i, 0, 0)),
            ],
            out_specs=[pl.BlockSpec((None, block, width), lambda m, i, *_: (m, i, 0))] * group,
            scratch_shapes=[
                pltpu.VMEM((block * QPK, pair), jnp.float32),
                pltpu.VMEM((block * QPK, window), jnp.float32),
                pltpu.VMEM((block * QPK, pair), jnp.float32),
            ],
        ),
        compiler_params=pltpu.CompilerParams(vmem_limit_bytes=60 << 20),
        name="attention",
    )(lengths, place, queries, new_kv, cache)


def project_kernel(group, masks, me_ref, *refs):
    held = refs[:group]
    weight, keep, send, wide, rows = refs[group:]
    batch, members, width = held[0].shape
    for r in range(group):
        wide[r] = held[r][...].astype(jnp.float32)
    me = me_ref[0]
    per_member = members // REQ_DEV
    for p, mask in enumerate(masks):
        block = me ^ mask
        member = (block // per_member) ^ (me % group)
        start = pl.multiple_of((block % per_member) * REQ_DEV, REQ_DEV)
        for m in range(batch):
            at = (p * batch + m) * REQ_DEV
            rows[at : at + REQ_DEV, :] = wide[member, m, pl.ds(start, REQ_DEV), :]
    half = keep.shape[0]
    send[...] = lax.dot_general(
        rows[half:, :].astype(jnp.bfloat16),
        weight[...],
        ROWS_LAST,
        preferred_element_type=jnp.float32,
    ).astype(jnp.bfloat16)
    keep[...] = lax.dot_general(
        rows[:half, :].astype(jnp.bfloat16),
        weight[...],
        ROWS_LAST,
        preferred_element_type=jnp.float32,
    )


def project(me, held, weight, masks):
    batch, members, width = held[0].shape
    group = len(held)
    count = len(masks) * batch * REQ_DEV
    whole = pl.BlockSpec(memory_space=pltpu.VMEM)
    return pl.pallas_call(
        functools.partial(project_kernel, group, masks),
        out_shape=[
            jax.ShapeDtypeStruct((count // 2, weight.shape[0]), jnp.float32),
            jax.ShapeDtypeStruct((count // 2, weight.shape[0]), jnp.bfloat16),
        ],
        in_specs=[pl.BlockSpec(memory_space=pltpu.SMEM)] + [whole] * (group + 1),
        out_specs=[whole] * 2,
        scratch_shapes=[
            pltpu.VMEM((group,) + held[0].shape, jnp.float32),
            pltpu.VMEM((count, width), jnp.float32),
        ],
        compiler_params=pltpu.CompilerParams(vmem_limit_bytes=32 << 20),
        name="project",
    )(me, *held, weight)


def expert_kernel(count, ahead, me_ref, *refs):
    pieces = refs[:count]
    sources = refs[count : count + 3]
    keep, send = refs[count + 3 : count + 5]
    rows, gates, ups, downs, active, total, done = refs[count + 5 :]
    entries, hidden, width = sources[0].shape
    order = [(k, e) for e in range(entries) for k in (0, 1)] + [(2, e) for e in range(entries)]
    stores = (gates, ups, downs)
    parts = pl.cdiv(hidden, CHUNK)
    copies = []
    for k, e in order:
        for s in range(parts):
            some = pl.ds(s * CHUNK, min(CHUNK, hidden - s * CHUNK))
            copies.append(
                pltpu.make_async_copy(
                    sources[k].at[e, some], stores[k].at[e, some], done.at[k, e, s]
                )
            )
    state = [0, 0]

    def issue():
        if state[0] < len(copies):
            copies[state[0]].start()
            state[0] += 1

    def finish():
        for _ in range(parts):
            copies[state[1]].wait()
            state[1] += 1
            issue()

    for _ in range(ahead):
        issue()
    at = 0
    for piece in pieces:
        rows[at : at + piece.shape[0], :] = piece[...]
        at += piece.shape[0]
    base = width // 128 * 128
    tail = rows[:, base:].astype(jnp.float32)
    lane = lax.broadcasted_iota(jnp.int32, tail.shape, 1) - (width - base)
    for e in range(entries):
        finish()
        gate = lax.dot_general(
            rows[:, :width], gates[e], ROWS_LAST, preferred_element_type=jnp.float32
        )
        finish()
        up = lax.dot_general(
            rows[:, :width], ups[e], ROWS_LAST, preferred_element_type=jnp.float32
        )
        active[e] = ((up + 1.0) * gate * jax.nn.sigmoid(1.702 * gate)).astype(jnp.bfloat16)
    half = keep.shape[0]
    local = max(1, entries // SPLIT)
    for e in range(entries):
        finish()
        out = jnp.dot(active[e], downs[e], preferred_element_type=jnp.float32)
        if e % SPLIT:
            out = out + total[...]
        if e + 1 < entries and (e + 1) % SPLIT:
            total[...] = out
            continue
        expert = me_ref[0] * entries // SPLIT + e // SPLIT
        picked = (lane == expert) | (lane == expert + EXPERTS)
        out = out * jnp.sum(jnp.where(picked, tail, 0.0), axis=1, keepdims=True)
        if e // SPLIT:
            keep[...] += out[:half]
            send[...] = (send[...].astype(jnp.float32) + out[half:]).astype(jnp.bfloat16)
        else:
            keep[...] = out[:half]
            send[...] = out[half:].astype(jnp.bfloat16)


def expert_sums(me, pieces, w_gate, w_up, w_down, ahead=9):
    entries, hidden, width = w_gate.shape
    count = sum(piece.shape[0] for piece in pieces)
    whole = pl.BlockSpec(memory_space=pltpu.VMEM)
    outside = pl.BlockSpec(memory_space=pl.ANY)
    parts = pl.cdiv(hidden, CHUNK)
    return pl.pallas_call(
        functools.partial(expert_kernel, len(pieces), ahead),
        out_shape=[
            jax.ShapeDtypeStruct((count // 2, width), jnp.float32),
            jax.ShapeDtypeStruct((count // 2, width), jnp.bfloat16),
        ],
        in_specs=[pl.BlockSpec(memory_space=pltpu.SMEM)]
        + [whole] * len(pieces)
        + [outside] * 3,
        out_specs=[whole] * 2,
        scratch_shapes=[
            pltpu.VMEM((count, pieces[0].shape[1]), jnp.bfloat16),
            pltpu.VMEM(w_gate.shape, jnp.bfloat16),
            pltpu.VMEM(w_up.shape, jnp.bfloat16),
            pltpu.VMEM(w_down.shape, jnp.bfloat16),
            pltpu.VMEM((entries, count, hidden), jnp.bfloat16),
            pltpu.VMEM((count, width), jnp.float32),
            pltpu.SemaphoreType.DMA((3, entries, parts)),
        ],
        compiler_params=pltpu.CompilerParams(vmem_limit_bytes=56 << 20),
        name="experts",
    )(me, *pieces, w_gate, w_up, w_down)


def shards(queries, new_kv, cache, lengths, residual, o_proj, router, w_gate, w_up, w_down, routes):
    device_count = lax.axis_size("req")
    device_index = lax.axis_index("req")
    stages, masks = plan(device_count)
    group_size = max(1, device_count // KVH)
    width = residual.shape[2]
    block_rows = residual.shape[0] * residual.shape[1]
    me = device_index.astype(jnp.int32)[None]

    held = attention(lengths, me % group_size, queries, new_kv, cache, group_size)
    held = [held[0]] + [from_mask(held[r], r) for r in range(1, group_size)]
    summed = scatter_sum(*project(me, held, o_proj.T, masks), stages)

    attended = (residual.reshape(block_rows, width).astype(jnp.float32) + summed).astype(
        jnp.bfloat16
    )
    attended_wide = attended.astype(jnp.float32)
    normed = (
        attended_wide
        * lax.rsqrt(jnp.mean(attended_wide * attended_wide, axis=1, keepdims=True) + 1e-05)
    ).astype(jnp.bfloat16)
    logits = jnp.dot(normed, router, preferred_element_type=jnp.float32)
    chosen_one = routes.reshape(block_rows, -1)[:, :, None] == jnp.arange(EXPERTS)[None, None, :]
    chosen = jnp.sum(jnp.where(chosen_one, logits[:, None, :], 0.0), axis=2)
    gates = 1.0 / jnp.sum(jnp.exp(chosen[:, None, :] - chosen[:, :, None]), axis=2)
    dense = jnp.sum(jnp.where(chosen_one, gates[:, :, None], 0.0), axis=1)
    high = lax.reduce_precision(dense, 8, 7)
    payload = jnp.concatenate(
        [normed, high.astype(jnp.bfloat16), (dense - high).astype(jnp.bfloat16)], axis=1
    )

    pieces = gather_rows(payload, stages)
    mixture = scatter_sum(
        *expert_sums(me, pieces, w_gate.swapaxes(1, 2), w_up.swapaxes(1, 2), w_down), stages
    )
    layer = (attended_wide + mixture).astype(jnp.bfloat16)
    return attended.reshape(residual.shape), layer.reshape(residual.shape)


def solution(mesh):
    placed = (
        P(None, ("groups", "req"), None),
        P(None, ("groups", "req"), None),
        P(None, ("groups", "req"), None, None),
        P(None, "groups"),
        P(None, ("groups", "req"), None),
        P("req", None),
        P(),
        P("req", None, None),
        P("req", None, None),
        P("req", None, None),
        P(None, ("groups", "req"), None),
    )
    return jax.shard_map(
        shards,
        mesh=mesh,
        in_specs=placed,
        out_specs=(P(None, ("groups", "req"), None), P(None, ("groups", "req"), None)),
        check_vma=False,
    )
```

time: 133 us -> 96.6 us (0.73)
  matrix products: 45.9 us -> 0.14 us
  Pallas kernels: 0 us -> 24.9 us
  local copies, waits for them, and re-layouts: 20.9 us -> 6.54 us
  other arithmetic: 5.18 us -> 1.74 us
  waiting for transfers between devices: 40.2 us -> 43 us
    dot_general x12 -> x0, matrix products: 45.8 us -> none  [the longest x4 29.5 us: shards(): out = jnp.dot(active, w_down[entry], preferred_element_type=jnp.float32)]
    pallas_call x0 -> x3, Pallas kernels: none -> 24.9 us  [the longest x1 16.6 us: expert_sums(): pl.pallas_call(functools.partial(expert_kernel, len(pieces), ahead), out_...]
    unnamed x26 -> x33, local copies, waits for them, and re-layouts: 10.8 us -> 2.43 us
    slice x14 -> x4, local copies, waits for them, and re-layouts: 5.37 us -> 0.11 us  [scatter_sum(): pieces = [total[r * size:(r + 1) * size] for r in range(1 << bits)]]
    pallas_call x0 -> x2, local copies, waits for them, and re-layouts: none -> 3.09 us  [the longest x1 1.6 us: expert_sums(): pl.pallas_call(functools.partial(expert_kernel, len(pieces), ahead), out_...]
    ppermute x16 -> x19, waiting for transfers between devices: 40.2 us -> 43 us  [from_mask(): return lax.ppermute(value, 'req', pairs)]
    another operation x3 -> x2, other arithmetic: 2.67 us -> 0.31 us
    dynamic_slice x3 -> x0, local copies, waits for them, and re-layouts: 1.53 us -> none  [the longest x1 0.86 us: shards(): lax.dynamic_slice_in_dim(lengths, block_index * local_rows, local_rows, 1)]
  transfers between devices with their start and end apart: 16 -> 19, of which waited for: 15 -> 15; matrix products, arithmetic and copies ran while one was open for 3% -> 0% of each run, Pallas kernels for 0% -> 0%
where the time goes in v2:
time: 96.6 us; the launch traced here: 96.2 us
  waiting for transfers between devices  43 us (45%)
  Pallas kernels  24.9 us (26%)
  starting transfers between devices  19 us (20%)
  local copies, waits for them, and re-layouts  6.54 us (7%)
  other arithmetic  1.74 us (2%)
    ppermute x19, waiting for transfers between devices, from_mask(): return lax.ppermute(value, 'req', pairs)  43 us
    ppermute x19, starting transfers between devices, from_mask(): return lax.ppermute(value, 'req', pairs)  19 us
    pallas_call x1, Pallas kernels, expert_sums(): pl.pallas_call(functools.partial(expert_kernel, len(pieces), ahead), out_...  16.6 us
    pallas_call x1, Pallas kernels, attention(): pl.pallas_call(functools.partial(attention_kernel, group, rows // block),...  7.29 us
    unnamed x33, local copies, waits for them, and re-layouts  2.43 us
  transfers between devices with their start and end apart: 19, of which 15 were waited for; matrix products, arithmetic and copies ran while one was open for 0% of the time, Pallas kernels for 0%

profile of v2, /device:TPU:0, one launch (start us, length us, event | category | flops | bytes accessed | tf_op | source)
XLA Modules:
  0.0 96.2 jit_solution(11366594968879510688)
XLA Ops:
  0.6 0.0 copy-start
  0.7 7.3 %attention.1 = (bf16[2,64,256]{2,1,0:T(8,128)(2,1)}, bf16[2,64,256]{2,1,0:T(8,128)(2,1)}) custom-call(s32[2,128]{1,0:T(2,128)} %lengths.1, s32[1]{0:T(128)S(6)} %select_n.15.place, bf16[2,64,512]{2,1,0:T(8,128)(2,1)} %q_ref.1, bf16[2,64,128]{2,1,0:T(8,128)(2,1)} %kv_ref.1, bf16[2,64,128,128]{3,2,1,0:T(8,128)(2,1)} %cache_ref.1), custom_call_target="tpu_custom_call" | custom-call | tf_op jit(solution)/shard_map/attention/pallas_call | solution.py:122
  8.0 0.5 collective-permute-start
  8.4 1.1 %collective-permute-done.refs_1_ = bf16[2,64,256]{2,1,0:T(8,128)(2,1)S(1)} collective-permute-done((bf16[2,64,256]{2,1,0:T(8,128)(2,1)}, bf16[2,64,256]{2,1,0:T(8,128)(2,1)S(1)}, u32[]{:S(2)}, u32[]{:S(2)}) %collective-permute-start) | collective-permute-done | bytes 65568 | tf_op jit(solution)/shard_map/ppermute | solution.py:37
  9.5 0.8 copy-done.3
  10.4 1.0 %project.1 = (f32[128,2880]{1,0:T(8,128)S(1)}, bf16[128,2880]{1,0:T(8,128)(2,1)S(1)}) custom-call(s32[1]{0:T(128)} %bitcast.1.me_ref, bf16[2,64,256]{2,1,0:T(8,128)(2,1)S(1)} %copy-done.3, bf16[2,64,256]{2,1,0:T(8,128)(2,1)S(1)} %collective-permute-done.refs_1_, bf16[2880,256]{1,0:T(8,128)(2,1)S(1)} %bitcast.15), custom_call_target="tpu_custom_call" | custom-call | tf_op jit(solution)/shard_map/project/pallas_call | solution.py:180
  11.4 0.9 copy-done.2
  12.3 1.5 %copy.21 = bf16[128,2880]{0,1:T(8,128)(2,1)S(1)} copy(bf16[128,2880]{1,0:T(8,128)(2,1)} %copy-done.2) | data formatting | bytes 1474560 | tf_op jit(solution)/shard_map/project/pallas_call | solution.py:180
  13.8 0.4 collective-permute-start.1
  14.2 1.9 %collective-permute-done.1 = bf16[128,2880]{0,1:T(8,128)(2,1)S(1)} collective-permute-done((bf16[128,2880]{0,1:T(8,128)(2,1)S(1)}, bf16[128,2880]{0,1:T(8,128)(2,1)S(1)}, u32[]{:S(2)}, u32[]{:S(2)}) %collective-permute-start.1) | collective-permute-done | bytes 737312 | tf_op jit(solution)/shard_map/ppermute | solution.py:37
  16.1 0.4 copy.22
  16.4 0.2 fusion.13
  16.6 0.0 copy-start.15
  16.6 0.0 copy-start.14
  16.7 2.9 %collective-permute-start.2 = (bf16[32,2880]{1,0:T(8,128)(2,1)S(1)}, bf16[32,2880]{1,0:T(8,128)(2,1)S(1)}, u32[]{:S(2)}, u32[]{:S(2)}) collective-permute-start(bf16[32,2880]{1,0:T(8,128)(2,1)S(1)} %get-tuple-element.23), channel_id=1, source_target_pairs={{0,2},{1,3},{2,0},{3,1},{4,6},{5,7},{6,4},{7,5},{8,10},{9,11},{10,... | collective-permute-start | bytes 552968 | tf_op jit(solution)/shard_map/ppermute | solution.py:37
  19.6 1.5 %collective-permute-start.4 = (bf16[32,2880]{1,0:T(8,128)(2,1)S(1)}, bf16[32,2880]{1,0:T(8,128)(2,1)S(1)}, u32[]{:S(2)}, u32[]{:S(2)}) collective-permute-start(bf16[32,2880]{1,0:T(8,128)(2,1)S(1)} %get-tuple-element.24), channel_id=1, source_target_pairs={{0,6},{1,7},{2,4},{3,5},{4,2},{5,3},{6,0},{7,1},{8,14},{9,15},{10,... | collective-permute-start | bytes 552968 | tf_op jit(solution)/shard_map/ppermute | solution.py:37
  21.1 0.1 collective-permute-start.3
  21.2 7.5 %collective-permute-done.2 = bf16[32,2880]{1,0:T(8,128)(2,1)S(1)} collective-permute-done((bf16[32,2880]{1,0:T(8,128)(2,1)S(1)}, bf16[32,2880]{1,0:T(8,128)(2,1)S(1)}, u32[]{:S(2)}, u32[]{:S(2)}) %collective-permute-start.2) | collective-permute-done | bytes 184352 | tf_op jit(solution)/shard_map/ppermute | solution.py:37
  28.7 0.0 collective-permute-done.4
  28.7 1.3 %collective-permute-done.3 = bf16[32,2880]{1,0:T(8,128)(2,1)S(1)} collective-permute-done((bf16[32,2880]{1,0:T(8,128)(2,1)S(1)}, bf16[32,2880]{1,0:T(8,128)(2,1)S(1)}, u32[]{:S(2)}, u32[]{:S(2)}) %collective-permute-start.3) | collective-permute-done | bytes 184352 | tf_op jit(solution)/shard_map/ppermute | solution.py:37
  30.0 0.1 fusion.3
  30.1 2.8 %collective-permute-start.5 = (bf16[16,2880]{1,0:T(8,128)(2,1)S(1)}, bf16[16,2880]{1,0:T(8,128)(2,1)S(1)}, u32[]{:S(2)}, u32[]{:S(2)}) collective-permute-start(bf16[16,2880]{1,0:T(8,128)(2,1)S(1)} %slice.91), channel_id=1, source_target_pairs={{0,8},{1,9},{2,10},{3,11},{4,12},{5,13},{6,14},{7,15},{8,0},{9,1},... | collective-permute-start | bytes 276488 | tf_op jit(solution)/shard_map/ppermute | solution.py:37
  32.9 0.1 eq.17
  33.0 4.1 %collective-permute-done.5 = bf16[16,2880]{1,0:T(8,128)(2,1)S(1)} collective-permute-done((bf16[16,2880]{1,0:T(8,128)(2,1)S(1)}, bf16[16,2880]{1,0:T(8,128)(2,1)S(1)}, u32[]{:S(2)}, u32[]{:S(2)}) %collective-permute-start.5) | collective-permute-done | bytes 92192 | tf_op jit(solution)/shard_map/ppermute | solution.py:37
  37.1 0.2 fusion.4
  37.2 0.1 fusion.5
  37.3 0.1 fusion.16
  37.5 0.2 select_reduce_fusion.1
  37.6 0.1 exponential_reduce_fusion
  37.7 0.1 select_reduce_fusion
  37.8 0.1 concatenate.6
  37.9 1.4 %collective-permute-start.6 = (bf16[16,2912]{1,0:T(8,128)(2,1)S(1)}, bf16[16,2912]{1,0:T(8,128)(2,1)S(1)}, u32[]{:S(2)}, u32[]{:S(2)}) collective-permute-start(bf16[16,2912]{1,0:T(8,128)(2,1)S(1)} %concatenate.6), channel_id=1, source_target_pairs={{0,8},{1,9},{2,10},{3,11},{4,12},{5,13},{6,14},{7,15},{8,0},{9,1},... | collective-permute-start | bytes 279560 | tf_op jit(solution)/shard_map/ppermute | solution.py:37
  39.3 5.2 %collective-permute-done.6 = bf16[16,2912]{1,0:T(8,128)(2,1)S(1)} collective-permute-done((bf16[16,2912]{1,0:T(8,128)(2,1)S(1)}, bf16[16,2912]{1,0:T(8,128)(2,1)S(1)}, u32[]{:S(2)}, u32[]{:S(2)}) %collective-permute-start.6) | collective-permute-done | bytes 93216 | tf_op jit(solution)/shard_map/ppermute | solution.py:37
  44.5 1.0 %collective-permute-start.9 = (bf16[32,2912]{1,0:T(8,128)(2,1)S(1)}, bf16[32,2912]{1,0:T(8,128)(2,1)S(1)}, u32[]{:S(2)}, u32[]{:S(2)}) collective-permute-start(bf16[32,2912]{1,0:T(8,128)(2,1)S(1)} %pad_maximum_fusion.refs_0_), channel_id=1, source_target_pairs={{0,6},{1,7},{2,4},{3,5},{4,2},{5,3},{6,0},{7,1},{8,14},{9,15},{10,... | collective-permute-start | bytes 559112 | tf_op jit(solution)/shard_map/ppermute | solution.py:37
  45.5 1.9 %collective-permute-start.8 = (bf16[32,2912]{1,0:T(8,128)(2,1)S(1)}, bf16[32,2912]{1,0:T(8,128)(2,1)S(1)}, u32[]{:S(2)}, u32[]{:S(2)}) collective-permute-start(bf16[32,2912]{1,0:T(8,128)(2,1)S(1)} %pad_maximum_fusion.refs_0_), channel_id=1, source_target_pairs={{0,4},{1,5},{2,6},{3,7},{4,0},{5,1},{6,2},{7,3},{8,12},{9,13},{10,... | collective-permute-start | bytes 559112 | tf_op jit(solution)/shard_map/ppermute | solution.py:37
  47.4 0.6 collective-permute-start.7
  48.1 0.0 collective-permute-start.10
  48.1 3.0 %collective-permute-done.9.refs_3_ = bf16[32,2912]{1,0:T(8,128)(2,1)S(1)} collective-permute-done((bf16[32,2912]{1,0:T(8,128)(2,1)S(1)}, bf16[32,2912]{1,0:T(8,128)(2,1)S(1)}, u32[]{:S(2)}, u32[]{:S(2)}) %collective-permute-start.9) | collective-permute-done | bytes 186400 | tf_op jit(solution)/shard_map/ppermute | solution.py:37
  51.1 0.0 collective-permute-start.13
  51.1 1.9 %collective-permute-done.8.refs_2_ = bf16[32,2912]{1,0:T(8,128)(2,1)S(1)} collective-permute-done((bf16[32,2912]{1,0:T(8,128)(2,1)S(1)}, bf16[32,2912]{1,0:T(8,128)(2,1)S(1)}, u32[]{:S(2)}, u32[]{:S(2)}) %collective-permute-start.8) | collective-permute-done | bytes 186400 | tf_op jit(solution)/shard_map/ppermute | solution.py:37
  53.0 0.0 collective-permute-start.12
  53.0 0.1 collective-permute-done.7.refs_1_
  53.1 0.4 collective-permute-start.11
  53.5 0.0 collective-permute-done.13.refs_7_
  53.5 0.9 collective-permute-done.12.refs_6_
  54.4 0.3 collective-permute-done.11.refs_5_
  54.7 0.4 copy-done.12
  55.1 0.3 copy-done.13
  55.4 16.6 %experts.1 = (f32[128,2880]{1,0:T(8,128)}, bf16[128,2880]{1,0:T(8,128)(2,1)}) custom-call(s32[1]{0:T(128)} %bitcast.1.me_ref, bf16[32,2912]{1,0:T(8,128)(2,1)} %copy-done.6, bf16[32,2912]{1,0:T(8,128)(2,1)} %copy-done.9, bf16[32,2912]{1,0:T(8,128)(2,1)} %copy-done.8, bf16[32,2912]{1,0:T(8,128)(2,1)} %copy-done.7, bf16[32,2912]{1,0:T(8,128)(2,1)} %copy-done.10, ...), custom_call_target="tpu_custom_call" | custom-call | tf_op jit(solution)/shard_map/experts/pallas_call | solution.py:274
  72.0 1.6 %copy.24 = bf16[128,2880]{0,1:T(8,128)(2,1)S(1)} copy(bf16[128,2880]{1,0:T(8,128)(2,1)} %get-tuple-element.13) | data formatting | bytes 1474560 | tf_op jit(solution)/shard_map/experts/pallas_call | solution.py:274
  73.6 0.3 collective-permute-start.14
  73.9 2.0 %collective-permute-done.14 = bf16[128,2880]{0,1:T(8,128)(2,1)S(1)} collective-permute-done((bf16[128,2880]{0,1:T(8,128)(2,1)S(1)}, bf16[128,2880]{0,1:T(8,128)(2,1)S(1)}, u32[]{:S(2)}, u32[]{:S(2)}) %collective-permute-start.14) | collective-permute-done | bytes 737312 | tf_op jit(solution)/shard_map/ppermute | solution.py:37
  75.9 0.4 copy.25
  76.3 0.2 fusion.11
  76.5 1.3 %collective-permute-start.15 = (bf16[32,2880]{1,0:T(8,128)(2,1)S(1)}, bf16[32,2880]{1,0:T(8,128)(2,1)S(1)}, u32[]{:S(2)}, u32[]{:S(2)}) collective-permute-start(bf16[32,2880]{1,0:T(8,128)(2,1)S(1)} %get-tuple-element.20), channel_id=1, source_target_pairs={{0,2},{1,3},{2,0},{3,1},{4,6},{5,7},{6,4},{7,5},{8,10},{9,11},{10,... | collective-permute-start | bytes 552968 | tf_op jit(solution)/shard_map/ppermute | solution.py:37
  77.8 1.3 %collective-permute-start.17 = (bf16[32,2880]{1,0:T(8,128)(2,1)S(1)}, bf16[32,2880]{1,0:T(8,128)(2,1)S(1)}, u32[]{:S(2)}, u32[]{:S(2)}) collective-permute-start(bf16[32,2880]{1,0:T(8,128)(2,1)S(1)} %get-tuple-element.21), channel_id=1, source_target_pairs={{0,6},{1,7},{2,4},{3,5},{4,2},{5,3},{6,0},{7,1},{8,14},{9,15},{10,... | collective-permute-start | bytes 552968 | tf_op jit(solution)/shard_map/ppermute | solution.py:37
  79.1 1.0 %collective-permute-start.16 = (bf16[32,2880]{1,0:T(8,128)(2,1)S(1)}, bf16[32,2880]{1,0:T(8,128)(2,1)S(1)}, u32[]{:S(2)}, u32[]{:S(2)}) collective-permute-start(bf16[32,2880]{1,0:T(8,128)(2,1)S(1)} %get-tuple-element.22), channel_id=1, source_target_pairs={{0,4},{1,5},{2,6},{3,7},{4,0},{5,1},{6,2},{7,3},{8,12},{9,13},{10,... | collective-permute-start | bytes 552968 | tf_op jit(solution)/shard_map/ppermute | solution.py:37
  80.0 7.4 %collective-permute-done.15 = bf16[32,2880]{1,0:T(8,128)(2,1)S(1)} collective-permute-done((bf16[32,2880]{1,0:T(8,128)(2,1)S(1)}, bf16[32,2880]{1,0:T(8,128)(2,1)S(1)}, u32[]{:S(2)}, u32[]{:S(2)}) %collective-permute-start.15) | collective-permute-done | bytes 184352 | tf_op jit(solution)/shard_map/ppermute | solution.py:37
  87.5 0.0 collective-permute-done.17
  87.5 1.2 %collective-permute-done.16 = bf16[32,2880]{1,0:T(8,128)(2,1)S(1)} collective-permute-done((bf16[32,2880]{1,0:T(8,128)(2,1)S(1)}, bf16[32,2880]{1,0:T(8,128)(2,1)S(1)}, u32[]{:S(2)}, u32[]{:S(2)}) %collective-permute-start.16) | collective-permute-done | bytes 184352 | tf_op jit(solution)/shard_map/ppermute | solution.py:37
  88.7 0.1 fusion.1
  88.8 1.6 %collective-permute-start.18 = (bf16[16,2880]{1,0:T(8,128)(2,1)S(1)}, bf16[16,2880]{1,0:T(8,128)(2,1)S(1)}, u32[]{:S(2)}, u32[]{:S(2)}) collective-permute-start(bf16[16,2880]{1,0:T(8,128)(2,1)S(1)} %slice.90), channel_id=1, source_target_pairs={{0,8},{1,9},{2,10},{3,11},{4,12},{5,13},{6,14},{7,15},{8,0},{9,1},... | collective-permute-start | bytes 276488 | tf_op jit(solution)/shard_map/ppermute | solution.py:37
  90.4 5.1 %collective-permute-done.18 = bf16[16,2880]{1,0:T(8,128)(2,1)S(1)} collective-permute-done((bf16[16,2880]{1,0:T(8,128)(2,1)S(1)}, bf16[16,2880]{1,0:T(8,128)(2,1)S(1)}, u32[]{:S(2)}, u32[]{:S(2)}) %collective-permute-start.18) | collective-permute-done | bytes 92192 | tf_op jit(solution)/shard_map/ppermute | solution.py:37
  95.6 0.7 fusion.9
  (35 shorter events, 0.2 us)
Async XLA Ops:
  0.6 36.7 %copy-start = (bf16[2880,16]{0,1:T(8,128)(2,1)S(1)}, bf16[2880,16]{0,1:T(8,128)(2,1)}, u32[]{:S(2)}) copy-start(bf16[2880,16]{0,1:T(8,128)(2,1)} %param.17) | copy-start | bytes 276484
  0.7 8.9 %copy-start.1 = (bf16[256,2880]{0,1:T(8,128)(2,1)S(1)}, bf16[256,2880]{0,1:T(8,128)(2,1)}, u32[]{:S(2)}) copy-start(bf16[256,2880]{0,1:T(8,128)(2,1)} %param.16) | copy-start | bytes 4423684
  8.0 1.6 %collective-permute-start = (bf16[2,64,256]{2,1,0:T(8,128)(2,1)}, bf16[2,64,256]{2,1,0:T(8,128)(2,1)S(1)}, u32[]{:S(2)}, u32[]{:S(2)}) collective-permute-start(bf16[2,64,256]{2,1,0:T(8,128)(2,1)} %get-tuple-element.9), channel_id=1, source_target_pairs={{0,1},{1,0},{2,3},{3,2},{4,5},{5,4},{6,7},{7,6},{8,9},{9,8},{10,11... | collective-permute-start | bytes 196616 | tf_op jit(solution)/shard_map/ppermute | solution.py:37
  9.5 0.8 copy-start.3
  11.4 0.9 copy-start.2
  13.8 2.3 %collective-permute-start.1 = (bf16[128,2880]{0,1:T(8,128)(2,1)S(1)}, bf16[128,2880]{0,1:T(8,128)(2,1)S(1)}, u32[]{:S(2)}, u32[]{:S(2)}) collective-permute-start(bf16[128,2880]{0,1:T(8,128)(2,1)S(1)} %copy.21), channel_id=1, source_target_pairs={{0,1},{1,0},{2,3},{3,2},{4,5},{5,4},{6,7},{7,6},{8,9},{9,8},{10,11... | collective-permute-start | bytes 2211848 | tf_op jit(solution)/shard_map/ppermute | solution.py:37
  16.6 16.3 %copy-start.15 = (s32[2,8,4]{1,2,0:T(4,128)S(1)}, s32[2,8,4]{1,2,0:T(4,128)}, u32[]{:S(2)}) copy-start(s32[2,8,4]{1,2,0:T(4,128)} %param.21) | copy-start | bytes 772
  16.6 20.5 %copy-start.14 = (bf16[2,8,2880]{2,1,0:T(8,128)(2,1)S(1)}, bf16[2,8,2880]{2,1,0:T(8,128)(2,1)}, u32[]{:S(2)}) copy-start(bf16[2,8,2880]{2,1,0:T(8,128)(2,1)} %param.15) | copy-start | bytes 276484
  16.7 12.0 %collective-permute-start.2 = (bf16[32,2880]{1,0:T(8,128)(2,1)S(1)}, bf16[32,2880]{1,0:T(8,128)(2,1)S(1)}, u32[]{:S(2)}, u32[]{:S(2)}) collective-permute-start(bf16[32,2880]{1,0:T(8,128)(2,1)S(1)} %get-tuple-element.23), channel_id=1, source_target_pairs={{0,2},{1,3},{2,0},{3,1},{4,6},{5,7},{6,4},{7,5},{8,10},{9,11},{10,... | collective-permute-start | bytes 552968 | tf_op jit(solution)/shard_map/ppermute | solution.py:37
  19.6 9.1 %collective-permute-start.4 = (bf16[32,2880]{1,0:T(8,128)(2,1)S(1)}, bf16[32,2880]{1,0:T(8,128)(2,1)S(1)}, u32[]{:S(2)}, u32[]{:S(2)}) collective-permute-start(bf16[32,2880]{1,0:T(8,128)(2,1)S(1)} %get-tuple-element.24), channel_id=1, source_target_pairs={{0,6},{1,7},{2,4},{3,5},{4,2},{5,3},{6,0},{7,1},{8,14},{9,15},{10,... | collective-permute-start | bytes 552968 | tf_op jit(solution)/shard_map/ppermute | solution.py:37
  21.1 8.9 %collective-permute-start.3 = (bf16[32,2880]{1,0:T(8,128)(2,1)S(1)}, bf16[32,2880]{1,0:T(8,128)(2,1)S(1)}, u32[]{:S(2)}, u32[]{:S(2)}) collective-permute-start(bf16[32,2880]{1,0:T(8,128)(2,1)S(1)} %get-tuple-element.25), channel_id=1, source_target_pairs={{0,4},{1,5},{2,6},{3,7},{4,0},{5,1},{6,2},{7,3},{8,12},{9,13},{10,... | collective-permute-start | bytes 552968 | tf_op jit(solution)/shard_map/ppermute | solution.py:37
  30.1 6.9 %collective-permute-start.5 = (bf16[16,2880]{1,0:T(8,128)(2,1)S(1)}, bf16[16,2880]{1,0:T(8,128)(2,1)S(1)}, u32[]{:S(2)}, u32[]{:S(2)}) collective-permute-start(bf16[16,2880]{1,0:T(8,128)(2,1)S(1)} %slice.91), channel_id=1, source_target_pairs={{0,8},{1,9},{2,10},{3,11},{4,12},{5,13},{6,14},{7,15},{8,0},{9,1},... | collective-permute-start | bytes 276488 | tf_op jit(solution)/shard_map/ppermute | solution.py:37
  37.2 58.3 %copy-start.5 = (bf16[16,2880]{1,0:T(8,128)(2,1)}, bf16[16,2880]{1,0:T(8,128)(2,1)S(1)}, u32[]{:S(2)}) copy-start(bf16[16,2880]{1,0:T(8,128)(2,1)S(1)} %get-tuple-element.17) | copy-start | bytes 276484
  37.9 6.6 %collective-permute-start.6 = (bf16[16,2912]{1,0:T(8,128)(2,1)S(1)}, bf16[16,2912]{1,0:T(8,128)(2,1)S(1)}, u32[]{:S(2)}, u32[]{:S(2)}) collective-permute-start(bf16[16,2912]{1,0:T(8,128)(2,1)S(1)} %concatenate.6), channel_id=1, source_target_pairs={{0,8},{1,9},{2,10},{3,11},{4,12},{5,13},{6,14},{7,15},{8,0},{9,1},... | collective-permute-start | bytes 279560 | tf_op jit(solution)/shard_map/ppermute | solution.py:37
  44.5 10.2 %copy-start.6 = (bf16[32,2912]{1,0:T(8,128)(2,1)}, bf16[32,2912]{1,0:T(8,128)(2,1)S(1)}, u32[]{:S(2)}) copy-start(bf16[32,2912]{1,0:T(8,128)(2,1)S(1)} %pad_maximum_fusion.refs_0_) | copy-start | bytes 559108
  44.5 6.6 %collective-permute-start.9 = (bf16[32,2912]{1,0:T(8,128)(2,1)S(1)}, bf16[32,2912]{1,0:T(8,128)(2,1)S(1)}, u32[]{:S(2)}, u32[]{:S(2)}) collective-permute-start(bf16[32,2912]{1,0:T(8,128)(2,1)S(1)} %pad_maximum_fusion.refs_0_), channel_id=1, source_target_pairs={{0,6},{1,7},{2,4},{3,5},{4,2},{5,3},{6,0},{7,1},{8,14},{9,15},{10,... | collective-permute-start | bytes 559112 | tf_op jit(solution)/shard_map/ppermute | solution.py:37
  45.5 7.5 %collective-permute-start.8 = (bf16[32,2912]{1,0:T(8,128)(2,1)S(1)}, bf16[32,2912]{1,0:T(8,128)(2,1)S(1)}, u32[]{:S(2)}, u32[]{:S(2)}) collective-permute-start(bf16[32,2912]{1,0:T(8,128)(2,1)S(1)} %pad_maximum_fusion.refs_0_), channel_id=1, source_target_pairs={{0,4},{1,5},{2,6},{3,7},{4,0},{5,1},{6,2},{7,3},{8,12},{9,13},{10,... | collective-permute-start | bytes 559112 | tf_op jit(solution)/shard_map/ppermute | solution.py:37
  47.4 5.7 %collective-permute-start.7 = (bf16[32,2912]{1,0:T(8,128)(2,1)S(1)}, bf16[32,2912]{1,0:T(8,128)(2,1)S(1)}, u32[]{:S(2)}, u32[]{:S(2)}) collective-permute-start(bf16[32,2912]{1,0:T(8,128)(2,1)S(1)} %pad_maximum_fusion.refs_0_), channel_id=1, source_target_pairs={{0,2},{1,3},{2,0},{3,1},{4,6},{5,7},{6,4},{7,5},{8,10},{9,11},{10,... | collective-permute-start | bytes 559112 | tf_op jit(solution)/shard_map/ppermute | solution.py:37
  48.1 5.4 %collective-permute-start.10 = (bf16[32,2912]{1,0:T(8,128)(2,1)S(1)}, bf16[32,2912]{1,0:T(8,128)(2,1)S(1)}, u32[]{:S(2)}, u32[]{:S(2)}) collective-permute-start(bf16[32,2912]{1,0:T(8,128)(2,1)S(1)} %pad_maximum_fusion.refs_0_), channel_id=1, source_target_pairs={{0,1},{1,0},{2,3},{3,2},{4,5},{5,4},{6,7},{7,6},{8,9},{9,8},{10,11... | collective-permute-start | bytes 559112 | tf_op jit(solution)/shard_map/ppermute | solution.py:37
  51.1 3.6 %copy-start.7 = (bf16[32,2912]{1,0:T(8,128)(2,1)}, bf16[32,2912]{1,0:T(8,128)(2,1)S(1)}, u32[]{:S(2)}) copy-start(bf16[32,2912]{1,0:T(8,128)(2,1)S(1)} %collective-permute-done.9.refs_3_) | copy-start | bytes 559108
  51.1 2.5 %collective-permute-start.13 = (bf16[32,2912]{1,0:T(8,128)(2,1)S(1)}, bf16[32,2912]{1,0:T(8,128)(2,1)S(1)}, u32[]{:S(2)}, u32[]{:S(2)}) collective-permute-start(bf16[32,2912]{1,0:T(8,128)(2,1)S(1)} %collective-permute-done.9.refs_3_), channel_id=1, source_target_pairs={{0,1},{1,0},{2,3},{3,2},{4,5},{5,4},{6,7},{7,6},{8,9},{9,8},{10,11... | collective-permute-start | bytes 559112 | tf_op jit(solution)/shard_map/ppermute | solution.py:37
  53.0 1.7 %copy-start.8 = (bf16[32,2912]{1,0:T(8,128)(2,1)}, bf16[32,2912]{1,0:T(8,128)(2,1)S(1)}, u32[]{:S(2)}) copy-start(bf16[32,2912]{1,0:T(8,128)(2,1)S(1)} %collective-permute-done.8.refs_2_) | copy-start | bytes 559108
  53.0 1.4 %collective-permute-start.12 = (bf16[32,2912]{1,0:T(8,128)(2,1)S(1)}, bf16[32,2912]{1,0:T(8,128)(2,1)S(1)}, u32[]{:S(2)}, u32[]{:S(2)}) collective-permute-start(bf16[32,2912]{1,0:T(8,128)(2,1)S(1)} %collective-permute-done.8.refs_2_), channel_id=1, source_target_pairs={{0,1},{1,0},{2,3},{3,2},{4,5},{5,4},{6,7},{7,6},{8,9},{9,8},{10,11... | collective-permute-start | bytes 559112 | tf_op jit(solution)/shard_map/ppermute | solution.py:37
  53.1 1.6 %copy-start.9 = (bf16[32,2912]{1,0:T(8,128)(2,1)}, bf16[32,2912]{1,0:T(8,128)(2,1)S(1)}, u32[]{:S(2)}) copy-start(bf16[32,2912]{1,0:T(8,128)(2,1)S(1)} %collective-permute-done.7.refs_1_) | copy-start | bytes 559108
  53.1 1.6 %collective-permute-start.11 = (bf16[32,2912]{1,0:T(8,128)(2,1)S(1)}, bf16[32,2912]{1,0:T(8,128)(2,1)S(1)}, u32[]{:S(2)}, u32[]{:S(2)}) collective-permute-start(bf16[32,2912]{1,0:T(8,128)(2,1)S(1)} %collective-permute-done.7.refs_1_), channel_id=1, source_target_pairs={{0,1},{1,0},{2,3},{3,2},{4,5},{5,4},{6,7},{7,6},{8,9},{9,8},{10,11... | collective-permute-start | bytes 559112 | tf_op jit(solution)/shard_map/ppermute | solution.py:37
  53.5 1.2 %copy-start.10 = (bf16[32,2912]{1,0:T(8,128)(2,1)}, bf16[32,2912]{1,0:T(8,128)(2,1)S(1)}, u32[]{:S(2)}) copy-start(bf16[32,2912]{1,0:T(8,128)(2,1)S(1)} %collective-permute-done.10.refs_4_) | copy-start | bytes 559108
  53.5 1.2 %copy-start.11 = (bf16[32,2912]{1,0:T(8,128)(2,1)}, bf16[32,2912]{1,0:T(8,128)(2,1)S(1)}, u32[]{:S(2)}) copy-start(bf16[32,2912]{1,0:T(8,128)(2,1)S(1)} %collective-permute-done.13.refs_7_) | copy-start | bytes 559108
  54.4 0.7 copy-start.12
  54.7 0.7 copy-start.13
  72.0 4.3 %copy-start.4 = (f32[128,2880]{1,0:T(8,128)S(1)}, f32[128,2880]{1,0:T(8,128)}, u32[]{:S(2)}) copy-start(f32[128,2880]{1,0:T(8,128)} %get-tuple-element.12) | copy-start | bytes 4423684
  73.6 2.3 %collective-permute-start.14 = (bf16[128,2880]{0,1:T(8,128)(2,1)S(1)}, bf16[128,2880]{0,1:T(8,128)(2,1)S(1)}, u32[]{:S(2)}, u32[]{:S(2)}) collective-permute-start(bf16[128,2880]{0,1:T(8,128)(2,1)S(1)} %copy.24), channel_id=1, source_target_pairs={{0,1},{1,0},{2,3},{3,2},{4,5},{5,4},{6,7},{7,6},{8,9},{9,8},{10,11... | collective-permute-start | bytes 2211848 | tf_op jit(solution)/shard_map/ppermute | solution.py:37
  76.5 11.0 %collective-permute-start.15 = (bf16[32,2880]{1,0:T(8,128)(2,1)S(1)}, bf16[32,2880]{1,0:T(8,128)(2,1)S(1)}, u32[]{:S(2)}, u32[]{:S(2)}) collective-permute-start(bf16[32,2880]{1,0:T(8,128)(2,1)S(1)} %get-tuple-element.20), channel_id=1, source_target_pairs={{0,2},{1,3},{2,0},{3,1},{4,6},{5,7},{6,4},{7,5},{8,10},{9,11},{10,... | collective-permute-start | bytes 552968 | tf_op jit(solution)/shard_map/ppermute | solution.py:37
  77.8 9.7 %collective-permute-start.17 = (bf16[32,2880]{1,0:T(8,128)(2,1)S(1)}, bf16[32,2880]{1,0:T(8,128)(2,1)S(1)}, u32[]{:S(2)}, u32[]{:S(2)}) collective-permute-start(bf16[32,2880]{1,0:T(8,128)(2,1)S(1)} %get-tuple-element.21), channel_id=1, source_target_pairs={{0,6},{1,7},{2,4},{3,5},{4,2},{5,3},{6,0},{7,1},{8,14},{9,15},{10,... | collective-permute-start | bytes 552968 | tf_op jit(solution)/shard_map/ppermute | solution.py:37
  79.1 9.6 %collective-permute-start.16 = (bf16[32,2880]{1,0:T(8,128)(2,1)S(1)}, bf16[32,2880]{1,0:T(8,128)(2,1)S(1)}, u32[]{:S(2)}, u32[]{:S(2)}) collective-permute-start(bf16[32,2880]{1,0:T(8,128)(2,1)S(1)} %get-tuple-element.22), channel_id=1, source_target_pairs={{0,4},{1,5},{2,6},{3,7},{4,0},{5,1},{6,2},{7,3},{8,12},{9,13},{10,... | collective-permute-start | bytes 552968 | tf_op jit(solution)/shard_map/ppermute | solution.py:37
  88.8 6.7 %collective-permute-start.18 = (bf16[16,2880]{1,0:T(8,128)(2,1)S(1)}, bf16[16,2880]{1,0:T(8,128)(2,1)S(1)}, u32[]{:S(2)}, u32[]{:S(2)}) collective-permute-start(bf16[16,2880]{1,0:T(8,128)(2,1)S(1)} %slice.90), channel_id=1, source_target_pairs={{0,8},{1,9},{2,10},{3,11},{4,12},{5,13},{6,14},{7,15},{8,0},{9,1},... | collective-permute-start | bytes 276488 | tf_op jit(solution)/shard_map/ppermute | solution.py:37

commit v3 on v2

--- a/solution.py
+++ b/solution.py
@@ -14,7 +14,8 @@
 EXPERTS = 16
 SPLIT = 4
 REQ_DEV = 8
-CHUNK = 128
+TILE = 256
+LIMIT = 16 << 20
 ROWS_LAST = (((1,), (1,)), ((), ()))
 
 
@@ -38,8 +39,8 @@
 
 
 def scatter_sum(keep, send, stages):
-    block_rows, width = keep.shape[0], keep.shape[1]
-    total = keep.astype(jnp.float32) + from_mask(send, 1).astype(jnp.float32)
+    width = keep.shape[1]
+    total = keep + from_mask(send, 1)[:, :width].astype(jnp.float32)
     for bit, bits in stages[1:]:
         size = total.shape[0] >> bits
         pieces = [total[r * size : (r + 1) * size] for r in range(1 << bits)]
@@ -137,7 +138,7 @@
                 pltpu.VMEM((block * QPK, pair), jnp.float32),
             ],
         ),
-        compiler_params=pltpu.CompilerParams(vmem_limit_bytes=60 << 20),
+        compiler_params=pltpu.CompilerParams(vmem_limit_bytes=61 << 20),
         name="attention",
     )(lengths, place, queries, new_kv, cache)
 
@@ -157,8 +158,8 @@
         for m in range(batch):
             at = (p * batch + m) * REQ_DEV
             rows[at : at + REQ_DEV, :] = wide[member, m, pl.ds(start, REQ_DEV), :]
-    half = keep.shape[0]
-    send[...] = lax.dot_general(
+    half, width = keep.shape
+    send[:, :width] = lax.dot_general(
         rows[half:, :].astype(jnp.bfloat16),
         weight[...],
         ROWS_LAST,
@@ -181,7 +182,7 @@
         functools.partial(project_kernel, group, masks),
         out_shape=[
             jax.ShapeDtypeStruct((count // 2, weight.shape[0]), jnp.float32),
-            jax.ShapeDtypeStruct((count // 2, weight.shape[0]), jnp.bfloat16),
+            jax.ShapeDtypeStruct((count // 2, pl.cdiv(weight.shape[0], 128) * 128), jnp.bfloat16),
         ],
         in_specs=[pl.BlockSpec(memory_space=pltpu.SMEM)] + [whole] * (group + 1),
         out_specs=[whole] * 2,
@@ -189,110 +190,105 @@
             pltpu.VMEM((group,) + held[0].shape, jnp.float32),
             pltpu.VMEM((count, width), jnp.float32),
         ],
-        compiler_params=pltpu.CompilerParams(vmem_limit_bytes=32 << 20),
+        compiler_params=pltpu.CompilerParams(vmem_limit_bytes=LIMIT),
         name="project",
     )(me, *held, weight)
 
 
-def expert_kernel(count, ahead, me_ref, *refs):
+def expert_kernel(count, hidden, me_ref, *refs):
     pieces = refs[:count]
-    sources = refs[count : count + 3]
+    w_gate, far_up, far_down = refs[count : count + 3]
     keep, send = refs[count + 3 : count + 5]
-    rows, gates, ups, downs, active, total, done = refs[count + 5 :]
-    entries, hidden, width = sources[0].shape
-    order = [(k, e) for e in range(entries) for k in (0, 1)] + [(2, e) for e in range(entries)]
-    stores = (gates, ups, downs)
-    parts = pl.cdiv(hidden, CHUNK)
-    copies = []
-    for k, e in order:
-        for s in range(parts):
-            some = pl.ds(s * CHUNK, min(CHUNK, hidden - s * CHUNK))
-            copies.append(
-                pltpu.make_async_copy(
-                    sources[k].at[e, some], stores[k].at[e, some], done.at[k, e, s]
-                )
+    rows, gates, active, w_up, w_down, up_done, down_done = refs[count + 5 :]
+    units, width = w_gate.shape
+    tiles = [slice(start, min(start + TILE, units)) for start in range(0, units, TILE)]
+    up_copies, down_copies = [
+        [
+            pltpu.make_async_copy(
+                far.at[pl.ds(some.start, some.stop - some.start)],
+                near.at[pl.ds(some.start, some.stop - some.start)],
+                done.at[index],
             )
-    state = [0, 0]
-
-    def issue():
-        if state[0] < len(copies):
-            copies[state[0]].start()
-            state[0] += 1
-
-    def finish():
-        for _ in range(parts):
-            copies[state[1]].wait()
-            state[1] += 1
-            issue()
-
-    for _ in range(ahead):
-        issue()
+            for index, some in enumerate(tiles)
+        ]
+        for far, near, done in ((far_up, w_up, up_done), (far_down, w_down, down_done))
+    ]
+    for copy in up_copies:
+        copy.start()
     at = 0
     for piece in pieces:
         rows[at : at + piece.shape[0], :] = piece[...]
         at += piece.shape[0]
+    for some in tiles:
+        gates[:, some] = lax.dot_general(
+            rows[:, :width], w_gate[some, :], ROWS_LAST, preferred_element_type=jnp.float32
+        )
+    for copy in down_copies:
+        copy.start()
+    for copy, some in zip(up_copies, tiles):
+        copy.wait()
+        gate = gates[:, some]
+        up = lax.dot_general(
+            rows[:, :width], w_up[some, :], ROWS_LAST, preferred_element_type=jnp.float32
+        )
+        active[:, some] = ((up + 1.0) * gate * jax.nn.sigmoid(1.702 * gate)).astype(jnp.bfloat16)
     base = width // 128 * 128
     tail = rows[:, base:].astype(jnp.float32)
     lane = lax.broadcasted_iota(jnp.int32, tail.shape, 1) - (width - base)
-    for e in range(entries):
-        finish()
-        gate = lax.dot_general(
-            rows[:, :width], gates[e], ROWS_LAST, preferred_element_type=jnp.float32
-        )
-        finish()
-        up = lax.dot_general(
-            rows[:, :width], ups[e], ROWS_LAST, preferred_element_type=jnp.float32
-        )
-        active[e] = ((up + 1.0) * gate * jax.nn.sigmoid(1.702 * gate)).astype(jnp.bfloat16)
+    deep = min(units, SPLIT * hidden)
+    weights = []
+    for start in range(0, units, deep):
+        expert = (me_ref[0] * units + start) // (SPLIT * hidden)
+        picked = (lane == expert) | (lane == expert + EXPERTS)
+        weights.append(jnp.sum(jnp.where(picked, tail, 0.0), axis=1, keepdims=True))
     half = keep.shape[0]
-    local = max(1, entries // SPLIT)
-    for e in range(entries):
-        finish()
-        out = jnp.dot(active[e], downs[e], preferred_element_type=jnp.float32)
-        if e % SPLIT:
-            out = out + total[...]
-        if e + 1 < entries and (e + 1) % SPLIT:
-            total[...] = out
-            continue
-        expert = me_ref[0] * entries // SPLIT + e // SPLIT
-        picked = (lane == expert) | (lane == expert + EXPERTS)
-        out = out * jnp.sum(jnp.where(picked, tail, 0.0), axis=1, keepdims=True)
-        if e // SPLIT:
-            keep[...] += out[:half]
-            send[...] = (send[...].astype(jnp.float32) + out[half:]).astype(jnp.bfloat16)
-        else:
-            keep[...] = out[:half]
-            send[...] = out[half:].astype(jnp.bfloat16)
-
-
-def expert_sums(me, pieces, w_gate, w_up, w_down, ahead=9):
-    entries, hidden, width = w_gate.shape
+    for copy in down_copies:
+        copy.wait()
+    for start in range(0, width, 2 * TILE):
+        some = slice(start, min(start + 2 * TILE, width))
+        out = 0.0
+        for index, weight in enumerate(weights):
+            part = slice(index * deep, (index + 1) * deep)
+            out = out + weight * jnp.dot(
+                active[:, part], w_down[part, some], preferred_element_type=jnp.float32
+            )
+        keep[:, some] = out[:half]
+        send[:, some] = out[half:].astype(jnp.bfloat16)
+
+
+def expert_sums(me, pieces, w_gate, w_up, w_down):
+    hidden, width = w_down.shape[1:]
+    units = w_down.shape[0] * hidden
     count = sum(piece.shape[0] for piece in pieces)
     whole = pl.BlockSpec(memory_space=pltpu.VMEM)
-    outside = pl.BlockSpec(memory_space=pl.ANY)
-    parts = pl.cdiv(hidden, CHUNK)
+    tiles = pl.cdiv(units, TILE)
     return pl.pallas_call(
-        functools.partial(expert_kernel, len(pieces), ahead),
+        functools.partial(expert_kernel, len(pieces), hidden),
         out_shape=[
             jax.ShapeDtypeStruct((count // 2, width), jnp.float32),
-            jax.ShapeDtypeStruct((count // 2, width), jnp.bfloat16),
+            jax.ShapeDtypeStruct((count // 2, pl.cdiv(width, 128) * 128), jnp.bfloat16),
         ],
-        in_specs=[pl.BlockSpec(memory_space=pltpu.SMEM)]
-        + [whole] * len(pieces)
-        + [outside] * 3,
+        in_specs=[pl.BlockSpec(memory_space=pltpu.SMEM)] + [whole] * (len(pieces) + 1)
+        + [pl.BlockSpec(memory_space=pl.ANY)] * 2,
         out_specs=[whole] * 2,
         scratch_shapes=[
             pltpu.VMEM((count, pieces[0].shape[1]), jnp.bfloat16),
-            pltpu.VMEM(w_gate.shape, jnp.bfloat16),
-            pltpu.VMEM(w_up.shape, jnp.bfloat16),
-            pltpu.VMEM(w_down.shape, jnp.bfloat16),
-            pltpu.VMEM((entries, count, hidden), jnp.bfloat16),
-            pltpu.VMEM((count, width), jnp.float32),
-            pltpu.SemaphoreType.DMA((3, entries, parts)),
+            pltpu.VMEM((count, units), jnp.float32),
+            pltpu.VMEM((count, units), jnp.bfloat16),
+            pltpu.VMEM((units, width), jnp.bfloat16),
+            pltpu.VMEM((units, width), jnp.bfloat16),
+            pltpu.SemaphoreType.DMA((tiles,)),
+            pltpu.SemaphoreType.DMA((tiles,)),
         ],
-        compiler_params=pltpu.CompilerParams(vmem_limit_bytes=56 << 20),
+        compiler_params=pltpu.CompilerParams(vmem_limit_bytes=50 << 20),
         name="experts",
-    )(me, *pieces, w_gate, w_up, w_down)
+    )(
+        me,
+        *pieces,
+        w_gate.swapaxes(1, 2).reshape(units, width),
+        w_up.swapaxes(1, 2).reshape(units, width),
+        w_down.reshape(units, width),
+    )
 
 
 def shards(queries, new_kv, cache, lengths, residual, o_proj, router, w_gate, w_up, w_down, routes):
@@ -328,7 +324,7 @@
 
     pieces = gather_rows(payload, stages)
     mixture = scatter_sum(
-        *expert_sums(me, pieces, w_gate.swapaxes(1, 2), w_up.swapaxes(1, 2), w_down), stages
+        *expert_sums(me, pieces, w_gate, w_up, w_down), stages
     )
     layer = (attended_wide + mixture).astype(jnp.bfloat16)
     return attended.reshape(residual.shape), layer.reshape(residual.shape)

time: 96.6 us -> 89.6 us (0.928)
  local copies, waits for them, and re-layouts: 6.54 us -> 1.16 us
  Pallas kernels: 24.9 us -> 23.5 us
    pallas_call x2 -> x0, local copies, waits for them, and re-layouts: 3.09 us -> none  [the longest x1 1.6 us: expert_sums(): pl.pallas_call(functools.partial(expert_kernel, len(pieces), ahead), out_...]
    unnamed x33 -> x13, local copies, waits for them, and re-layouts: 2.43 us -> 0.87 us
    pallas_call x1, Pallas kernels: 16.6 us -> 15.2 us  [expert_sums(): pl.pallas_call(functools.partial(expert_kernel, len(pieces), hidden), out...]
where the time goes in v3:
time: 89.6 us; the launch traced here: 89.3 us
  waiting for transfers between devices  43.5 us (49%)
  Pallas kernels  23.5 us (26%)
  starting transfers between devices  18.5 us (21%)
  other arithmetic  1.74 us (2%)
  local copies, waits for them, and re-layouts  1.16 us (1%)
    ppermute x19, waiting for transfers between devices, from_mask(): return lax.ppermute(value, 'req', pairs)  43.5 us
    ppermute x19, starting transfers between devices, from_mask(): return lax.ppermute(value, 'req', pairs)  18.5 us
    pallas_call x1, Pallas kernels, expert_sums(): pl.pallas_call(functools.partial(expert_kernel, len(pieces), hidden), out...  15.2 us
    pallas_call x1, Pallas kernels, attention(): pl.pallas_call(functools.partial(attention_kernel, group, rows // block),...  7.29 us
  transfers between devices with their start and end apart: 19, of which 15 were waited for; matrix products, arithmetic and copies ran while one was open for 0% of the time, Pallas kernels for 0%

profile of v3, /device:TPU:0, one launch (start us, length us, event | category | flops | bytes accessed | tf_op | source)
XLA Modules:
  0.0 89.3 jit_solution(8731282242034198682)
XLA Ops:
  0.6 0.0 copy-start
  0.7 0.0 copy-start.1
  0.7 7.3 %attention.1 = (bf16[2,64,256]{2,1,0:T(8,128)(2,1)}, bf16[2,64,256]{2,1,0:T(8,128)(2,1)}) custom-call(s32[2,128]{1,0:T(2,128)} %lengths.1, s32[1]{0:T(128)S(6)} %select_n.15.place, bf16[2,64,512]{2,1,0:T(8,128)(2,1)} %q_ref.1, bf16[2,64,128]{2,1,0:T(8,128)(2,1)} %kv_ref.1, bf16[2,64,128,128]{3,2,1,0:T(8,128)(2,1)} %cache_ref.1), custom_call_target="tpu_custom_call" | custom-call | tf_op jit(solution)/shard_map/attention/pallas_call | solution.py:123
  8.0 0.5 collective-permute-start
  8.4 1.1 %collective-permute-done.refs_1_ = bf16[2,64,256]{2,1,0:T(8,128)(2,1)S(1)} collective-permute-done((bf16[2,64,256]{2,1,0:T(8,128)(2,1)}, bf16[2,64,256]{2,1,0:T(8,128)(2,1)S(1)}, u32[]{:S(2)}, u32[]{:S(2)}) %collective-permute-start) | collective-permute-done | bytes 65568 | tf_op jit(solution)/shard_map/ppermute | solution.py:38
  9.5 0.0 copy-done.1
  9.5 0.8 copy-done.2
  10.4 1.0 %project.1 = (f32[128,2880]{1,0:T(8,128)S(1)}, bf16[128,2944]{1,0:T(8,128)(2,1)S(1)}) custom-call(s32[1]{0:T(128)} %bitcast.1.me_ref, bf16[2,64,256]{2,1,0:T(8,128)(2,1)S(1)} %copy-done.2, bf16[2,64,256]{2,1,0:T(8,128)(2,1)S(1)} %collective-permute-done.refs_1_, bf16[2880,256]{1,0:T(8,128)(2,1)S(1)} %bitcast.20), custom_call_target="tpu_custom_call" | custom-call | tf_op jit(solution)/shard_map/project/pallas_call | solution.py:181
  11.4 0.4 collective-permute-start.1
  11.8 1.9 %collective-permute-done.1 = bf16[128,2944]{1,0:T(8,128)(2,1)S(1)} collective-permute-done((bf16[128,2944]{1,0:T(8,128)(2,1)S(1)}, bf16[128,2944]{1,0:T(8,128)(2,1)S(1)}, u32[]{:S(2)}, u32[]{:S(2)}) %collective-permute-start.1) | collective-permute-done | bytes 753696 | tf_op jit(solution)/shard_map/ppermute | solution.py:38
  13.7 0.2 fusion.13
  13.9 0.0 copy-start.5
  13.9 0.0 copy-start.4
  13.9 2.9 %collective-permute-start.2 = (bf16[32,2880]{1,0:T(8,128)(2,1)S(1)}, bf16[32,2880]{1,0:T(8,128)(2,1)S(1)}, u32[]{:S(2)}, u32[]{:S(2)}) collective-permute-start(bf16[32,2880]{1,0:T(8,128)(2,1)S(1)} %get-tuple-element.23), channel_id=1, source_target_pairs={{0,2},{1,3},{2,0},{3,1},{4,6},{5,7},{6,4},{7,5},{8,10},{9,11},{10,... | collective-permute-start | bytes 552968 | tf_op jit(solution)/shard_map/ppermute | solution.py:38
  16.9 1.5 %collective-permute-start.4 = (bf16[32,2880]{1,0:T(8,128)(2,1)S(1)}, bf16[32,2880]{1,0:T(8,128)(2,1)S(1)}, u32[]{:S(2)}, u32[]{:S(2)}) collective-permute-start(bf16[32,2880]{1,0:T(8,128)(2,1)S(1)} %get-tuple-element.24), channel_id=1, source_target_pairs={{0,6},{1,7},{2,4},{3,5},{4,2},{5,3},{6,0},{7,1},{8,14},{9,15},{10,... | collective-permute-start | bytes 552968 | tf_op jit(solution)/shard_map/ppermute | solution.py:38
  18.4 0.1 collective-permute-start.3
  18.4 7.5 %collective-permute-done.2 = bf16[32,2880]{1,0:T(8,128)(2,1)S(1)} collective-permute-done((bf16[32,2880]{1,0:T(8,128)(2,1)S(1)}, bf16[32,2880]{1,0:T(8,128)(2,1)S(1)}, u32[]{:S(2)}, u32[]{:S(2)}) %collective-permute-start.2) | collective-permute-done | bytes 184352 | tf_op jit(solution)/shard_map/ppermute | solution.py:38
  25.9 0.0 collective-permute-done.4
  25.9 1.3 %collective-permute-done.3 = bf16[32,2880]{1,0:T(8,128)(2,1)S(1)} collective-permute-done((bf16[32,2880]{1,0:T(8,128)(2,1)S(1)}, bf16[32,2880]{1,0:T(8,128)(2,1)S(1)}, u32[]{:S(2)}, u32[]{:S(2)}) %collective-permute-start.3) | collective-permute-done | bytes 184352 | tf_op jit(solution)/shard_map/ppermute | solution.py:38
  27.3 0.1 fusion.3
  27.4 2.8 %collective-permute-start.5 = (bf16[16,2880]{1,0:T(8,128)(2,1)S(1)}, bf16[16,2880]{1,0:T(8,128)(2,1)S(1)}, u32[]{:S(2)}, u32[]{:S(2)}) collective-permute-start(bf16[16,2880]{1,0:T(8,128)(2,1)S(1)} %slice.103), channel_id=1, source_target_pairs={{0,8},{1,9},{2,10},{3,11},{4,12},{5,13},{6,14},{7,15},{8,0},{9,1},... | collective-permute-start | bytes 276488 | tf_op jit(solution)/shard_map/ppermute | solution.py:38
  30.2 0.0 copy-done.5
  30.2 0.1 eq.17
  30.3 4.1 %collective-permute-done.5 = bf16[16,2880]{1,0:T(8,128)(2,1)S(1)} collective-permute-done((bf16[16,2880]{1,0:T(8,128)(2,1)S(1)}, bf16[16,2880]{1,0:T(8,128)(2,1)S(1)}, u32[]{:S(2)}, u32[]{:S(2)}) %collective-permute-start.5) | collective-permute-done | bytes 92192 | tf_op jit(solution)/shard_map/ppermute | solution.py:38
  34.3 0.0 copy-done.4
  34.3 0.2 fusion.4
  34.5 0.1 fusion.5
  34.6 0.0 copy-done
  34.6 0.1 fusion.16
  34.7 0.2 select_reduce_fusion.1
  34.9 0.1 exponential_reduce_fusion
  35.0 0.1 select_reduce_fusion
  35.1 0.1 concatenate.6
  35.2 1.4 %collective-permute-start.6 = (bf16[16,2912]{1,0:T(8,128)(2,1)S(1)}, bf16[16,2912]{1,0:T(8,128)(2,1)S(1)}, u32[]{:S(2)}, u32[]{:S(2)}) collective-permute-start(bf16[16,2912]{1,0:T(8,128)(2,1)S(1)} %concatenate.6), channel_id=1, source_target_pairs={{0,8},{1,9},{2,10},{3,11},{4,12},{5,13},{6,14},{7,15},{8,0},{9,1},... | collective-permute-start | bytes 279560 | tf_op jit(solution)/shard_map/ppermute | solution.py:38
  36.6 5.2 %collective-permute-done.6 = bf16[16,2912]{1,0:T(8,128)(2,1)S(1)} collective-permute-done((bf16[16,2912]{1,0:T(8,128)(2,1)S(1)}, bf16[16,2912]{1,0:T(8,128)(2,1)S(1)}, u32[]{:S(2)}, u32[]{:S(2)}) %collective-permute-start.6) | collective-permute-done | bytes 93216 | tf_op jit(solution)/shard_map/ppermute | solution.py:38
  41.8 1.0 %collective-permute-start.9 = (bf16[32,2912]{1,0:T(8,128)(2,1)S(1)}, bf16[32,2912]{1,0:T(8,128)(2,1)S(1)}, u32[]{:S(2)}, u32[]{:S(2)}) collective-permute-start(bf16[32,2912]{1,0:T(8,128)(2,1)S(1)} %pad_maximum_fusion.refs_0_), channel_id=1, source_target_pairs={{0,6},{1,7},{2,4},{3,5},{4,2},{5,3},{6,0},{7,1},{8,14},{9,15},{10,... | collective-permute-start | bytes 559112 | tf_op jit(solution)/shard_map/ppermute | solution.py:38
  42.8 1.9 %collective-permute-start.8 = (bf16[32,2912]{1,0:T(8,128)(2,1)S(1)}, bf16[32,2912]{1,0:T(8,128)(2,1)S(1)}, u32[]{:S(2)}, u32[]{:S(2)}) collective-permute-start(bf16[32,2912]{1,0:T(8,128)(2,1)S(1)} %pad_maximum_fusion.refs_0_), channel_id=1, source_target_pairs={{0,4},{1,5},{2,6},{3,7},{4,0},{5,1},{6,2},{7,3},{8,12},{9,13},{10,... | collective-permute-start | bytes 559112 | tf_op jit(solution)/shard_map/ppermute | solution.py:38
  44.7 0.7 collective-permute-start.7
  45.3 0.0 collective-permute-start.10
  45.3 3.0 %collective-permute-done.9.refs_3_ = bf16[32,2912]{1,0:T(8,128)(2,1)S(1)} collective-permute-done((bf16[32,2912]{1,0:T(8,128)(2,1)S(1)}, bf16[32,2912]{1,0:T(8,128)(2,1)S(1)}, u32[]{:S(2)}, u32[]{:S(2)}) %collective-permute-start.9) | collective-permute-done | bytes 186400 | tf_op jit(solution)/shard_map/ppermute | solution.py:38
  48.3 0.0 collective-permute-start.13
  48.3 1.9 %collective-permute-done.8.refs_2_ = bf16[32,2912]{1,0:T(8,128)(2,1)S(1)} collective-permute-done((bf16[32,2912]{1,0:T(8,128)(2,1)S(1)}, bf16[32,2912]{1,0:T(8,128)(2,1)S(1)}, u32[]{:S(2)}, u32[]{:S(2)}) %collective-permute-start.8) | collective-permute-done | bytes 186400 | tf_op jit(solution)/shard_map/ppermute | solution.py:38
  50.2 0.0 collective-permute-start.12
  50.2 0.1 collective-permute-done.7.refs_1_
  50.3 0.4 collective-permute-start.11
  50.7 0.0 collective-permute-done.10.refs_4_
  50.8 0.0 collective-permute-done.13.refs_7_
  50.8 0.9 %collective-permute-done.12.refs_6_ = bf16[32,2912]{1,0:T(8,128)(2,1)S(1)} collective-permute-done((bf16[32,2912]{1,0:T(8,128)(2,1)S(1)}, bf16[32,2912]{1,0:T(8,128)(2,1)S(1)}, u32[]{:S(2)}, u32[]{:S(2)}) %collective-permute-start.12) | collective-permute-done | bytes 186400 | tf_op jit(solution)/shard_map/ppermute | solution.py:38
  51.7 0.3 collective-permute-done.11.refs_5_
  51.9 15.2 %experts.1 = (f32[128,2880]{1,0:T(8,128)S(1)}, bf16[128,2944]{1,0:T(8,128)(2,1)S(1)}) custom-call(s32[1]{0:T(128)} %bitcast.1.me_ref, bf16[32,2912]{1,0:T(8,128)(2,1)S(1)} %pad_maximum_fusion.refs_0_, bf16[32,2912]{1,0:T(8,128)(2,1)S(1)} %collective-permute-done.7.refs_1_, bf16[32,2912]{1,0:T(8,128)(2,1)S(1)} %collective-permute-done.8.refs_2_, ...), custom_call_target="tpu_custom_call" | custom-call | tf_op jit(solution)/shard_map/experts/pallas_call | solution.py:265
  67.1 0.3 collective-permute-start.14
  67.4 2.0 %collective-permute-done.14 = bf16[128,2944]{1,0:T(8,128)(2,1)S(1)} collective-permute-done((bf16[128,2944]{1,0:T(8,128)(2,1)S(1)}, bf16[128,2944]{1,0:T(8,128)(2,1)S(1)}, u32[]{:S(2)}, u32[]{:S(2)}) %collective-permute-start.14) | collective-permute-done | bytes 753696 | tf_op jit(solution)/shard_map/ppermute | solution.py:38
  69.4 0.2 fusion.11
  69.6 1.3 %collective-permute-start.15 = (bf16[32,2880]{1,0:T(8,128)(2,1)S(1)}, bf16[32,2880]{1,0:T(8,128)(2,1)S(1)}, u32[]{:S(2)}, u32[]{:S(2)}) collective-permute-start(bf16[32,2880]{1,0:T(8,128)(2,1)S(1)} %get-tuple-element.20), channel_id=1, source_target_pairs={{0,2},{1,3},{2,0},{3,1},{4,6},{5,7},{6,4},{7,5},{8,10},{9,11},{10,... | collective-permute-start | bytes 552968 | tf_op jit(solution)/shard_map/ppermute | solution.py:38
  70.9 1.0 %collective-permute-start.17 = (bf16[32,2880]{1,0:T(8,128)(2,1)S(1)}, bf16[32,2880]{1,0:T(8,128)(2,1)S(1)}, u32[]{:S(2)}, u32[]{:S(2)}) collective-permute-start(bf16[32,2880]{1,0:T(8,128)(2,1)S(1)} %get-tuple-element.21), channel_id=1, source_target_pairs={{0,6},{1,7},{2,4},{3,5},{4,2},{5,3},{6,0},{7,1},{8,14},{9,15},{10,... | collective-permute-start | bytes 552968 | tf_op jit(solution)/shard_map/ppermute | solution.py:38
  71.9 1.3 %collective-permute-start.16 = (bf16[32,2880]{1,0:T(8,128)(2,1)S(1)}, bf16[32,2880]{1,0:T(8,128)(2,1)S(1)}, u32[]{:S(2)}, u32[]{:S(2)}) collective-permute-start(bf16[32,2880]{1,0:T(8,128)(2,1)S(1)} %get-tuple-element.22), channel_id=1, source_target_pairs={{0,4},{1,5},{2,6},{3,7},{4,0},{5,1},{6,2},{7,3},{8,12},{9,13},{10,... | collective-permute-start | bytes 552968 | tf_op jit(solution)/shard_map/ppermute | solution.py:38
  73.2 7.4 %collective-permute-done.15 = bf16[32,2880]{1,0:T(8,128)(2,1)S(1)} collective-permute-done((bf16[32,2880]{1,0:T(8,128)(2,1)S(1)}, bf16[32,2880]{1,0:T(8,128)(2,1)S(1)}, u32[]{:S(2)}, u32[]{:S(2)}) %collective-permute-start.15) | collective-permute-done | bytes 184352 | tf_op jit(solution)/shard_map/ppermute | solution.py:38
  80.6 0.0 collective-permute-done.17
  80.6 1.2 %collective-permute-done.16 = bf16[32,2880]{1,0:T(8,128)(2,1)S(1)} collective-permute-done((bf16[32,2880]{1,0:T(8,128)(2,1)S(1)}, bf16[32,2880]{1,0:T(8,128)(2,1)S(1)}, u32[]{:S(2)}, u32[]{:S(2)}) %collective-permute-start.16) | collective-permute-done | bytes 184352 | tf_op jit(solution)/shard_map/ppermute | solution.py:38
  81.8 0.1 fusion.1
  81.9 1.1 %collective-permute-start.18 = (bf16[16,2880]{1,0:T(8,128)(2,1)S(1)}, bf16[16,2880]{1,0:T(8,128)(2,1)S(1)}, u32[]{:S(2)}, u32[]{:S(2)}) collective-permute-start(bf16[16,2880]{1,0:T(8,128)(2,1)S(1)} %slice.102), channel_id=1, source_target_pairs={{0,8},{1,9},{2,10},{3,11},{4,12},{5,13},{6,14},{7,15},{8,0},{9,1},... | collective-permute-start | bytes 276488 | tf_op jit(solution)/shard_map/ppermute | solution.py:38
  83.0 5.6 %collective-permute-done.18 = bf16[16,2880]{1,0:T(8,128)(2,1)S(1)} collective-permute-done((bf16[16,2880]{1,0:T(8,128)(2,1)S(1)}, bf16[16,2880]{1,0:T(8,128)(2,1)S(1)}, u32[]{:S(2)}, u32[]{:S(2)}) %collective-permute-start.18) | collective-permute-done | bytes 92192 | tf_op jit(solution)/shard_map/ppermute | solution.py:38
  88.6 0.0 copy-done.3
  88.6 0.7 fusion.9
  (11 shorter events, 0.1 us)
Async XLA Ops:
  0.6 34.0 %copy-start = (bf16[2880,16]{0,1:T(8,128)(2,1)S(1)}, bf16[2880,16]{0,1:T(8,128)(2,1)}, u32[]{:S(2)}) copy-start(bf16[2880,16]{0,1:T(8,128)(2,1)} %param.17) | copy-start | bytes 276484
  0.7 8.9 %copy-start.1 = (bf16[256,2880]{0,1:T(8,128)(2,1)S(1)}, bf16[256,2880]{0,1:T(8,128)(2,1)}, u32[]{:S(2)}) copy-start(bf16[256,2880]{0,1:T(8,128)(2,1)} %param.16) | copy-start | bytes 4423684
  8.0 1.6 %collective-permute-start = (bf16[2,64,256]{2,1,0:T(8,128)(2,1)}, bf16[2,64,256]{2,1,0:T(8,128)(2,1)S(1)}, u32[]{:S(2)}, u32[]{:S(2)}) collective-permute-start(bf16[2,64,256]{2,1,0:T(8,128)(2,1)} %get-tuple-element.9), channel_id=1, source_target_pairs={{0,1},{1,0},{2,3},{3,2},{4,5},{5,4},{6,7},{7,6},{8,9},{9,8},{10,11... | collective-permute-start | bytes 196616 | tf_op jit(solution)/shard_map/ppermute | solution.py:38
  9.5 0.8 copy-start.2
  11.4 2.3 %collective-permute-start.1 = (bf16[128,2944]{1,0:T(8,128)(2,1)S(1)}, bf16[128,2944]{1,0:T(8,128)(2,1)S(1)}, u32[]{:S(2)}, u32[]{:S(2)}) collective-permute-start(bf16[128,2944]{1,0:T(8,128)(2,1)S(1)} %get-tuple-element.11), channel_id=1, source_target_pairs={{0,1},{1,0},{2,3},{3,2},{4,5},{5,4},{6,7},{7,6},{8,9},{9,8},{10,11... | collective-permute-start | bytes 2261000 | tf_op jit(solution)/shard_map/ppermute | solution.py:38
  13.9 16.3 %copy-start.5 = (s32[2,8,4]{1,2,0:T(4,128)S(1)}, s32[2,8,4]{1,2,0:T(4,128)}, u32[]{:S(2)}) copy-start(s32[2,8,4]{1,2,0:T(4,128)} %param.21) | copy-start | bytes 772
  13.9 20.5 %copy-start.4 = (bf16[2,8,2880]{2,1,0:T(8,128)(2,1)S(1)}, bf16[2,8,2880]{2,1,0:T(8,128)(2,1)}, u32[]{:S(2)}) copy-start(bf16[2,8,2880]{2,1,0:T(8,128)(2,1)} %param.15) | copy-start | bytes 276484
  13.9 12.0 %collective-permute-start.2 = (bf16[32,2880]{1,0:T(8,128)(2,1)S(1)}, bf16[32,2880]{1,0:T(8,128)(2,1)S(1)}, u32[]{:S(2)}, u32[]{:S(2)}) collective-permute-start(bf16[32,2880]{1,0:T(8,128)(2,1)S(1)} %get-tuple-element.23), channel_id=1, source_target_pairs={{0,2},{1,3},{2,0},{3,1},{4,6},{5,7},{6,4},{7,5},{8,10},{9,11},{10,... | collective-permute-start | bytes 552968 | tf_op jit(solution)/shard_map/ppermute | solution.py:38
  16.9 9.1 %collective-permute-start.4 = (bf16[32,2880]{1,0:T(8,128)(2,1)S(1)}, bf16[32,2880]{1,0:T(8,128)(2,1)S(1)}, u32[]{:S(2)}, u32[]{:S(2)}) collective-permute-start(bf16[32,2880]{1,0:T(8,128)(2,1)S(1)} %get-tuple-element.24), channel_id=1, source_target_pairs={{0,6},{1,7},{2,4},{3,5},{4,2},{5,3},{6,0},{7,1},{8,14},{9,15},{10,... | collective-permute-start | bytes 552968 | tf_op jit(solution)/shard_map/ppermute | solution.py:38
  18.4 8.9 %collective-permute-start.3 = (bf16[32,2880]{1,0:T(8,128)(2,1)S(1)}, bf16[32,2880]{1,0:T(8,128)(2,1)S(1)}, u32[]{:S(2)}, u32[]{:S(2)}) collective-permute-start(bf16[32,2880]{1,0:T(8,128)(2,1)S(1)} %get-tuple-element.25), channel_id=1, source_target_pairs={{0,4},{1,5},{2,6},{3,7},{4,0},{5,1},{6,2},{7,3},{8,12},{9,13},{10,... | collective-permute-start | bytes 552968 | tf_op jit(solution)/shard_map/ppermute | solution.py:38
  27.4 6.9 %collective-permute-start.5 = (bf16[16,2880]{1,0:T(8,128)(2,1)S(1)}, bf16[16,2880]{1,0:T(8,128)(2,1)S(1)}, u32[]{:S(2)}, u32[]{:S(2)}) collective-permute-start(bf16[16,2880]{1,0:T(8,128)(2,1)S(1)} %slice.103), channel_id=1, source_target_pairs={{0,8},{1,9},{2,10},{3,11},{4,12},{5,13},{6,14},{7,15},{8,0},{9,1},... | collective-permute-start | bytes 276488 | tf_op jit(solution)/shard_map/ppermute | solution.py:38
  34.5 54.1 %copy-start.3 = (bf16[16,2880]{1,0:T(8,128)(2,1)}, bf16[16,2880]{1,0:T(8,128)(2,1)S(1)}, u32[]{:S(2)}) copy-start(bf16[16,2880]{1,0:T(8,128)(2,1)S(1)} %get-tuple-element.17) | copy-start | bytes 276484
  35.2 6.6 %collective-permute-start.6 = (bf16[16,2912]{1,0:T(8,128)(2,1)S(1)}, bf16[16,2912]{1,0:T(8,128)(2,1)S(1)}, u32[]{:S(2)}, u32[]{:S(2)}) collective-permute-start(bf16[16,2912]{1,0:T(8,128)(2,1)S(1)} %concatenate.6), channel_id=1, source_target_pairs={{0,8},{1,9},{2,10},{3,11},{4,12},{5,13},{6,14},{7,15},{8,0},{9,1},... | collective-permute-start | bytes 279560 | tf_op jit(solution)/shard_map/ppermute | solution.py:38
  41.8 6.6 %collective-permute-start.9 = (bf16[32,2912]{1,0:T(8,128)(2,1)S(1)}, bf16[32,2912]{1,0:T(8,128)(2,1)S(1)}, u32[]{:S(2)}, u32[]{:S(2)}) collective-permute-start(bf16[32,2912]{1,0:T(8,128)(2,1)S(1)} %pad_maximum_fusion.refs_0_), channel_id=1, source_target_pairs={{0,6},{1,7},{2,4},{3,5},{4,2},{5,3},{6,0},{7,1},{8,14},{9,15},{10,... | collective-permute-start | bytes 559112 | tf_op jit(solution)/shard_map/ppermute | solution.py:38
  42.8 7.5 %collective-permute-start.8 = (bf16[32,2912]{1,0:T(8,128)(2,1)S(1)}, bf16[32,2912]{1,0:T(8,128)(2,1)S(1)}, u32[]{:S(2)}, u32[]{:S(2)}) collective-permute-start(bf16[32,2912]{1,0:T(8,128)(2,1)S(1)} %pad_maximum_fusion.refs_0_), channel_id=1, source_target_pairs={{0,4},{1,5},{2,6},{3,7},{4,0},{5,1},{6,2},{7,3},{8,12},{9,13},{10,... | collective-permute-start | bytes 559112 | tf_op jit(solution)/shard_map/ppermute | solution.py:38
  44.7 5.7 %collective-permute-start.7 = (bf16[32,2912]{1,0:T(8,128)(2,1)S(1)}, bf16[32,2912]{1,0:T(8,128)(2,1)S(1)}, u32[]{:S(2)}, u32[]{:S(2)}) collective-permute-start(bf16[32,2912]{1,0:T(8,128)(2,1)S(1)} %pad_maximum_fusion.refs_0_), channel_id=1, source_target_pairs={{0,2},{1,3},{2,0},{3,1},{4,6},{5,7},{6,4},{7,5},{8,10},{9,11},{10,... | collective-permute-start | bytes 559112 | tf_op jit(solution)/shard_map/ppermute | solution.py:38
  45.3 5.4 %collective-permute-start.10 = (bf16[32,2912]{1,0:T(8,128)(2,1)S(1)}, bf16[32,2912]{1,0:T(8,128)(2,1)S(1)}, u32[]{:S(2)}, u32[]{:S(2)}) collective-permute-start(bf16[32,2912]{1,0:T(8,128)(2,1)S(1)} %pad_maximum_fusion.refs_0_), channel_id=1, source_target_pairs={{0,1},{1,0},{2,3},{3,2},{4,5},{5,4},{6,7},{7,6},{8,9},{9,8},{10,11... | collective-permute-start | bytes 559112 | tf_op jit(solution)/shard_map/ppermute | solution.py:38
  48.3 2.4 %collective-permute-start.13 = (bf16[32,2912]{1,0:T(8,128)(2,1)S(1)}, bf16[32,2912]{1,0:T(8,128)(2,1)S(1)}, u32[]{:S(2)}, u32[]{:S(2)}) collective-permute-start(bf16[32,2912]{1,0:T(8,128)(2,1)S(1)} %collective-permute-done.9.refs_3_), channel_id=1, source_target_pairs={{0,1},{1,0},{2,3},{3,2},{4,5},{5,4},{6,7},{7,6},{8,9},{9,8},{10,11... | collective-permute-start | bytes 559112 | tf_op jit(solution)/shard_map/ppermute | solution.py:38
  50.2 1.4 %collective-permute-start.12 = (bf16[32,2912]{1,0:T(8,128)(2,1)S(1)}, bf16[32,2912]{1,0:T(8,128)(2,1)S(1)}, u32[]{:S(2)}, u32[]{:S(2)}) collective-permute-start(bf16[32,2912]{1,0:T(8,128)(2,1)S(1)} %collective-permute-done.8.refs_2_), channel_id=1, source_target_pairs={{0,1},{1,0},{2,3},{3,2},{4,5},{5,4},{6,7},{7,6},{8,9},{9,8},{10,11... | collective-permute-start | bytes 559112 | tf_op jit(solution)/shard_map/ppermute | solution.py:38
  50.3 1.6 %collective-permute-start.11 = (bf16[32,2912]{1,0:T(8,128)(2,1)S(1)}, bf16[32,2912]{1,0:T(8,128)(2,1)S(1)}, u32[]{:S(2)}, u32[]{:S(2)}) collective-permute-start(bf16[32,2912]{1,0:T(8,128)(2,1)S(1)} %collective-permute-done.7.refs_1_), channel_id=1, source_target_pairs={{0,1},{1,0},{2,3},{3,2},{4,5},{5,4},{6,7},{7,6},{8,9},{9,8},{10,11... | collective-permute-start | bytes 559112 | tf_op jit(solution)/shard_map/ppermute | solution.py:38
  67.1 2.3 %collective-permute-start.14 = (bf16[128,2944]{1,0:T(8,128)(2,1)S(1)}, bf16[128,2944]{1,0:T(8,128)(2,1)S(1)}, u32[]{:S(2)}, u32[]{:S(2)}) collective-permute-start(bf16[128,2944]{1,0:T(8,128)(2,1)S(1)} %get-tuple-element.13), channel_id=1, source_target_pairs={{0,1},{1,0},{2,3},{3,2},{4,5},{5,4},{6,7},{7,6},{8,9},{9,8},{10,11... | collective-permute-start | bytes 2261000 | tf_op jit(solution)/shard_map/ppermute | solution.py:38
  69.6 11.0 %collective-permute-start.15 = (bf16[32,2880]{1,0:T(8,128)(2,1)S(1)}, bf16[32,2880]{1,0:T(8,128)(2,1)S(1)}, u32[]{:S(2)}, u32[]{:S(2)}) collective-permute-start(bf16[32,2880]{1,0:T(8,128)(2,1)S(1)} %get-tuple-element.20), channel_id=1, source_target_pairs={{0,2},{1,3},{2,0},{3,1},{4,6},{5,7},{6,4},{7,5},{8,10},{9,11},{10,... | collective-permute-start | bytes 552968 | tf_op jit(solution)/shard_map/ppermute | solution.py:38
  70.9 9.7 %collective-permute-start.17 = (bf16[32,2880]{1,0:T(8,128)(2,1)S(1)}, bf16[32,2880]{1,0:T(8,128)(2,1)S(1)}, u32[]{:S(2)}, u32[]{:S(2)}) collective-permute-start(bf16[32,2880]{1,0:T(8,128)(2,1)S(1)} %get-tuple-element.21), channel_id=1, source_target_pairs={{0,6},{1,7},{2,4},{3,5},{4,2},{5,3},{6,0},{7,1},{8,14},{9,15},{10,... | collective-permute-start | bytes 552968 | tf_op jit(solution)/shard_map/ppermute | solution.py:38
  71.9 10.0 %collective-permute-start.16 = (bf16[32,2880]{1,0:T(8,128)(2,1)S(1)}, bf16[32,2880]{1,0:T(8,128)(2,1)S(1)}, u32[]{:S(2)}, u32[]{:S(2)}) collective-permute-start(bf16[32,2880]{1,0:T(8,128)(2,1)S(1)} %get-tuple-element.22), channel_id=1, source_target_pairs={{0,4},{1,5},{2,6},{3,7},{4,0},{5,1},{6,2},{7,3},{8,12},{9,13},{10,... | collective-permute-start | bytes 552968 | tf_op jit(solution)/shard_map/ppermute | solution.py:38
  81.9 6.7 %collective-permute-start.18 = (bf16[16,2880]{1,0:T(8,128)(2,1)S(1)}, bf16[16,2880]{1,0:T(8,128)(2,1)S(1)}, u32[]{:S(2)}, u32[]{:S(2)}) collective-permute-start(bf16[16,2880]{1,0:T(8,128)(2,1)S(1)} %slice.102), channel_id=1, source_target_pairs={{0,8},{1,9},{2,10},{3,11},{4,12},{5,13},{6,14},{7,15},{8,0},{9,1},... | collective-permute-start | bytes 276488 | tf_op jit(solution)/shard_map/ppermute | solution.py:38

commit v4 on v3

--- a/solution.py
+++ b/solution.py
@@ -191,43 +191,26 @@
             pltpu.VMEM((count, width), jnp.float32),
         ],
         compiler_params=pltpu.CompilerParams(vmem_limit_bytes=LIMIT),
+        cost_estimate=pl.CostEstimate(flops=60000000000, bytes_accessed=150000000, transcendentals=0),
         name="project",
     )(me, *held, weight)
 
 
 def expert_kernel(count, hidden, me_ref, *refs):
     pieces = refs[:count]
-    w_gate, far_up, far_down = refs[count : count + 3]
+    w_gate, w_up, w_down = refs[count : count + 3]
     keep, send = refs[count + 3 : count + 5]
-    rows, gates, active, w_up, w_down, up_done, down_done = refs[count + 5 :]
+    rows, active = refs[count + 5 :]
     units, width = w_gate.shape
-    tiles = [slice(start, min(start + TILE, units)) for start in range(0, units, TILE)]
-    up_copies, down_copies = [
-        [
-            pltpu.make_async_copy(
-                far.at[pl.ds(some.start, some.stop - some.start)],
-                near.at[pl.ds(some.start, some.stop - some.start)],
-                done.at[index],
-            )
-            for index, some in enumerate(tiles)
-        ]
-        for far, near, done in ((far_up, w_up, up_done), (far_down, w_down, down_done))
-    ]
-    for copy in up_copies:
-        copy.start()
     at = 0
     for piece in pieces:
         rows[at : at + piece.shape[0], :] = piece[...]
         at += piece.shape[0]
-    for some in tiles:
-        gates[:, some] = lax.dot_general(
+    for start in range(0, units, TILE):
+        some = slice(start, min(start + TILE, units))
+        gate = lax.dot_general(
             rows[:, :width], w_gate[some, :], ROWS_LAST, preferred_element_type=jnp.float32
         )
-    for copy in down_copies:
-        copy.start()
-    for copy, some in zip(up_copies, tiles):
-        copy.wait()
-        gate = gates[:, some]
         up = lax.dot_general(
             rows[:, :width], w_up[some, :], ROWS_LAST, preferred_element_type=jnp.float32
         )
@@ -242,8 +225,6 @@
         picked = (lane == expert) | (lane == expert + EXPERTS)
         weights.append(jnp.sum(jnp.where(picked, tail, 0.0), axis=1, keepdims=True))
     half = keep.shape[0]
-    for copy in down_copies:
-        copy.wait()
     for start in range(0, width, 2 * TILE):
         some = slice(start, min(start + 2 * TILE, width))
         out = 0.0
@@ -261,26 +242,19 @@
     units = w_down.shape[0] * hidden
     count = sum(piece.shape[0] for piece in pieces)
     whole = pl.BlockSpec(memory_space=pltpu.VMEM)
-    tiles = pl.cdiv(units, TILE)
     return pl.pallas_call(
         functools.partial(expert_kernel, len(pieces), hidden),
         out_shape=[
             jax.ShapeDtypeStruct((count // 2, width), jnp.float32),
             jax.ShapeDtypeStruct((count // 2, pl.cdiv(width, 128) * 128), jnp.bfloat16),
         ],
-        in_specs=[pl.BlockSpec(memory_space=pltpu.SMEM)] + [whole] * (len(pieces) + 1)
-        + [pl.BlockSpec(memory_space=pl.ANY)] * 2,
+        in_specs=[pl.BlockSpec(memory_space=pltpu.SMEM)] + [whole] * (len(pieces) + 3),
         out_specs=[whole] * 2,
         scratch_shapes=[
             pltpu.VMEM((count, pieces[0].shape[1]), jnp.bfloat16),
-            pltpu.VMEM((count, units), jnp.float32),
             pltpu.VMEM((count, units), jnp.bfloat16),
-            pltpu.VMEM((units, width), jnp.bfloat16),
-            pltpu.VMEM((units, width), jnp.bfloat16),
-            pltpu.SemaphoreType.DMA((tiles,)),
-            pltpu.SemaphoreType.DMA((tiles,)),
         ],
-        compiler_params=pltpu.CompilerParams(vmem_limit_bytes=50 << 20),
+        compiler_params=pltpu.CompilerParams(vmem_limit_bytes=LIMIT),
         name="experts",
     )(
         me,

time: 89.6 us -> 92.4 us (1.031)
  local copies, waits for them, and re-layouts: 1.16 us -> 11.4 us
  Pallas kernels: 23.5 us -> 15.9 us
    unnamed x13 -> x19, local copies, waits for them, and re-layouts: 0.87 us -> 11.1 us
    pallas_call x1, Pallas kernels: 15.2 us -> 7.62 us  [expert_sums(): pl.pallas_call(functools.partial(expert_kernel, len(pieces), hidden), out...]
where the time goes in v4:
time: 92.4 us; the launch traced here: 92 us
  waiting for transfers between devices  43.5 us (47%)
  starting transfers between devices  18.5 us (20%)
  Pallas kernels  15.9 us (17%)
  local copies, waits for them, and re-layouts  11.4 us (12%)
  other arithmetic  1.74 us (2%)
    ppermute x19, waiting for transfers between devices, from_mask(): return lax.ppermute(value, 'req', pairs)  43.5 us
    ppermute x19, starting transfers between devices, from_mask(): return lax.ppermute(value, 'req', pairs)  18.5 us
    unnamed x19, local copies, waits for them, and re-layouts  11.1 us
    pallas_call x1, Pallas kernels, expert_sums(): pl.pallas_call(functools.partial(expert_kernel, len(pieces), hidden), out...  7.62 us
    pallas_call x1, Pallas kernels, attention(): pl.pallas_call(functools.partial(attention_kernel, group, rows // block),...  7.29 us
  transfers between devices with their start and end apart: 19, of which 15 were waited for; matrix products, arithmetic and copies ran while one was open for 0% of the time, Pallas kernels for 0%

profile of v4, /device:TPU:0, one launch (start us, length us, event | category | flops | bytes accessed | tf_op | source)
XLA Modules:
  0.0 92.0 jit_solution(1987762799699200961)
XLA Ops:
  0.6 0.0 copy-start
  0.7 0.0 copy-start.4
  0.7 7.3 %attention.1 = (bf16[2,64,256]{2,1,0:T(8,128)(2,1)}, bf16[2,64,256]{2,1,0:T(8,128)(2,1)}) custom-call(s32[2,128]{1,0:T(2,128)} %lengths.1, s32[1]{0:T(128)S(6)} %select_n.15.place, bf16[2,64,512]{2,1,0:T(8,128)(2,1)} %q_ref.1, bf16[2,64,128]{2,1,0:T(8,128)(2,1)} %kv_ref.1, bf16[2,64,128,128]{3,2,1,0:T(8,128)(2,1)} %cache_ref.1), custom_call_target="tpu_custom_call" | custom-call | tf_op jit(solution)/shard_map/attention/pallas_call | solution.py:123
  8.0 0.5 collective-permute-start
  8.4 1.1 %collective-permute-done.refs_1_ = bf16[2,64,256]{2,1,0:T(8,128)(2,1)S(1)} collective-permute-done((bf16[2,64,256]{2,1,0:T(8,128)(2,1)}, bf16[2,64,256]{2,1,0:T(8,128)(2,1)S(1)}, u32[]{:S(2)}, u32[]{:S(2)}) %collective-permute-start) | collective-permute-done | bytes 65568 | tf_op jit(solution)/shard_map/ppermute | solution.py:38
  9.5 0.0 copy-done.4
  9.5 0.8 copy-done.5
  10.4 1.0 %project.1 = (f32[128,2880]{1,0:T(8,128)S(1)}, bf16[128,2944]{1,0:T(8,128)(2,1)S(1)}) custom-call(s32[1]{0:T(128)} %bitcast.1.me_ref, bf16[2,64,256]{2,1,0:T(8,128)(2,1)S(1)} %copy-done.5, bf16[2,64,256]{2,1,0:T(8,128)(2,1)S(1)} %collective-permute-done.refs_1_, bf16[2880,256]{1,0:T(8,128)(2,1)S(1)} %bitcast.23), custom_call_target="tpu_custom_call" | custom-call | flops 60000002048 | bytes 150000000 | tf_op jit(solution)/shard_map/project/pallas_call | solution.py:181
  11.4 0.4 collective-permute-start.1
  11.8 1.9 %collective-permute-done.1 = bf16[128,2944]{1,0:T(8,128)(2,1)S(1)} collective-permute-done((bf16[128,2944]{1,0:T(8,128)(2,1)S(1)}, bf16[128,2944]{1,0:T(8,128)(2,1)S(1)}, u32[]{:S(2)}, u32[]{:S(2)}) %collective-permute-start.1) | collective-permute-done | bytes 753696 | tf_op jit(solution)/shard_map/ppermute | solution.py:38
  13.7 0.2 fusion.13
  13.9 0.0 copy-start.8
  13.9 0.0 copy-start.7
  13.9 2.9 %collective-permute-start.2 = (bf16[32,2880]{1,0:T(8,128)(2,1)S(1)}, bf16[32,2880]{1,0:T(8,128)(2,1)S(1)}, u32[]{:S(2)}, u32[]{:S(2)}) collective-permute-start(bf16[32,2880]{1,0:T(8,128)(2,1)S(1)} %get-tuple-element.23), channel_id=1, source_target_pairs={{0,2},{1,3},{2,0},{3,1},{4,6},{5,7},{6,4},{7,5},{8,10},{9,11},{10,... | collective-permute-start | bytes 552968 | tf_op jit(solution)/shard_map/ppermute | solution.py:38
  16.9 1.5 %collective-permute-start.4 = (bf16[32,2880]{1,0:T(8,128)(2,1)S(1)}, bf16[32,2880]{1,0:T(8,128)(2,1)S(1)}, u32[]{:S(2)}, u32[]{:S(2)}) collective-permute-start(bf16[32,2880]{1,0:T(8,128)(2,1)S(1)} %get-tuple-element.24), channel_id=1, source_target_pairs={{0,6},{1,7},{2,4},{3,5},{4,2},{5,3},{6,0},{7,1},{8,14},{9,15},{10,... | collective-permute-start | bytes 552968 | tf_op jit(solution)/shard_map/ppermute | solution.py:38
  18.4 0.1 collective-permute-start.3
  18.4 7.5 %collective-permute-done.2 = bf16[32,2880]{1,0:T(8,128)(2,1)S(1)} collective-permute-done((bf16[32,2880]{1,0:T(8,128)(2,1)S(1)}, bf16[32,2880]{1,0:T(8,128)(2,1)S(1)}, u32[]{:S(2)}, u32[]{:S(2)}) %collective-permute-start.2) | collective-permute-done | bytes 184352 | tf_op jit(solution)/shard_map/ppermute | solution.py:38
  25.9 0.0 collective-permute-done.4
  25.9 1.3 %collective-permute-done.3 = bf16[32,2880]{1,0:T(8,128)(2,1)S(1)} collective-permute-done((bf16[32,2880]{1,0:T(8,128)(2,1)S(1)}, bf16[32,2880]{1,0:T(8,128)(2,1)S(1)}, u32[]{:S(2)}, u32[]{:S(2)}) %collective-permute-start.3) | collective-permute-done | bytes 184352 | tf_op jit(solution)/shard_map/ppermute | solution.py:38
  27.3 0.1 fusion.3
  27.4 2.8 %collective-permute-start.5 = (bf16[16,2880]{1,0:T(8,128)(2,1)S(1)}, bf16[16,2880]{1,0:T(8,128)(2,1)S(1)}, u32[]{:S(2)}, u32[]{:S(2)}) collective-permute-start(bf16[16,2880]{1,0:T(8,128)(2,1)S(1)} %slice.103), channel_id=1, source_target_pairs={{0,8},{1,9},{2,10},{3,11},{4,12},{5,13},{6,14},{7,15},{8,0},{9,1},... | collective-permute-start | bytes 276488 | tf_op jit(solution)/shard_map/ppermute | solution.py:38
  30.2 0.0 copy-done.8
  30.2 0.1 eq.17
  30.3 4.1 %collective-permute-done.5 = bf16[16,2880]{1,0:T(8,128)(2,1)S(1)} collective-permute-done((bf16[16,2880]{1,0:T(8,128)(2,1)S(1)}, bf16[16,2880]{1,0:T(8,128)(2,1)S(1)}, u32[]{:S(2)}, u32[]{:S(2)}) %collective-permute-start.5) | collective-permute-done | bytes 92192 | tf_op jit(solution)/shard_map/ppermute | solution.py:38
  34.3 0.2 fusion.4
  34.5 0.1 fusion.5
  34.6 0.1 fusion.16
  34.7 0.2 select_reduce_fusion.1
  34.9 0.1 exponential_reduce_fusion
  35.0 0.1 select_reduce_fusion
  35.1 0.1 concatenate.6
  35.2 1.4 %collective-permute-start.6 = (bf16[16,2912]{1,0:T(8,128)(2,1)S(1)}, bf16[16,2912]{1,0:T(8,128)(2,1)S(1)}, u32[]{:S(2)}, u32[]{:S(2)}) collective-permute-start(bf16[16,2912]{1,0:T(8,128)(2,1)S(1)} %concatenate.6), channel_id=1, source_target_pairs={{0,8},{1,9},{2,10},{3,11},{4,12},{5,13},{6,14},{7,15},{8,0},{9,1},... | collective-permute-start | bytes 279560 | tf_op jit(solution)/shard_map/ppermute | solution.py:38
  36.6 5.2 %collective-permute-done.6 = bf16[16,2912]{1,0:T(8,128)(2,1)S(1)} collective-permute-done((bf16[16,2912]{1,0:T(8,128)(2,1)S(1)}, bf16[16,2912]{1,0:T(8,128)(2,1)S(1)}, u32[]{:S(2)}, u32[]{:S(2)}) %collective-permute-start.6) | collective-permute-done | bytes 93216 | tf_op jit(solution)/shard_map/ppermute | solution.py:38
  41.8 1.0 %collective-permute-start.9 = (bf16[32,2912]{1,0:T(8,128)(2,1)S(1)}, bf16[32,2912]{1,0:T(8,128)(2,1)S(1)}, u32[]{:S(2)}, u32[]{:S(2)}) collective-permute-start(bf16[32,2912]{1,0:T(8,128)(2,1)S(1)} %pad_maximum_fusion.refs_0_), channel_id=1, source_target_pairs={{0,6},{1,7},{2,4},{3,5},{4,2},{5,3},{6,0},{7,1},{8,14},{9,15},{10,... | collective-permute-start | bytes 559112 | tf_op jit(solution)/shard_map/ppermute | solution.py:38
  42.8 1.9 %collective-permute-start.8 = (bf16[32,2912]{1,0:T(8,128)(2,1)S(1)}, bf16[32,2912]{1,0:T(8,128)(2,1)S(1)}, u32[]{:S(2)}, u32[]{:S(2)}) collective-permute-start(bf16[32,2912]{1,0:T(8,128)(2,1)S(1)} %pad_maximum_fusion.refs_0_), channel_id=1, source_target_pairs={{0,4},{1,5},{2,6},{3,7},{4,0},{5,1},{6,2},{7,3},{8,12},{9,13},{10,... | collective-permute-start | bytes 559112 | tf_op jit(solution)/shard_map/ppermute | solution.py:38
  44.7 0.7 collective-permute-start.7
  45.3 0.0 collective-permute-start.10
  45.3 3.0 %collective-permute-done.9.refs_3_ = bf16[32,2912]{1,0:T(8,128)(2,1)S(1)} collective-permute-done((bf16[32,2912]{1,0:T(8,128)(2,1)S(1)}, bf16[32,2912]{1,0:T(8,128)(2,1)S(1)}, u32[]{:S(2)}, u32[]{:S(2)}) %collective-permute-start.9) | collective-permute-done | bytes 186400 | tf_op jit(solution)/shard_map/ppermute | solution.py:38
  48.3 0.0 collective-permute-start.13
  48.3 1.9 %collective-permute-done.8.refs_2_ = bf16[32,2912]{1,0:T(8,128)(2,1)S(1)} collective-permute-done((bf16[32,2912]{1,0:T(8,128)(2,1)S(1)}, bf16[32,2912]{1,0:T(8,128)(2,1)S(1)}, u32[]{:S(2)}, u32[]{:S(2)}) %collective-permute-start.8) | collective-permute-done | bytes 186400 | tf_op jit(solution)/shard_map/ppermute | solution.py:38
  50.2 0.0 collective-permute-start.12
  50.2 0.1 collective-permute-done.7.refs_1_
  50.3 0.4 collective-permute-start.11
  50.7 0.0 collective-permute-done.10.refs_4_
  50.8 0.0 collective-permute-done.13.refs_7_
  50.8 0.9 collective-permute-done.12.refs_6_
  51.7 0.3 collective-permute-done.11.refs_5_
  51.9 3.4 %copy-done.1 = bf16[4,2880,360]{1,2,0:T(8,128)(2,1)S(1)} copy-done((bf16[4,2880,360]{1,2,0:T(8,128)(2,1)S(1)}, bf16[4,2880,360]{1,2,0:T(8,128)(2,1)}, u32[]{:S(2)}) %copy-start.1) | copy-done | bytes 8294424
  55.3 3.4 %copy-done.2 = bf16[4,2880,360]{1,2,0:T(8,128)(2,1)S(1)} copy-done((bf16[4,2880,360]{1,2,0:T(8,128)(2,1)S(1)}, bf16[4,2880,360]{1,2,0:T(8,128)(2,1)}, u32[]{:S(2)}) %copy-start.2) | copy-done | bytes 8294424
  58.8 3.4 %copy-done.3 = bf16[4,360,2880]{2,1,0:T(8,128)(2,1)S(1)} copy-done((bf16[4,360,2880]{2,1,0:T(8,128)(2,1)S(1)}, bf16[4,360,2880]{2,1,0:T(8,128)(2,1)}, u32[]{:S(2)}) %copy-start.3) | copy-done | bytes 8294424
  62.2 7.6 %experts.1 = (f32[128,2880]{1,0:T(8,128)S(1)}, bf16[128,2944]{1,0:T(8,128)(2,1)S(1)}) custom-call(s32[1]{0:T(128)} %bitcast.1.me_ref, bf16[32,2912]{1,0:T(8,128)(2,1)S(1)} %pad_maximum_fusion.refs_0_, bf16[32,2912]{1,0:T(8,128)(2,1)S(1)} %collective-permute-done.7.refs_1_, bf16[32,2912]{1,0:T(8,128)(2,1)S(1)} %collective-permute-done.8.refs_2_, ...), custom_call_target="tpu_custom_call" | custom-call | tf_op jit(solution)/shard_map/experts/pallas_call | solution.py:245
  69.8 0.3 collective-permute-start.14
  70.1 2.0 %collective-permute-done.14 = bf16[128,2944]{1,0:T(8,128)(2,1)S(1)} collective-permute-done((bf16[128,2944]{1,0:T(8,128)(2,1)S(1)}, bf16[128,2944]{1,0:T(8,128)(2,1)S(1)}, u32[]{:S(2)}, u32[]{:S(2)}) %collective-permute-start.14) | collective-permute-done | bytes 753696 | tf_op jit(solution)/shard_map/ppermute | solution.py:38
  72.1 0.2 fusion.11
  72.3 1.3 %collective-permute-start.15 = (bf16[32,2880]{1,0:T(8,128)(2,1)S(1)}, bf16[32,2880]{1,0:T(8,128)(2,1)S(1)}, u32[]{:S(2)}, u32[]{:S(2)}) collective-permute-start(bf16[32,2880]{1,0:T(8,128)(2,1)S(1)} %get-tuple-element.20), channel_id=1, source_target_pairs={{0,2},{1,3},{2,0},{3,1},{4,6},{5,7},{6,4},{7,5},{8,10},{9,11},{10,... | collective-permute-start | bytes 552968 | tf_op jit(solution)/shard_map/ppermute | solution.py:38
  73.6 1.0 %collective-permute-start.17 = (bf16[32,2880]{1,0:T(8,128)(2,1)S(1)}, bf16[32,2880]{1,0:T(8,128)(2,1)S(1)}, u32[]{:S(2)}, u32[]{:S(2)}) collective-permute-start(bf16[32,2880]{1,0:T(8,128)(2,1)S(1)} %get-tuple-element.21), channel_id=1, source_target_pairs={{0,6},{1,7},{2,4},{3,5},{4,2},{5,3},{6,0},{7,1},{8,14},{9,15},{10,... | collective-permute-start | bytes 552968 | tf_op jit(solution)/shard_map/ppermute | solution.py:38
  74.5 1.3 %collective-permute-start.16 = (bf16[32,2880]{1,0:T(8,128)(2,1)S(1)}, bf16[32,2880]{1,0:T(8,128)(2,1)S(1)}, u32[]{:S(2)}, u32[]{:S(2)}) collective-permute-start(bf16[32,2880]{1,0:T(8,128)(2,1)S(1)} %get-tuple-element.22), channel_id=1, source_target_pairs={{0,4},{1,5},{2,6},{3,7},{4,0},{5,1},{6,2},{7,3},{8,12},{9,13},{10,... | collective-permute-start | bytes 552968 | tf_op jit(solution)/shard_map/ppermute | solution.py:38
  75.8 7.4 %collective-permute-done.15 = bf16[32,2880]{1,0:T(8,128)(2,1)S(1)} collective-permute-done((bf16[32,2880]{1,0:T(8,128)(2,1)S(1)}, bf16[32,2880]{1,0:T(8,128)(2,1)S(1)}, u32[]{:S(2)}, u32[]{:S(2)}) %collective-permute-start.15) | collective-permute-done | bytes 184352 | tf_op jit(solution)/shard_map/ppermute | solution.py:38
  83.3 0.0 collective-permute-done.17
  83.3 1.2 %collective-permute-done.16 = bf16[32,2880]{1,0:T(8,128)(2,1)S(1)} collective-permute-done((bf16[32,2880]{1,0:T(8,128)(2,1)S(1)}, bf16[32,2880]{1,0:T(8,128)(2,1)S(1)}, u32[]{:S(2)}, u32[]{:S(2)}) %collective-permute-start.16) | collective-permute-done | bytes 184352 | tf_op jit(solution)/shard_map/ppermute | solution.py:38
  84.5 0.1 fusion.1
  84.6 1.1 %collective-permute-start.18 = (bf16[16,2880]{1,0:T(8,128)(2,1)S(1)}, bf16[16,2880]{1,0:T(8,128)(2,1)S(1)}, u32[]{:S(2)}, u32[]{:S(2)}) collective-permute-start(bf16[16,2880]{1,0:T(8,128)(2,1)S(1)} %slice.102), channel_id=1, source_target_pairs={{0,8},{1,9},{2,10},{3,11},{4,12},{5,13},{6,14},{7,15},{8,0},{9,1},... | collective-permute-start | bytes 276488 | tf_op jit(solution)/shard_map/ppermute | solution.py:38
  85.7 5.6 %collective-permute-done.18 = bf16[16,2880]{1,0:T(8,128)(2,1)S(1)} collective-permute-done((bf16[16,2880]{1,0:T(8,128)(2,1)S(1)}, bf16[16,2880]{1,0:T(8,128)(2,1)S(1)}, u32[]{:S(2)}, u32[]{:S(2)}) %collective-permute-start.18) | collective-permute-done | bytes 92192 | tf_op jit(solution)/shard_map/ppermute | solution.py:38
  91.3 0.7 fusion.9
  (17 shorter events, 0.2 us)
Async XLA Ops:
  0.6 34.0 %copy-start = (bf16[2880,16]{0,1:T(8,128)(2,1)S(1)}, bf16[2880,16]{0,1:T(8,128)(2,1)}, u32[]{:S(2)}) copy-start(bf16[2880,16]{0,1:T(8,128)(2,1)} %param.17) | copy-start | bytes 276484
  0.7 8.9 %copy-start.4 = (bf16[256,2880]{0,1:T(8,128)(2,1)S(1)}, bf16[256,2880]{0,1:T(8,128)(2,1)}, u32[]{:S(2)}) copy-start(bf16[256,2880]{0,1:T(8,128)(2,1)} %param.16) | copy-start | bytes 4423684
  8.0 1.6 %collective-permute-start = (bf16[2,64,256]{2,1,0:T(8,128)(2,1)}, bf16[2,64,256]{2,1,0:T(8,128)(2,1)S(1)}, u32[]{:S(2)}, u32[]{:S(2)}) collective-permute-start(bf16[2,64,256]{2,1,0:T(8,128)(2,1)} %get-tuple-element.9), channel_id=1, source_target_pairs={{0,1},{1,0},{2,3},{3,2},{4,5},{5,4},{6,7},{7,6},{8,9},{9,8},{10,11... | collective-permute-start | bytes 196616 | tf_op jit(solution)/shard_map/ppermute | solution.py:38
  9.5 0.8 copy-start.5
  11.4 2.3 %collective-permute-start.1 = (bf16[128,2944]{1,0:T(8,128)(2,1)S(1)}, bf16[128,2944]{1,0:T(8,128)(2,1)S(1)}, u32[]{:S(2)}, u32[]{:S(2)}) collective-permute-start(bf16[128,2944]{1,0:T(8,128)(2,1)S(1)} %get-tuple-element.11), channel_id=1, source_target_pairs={{0,1},{1,0},{2,3},{3,2},{4,5},{5,4},{6,7},{7,6},{8,9},{9,8},{10,11... | collective-permute-start | bytes 2261000 | tf_op jit(solution)/shard_map/ppermute | solution.py:38
  13.9 16.3 %copy-start.8 = (s32[2,8,4]{1,2,0:T(4,128)S(1)}, s32[2,8,4]{1,2,0:T(4,128)}, u32[]{:S(2)}) copy-start(s32[2,8,4]{1,2,0:T(4,128)} %param.21) | copy-start | bytes 772
  13.9 20.5 %copy-start.7 = (bf16[2,8,2880]{2,1,0:T(8,128)(2,1)S(1)}, bf16[2,8,2880]{2,1,0:T(8,128)(2,1)}, u32[]{:S(2)}) copy-start(bf16[2,8,2880]{2,1,0:T(8,128)(2,1)} %param.15) | copy-start | bytes 276484
  13.9 12.0 %collective-permute-start.2 = (bf16[32,2880]{1,0:T(8,128)(2,1)S(1)}, bf16[32,2880]{1,0:T(8,128)(2,1)S(1)}, u32[]{:S(2)}, u32[]{:S(2)}) collective-permute-start(bf16[32,2880]{1,0:T(8,128)(2,1)S(1)} %get-tuple-element.23), channel_id=1, source_target_pairs={{0,2},{1,3},{2,0},{3,1},{4,6},{5,7},{6,4},{7,5},{8,10},{9,11},{10,... | collective-permute-start | bytes 552968 | tf_op jit(solution)/shard_map/ppermute | solution.py:38
  16.9 9.1 %collective-permute-start.4 = (bf16[32,2880]{1,0:T(8,128)(2,1)S(1)}, bf16[32,2880]{1,0:T(8,128)(2,1)S(1)}, u32[]{:S(2)}, u32[]{:S(2)}) collective-permute-start(bf16[32,2880]{1,0:T(8,128)(2,1)S(1)} %get-tuple-element.24), channel_id=1, source_target_pairs={{0,6},{1,7},{2,4},{3,5},{4,2},{5,3},{6,0},{7,1},{8,14},{9,15},{10,... | collective-permute-start | bytes 552968 | tf_op jit(solution)/shard_map/ppermute | solution.py:38
  18.4 8.9 %collective-permute-start.3 = (bf16[32,2880]{1,0:T(8,128)(2,1)S(1)}, bf16[32,2880]{1,0:T(8,128)(2,1)S(1)}, u32[]{:S(2)}, u32[]{:S(2)}) collective-permute-start(bf16[32,2880]{1,0:T(8,128)(2,1)S(1)} %get-tuple-element.25), channel_id=1, source_target_pairs={{0,4},{1,5},{2,6},{3,7},{4,0},{5,1},{6,2},{7,3},{8,12},{9,13},{10,... | collective-permute-start | bytes 552968 | tf_op jit(solution)/shard_map/ppermute | solution.py:38
  27.4 6.9 %collective-permute-start.5 = (bf16[16,2880]{1,0:T(8,128)(2,1)S(1)}, bf16[16,2880]{1,0:T(8,128)(2,1)S(1)}, u32[]{:S(2)}, u32[]{:S(2)}) collective-permute-start(bf16[16,2880]{1,0:T(8,128)(2,1)S(1)} %slice.103), channel_id=1, source_target_pairs={{0,8},{1,9},{2,10},{3,11},{4,12},{5,13},{6,14},{7,15},{8,0},{9,1},... | collective-permute-start | bytes 276488 | tf_op jit(solution)/shard_map/ppermute | solution.py:38
  34.5 56.8 %copy-start.6 = (bf16[16,2880]{1,0:T(8,128)(2,1)}, bf16[16,2880]{1,0:T(8,128)(2,1)S(1)}, u32[]{:S(2)}) copy-start(bf16[16,2880]{1,0:T(8,128)(2,1)S(1)} %get-tuple-element.17) | copy-start | bytes 276484
  35.2 6.6 %collective-permute-start.6 = (bf16[16,2912]{1,0:T(8,128)(2,1)S(1)}, bf16[16,2912]{1,0:T(8,128)(2,1)S(1)}, u32[]{:S(2)}, u32[]{:S(2)}) collective-permute-start(bf16[16,2912]{1,0:T(8,128)(2,1)S(1)} %concatenate.6), channel_id=1, source_target_pairs={{0,8},{1,9},{2,10},{3,11},{4,12},{5,13},{6,14},{7,15},{8,0},{9,1},... | collective-permute-start | bytes 279560 | tf_op jit(solution)/shard_map/ppermute | solution.py:38
  41.8 6.6 %collective-permute-start.9 = (bf16[32,2912]{1,0:T(8,128)(2,1)S(1)}, bf16[32,2912]{1,0:T(8,128)(2,1)S(1)}, u32[]{:S(2)}, u32[]{:S(2)}) collective-permute-start(bf16[32,2912]{1,0:T(8,128)(2,1)S(1)} %pad_maximum_fusion.refs_0_), channel_id=1, source_target_pairs={{0,6},{1,7},{2,4},{3,5},{4,2},{5,3},{6,0},{7,1},{8,14},{9,15},{10,... | collective-permute-start | bytes 559112 | tf_op jit(solution)/shard_map/ppermute | solution.py:38
  42.8 7.5 %collective-permute-start.8 = (bf16[32,2912]{1,0:T(8,128)(2,1)S(1)}, bf16[32,2912]{1,0:T(8,128)(2,1)S(1)}, u32[]{:S(2)}, u32[]{:S(2)}) collective-permute-start(bf16[32,2912]{1,0:T(8,128)(2,1)S(1)} %pad_maximum_fusion.refs_0_), channel_id=1, source_target_pairs={{0,4},{1,5},{2,6},{3,7},{4,0},{5,1},{6,2},{7,3},{8,12},{9,13},{10,... | collective-permute-start | bytes 559112 | tf_op jit(solution)/shard_map/ppermute | solution.py:38
  44.7 5.7 %collective-permute-start.7 = (bf16[32,2912]{1,0:T(8,128)(2,1)S(1)}, bf16[32,2912]{1,0:T(8,128)(2,1)S(1)}, u32[]{:S(2)}, u32[]{:S(2)}) collective-permute-start(bf16[32,2912]{1,0:T(8,128)(2,1)S(1)} %pad_maximum_fusion.refs_0_), channel_id=1, source_target_pairs={{0,2},{1,3},{2,0},{3,1},{4,6},{5,7},{6,4},{7,5},{8,10},{9,11},{10,... | collective-permute-start | bytes 559112 | tf_op jit(solution)/shard_map/ppermute | solution.py:38
  45.3 5.4 %collective-permute-start.10 = (bf16[32,2912]{1,0:T(8,128)(2,1)S(1)}, bf16[32,2912]{1,0:T(8,128)(2,1)S(1)}, u32[]{:S(2)}, u32[]{:S(2)}) collective-permute-start(bf16[32,2912]{1,0:T(8,128)(2,1)S(1)} %pad_maximum_fusion.refs_0_), channel_id=1, source_target_pairs={{0,1},{1,0},{2,3},{3,2},{4,5},{5,4},{6,7},{7,6},{8,9},{9,8},{10,11... | collective-permute-start | bytes 559112 | tf_op jit(solution)/shard_map/ppermute | solution.py:38
  48.3 2.4 %collective-permute-start.13 = (bf16[32,2912]{1,0:T(8,128)(2,1)S(1)}, bf16[32,2912]{1,0:T(8,128)(2,1)S(1)}, u32[]{:S(2)}, u32[]{:S(2)}) collective-permute-start(bf16[32,2912]{1,0:T(8,128)(2,1)S(1)} %collective-permute-done.9.refs_3_), channel_id=1, source_target_pairs={{0,1},{1,0},{2,3},{3,2},{4,5},{5,4},{6,7},{7,6},{8,9},{9,8},{10,11... | collective-permute-start | bytes 559112 | tf_op jit(solution)/shard_map/ppermute | solution.py:38
  50.2 1.4 %collective-permute-start.12 = (bf16[32,2912]{1,0:T(8,128)(2,1)S(1)}, bf16[32,2912]{1,0:T(8,128)(2,1)S(1)}, u32[]{:S(2)}, u32[]{:S(2)}) collective-permute-start(bf16[32,2912]{1,0:T(8,128)(2,1)S(1)} %collective-permute-done.8.refs_2_), channel_id=1, source_target_pairs={{0,1},{1,0},{2,3},{3,2},{4,5},{5,4},{6,7},{7,6},{8,9},{9,8},{10,11... | collective-permute-start | bytes 559112 | tf_op jit(solution)/shard_map/ppermute | solution.py:38
  50.3 1.6 %collective-permute-start.11 = (bf16[32,2912]{1,0:T(8,128)(2,1)S(1)}, bf16[32,2912]{1,0:T(8,128)(2,1)S(1)}, u32[]{:S(2)}, u32[]{:S(2)}) collective-permute-start(bf16[32,2912]{1,0:T(8,128)(2,1)S(1)} %collective-permute-done.7.refs_1_), channel_id=1, source_target_pairs={{0,1},{1,0},{2,3},{3,2},{4,5},{5,4},{6,7},{7,6},{8,9},{9,8},{10,11... | collective-permute-start | bytes 559112 | tf_op jit(solution)/shard_map/ppermute | solution.py:38
  51.9 3.4 %copy-start.1 = (bf16[4,2880,360]{1,2,0:T(8,128)(2,1)S(1)}, bf16[4,2880,360]{1,2,0:T(8,128)(2,1)}, u32[]{:S(2)}) copy-start(bf16[4,2880,360]{1,2,0:T(8,128)(2,1)} %param.18) | copy-start | bytes 24883204
  55.3 3.4 %copy-start.2 = (bf16[4,2880,360]{1,2,0:T(8,128)(2,1)S(1)}, bf16[4,2880,360]{1,2,0:T(8,128)(2,1)}, u32[]{:S(2)}) copy-start(bf16[4,2880,360]{1,2,0:T(8,128)(2,1)} %param.19) | copy-start | bytes 24883204
  58.7 3.4 %copy-start.3 = (bf16[4,360,2880]{2,1,0:T(8,128)(2,1)S(1)}, bf16[4,360,2880]{2,1,0:T(8,128)(2,1)}, u32[]{:S(2)}) copy-start(bf16[4,360,2880]{2,1,0:T(8,128)(2,1)} %param.20) | copy-start | bytes 24883204
  69.8 2.3 %collective-permute-start.14 = (bf16[128,2944]{1,0:T(8,128)(2,1)S(1)}, bf16[128,2944]{1,0:T(8,128)(2,1)S(1)}, u32[]{:S(2)}, u32[]{:S(2)}) collective-permute-start(bf16[128,2944]{1,0:T(8,128)(2,1)S(1)} %get-tuple-element.13), channel_id=1, source_target_pairs={{0,1},{1,0},{2,3},{3,2},{4,5},{5,4},{6,7},{7,6},{8,9},{9,8},{10,11... | collective-permute-start | bytes 2261000 | tf_op jit(solution)/shard_map/ppermute | solution.py:38
  72.3 11.0 %collective-permute-start.15 = (bf16[32,2880]{1,0:T(8,128)(2,1)S(1)}, bf16[32,2880]{1,0:T(8,128)(2,1)S(1)}, u32[]{:S(2)}, u32[]{:S(2)}) collective-permute-start(bf16[32,2880]{1,0:T(8,128)(2,1)S(1)} %get-tuple-element.20), channel_id=1, source_target_pairs={{0,2},{1,3},{2,0},{3,1},{4,6},{5,7},{6,4},{7,5},{8,10},{9,11},{10,... | collective-permute-start | bytes 552968 | tf_op jit(solution)/shard_map/ppermute | solution.py:38
  73.6 9.7 %collective-permute-start.17 = (bf16[32,2880]{1,0:T(8,128)(2,1)S(1)}, bf16[32,2880]{1,0:T(8,128)(2,1)S(1)}, u32[]{:S(2)}, u32[]{:S(2)}) collective-permute-start(bf16[32,2880]{1,0:T(8,128)(2,1)S(1)} %get-tuple-element.21), channel_id=1, source_target_pairs={{0,6},{1,7},{2,4},{3,5},{4,2},{5,3},{6,0},{7,1},{8,14},{9,15},{10,... | collective-permute-start | bytes 552968 | tf_op jit(solution)/shard_map/ppermute | solution.py:38
  74.5 10.0 %collective-permute-start.16 = (bf16[32,2880]{1,0:T(8,128)(2,1)S(1)}, bf16[32,2880]{1,0:T(8,128)(2,1)S(1)}, u32[]{:S(2)}, u32[]{:S(2)}) collective-permute-start(bf16[32,2880]{1,0:T(8,128)(2,1)S(1)} %get-tuple-element.22), channel_id=1, source_target_pairs={{0,4},{1,5},{2,6},{3,7},{4,0},{5,1},{6,2},{7,3},{8,12},{9,13},{10,... | collective-permute-start | bytes 552968 | tf_op jit(solution)/shard_map/ppermute | solution.py:38
  84.6 6.7 %collective-permute-start.18 = (bf16[16,2880]{1,0:T(8,128)(2,1)S(1)}, bf16[16,2880]{1,0:T(8,128)(2,1)S(1)}, u32[]{:S(2)}, u32[]{:S(2)}) collective-permute-start(bf16[16,2880]{1,0:T(8,128)(2,1)S(1)} %slice.102), channel_id=1, source_target_pairs={{0,8},{1,9},{2,10},{3,11},{4,12},{5,13},{6,14},{7,15},{8,0},{9,1},... | collective-permute-start | bytes 276488 | tf_op jit(solution)/shard_map/ppermute | solution.py:38

commit v5 on v4

--- a/solution.py
+++ b/solution.py
@@ -15,18 +15,19 @@
 SPLIT = 4
 REQ_DEV = 8
 TILE = 256
+LANES = 128
 LIMIT = 16 << 20
 ROWS_LAST = (((1,), (1,)), ((), ()))
 
 
 def plan(device_count):
     bits = device_count.bit_length() - 1
-    stages = [(0, 1)] if bits else []
-    bit = 1
-    while bit < bits:
-        width = min(2, bits - bit)
+    stages, bit = [(0, 1)], 1
+    while bit < bits - 1:
+        width = min(2, bits - 1 - bit)
         stages.append((bit, width))
         bit += width
+    stages.append((bits - 1, 1))
     masks = [0]
     for bit, width in stages:
         masks = [mask | (r << bit) for mask in masks for r in range(1 << width)]
@@ -38,21 +39,58 @@
     return lax.ppermute(value, "req", pairs)
 
 
+def padded(width):
+    return pl.cdiv(width, LANES) * LANES
+
+
+def whole_call(kernel, name, outs, inputs, scratch=(), scalars=(), **options):
+    return pl.pallas_call(
+        kernel,
+        out_shape=outs,
+        in_specs=[pl.BlockSpec(memory_space=pltpu.SMEM)] * len(scalars)
+        + [pl.BlockSpec(memory_space=pltpu.VMEM)] * len(inputs),
+        out_specs=[pl.BlockSpec(memory_space=pltpu.VMEM)] * len(outs),
+        scratch_shapes=list(scratch),
+        compiler_params=pltpu.CompilerParams(vmem_limit_bytes=LIMIT),
+        name=name,
+        **options,
+    )(*scalars, *inputs)
+
+
+def split_kernel(count, *refs):
+    total = refs[0][...]
+    width = total.shape[1]
+    for ref in refs[1:count]:
+        total = total + ref[:, :width].astype(jnp.float32)
+    outs = refs[count:]
+    size = outs[0].shape[0]
+    for r, out in enumerate(outs):
+        out[...] = total[r * size : (r + 1) * size].astype(out.dtype)
+
+
+def add_split(total, received, pieces):
+    shape = (total.shape[0] // pieces, total.shape[1])
+    return whole_call(
+        functools.partial(split_kernel, 1 + len(received)),
+        "add_split",
+        [
+            jax.ShapeDtypeStruct(shape, jnp.bfloat16 if r else jnp.float32)
+            for r in range(pieces)
+        ],
+        [total, *received],
+    )
+
+
 def scatter_sum(keep, send, stages):
-    width = keep.shape[1]
-    total = keep + from_mask(send, 1)[:, :width].astype(jnp.float32)
-    for bit, bits in stages[1:]:
-        size = total.shape[0] >> bits
-        pieces = [total[r * size : (r + 1) * size] for r in range(1 << bits)]
-        total = pieces[0]
-        for r in range(1, 1 << bits):
-            moved = from_mask(pieces[r].astype(jnp.bfloat16), r << bit)
-            total = total + moved.astype(jnp.float32)
-    return total
-
-
-def gather_rows(rows, stages):
-    pieces = [rows]
+    pieces = [keep, send]
+    for index, (bit, bits) in enumerate(stages[:-1]):
+        received = [from_mask(pieces[r], r << bit) for r in range(1, 1 << bits)]
+        if index + 2 < len(stages):
+            pieces = add_split(pieces[0], received, 1 << stages[index + 1][1])
+    return pieces[0], received
+
+
+def gather_rows(pieces, stages):
     for bit, bits in reversed(stages):
         if bit:
             held = jnp.concatenate(pieces, axis=0) if len(pieces) > 1 else pieces[0]
@@ -60,6 +98,100 @@
         else:
             pieces = pieces + [from_mask(piece, 1) for piece in pieces]
     return pieces
+
+
+def share_kernel(count, routes, *refs):
+    received, residual = refs[:count], refs[count]
+    total, message = refs[count + 1 :]
+    rows, width = residual.shape
+    value = received[0][...]
+    for ref in received[1:]:
+        value = value + ref[:, :width].astype(jnp.float32)
+    total[:rows, :width] = value[:rows] + residual[...].astype(jnp.float32)
+    total[rows:, :width] = value[rows:]
+    message[:, :width] = total[:, :width].astype(jnp.bfloat16)
+    base = width // LANES * LANES
+    used = width - base
+    lane = lax.broadcasted_iota(jnp.int32, (rows, LANES), 1)
+    row = lax.broadcasted_iota(jnp.int32, (rows, LANES), 0)
+    named = lane < 0
+    batch, top, each = routes.shape
+    for m in range(batch):
+        for i in range(each):
+            for t in range(top):
+                named |= (row == m * each + i) & (lane == used + routes[m, t, i])
+    end = jnp.where(lane < used, total[:rows, base:], jnp.where(named, 1.0, 0.0))
+    message[:rows, base:] = end.astype(jnp.bfloat16)
+    end = jnp.where(lane < used, total[rows:, base:], 0.0)
+    message[rows:, base:] = end.astype(jnp.bfloat16)
+
+
+def norm_kernel(total, mine, theirs, router, attended, payload):
+    rows, width = attended.shape
+    base = width // LANES * LANES
+    used = width - base
+    lane = lax.broadcasted_iota(jnp.int32, (rows, LANES), 1)
+    place = lax.broadcasted_iota(jnp.int32, (EXPERTS, LANES), 1) - used
+    place -= lax.broadcasted_iota(jnp.int32, (EXPERTS, LANES), 0)
+    first = jnp.where(place == 0, 1.0, 0.0).astype(jnp.bfloat16)
+    second = jnp.where(place == EXPERTS, 1.0, 0.0).astype(jnp.bfloat16)
+    for half, source in enumerate((mine, theirs)):
+        own = slice(half * rows, (half + 1) * rows)
+        other = slice((1 - half) * rows, (2 - half) * rows)
+        value = total[own, :width] + theirs[other, :width].astype(jnp.float32)
+        value = value.astype(jnp.bfloat16)
+        if half == 0:
+            attended[...] = value
+        value = value.astype(jnp.float32)
+        mean = jnp.sum(value * value, axis=1, keepdims=True) * (1.0 / width)
+        normed = (value * lax.rsqrt(mean + 1e-05)).astype(jnp.bfloat16)
+        payload[own, :width] = normed
+        logits = lax.dot_general(
+            normed, router[...], ROWS_LAST, preferred_element_type=jnp.float32
+        )
+        named = lax.dot_general(
+            source[:rows, base:], first, ROWS_LAST, preferred_element_type=jnp.float32
+        )
+        named = named > 0.5
+        top = jnp.max(jnp.where(named, logits, -jnp.inf), axis=1, keepdims=True)
+        weight = jnp.where(named, jnp.exp(jnp.where(named, logits - top, 0.0)), 0.0)
+        gate = weight / jnp.sum(weight, axis=1, keepdims=True)
+        high = gate.astype(jnp.bfloat16)
+        low = (gate - high.astype(jnp.float32)).astype(jnp.bfloat16)
+        end = jnp.dot(high, first, preferred_element_type=jnp.float32)
+        end = end + jnp.dot(low, second, preferred_element_type=jnp.float32)
+        kept = payload[own, base:].astype(jnp.float32)
+        payload[own, base:] = jnp.where(lane < used, kept, end).astype(jnp.bfloat16)
+
+
+def attend(total, received, residual, routes, router, stages):
+    rows, width = residual.shape
+    wide = padded(width)
+    total, message = whole_call(
+        functools.partial(share_kernel, 1 + len(received)),
+        "share",
+        [
+            jax.ShapeDtypeStruct((2 * rows, wide), jnp.float32),
+            jax.ShapeDtypeStruct((2 * rows, wide), jnp.bfloat16),
+        ],
+        [total, *received, residual],
+        scalars=[routes],
+    )
+    theirs = from_mask(message, 1 << stages[-1][0])
+    return whole_call(
+        norm_kernel,
+        "norm",
+        [
+            jax.ShapeDtypeStruct((rows, width), jnp.bfloat16),
+            jax.ShapeDtypeStruct((2 * rows, wide), jnp.bfloat16),
+        ],
+        [total, message, theirs, router],
+    )
+
+
+def finish_kernel(total, received, attended, layer):
+    value = total[...] + received[...].astype(jnp.float32)
+    layer[...] = (attended[...].astype(jnp.float32) + value).astype(jnp.bfloat16)
 
 
 def attention_kernel(
@@ -182,7 +314,7 @@
         functools.partial(project_kernel, group, masks),
         out_shape=[
             jax.ShapeDtypeStruct((count // 2, weight.shape[0]), jnp.float32),
-            jax.ShapeDtypeStruct((count // 2, pl.cdiv(weight.shape[0], 128) * 128), jnp.bfloat16),
+            jax.ShapeDtypeStruct((count // 2, padded(weight.shape[0])), jnp.bfloat16),
         ],
         in_specs=[pl.BlockSpec(memory_space=pltpu.SMEM)] + [whole] * (group + 1),
         out_specs=[whole] * 2,
@@ -191,7 +323,7 @@
             pltpu.VMEM((count, width), jnp.float32),
         ],
         compiler_params=pltpu.CompilerParams(vmem_limit_bytes=LIMIT),
-        cost_estimate=pl.CostEstimate(flops=60000000000, bytes_accessed=150000000, transcendentals=0),
+        cost_estimate=pl.CostEstimate(flops=60_000_000_000, bytes_accessed=150_000_000, transcendentals=0),
         name="project",
     )(me, *held, weight)
 
@@ -246,7 +378,7 @@
         functools.partial(expert_kernel, len(pieces), hidden),
         out_shape=[
             jax.ShapeDtypeStruct((count // 2, width), jnp.float32),
-            jax.ShapeDtypeStruct((count // 2, pl.cdiv(width, 128) * 128), jnp.bfloat16),
+            jax.ShapeDtypeStruct((count // 2, padded(width)), jnp.bfloat16),
         ],
         in_specs=[pl.BlockSpec(memory_space=pltpu.SMEM)] + [whole] * (len(pieces) + 3),
         out_specs=[whole] * 2,
@@ -270,37 +402,29 @@
     device_index = lax.axis_index("req")
     stages, masks = plan(device_count)
     group_size = max(1, device_count // KVH)
-    width = residual.shape[2]
-    block_rows = residual.shape[0] * residual.shape[1]
+    batch, each, width = residual.shape
     me = device_index.astype(jnp.int32)[None]
 
     held = attention(lengths, me % group_size, queries, new_kv, cache, group_size)
     held = [held[0]] + [from_mask(held[r], r) for r in range(1, group_size)]
-    summed = scatter_sum(*project(me, held, o_proj.T, masks), stages)
-
-    attended = (residual.reshape(block_rows, width).astype(jnp.float32) + summed).astype(
-        jnp.bfloat16
-    )
-    attended_wide = attended.astype(jnp.float32)
-    normed = (
-        attended_wide
-        * lax.rsqrt(jnp.mean(attended_wide * attended_wide, axis=1, keepdims=True) + 1e-05)
-    ).astype(jnp.bfloat16)
-    logits = jnp.dot(normed, router, preferred_element_type=jnp.float32)
-    chosen_one = routes.reshape(block_rows, -1)[:, :, None] == jnp.arange(EXPERTS)[None, None, :]
-    chosen = jnp.sum(jnp.where(chosen_one, logits[:, None, :], 0.0), axis=2)
-    gates = 1.0 / jnp.sum(jnp.exp(chosen[:, None, :] - chosen[:, :, None]), axis=2)
-    dense = jnp.sum(jnp.where(chosen_one, gates[:, :, None], 0.0), axis=1)
-    high = lax.reduce_precision(dense, 8, 7)
-    payload = jnp.concatenate(
-        [normed, high.astype(jnp.bfloat16), (dense - high).astype(jnp.bfloat16)], axis=1
-    )
-
-    pieces = gather_rows(payload, stages)
-    mixture = scatter_sum(
-        *expert_sums(me, pieces, w_gate, w_up, w_down), stages
-    )
-    layer = (attended_wide + mixture).astype(jnp.bfloat16)
+    total, received = scatter_sum(*project(me, held, o_proj.T, masks), stages)
+    attended, payload = attend(
+        total,
+        received,
+        residual.reshape(batch * each, width),
+        routes.swapaxes(1, 2),
+        router.T,
+        stages,
+    )
+    pieces = gather_rows([payload], stages[:-1])
+    total, received = scatter_sum(*expert_sums(me, pieces, w_gate, w_up, w_down), stages)
+    kept, sent = add_split(total, received, 2)
+    (layer,) = whole_call(
+        finish_kernel,
+        "finish",
+        [jax.ShapeDtypeStruct(attended.shape, jnp.bfloat16)],
+        [kept, from_mask(sent, 1 << stages[-1][0]), attended],
+    )
     return attended.reshape(residual.shape), layer.reshape(residual.shape)
 
 

time: 92.4 us -> 83.4 us (0.903)
  local copies, waits for them, and re-layouts: 11.4 us -> 1.04 us
  Pallas kernels: 15.9 us -> 18.8 us
  other arithmetic: 1.74 us -> 0.01 us
    unnamed x19 -> x30, local copies, waits for them, and re-layouts: 11.1 us -> 1.04 us
    pallas_call x0 -> x6, Pallas kernels: none -> 2.86 us  [whole_call(): pl.pallas_call(kernel, out_shape=outs, in_specs=[pl.BlockSpec(memory_spac...]
    ppermute x19 -> x18, starting transfers between devices: 18.5 us -> 19.2 us  [from_mask(): return lax.ppermute(value, 'req', pairs)]
    ppermute x19 -> x18, waiting for transfers between devices: 43.5 us -> 43.3 us  [from_mask(): return lax.ppermute(value, 'req', pairs)]
  transfers between devices with their start and end apart: 19 -> 18, of which waited for: 15 -> 16; matrix products, arithmetic and copies ran while one was open for 0% -> 0% of each run, Pallas kernels for 0% -> 0%
where the time goes in v5:
time: 83.4 us; the launch traced here: 83.2 us
  waiting for transfers between devices  43.3 us (52%)
  starting transfers between devices  19.2 us (23%)
  Pallas kernels  18.8 us (23%)
  local copies, waits for them, and re-layouts  1.04 us (1%)
    ppermute x18, waiting for transfers between devices, from_mask(): return lax.ppermute(value, 'req', pairs)  43.3 us
    ppermute x18, starting transfers between devices, from_mask(): return lax.ppermute(value, 'req', pairs)  19.2 us
    pallas_call x1, Pallas kernels, expert_sums(): pl.pallas_call(functools.partial(expert_kernel, len(pieces), hidden), out...  7.63 us
    pallas_call x1, Pallas kernels, attention(): pl.pallas_call(functools.partial(attention_kernel, group, rows // block),...  7.29 us
    pallas_call x6, Pallas kernels, whole_call(): pl.pallas_call(kernel, out_shape=outs, in_specs=[pl.BlockSpec(memory_spac...  2.86 us
  transfers between devices with their start and end apart: 18, of which 16 were waited for; matrix products, arithmetic and copies ran while one was open for 0% of the time, Pallas kernels for 0%

profile of v5, /device:TPU:0, one launch (start us, length us, event | category | flops | bytes accessed | tf_op | source)
XLA Modules:
  0.0 83.2 jit_solution(10033094834918063382)
XLA Ops:
  0.6 0.0 copy-start.4
  0.7 7.3 %attention.1 = (bf16[2,64,256]{2,1,0:T(8,128)(2,1)}, bf16[2,64,256]{2,1,0:T(8,128)(2,1)}) custom-call(s32[2,128]{1,0:T(2,128)} %lengths.1, s32[1]{0:T(128)S(6)} %select_n.7.place, bf16[2,64,512]{2,1,0:T(8,128)(2,1)} %q_ref.1, bf16[2,64,128]{2,1,0:T(8,128)(2,1)} %kv_ref.1, bf16[2,64,128,128]{3,2,1,0:T(8,128)(2,1)} %cache_ref.1), custom_call_target="tpu_custom_call" | custom-call | tf_op jit(solution)/shard_map/attention/pallas_call | solution.py:255
  7.9 0.5 collective-permute-start
  8.4 1.1 %collective-permute-done.refs_1_ = bf16[2,64,256]{2,1,0:T(8,128)(2,1)S(1)} collective-permute-done((bf16[2,64,256]{2,1,0:T(8,128)(2,1)}, bf16[2,64,256]{2,1,0:T(8,128)(2,1)S(1)}, u32[]{:S(2)}, u32[]{:S(2)}) %collective-permute-start) | collective-permute-done | bytes 65568 | tf_op jit(solution)/shard_map/ppermute | solution.py:39
  9.5 0.0 copy-done.4
  9.5 0.0 copy-start.5
  9.5 1.0 %copy-done.5 = bf16[2,64,256]{2,1,0:T(8,128)(2,1)S(1)} copy-done((bf16[2,64,256]{2,1,0:T(8,128)(2,1)S(1)}, bf16[2,64,256]{2,1,0:T(8,128)(2,1)}, u32[]{:S(2)}) %copy-start.5) | copy-done | bytes 65560
  10.5 0.0 slice-start.2
  10.5 0.0 slice-start.4
  10.5 0.0 slice-start.5
  10.6 0.0 slice-start.7
  10.6 0.0 slice-start.8
  10.6 1.0 %project.1 = (f32[128,2880]{1,0:T(8,128)S(1)}, bf16[128,2944]{1,0:T(8,128)(2,1)S(1)}) custom-call(s32[1]{0:T(128)} %bitcast.1.me_ref, bf16[2,64,256]{2,1,0:T(8,128)(2,1)S(1)} %copy-done.5, bf16[2,64,256]{2,1,0:T(8,128)(2,1)S(1)} %collective-permute-done.refs_1_, bf16[2880,256]{1,0:T(8,128)(2,1)S(1)} %bitcast.27), custom_call_target="tpu_custom_call" | custom-call | flops 60000002048 | bytes 150000000 | tf_op jit(solution)/shard_map/project/pallas_call | solution.py:313
  11.6 0.4 collective-permute-start.1
  12.0 1.9 %collective-permute-done.1.refs_1_ = bf16[128,2944]{1,0:T(8,128)(2,1)S(1)} collective-permute-done((bf16[128,2944]{1,0:T(8,128)(2,1)S(1)}, bf16[128,2944]{1,0:T(8,128)(2,1)S(1)}, u32[]{:S(2)}, u32[]{:S(2)}) %collective-permute-start.1) | collective-permute-done | bytes 753696 | tf_op jit(solution)/shard_map/ppermute | solution.py:39
  13.9 0.2 add_split.3
  14.1 2.9 %collective-permute-start.2 = (bf16[32,2880]{1,0:T(8,128)(2,1)S(1)}, bf16[32,2880]{1,0:T(8,128)(2,1)S(1)}, u32[]{:S(2)}, u32[]{:S(2)}) collective-permute-start(bf16[32,2880]{1,0:T(8,128)(2,1)S(1)} %get-tuple-element.27), channel_id=1, source_target_pairs={{0,2},{1,3},{2,0},{3,1},{4,6},{5,7},{6,4},{7,5},{8,10},{9,11},{10,... | collective-permute-start | bytes 552968 | tf_op jit(solution)/shard_map/ppermute | solution.py:39
  17.0 1.6 %collective-permute-start.3 = (bf16[32,2880]{1,0:T(8,128)(2,1)S(1)}, bf16[32,2880]{1,0:T(8,128)(2,1)S(1)}, u32[]{:S(2)}, u32[]{:S(2)}) collective-permute-start(bf16[32,2880]{1,0:T(8,128)(2,1)S(1)} %get-tuple-element.28), channel_id=1, source_target_pairs={{0,4},{1,5},{2,6},{3,7},{4,0},{5,1},{6,2},{7,3},{8,12},{9,13},{10,... | collective-permute-start | bytes 552968 | tf_op jit(solution)/shard_map/ppermute | solution.py:39
  18.6 0.0 collective-permute-start.4
  18.6 3.5 %collective-permute-done.2.refs_1_ = bf16[32,2880]{1,0:T(8,128)(2,1)S(1)} collective-permute-done((bf16[32,2880]{1,0:T(8,128)(2,1)S(1)}, bf16[32,2880]{1,0:T(8,128)(2,1)S(1)}, u32[]{:S(2)}, u32[]{:S(2)}) %collective-permute-start.2) | collective-permute-done | bytes 184352 | tf_op jit(solution)/shard_map/ppermute | solution.py:39
  22.1 2.5 %collective-permute-done.3.refs_2_ = bf16[32,2880]{1,0:T(8,128)(2,1)S(1)} collective-permute-done((bf16[32,2880]{1,0:T(8,128)(2,1)S(1)}, bf16[32,2880]{1,0:T(8,128)(2,1)S(1)}, u32[]{:S(2)}, u32[]{:S(2)}) %collective-permute-start.3) | collective-permute-done | bytes 184352 | tf_op jit(solution)/shard_map/ppermute | solution.py:39
  24.6 2.7 %collective-permute-done.4.refs_3_ = bf16[32,2880]{1,0:T(8,128)(2,1)S(1)} collective-permute-done((bf16[32,2880]{1,0:T(8,128)(2,1)S(1)}, bf16[32,2880]{1,0:T(8,128)(2,1)S(1)}, u32[]{:S(2)}, u32[]{:S(2)}) %collective-permute-start.4) | collective-permute-done | bytes 184352 | tf_op jit(solution)/shard_map/ppermute | solution.py:39
  27.4 0.0 copy-done.1
  27.4 0.0 copy-done.3
  27.4 0.8 share.1
  28.2 2.8 %collective-permute-start.5 = (bf16[32,2944]{1,0:T(8,128)(2,1)S(1)}, bf16[32,2944]{1,0:T(8,128)(2,1)S(1)}, u32[]{:S(2)}, u32[]{:S(2)}) collective-permute-start(bf16[32,2944]{1,0:T(8,128)(2,1)S(1)} %get-tuple-element.31.mine), channel_id=1, source_target_pairs={{0,8},{1,9},{2,10},{3,11},{4,12},{5,13},{6,14},{7,15},{8,0},{9,1},... | collective-permute-start | bytes 565256 | tf_op jit(solution)/shard_map/ppermute | solution.py:39
  31.0 8.2 %collective-permute-done.5.theirs = bf16[32,2944]{1,0:T(8,128)(2,1)S(1)} collective-permute-done((bf16[32,2944]{1,0:T(8,128)(2,1)S(1)}, bf16[32,2944]{1,0:T(8,128)(2,1)S(1)}, u32[]{:S(2)}, u32[]{:S(2)}) %collective-permute-start.5) | collective-permute-done | bytes 188448 | tf_op jit(solution)/shard_map/ppermute | solution.py:39
  39.2 0.0 copy-done.2
  39.2 0.9 %norm.1 = (bf16[16,2880]{1,0:T(8,128)(2,1)}, bf16[32,2944]{1,0:T(8,128)(2,1)S(1)}) custom-call(f32[32,2944]{1,0:T(8,128)S(1)} %get-tuple-element.30.total, bf16[32,2944]{1,0:T(8,128)(2,1)S(1)} %get-tuple-element.31.mine, bf16[32,2944]{1,0:T(8,128)(2,1)S(1)} %collective-permute-done.5.theirs, bf16[16,2880]{1,0:T(8,128)(2,1)S(1)} %bitcast.25), custom_call_target="tpu_custom_call" | custom-call | tf_op jit(solution)/shard_map/norm/pallas_call | solution.py:47
  40.1 1.5 %collective-permute-start.8 = (bf16[32,2944]{1,0:T(8,128)(2,1)S(1)}, bf16[32,2944]{1,0:T(8,128)(2,1)S(1)}, u32[]{:S(2)}, u32[]{:S(2)}) collective-permute-start(bf16[32,2944]{1,0:T(8,128)(2,1)S(1)} %get-tuple-element.33.refs_0_), channel_id=1, source_target_pairs={{0,6},{1,7},{2,4},{3,5},{4,2},{5,3},{6,0},{7,1},{8,14},{9,15},{10,... | collective-permute-start | bytes 565256 | tf_op jit(solution)/shard_map/ppermute | solution.py:39
  41.6 1.4 %collective-permute-start.7 = (bf16[32,2944]{1,0:T(8,128)(2,1)S(1)}, bf16[32,2944]{1,0:T(8,128)(2,1)S(1)}, u32[]{:S(2)}, u32[]{:S(2)}) collective-permute-start(bf16[32,2944]{1,0:T(8,128)(2,1)S(1)} %get-tuple-element.33.refs_0_), channel_id=1, source_target_pairs={{0,4},{1,5},{2,6},{3,7},{4,0},{5,1},{6,2},{7,3},{8,12},{9,13},{10,... | collective-permute-start | bytes 565256 | tf_op jit(solution)/shard_map/ppermute | solution.py:39
  42.9 0.7 collective-permute-start.6
  43.6 0.0 collective-permute-start.9
  43.6 5.1 %collective-permute-done.8.refs_3_ = bf16[32,2944]{1,0:T(8,128)(2,1)S(1)} collective-permute-done((bf16[32,2944]{1,0:T(8,128)(2,1)S(1)}, bf16[32,2944]{1,0:T(8,128)(2,1)S(1)}, u32[]{:S(2)}, u32[]{:S(2)}) %collective-permute-start.8) | collective-permute-done | bytes 188448 | tf_op jit(solution)/shard_map/ppermute | solution.py:39
  48.7 0.0 collective-permute-start.12
  48.7 1.8 %collective-permute-done.7.refs_2_ = bf16[32,2944]{1,0:T(8,128)(2,1)S(1)} collective-permute-done((bf16[32,2944]{1,0:T(8,128)(2,1)S(1)}, bf16[32,2944]{1,0:T(8,128)(2,1)S(1)}, u32[]{:S(2)}, u32[]{:S(2)}) %collective-permute-start.7) | collective-permute-done | bytes 188448 | tf_op jit(solution)/shard_map/ppermute | solution.py:39
  50.5 0.0 collective-permute-start.11
  50.6 0.3 collective-permute-done.6.refs_1_
  50.8 0.2 collective-permute-start.10
  51.1 0.0 collective-permute-done.9.refs_4_
  51.1 0.0 collective-permute-done.12.refs_7_
  51.1 0.9 %collective-permute-done.11.refs_6_ = bf16[32,2944]{1,0:T(8,128)(2,1)S(1)} collective-permute-done((bf16[32,2944]{1,0:T(8,128)(2,1)S(1)}, bf16[32,2944]{1,0:T(8,128)(2,1)S(1)}, u32[]{:S(2)}, u32[]{:S(2)}) %collective-permute-start.11) | collective-permute-done | bytes 188448 | tf_op jit(solution)/shard_map/ppermute | solution.py:39
  52.0 0.3 collective-permute-done.10.refs_5_
  52.3 0.0 slice-done.1
  52.3 0.0 slice-done.2
  52.3 0.0 slice-done.4
  52.3 0.0 slice-done.5
  52.3 0.0 slice-done.7
  52.3 0.0 slice-done.8
  52.4 0.0 copy-start
  52.4 7.6 %experts.1 = (f32[128,2880]{1,0:T(8,128)S(1)}, bf16[128,2944]{1,0:T(8,128)(2,1)S(1)}) custom-call(s32[1]{0:T(128)} %bitcast.1.me_ref, bf16[32,2944]{1,0:T(8,128)(2,1)S(1)} %get-tuple-element.33.refs_0_, bf16[32,2944]{1,0:T(8,128)(2,1)S(1)} %collective-permute-done.6.refs_1_, bf16[32,2944]{1,0:T(8,128)(2,1)S(1)} %collective-permute-done.7.refs_2_, ...), custom_call_target="tpu_custom_call" | custom-call | tf_op jit(solution)/shard_map/experts/pallas_call | solution.py:377
  60.0 0.3 collective-permute-start.13
  60.3 2.0 %collective-permute-done.13.refs_1_ = bf16[128,2944]{1,0:T(8,128)(2,1)S(1)} collective-permute-done((bf16[128,2944]{1,0:T(8,128)(2,1)S(1)}, bf16[128,2944]{1,0:T(8,128)(2,1)S(1)}, u32[]{:S(2)}, u32[]{:S(2)}) %collective-permute-start.13) | collective-permute-done | bytes 753696 | tf_op jit(solution)/shard_map/ppermute | solution.py:39
  62.3 0.2 add_split.4
  62.5 1.2 %collective-permute-start.14 = (bf16[32,2880]{1,0:T(8,128)(2,1)S(1)}, bf16[32,2880]{1,0:T(8,128)(2,1)S(1)}, u32[]{:S(2)}, u32[]{:S(2)}) collective-permute-start(bf16[32,2880]{1,0:T(8,128)(2,1)S(1)} %get-tuple-element.37), channel_id=1, source_target_pairs={{0,2},{1,3},{2,0},{3,1},{4,6},{5,7},{6,4},{7,5},{8,10},{9,11},{10,... | collective-permute-start | bytes 552968 | tf_op jit(solution)/shard_map/ppermute | solution.py:39
  63.7 1.7 %collective-permute-start.15 = (bf16[32,2880]{1,0:T(8,128)(2,1)S(1)}, bf16[32,2880]{1,0:T(8,128)(2,1)S(1)}, u32[]{:S(2)}, u32[]{:S(2)}) collective-permute-start(bf16[32,2880]{1,0:T(8,128)(2,1)S(1)} %get-tuple-element.38), channel_id=1, source_target_pairs={{0,4},{1,5},{2,6},{3,7},{4,0},{5,1},{6,2},{7,3},{8,12},{9,13},{10,... | collective-permute-start | bytes 552968 | tf_op jit(solution)/shard_map/ppermute | solution.py:39
  65.4 0.6 collective-permute-start.16
  66.0 3.4 %collective-permute-done.14.refs_1_ = bf16[32,2880]{1,0:T(8,128)(2,1)S(1)} collective-permute-done((bf16[32,2880]{1,0:T(8,128)(2,1)S(1)}, bf16[32,2880]{1,0:T(8,128)(2,1)S(1)}, u32[]{:S(2)}, u32[]{:S(2)}) %collective-permute-start.14) | collective-permute-done | bytes 184352 | tf_op jit(solution)/shard_map/ppermute | solution.py:39
  69.4 1.9 %collective-permute-done.15.refs_2_ = bf16[32,2880]{1,0:T(8,128)(2,1)S(1)} collective-permute-done((bf16[32,2880]{1,0:T(8,128)(2,1)S(1)}, bf16[32,2880]{1,0:T(8,128)(2,1)S(1)}, u32[]{:S(2)}, u32[]{:S(2)}) %collective-permute-start.15) | collective-permute-done | bytes 184352 | tf_op jit(solution)/shard_map/ppermute | solution.py:39
  71.3 3.3 %collective-permute-done.16.refs_3_ = bf16[32,2880]{1,0:T(8,128)(2,1)S(1)} collective-permute-done((bf16[32,2880]{1,0:T(8,128)(2,1)S(1)}, bf16[32,2880]{1,0:T(8,128)(2,1)S(1)}, u32[]{:S(2)}, u32[]{:S(2)}) %collective-permute-start.16) | collective-permute-done | bytes 184352 | tf_op jit(solution)/shard_map/ppermute | solution.py:39
  74.6 0.1 add_split.5
  74.7 3.4 %collective-permute-start.17 = (bf16[16,2880]{1,0:T(8,128)(2,1)S(1)}, bf16[16,2880]{1,0:T(8,128)(2,1)S(1)}, u32[]{:S(2)}, u32[]{:S(2)}) collective-permute-start(bf16[16,2880]{1,0:T(8,128)(2,1)S(1)} %get-tuple-element.41), channel_id=1, source_target_pairs={{0,8},{1,9},{2,10},{3,11},{4,12},{5,13},{6,14},{7,15},{8,0},{9,1},... | collective-permute-start | bytes 276488 | tf_op jit(solution)/shard_map/ppermute | solution.py:39
  78.2 4.3 %collective-permute-done.17.received = bf16[16,2880]{1,0:T(8,128)(2,1)S(1)} collective-permute-done((bf16[16,2880]{1,0:T(8,128)(2,1)S(1)}, bf16[16,2880]{1,0:T(8,128)(2,1)S(1)}, u32[]{:S(2)}, u32[]{:S(2)}) %collective-permute-start.17) | collective-permute-done | bytes 92192 | tf_op jit(solution)/shard_map/ppermute | solution.py:39
  82.5 0.7 finish.1
  (14 shorter events, 0.0 us)
Async XLA Ops:
  0.6 8.9 %copy-start.4 = (bf16[256,2880]{0,1:T(8,128)(2,1)S(1)}, bf16[256,2880]{0,1:T(8,128)(2,1)}, u32[]{:S(2)}) copy-start(bf16[256,2880]{0,1:T(8,128)(2,1)} %param.16) | copy-start | bytes 4423684
  7.9 1.6 %collective-permute-start = (bf16[2,64,256]{2,1,0:T(8,128)(2,1)}, bf16[2,64,256]{2,1,0:T(8,128)(2,1)S(1)}, u32[]{:S(2)}, u32[]{:S(2)}) collective-permute-start(bf16[2,64,256]{2,1,0:T(8,128)(2,1)} %get-tuple-element.23), channel_id=1, source_target_pairs={{0,1},{1,0},{2,3},{3,2},{4,5},{5,4},{6,7},{7,6},{8,9},{9,8},{10,11... | collective-permute-start | bytes 196616 | tf_op jit(solution)/shard_map/ppermute | solution.py:39
  9.5 42.8 %slice-start = ((s8[8478720]{0:T(1024)(128)(4,1)}), s8[4194304]{0:T(1024)(128)(4,1)S(1)}, s32[]{:S(2)}) async-start(s8[8478720]{0:T(1024)(128)(4,1)} %bitcast.14), calls=%async_computation | async-start | bytes 8388608
  9.5 42.8 %slice-start.3 = ((s8[8478720]{0:T(1024)(128)(4,1)}), s8[4194304]{0:T(1024)(128)(4,1)S(1)}, s32[]{:S(2)}) async-start(s8[8478720]{0:T(1024)(128)(4,1)} %bitcast.17), calls=%async_computation.3 | async-start | bytes 8388608
  9.5 42.8 %slice-start.6 = ((s8[8478720]{0:T(1024)(128)(4,1)}), s8[4194304]{0:T(1024)(128)(4,1)S(1)}, s32[]{:S(2)}) async-start(s8[8478720]{0:T(1024)(128)(4,1)} %bitcast.20), calls=%async_computation.6 | async-start | bytes 8388608
  9.5 1.0 %copy-start.5 = (bf16[2,64,256]{2,1,0:T(8,128)(2,1)S(1)}, bf16[2,64,256]{2,1,0:T(8,128)(2,1)}, u32[]{:S(2)}) copy-start(bf16[2,64,256]{2,1,0:T(8,128)(2,1)} %get-tuple-element.22.refs_0_) | copy-start | bytes 196612
  10.5 16.8 %copy-start.1 = (bf16[2,8,2880]{2,1,0:T(8,128)(2,1)S(1)}, bf16[2,8,2880]{2,1,0:T(8,128)(2,1)}, u32[]{:S(2)}) copy-start(bf16[2,8,2880]{2,1,0:T(8,128)(2,1)} %param.15) | copy-start | bytes 276484
  10.5 16.8 %copy-start.3 = (s32[2,8,4]{1,2,0:T(4,128)S(1)}, s32[2,8,4]{1,2,0:T(4,128)}, u32[]{:S(2)}) copy-start(s32[2,8,4]{1,2,0:T(4,128)} %param.21) | copy-start | bytes 772
  10.5 28.7 %copy-start.2 = (bf16[2880,16]{0,1:T(8,128)(2,1)S(1)}, bf16[2880,16]{0,1:T(8,128)(2,1)}, u32[]{:S(2)}) copy-start(bf16[2880,16]{0,1:T(8,128)(2,1)} %param.17) | copy-start | bytes 276484
  10.5 41.8 %slice-start.1 = ((s8[8478720]{0:T(1024)(128)(4,1)}), s8[4194304]{0:T(1024)(128)(4,1)S(1)}, s32[]{:S(2)}) async-start(s8[8478720]{0:T(1024)(128)(4,1)} %bitcast.14), calls=%async_computation.1 | async-start | bytes 8388608
  10.5 41.8 %slice-start.2 = ((s8[8478720]{0:T(1024)(128)(4,1)}), s8[90112]{0:T(1024)(128)(4,1)S(1)}, s32[]{:S(2)}) async-start(s8[8478720]{0:T(1024)(128)(4,1)} %bitcast.14), calls=%async_computation.2 | async-start | bytes 180224
  10.5 41.8 %slice-start.4 = ((s8[8478720]{0:T(1024)(128)(4,1)}), s8[4194304]{0:T(1024)(128)(4,1)S(1)}, s32[]{:S(2)}) async-start(s8[8478720]{0:T(1024)(128)(4,1)} %bitcast.17), calls=%async_computation.4 | async-start | bytes 8388608
  10.5 41.8 %slice-start.5 = ((s8[8478720]{0:T(1024)(128)(4,1)}), s8[90112]{0:T(1024)(128)(4,1)S(1)}, s32[]{:S(2)}) async-start(s8[8478720]{0:T(1024)(128)(4,1)} %bitcast.17), calls=%async_computation.5 | async-start | bytes 180224
  10.6 41.8 %slice-start.7 = ((s8[8478720]{0:T(1024)(128)(4,1)}), s8[4194304]{0:T(1024)(128)(4,1)S(1)}, s32[]{:S(2)}) async-start(s8[8478720]{0:T(1024)(128)(4,1)} %bitcast.20), calls=%async_computation.7 | async-start | bytes 8388608
  10.6 41.8 %slice-start.8 = ((s8[8478720]{0:T(1024)(128)(4,1)}), s8[90112]{0:T(1024)(128)(4,1)S(1)}, s32[]{:S(2)}) async-start(s8[8478720]{0:T(1024)(128)(4,1)} %bitcast.20), calls=%async_computation.8 | async-start | bytes 180224
  11.6 2.3 %collective-permute-start.1 = (bf16[128,2944]{1,0:T(8,128)(2,1)S(1)}, bf16[128,2944]{1,0:T(8,128)(2,1)S(1)}, u32[]{:S(2)}, u32[]{:S(2)}) collective-permute-start(bf16[128,2944]{1,0:T(8,128)(2,1)S(1)} %get-tuple-element.25), channel_id=1, source_target_pairs={{0,1},{1,0},{2,3},{3,2},{4,5},{5,4},{6,7},{7,6},{8,9},{9,8},{10,11... | collective-permute-start | bytes 2261000 | tf_op jit(solution)/shard_map/ppermute | solution.py:39
  14.1 8.0 %collective-permute-start.2 = (bf16[32,2880]{1,0:T(8,128)(2,1)S(1)}, bf16[32,2880]{1,0:T(8,128)(2,1)S(1)}, u32[]{:S(2)}, u32[]{:S(2)}) collective-permute-start(bf16[32,2880]{1,0:T(8,128)(2,1)S(1)} %get-tuple-element.27), channel_id=1, source_target_pairs={{0,2},{1,3},{2,0},{3,1},{4,6},{5,7},{6,4},{7,5},{8,10},{9,11},{10,... | collective-permute-start | bytes 552968 | tf_op jit(solution)/shard_map/ppermute | solution.py:39
  17.0 7.6 %collective-permute-start.3 = (bf16[32,2880]{1,0:T(8,128)(2,1)S(1)}, bf16[32,2880]{1,0:T(8,128)(2,1)S(1)}, u32[]{:S(2)}, u32[]{:S(2)}) collective-permute-start(bf16[32,2880]{1,0:T(8,128)(2,1)S(1)} %get-tuple-element.28), channel_id=1, source_target_pairs={{0,4},{1,5},{2,6},{3,7},{4,0},{5,1},{6,2},{7,3},{8,12},{9,13},{10,... | collective-permute-start | bytes 552968 | tf_op jit(solution)/shard_map/ppermute | solution.py:39
  18.6 8.8 %collective-permute-start.4 = (bf16[32,2880]{1,0:T(8,128)(2,1)S(1)}, bf16[32,2880]{1,0:T(8,128)(2,1)S(1)}, u32[]{:S(2)}, u32[]{:S(2)}) collective-permute-start(bf16[32,2880]{1,0:T(8,128)(2,1)S(1)} %get-tuple-element.29), channel_id=1, source_target_pairs={{0,6},{1,7},{2,4},{3,5},{4,2},{5,3},{6,0},{7,1},{8,14},{9,15},{10,... | collective-permute-start | bytes 552968 | tf_op jit(solution)/shard_map/ppermute | solution.py:39
  28.2 11.0 %collective-permute-start.5 = (bf16[32,2944]{1,0:T(8,128)(2,1)S(1)}, bf16[32,2944]{1,0:T(8,128)(2,1)S(1)}, u32[]{:S(2)}, u32[]{:S(2)}) collective-permute-start(bf16[32,2944]{1,0:T(8,128)(2,1)S(1)} %get-tuple-element.31.mine), channel_id=1, source_target_pairs={{0,8},{1,9},{2,10},{3,11},{4,12},{5,13},{6,14},{7,15},{8,0},{9,1},... | collective-permute-start | bytes 565256 | tf_op jit(solution)/shard_map/ppermute | solution.py:39
  40.1 8.6 %collective-permute-start.8 = (bf16[32,2944]{1,0:T(8,128)(2,1)S(1)}, bf16[32,2944]{1,0:T(8,128)(2,1)S(1)}, u32[]{:S(2)}, u32[]{:S(2)}) collective-permute-start(bf16[32,2944]{1,0:T(8,128)(2,1)S(1)} %get-tuple-element.33.refs_0_), channel_id=1, source_target_pairs={{0,6},{1,7},{2,4},{3,5},{4,2},{5,3},{6,0},{7,1},{8,14},{9,15},{10,... | collective-permute-start | bytes 565256 | tf_op jit(solution)/shard_map/ppermute | solution.py:39
  41.6 9.0 %collective-permute-start.7 = (bf16[32,2944]{1,0:T(8,128)(2,1)S(1)}, bf16[32,2944]{1,0:T(8,128)(2,1)S(1)}, u32[]{:S(2)}, u32[]{:S(2)}) collective-permute-start(bf16[32,2944]{1,0:T(8,128)(2,1)S(1)} %get-tuple-element.33.refs_0_), channel_id=1, source_target_pairs={{0,4},{1,5},{2,6},{3,7},{4,0},{5,1},{6,2},{7,3},{8,12},{9,13},{10,... | collective-permute-start | bytes 565256 | tf_op jit(solution)/shard_map/ppermute | solution.py:39
  42.9 7.9 %collective-permute-start.6 = (bf16[32,2944]{1,0:T(8,128)(2,1)S(1)}, bf16[32,2944]{1,0:T(8,128)(2,1)S(1)}, u32[]{:S(2)}, u32[]{:S(2)}) collective-permute-start(bf16[32,2944]{1,0:T(8,128)(2,1)S(1)} %get-tuple-element.33.refs_0_), channel_id=1, source_target_pairs={{0,2},{1,3},{2,0},{3,1},{4,6},{5,7},{6,4},{7,5},{8,10},{9,11},{10,... | collective-permute-start | bytes 565256 | tf_op jit(solution)/shard_map/ppermute | solution.py:39
  43.6 7.4 %collective-permute-start.9 = (bf16[32,2944]{1,0:T(8,128)(2,1)S(1)}, bf16[32,2944]{1,0:T(8,128)(2,1)S(1)}, u32[]{:S(2)}, u32[]{:S(2)}) collective-permute-start(bf16[32,2944]{1,0:T(8,128)(2,1)S(1)} %get-tuple-element.33.refs_0_), channel_id=1, source_target_pairs={{0,1},{1,0},{2,3},{3,2},{4,5},{5,4},{6,7},{7,6},{8,9},{9,8},{10,11... | collective-permute-start | bytes 565256 | tf_op jit(solution)/shard_map/ppermute | solution.py:39
  48.7 2.4 %collective-permute-start.12 = (bf16[32,2944]{1,0:T(8,128)(2,1)S(1)}, bf16[32,2944]{1,0:T(8,128)(2,1)S(1)}, u32[]{:S(2)}, u32[]{:S(2)}) collective-permute-start(bf16[32,2944]{1,0:T(8,128)(2,1)S(1)} %collective-permute-done.8.refs_3_), channel_id=1, source_target_pairs={{0,1},{1,0},{2,3},{3,2},{4,5},{5,4},{6,7},{7,6},{8,9},{9,8},{10,11... | collective-permute-start | bytes 565256 | tf_op jit(solution)/shard_map/ppermute | solution.py:39
  50.5 1.4 %collective-permute-start.11 = (bf16[32,2944]{1,0:T(8,128)(2,1)S(1)}, bf16[32,2944]{1,0:T(8,128)(2,1)S(1)}, u32[]{:S(2)}, u32[]{:S(2)}) collective-permute-start(bf16[32,2944]{1,0:T(8,128)(2,1)S(1)} %collective-permute-done.7.refs_2_), channel_id=1, source_target_pairs={{0,1},{1,0},{2,3},{3,2},{4,5},{5,4},{6,7},{7,6},{8,9},{9,8},{10,11... | collective-permute-start | bytes 565256 | tf_op jit(solution)/shard_map/ppermute | solution.py:39
  50.8 1.4 %collective-permute-start.10 = (bf16[32,2944]{1,0:T(8,128)(2,1)S(1)}, bf16[32,2944]{1,0:T(8,128)(2,1)S(1)}, u32[]{:S(2)}, u32[]{:S(2)}) collective-permute-start(bf16[32,2944]{1,0:T(8,128)(2,1)S(1)} %collective-permute-done.6.refs_1_), channel_id=1, source_target_pairs={{0,1},{1,0},{2,3},{3,2},{4,5},{5,4},{6,7},{7,6},{8,9},{9,8},{10,11... | collective-permute-start | bytes 565256 | tf_op jit(solution)/shard_map/ppermute | solution.py:39
  52.4 30.1 %copy-start = (bf16[16,2880]{1,0:T(8,128)(2,1)S(1)}, bf16[16,2880]{1,0:T(8,128)(2,1)}, u32[]{:S(2)}) copy-start(bf16[16,2880]{1,0:T(8,128)(2,1)} %get-tuple-element.32.attended) | copy-start | bytes 276484
  60.0 2.3 %collective-permute-start.13 = (bf16[128,2944]{1,0:T(8,128)(2,1)S(1)}, bf16[128,2944]{1,0:T(8,128)(2,1)S(1)}, u32[]{:S(2)}, u32[]{:S(2)}) collective-permute-start(bf16[128,2944]{1,0:T(8,128)(2,1)S(1)} %get-tuple-element.35), channel_id=1, source_target_pairs={{0,1},{1,0},{2,3},{3,2},{4,5},{5,4},{6,7},{7,6},{8,9},{9,8},{10,11... | collective-permute-start | bytes 2261000 | tf_op jit(solution)/shard_map/ppermute | solution.py:39
  62.5 6.9 %collective-permute-start.14 = (bf16[32,2880]{1,0:T(8,128)(2,1)S(1)}, bf16[32,2880]{1,0:T(8,128)(2,1)S(1)}, u32[]{:S(2)}, u32[]{:S(2)}) collective-permute-start(bf16[32,2880]{1,0:T(8,128)(2,1)S(1)} %get-tuple-element.37), channel_id=1, source_target_pairs={{0,2},{1,3},{2,0},{3,1},{4,6},{5,7},{6,4},{7,5},{8,10},{9,11},{10,... | collective-permute-start | bytes 552968 | tf_op jit(solution)/shard_map/ppermute | solution.py:39
  63.7 7.6 %collective-permute-start.15 = (bf16[32,2880]{1,0:T(8,128)(2,1)S(1)}, bf16[32,2880]{1,0:T(8,128)(2,1)S(1)}, u32[]{:S(2)}, u32[]{:S(2)}) collective-permute-start(bf16[32,2880]{1,0:T(8,128)(2,1)S(1)} %get-tuple-element.38), channel_id=1, source_target_pairs={{0,4},{1,5},{2,6},{3,7},{4,0},{5,1},{6,2},{7,3},{8,12},{9,13},{10,... | collective-permute-start | bytes 552968 | tf_op jit(solution)/shard_map/ppermute | solution.py:39
  65.4 9.2 %collective-permute-start.16 = (bf16[32,2880]{1,0:T(8,128)(2,1)S(1)}, bf16[32,2880]{1,0:T(8,128)(2,1)S(1)}, u32[]{:S(2)}, u32[]{:S(2)}) collective-permute-start(bf16[32,2880]{1,0:T(8,128)(2,1)S(1)} %get-tuple-element.39), channel_id=1, source_target_pairs={{0,6},{1,7},{2,4},{3,5},{4,2},{5,3},{6,0},{7,1},{8,14},{9,15},{10,... | collective-permute-start | bytes 552968 | tf_op jit(solution)/shard_map/ppermute | solution.py:39
  74.7 7.8 %collective-permute-start.17 = (bf16[16,2880]{1,0:T(8,128)(2,1)S(1)}, bf16[16,2880]{1,0:T(8,128)(2,1)S(1)}, u32[]{:S(2)}, u32[]{:S(2)}) collective-permute-start(bf16[16,2880]{1,0:T(8,128)(2,1)S(1)} %get-tuple-element.41), channel_id=1, source_target_pairs={{0,8},{1,9},{2,10},{3,11},{4,12},{5,13},{6,14},{7,15},{8,0},{9,1},... | collective-permute-start | bytes 276488 | tf_op jit(solution)/shard_map/ppermute | solution.py:39

commit v6 on v5

v6 whole, which is shorter than its diff:
```python
import functools
import math

import jax
import jax.numpy as jnp
from jax import lax
from jax.experimental import pallas as pl
from jax.experimental.pallas import tpu as pltpu
from jax.sharding import PartitionSpec as P

HD = 64
KVH = 8
QPK = 8
EXPERTS = 16
SPLIT = 4
REQ_DEV = 8
TILE = 256
LANES = 128
COPY_ROWS = 16
COPIES_AHEAD = 8
LIMIT = 16 << 20
AHEAD = pl.CostEstimate(flops=60_000_000_000, bytes_accessed=150_000_000, transcendentals=0)
ROWS_LAST = (((1,), (1,)), ((), ()))


def plan(device_count):
    bits = device_count.bit_length() - 1
    stages, bit = [(0, 1)], 1
    while bit < bits - 1:
        width = min(2, bits - 1 - bit)
        stages.append((bit, width))
        bit += width
    stages.append((bits - 1, 1))
    masks = [0]
    for bit, width in stages:
        masks = [mask | (r << bit) for mask in masks for r in range(1 << width)]
    return stages, masks


def from_mask(value, mask):
    pairs = [(source, source ^ mask) for source in range(lax.axis_size("req"))]
    return lax.ppermute(value, "req", pairs)


def padded(width):
    return pl.cdiv(width, LANES) * LANES


def whole_call(kernel, name, outs, inputs, scratch=(), scalars=(), **options):
    return pl.pallas_call(
        kernel,
        out_shape=outs,
        in_specs=[pl.BlockSpec(memory_space=pltpu.SMEM)] * len(scalars)
        + [pl.BlockSpec(memory_space=pltpu.VMEM)] * len(inputs),
        out_specs=[pl.BlockSpec(memory_space=pltpu.VMEM)] * len(outs),
        scratch_shapes=list(scratch),
        compiler_params=pltpu.CompilerParams(vmem_limit_bytes=LIMIT),
        name=name,
        **options,
    )(*scalars, *inputs)


def split_kernel(count, pieces, *refs):
    total = refs[0][...]
    width = total.shape[1]
    for ref in refs[1:count]:
        total = total + ref[:, :width].astype(jnp.float32)
    outs = refs[count:]
    size = outs[0].shape[0]
    for index, out in enumerate(outs):
        out[...] = total[index * size : (index + 1) * size].astype(out.dtype)


def add_split(total, received, pieces, chunks=1):
    shape = (total.shape[0] // (pieces * chunks), total.shape[1])
    types = [jnp.float32] + [jnp.bfloat16] * (pieces - 1)
    found = whole_call(
        functools.partial(split_kernel, 1 + len(received), pieces),
        "add_split",
        [jax.ShapeDtypeStruct(shape, dtype) for dtype in types] * chunks,
        [total, *received],
    )
    return [found[c * pieces : (c + 1) * pieces] for c in range(chunks)]


def scatter_sum(pieces, stages):
    for index, (bit, bits) in enumerate(stages):
        received = [from_mask(pieces[r], r << bit) for r in range(1, 1 << bits)]
        if index + 1 < len(stages):
            (pieces,) = add_split(pieces[0], received, 1 << stages[index + 1][1])
    return pieces[0], received


def gather_rows(pieces, stages):
    for bit, bits in reversed(stages):
        if bit:
            held = jnp.concatenate(pieces, axis=0) if len(pieces) > 1 else pieces[0]
            pieces = [held] + [from_mask(held, r << bit) for r in range(1, 1 << bits)]
        else:
            pieces = pieces + [from_mask(piece, 1) for piece in pieces]
    return pieces


def share_kernel(batch, count, routes, *refs):
    received, residual = refs[:count], refs[count]
    total, message = refs[count + 1 :]
    rows, width = residual.shape[1:]
    value = received[0][...]
    for ref in received[1:]:
        value = value + ref[:, :width].astype(jnp.float32)
    total[:rows, :width] = value[:rows] + residual[batch].astype(jnp.float32)
    total[rows:, :width] = value[rows:]
    message[:, :width] = total[:, :width].astype(jnp.bfloat16)
    base = width // LANES * LANES
    used = width - base
    lane = lax.broadcasted_iota(jnp.int32, (2 * rows, LANES), 1)
    row = lax.broadcasted_iota(jnp.int32, (2 * rows, LANES), 0)
    named = lane < 0
    for i in range(routes.shape[2]):
        for t in range(routes.shape[1]):
            named |= (row == i) & (lane == used + routes[batch, t, i])
    end = jnp.where(lane < used, total[:, base:], jnp.where(named, 1.0, 0.0))
    message[:, base:] = end.astype(jnp.bfloat16)


def norm_kernel(total, mine, theirs, router, attended, payload):
    rows, width = attended.shape
    base = width // LANES * LANES
    used = width - base
    lane = lax.broadcasted_iota(jnp.int32, (2 * rows, LANES), 1)
    place = lax.broadcasted_iota(jnp.int32, (EXPERTS, LANES), 1) - used
    place -= lax.broadcasted_iota(jnp.int32, (EXPERTS, LANES), 0)
    first = jnp.where(place == 0, 1.0, 0.0).astype(jnp.bfloat16)
    second = jnp.where(place == EXPERTS, 1.0, 0.0).astype(jnp.bfloat16)
    other = theirs[...].astype(jnp.float32)
    swapped = jnp.concatenate([other[rows:, :width], other[:rows, :width]], axis=0)
    value = total[:, :width] + swapped
    attended[...] = value[:rows].astype(jnp.bfloat16)
    value = value.astype(jnp.bfloat16).astype(jnp.float32)
    mean = jnp.sum(value * value, axis=1, keepdims=True) * (1.0 / width)
    normed = (value * lax.rsqrt(mean + 1e-05)).astype(jnp.bfloat16)
    payload[:, :width] = normed
    logits = lax.dot_general(normed, router[...], ROWS_LAST, preferred_element_type=jnp.float32)
    ends = jnp.concatenate(
        [mine[:, base:].astype(jnp.float32)[:rows], other[:rows, base:]], axis=0
    )
    named = lax.dot_general(
        ends.astype(jnp.bfloat16), first, ROWS_LAST, preferred_element_type=jnp.float32
    )
    named = named > 0.5
    top = jnp.max(jnp.where(named, logits, -jnp.inf), axis=1, keepdims=True)
    weight = jnp.where(named, jnp.exp(jnp.where(named, logits - top, 0.0)), 0.0)
    gate = weight / jnp.sum(weight, axis=1, keepdims=True)
    high = gate.astype(jnp.bfloat16)
    low = (gate - high.astype(jnp.float32)).astype(jnp.bfloat16)
    end = jnp.dot(high, first, preferred_element_type=jnp.float32)
    end = end + jnp.dot(low, second, preferred_element_type=jnp.float32)
    kept = payload[:, base:].astype(jnp.float32)
    payload[:, base:] = jnp.where(lane < used, kept, end).astype(jnp.bfloat16)


def attend(batch, total, received, residual, routes, router, stages):
    rows, width = residual.shape[1:]
    wide = padded(width)
    total, message = whole_call(
        functools.partial(share_kernel, batch, 1 + len(received)),
        "share",
        [
            jax.ShapeDtypeStruct((2 * rows, wide), jnp.float32),
            jax.ShapeDtypeStruct((2 * rows, wide), jnp.bfloat16),
        ],
        [total, *received, residual],
        scalars=[routes],
        cost_estimate=pl.CostEstimate(flops=60000000000, bytes_accessed=180000000, transcendentals=0),
    )
    theirs = from_mask(message, 1 << stages[-1][0])
    return whole_call(
        norm_kernel,
        "norm",
        [
            jax.ShapeDtypeStruct((rows, width), jnp.bfloat16),
            jax.ShapeDtypeStruct((2 * rows, wide), jnp.bfloat16),
        ],
        [total, message, theirs, router],
    )


def finish_kernel(batch, *refs):
    rows = refs[:batch]
    sums = refs[batch:-2]
    attended, layer = refs[-2:]
    each = rows[0].shape[0]
    begin = 0
    for total, received in zip(sums[::2], sums[1::2]):
        size = total.shape[1]
        some = slice(begin, begin + size)
        value = total[...] + received[:, :size].astype(jnp.float32)
        for m in range(batch):
            mixture = value[m * each : (m + 1) * each]
            layer[m, :, some] = (rows[m][:, some].astype(jnp.float32) + mixture).astype(
                jnp.bfloat16
            )
        begin += size
    for m in range(batch):
        attended[m] = rows[m][...]


def attention_kernel(group, block, lengths, place, far_q, far_kv, far, *refs):
    outs = refs[:group]
    q_ref, kv_ref, near, query, scores, mixed, done = refs[group:]
    small = [
        pltpu.make_async_copy(far_q, q_ref, done.at[0]),
        pltpu.make_async_copy(far_kv, kv_ref, done.at[1]),
    ]
    for copy in small:
        copy.start()
    batch, rows, window, pair = near.shape
    steps = [(m, i) for m in range(batch) for i in range(0, rows, block)]
    size = min(COPY_ROWS, block)
    copies = [
        pltpu.make_async_copy(
            far.at[m, pl.ds(i, size)], near.at[m, pl.ds(i, size)], done.at[index + 2]
        )
        for index, (m, i) in enumerate((m, i) for m in range(batch) for i in range(0, rows, size))
    ]
    started = finished = 0
    low = lax.broadcasted_iota(jnp.int32, (block, pair), 1) < HD
    position = lax.broadcasted_iota(jnp.int32, (QPK, window), 1)
    heads = QPK // group
    for m, i in steps:
        while started < min(finished + COPIES_AHEAD, len(copies)):
            copies[started].start()
            started += 1
        some = slice(i, i + block)
        if finished == 0:
            for copy in small:
                copy.wait()
        for h in range(QPK):
            tile = q_ref[m, some, (h // 2) * pair : (h // 2 + 1) * pair].astype(jnp.float32)
            tile = tile * (1.0 / math.sqrt(HD))
            if h % 2:
                tile = pltpu.roll(tile, HD, 1)
            query[pl.ds(h, block, stride=QPK), :] = jnp.where(low, tile, 0.0)
        fresh = kv_ref[m, some, :].astype(jnp.float32)
        fresh = jnp.broadcast_to(fresh[:, None, :], (block, QPK, pair))
        fresh = fresh.reshape(block * QPK, pair)
        own = jnp.sum(query[...] * fresh, axis=1, keepdims=True)
        first = place[0] * rows + i
        for _ in range(block // size):
            copies[finished].wait()
            finished += 1
            if started < len(copies):
                copies[started].start()
                started += 1
        for r in range(block):
            part = slice(r * QPK, (r + 1) * QPK)
            found = lax.dot_general(
                query[part, :].astype(jnp.bfloat16),
                near[m, i + r],
                ROWS_LAST,
                preferred_element_type=jnp.float32,
            )
            scores[part, :] = jnp.where(position < lengths[m, first + r], found, -jnp.inf)
        top = jnp.maximum(jnp.max(scores[...], axis=1, keepdims=True), own)
        weight = jnp.exp(scores[...] - top)
        weight_own = jnp.exp(own - top)
        total = jnp.sum(weight, axis=1, keepdims=True) + weight_own
        scores[...] = weight / total
        prob_own = (weight_own / total).astype(jnp.bfloat16).astype(jnp.float32)
        for r in range(block):
            part = slice(r * QPK, (r + 1) * QPK)
            mixed[part, :] = jnp.dot(
                scores[part, :].astype(jnp.bfloat16),
                near[m, i + r],
                preferred_element_type=jnp.float32,
            )
        mixed[...] = mixed[...] + prob_own * fresh
        for r in range(group):
            start = (place[0] ^ r) * heads
            for j in range(0, heads, 2):
                left = pltpu.roll(mixed[pl.ds(start + j, block, stride=QPK), :], HD, 1)
                if heads == 1:
                    outs[r][m, some, :] = left[:, :HD].astype(jnp.bfloat16)
                else:
                    right = mixed[pl.ds(start + j + 1, block, stride=QPK), :]
                    outs[r][m, some, j * HD : (j + 2) * HD] = jnp.where(low, left, right).astype(
                        jnp.bfloat16
                    )


def attention(lengths, place, queries, new_kv, cache, group, block=64):
    batch, rows, window, pair = cache.shape
    block = min(block, rows)
    width = QPK // group * HD
    small = pl.BlockSpec(memory_space=pltpu.SMEM)
    whole = pl.BlockSpec(memory_space=pltpu.VMEM)
    return pl.pallas_call(
        functools.partial(attention_kernel, group, block),
        out_shape=[pltpu.VMEM((batch, rows, width), jnp.bfloat16)] * group,
        in_specs=[small] * 2 + [pl.BlockSpec(memory_space=pl.ANY)] * 3,
        out_specs=[whole] * group,
        scratch_shapes=[
            pltpu.VMEM(queries.shape, jnp.bfloat16),
            pltpu.VMEM(new_kv.shape, jnp.bfloat16),
            pltpu.VMEM(cache.shape, jnp.bfloat16),
            pltpu.VMEM((block * QPK, pair), jnp.float32),
            pltpu.VMEM((block * QPK, window), jnp.float32),
            pltpu.VMEM((block * QPK, pair), jnp.float32),
            pltpu.SemaphoreType.DMA((2 + batch * rows // min(COPY_ROWS, block),)),
        ],
        compiler_params=pltpu.CompilerParams(vmem_limit_bytes=56 << 20),
        cost_estimate=pl.CostEstimate(
            flops=10000000000, bytes_accessed=30000000, transcendentals=0
        ),
        name="attention",
    )(lengths, place, queries, new_kv, cache)


def project_kernel(group, masks, me_ref, *refs):
    held = refs[:group]
    weight, outs, wide, rows = refs[group], refs[group + 1 : -2], *refs[-2:]
    batch, members, width = held[0].shape
    for r in range(group):
        wide[r] = held[r][...].astype(jnp.float32)
    me = me_ref[0]
    per_member = members // REQ_DEV
    for p, mask in enumerate(masks):
        block = me ^ mask
        member = (block // per_member) ^ (me % group)
        start = pl.multiple_of((block % per_member) * REQ_DEV, REQ_DEV)
        for m in range(batch):
            at = (m * len(masks) + p) * REQ_DEV
            rows[at : at + REQ_DEV, :] = wide[member, m, pl.ds(start, REQ_DEV), :]
    half, width = outs[0].shape
    found = lax.dot_general(
        rows[...].astype(jnp.bfloat16),
        weight[...],
        ROWS_LAST,
        preferred_element_type=jnp.float32,
    )
    for index, out in enumerate(outs):
        out[:, :width] = found[index * half : (index + 1) * half].astype(out.dtype)


def project(me, held, weight, masks):
    batch, members, width = held[0].shape
    group = len(held)
    half = len(masks) * REQ_DEV // 2
    found = whole_call(
        functools.partial(project_kernel, group, masks),
        "project",
        [
            jax.ShapeDtypeStruct((half, weight.shape[0]), jnp.float32),
            jax.ShapeDtypeStruct((half, padded(weight.shape[0])), jnp.bfloat16),
        ]
        * batch,
        [*held, weight],
        scratch=[
            pltpu.VMEM((group,) + held[0].shape, jnp.float32),
            pltpu.VMEM((2 * batch * half, width), jnp.float32),
        ],
        scalars=[me],
    )
    return [found[2 * m : 2 * m + 2] for m in range(batch)]


def expert_kernel(batch, count, hidden, me_ref, *refs):
    pieces = refs[:count]
    w_gate, w_up, w_down = refs[count : count + 3]
    keep, send, active, weights, rows = refs[count + 3 :]
    units, width = w_gate.shape
    at = 0
    for piece in pieces:
        rows[at : at + piece.shape[0], :] = piece[...]
        at += piece.shape[0]
    for start in range(0, units, TILE):
        some = slice(start, min(start + TILE, units))
        gate = lax.dot_general(
            rows[:, :width], w_gate[some, :], ROWS_LAST, preferred_element_type=jnp.float32
        )
        up = lax.dot_general(
            rows[:, :width], w_up[some, :], ROWS_LAST, preferred_element_type=jnp.float32
        )
        active[:, some] = ((up + 1.0) * gate * jax.nn.sigmoid(1.702 * gate)).astype(jnp.bfloat16)
    base = width // LANES * LANES
    tail = rows[:, base:].astype(jnp.float32)
    lane = lax.broadcasted_iota(jnp.int32, tail.shape, 1) - (width - base)
    deep = min(units, SPLIT * hidden)
    for index in range(units // deep):
        expert = (me_ref[0] * units + index * deep) // (SPLIT * hidden)
        picked = (lane == expert) | (lane == expert + EXPERTS)
        weight = jnp.sum(jnp.where(picked, tail, 0.0), axis=1, keepdims=True)
        weights[index] = jnp.broadcast_to(weight, weights.shape[1:])
    down_kernel(batch, hidden, 0, active, weights, w_down, keep, send)


def down_kernel(batch, hidden, begin, active, weights, w_down, keep, send):
    units = w_down.shape[0]
    deep = min(units, SPLIT * hidden)
    half, width = keep.shape
    for start in range(0, width, 2 * TILE):
        some = slice(start, min(start + 2 * TILE, width))
        out = 0.0
        for index in range(units // deep):
            part = slice(index * deep, (index + 1) * deep)
            out = out + weights[index, :, :1] * jnp.dot(
                active[:, part],
                w_down[part, begin + some.start : begin + some.stop],
                preferred_element_type=jnp.float32,
            )
        blocks = half // (batch * REQ_DEV)
        for side, ref in enumerate((keep, send)):
            ordered = []
            for p in range(side * blocks, (side + 1) * blocks):
                for m in range(batch):
                    at = (m * 2 * blocks + p) * REQ_DEV
                    ordered.append(out[at : at + REQ_DEV])
            ref[:, some] = jnp.concatenate(ordered, axis=0).astype(ref.dtype)


def expert_sums(me, batch, pieces, w_gate, w_up, w_down):
    hidden, width = w_down.shape[1:]
    units = w_down.shape[0] * hidden
    count = sum(piece.shape[0] for piece in pieces)
    parts = max(1, units // (SPLIT * hidden))
    first = padded(pl.cdiv(width, 2))

    def halves(columns):
        return [
            jax.ShapeDtypeStruct((count // 2, columns), jnp.float32),
            jax.ShapeDtypeStruct((count // 2, padded(columns)), jnp.bfloat16),
        ]

    down = w_down.reshape(units, width)
    keep, send, active, weights = whole_call(
        functools.partial(expert_kernel, batch, len(pieces), hidden),
        "experts",
        halves(first)
        + [
            jax.ShapeDtypeStruct((count, units), jnp.bfloat16),
            jax.ShapeDtypeStruct((parts, count, LANES), jnp.float32),
        ],
        [
            *pieces,
            w_gate.swapaxes(1, 2).reshape(units, width),
            w_up.swapaxes(1, 2).reshape(units, width),
            down,
        ],
        scratch=[pltpu.VMEM((count, pieces[0].shape[1]), jnp.bfloat16)],
        scalars=[me],
    )
    rest = whole_call(
        functools.partial(down_kernel, batch, hidden, first),
        "down",
        halves(width - first),
        [active, weights, down],
    )
    return [(keep, send), rest]


def shards(queries, new_kv, cache, lengths, residual, o_proj, router, w_gate, w_up, w_down, routes):
    device_count = lax.axis_size("req")
    device_index = lax.axis_index("req")
    stages, masks = plan(device_count)
    group_size = max(1, device_count // KVH)
    batch = residual.shape[0]
    me = device_index.astype(jnp.int32)[None]

    held = attention(lengths, me % group_size, queries, new_kv, cache, group_size)
    held = [held[0]] + [from_mask(held[r], r) for r in range(1, group_size)]
    halves = project(me, held, o_proj.T, masks)
    attended, pieces = [], []
    for m in range(batch):
        total, received = scatter_sum(halves[m], stages[:-1])
        rows, payload = attend(
            m, total, received, residual, routes.swapaxes(1, 2), router.T, stages
        )
        attended.append(rows)
        pieces += gather_rows([payload], stages[:-1])
    sums = []
    for halves in expert_sums(me, batch, pieces, w_gate, w_up, w_down):
        total, (received,) = scatter_sum(halves, stages)
        sums += [total, received]
    return whole_call(
        functools.partial(finish_kernel, batch),
        "finish",
        [jax.ShapeDtypeStruct(residual.shape, jnp.bfloat16)] * 2,
        [*attended, *sums],
    )


def solution(mesh):
    placed = (
        P(None, ("groups", "req"), None),
        P(None, ("groups", "req"), None),
        P(None, ("groups", "req"), None, None),
        P(None, "groups"),
        P(None, ("groups", "req"), None),
        P("req", None),
        P(),
        P("req", None, None),
        P("req", None, None),
        P("req", None, None),
        P(None, ("groups", "req"), None),
    )
    return jax.shard_map(
        shards,
        mesh=mesh,
        in_specs=placed,
        out_specs=(P(None, ("groups", "req"), None), P(None, ("groups", "req"), None)),
        check_vma=False,
    )
```

time: 83.4 us -> 74.1 us (0.89)
  waiting for transfers between devices: 43.3 us -> 22.5 us
  starting transfers between devices: 19.2 us -> 32.2 us
  local copies, waits for them, and re-layouts: 1.04 us -> 0.08 us
    ppermute x18 -> x35, waiting for transfers between devices: 43.3 us -> 22.5 us  [from_mask(): return lax.ppermute(value, 'req', pairs)]
    ppermute x18 -> x35, starting transfers between devices: 19.2 us -> 32.2 us  [from_mask(): return lax.ppermute(value, 'req', pairs)]
    pallas_call x3 -> x1, Pallas kernels: 15.9 us -> 6.24 us  [attention(): pl.pallas_call(functools.partial(attention_kernel, group, block), out_sha...]
    pallas_call x6 -> x14, Pallas kernels: 2.86 us -> 11.9 us  [whole_call(): pl.pallas_call(kernel, out_shape=outs, in_specs=[pl.BlockSpec(memory_spac...]
    unnamed x30 -> x26, local copies, waits for them, and re-layouts: 1.04 us -> 0.08 us
  transfers between devices with their start and end apart: 18 -> 35, of which waited for: 16 -> 15; matrix products, arithmetic and copies ran while one was open for 0% -> 0% of each run, Pallas kernels for 0% -> 6%
where the time goes in v6:
time: 74.1 us; the launch traced here: 73.9 us
  starting transfers between devices  32.2 us (43%)
  waiting for transfers between devices  22.5 us (30%)
  Pallas kernels  18.2 us (25%)
  between operations  0.98 us (1%)
    ppermute x35, starting transfers between devices, from_mask(): return lax.ppermute(value, 'req', pairs)  32.2 us
    ppermute x35, waiting for transfers between devices, from_mask(): return lax.ppermute(value, 'req', pairs)  22.5 us
    pallas_call x14, Pallas kernels, whole_call(): pl.pallas_call(kernel, out_shape=outs, in_specs=[pl.BlockSpec(memory_spac...  11.9 us
    pallas_call x1, Pallas kernels, attention(): pl.pallas_call(functools.partial(attention_kernel, group, block), out_sha...  6.24 us
  transfers between devices with their start and end apart: 35, of which 15 were waited for; matrix products, arithmetic and copies ran while one was open for 0% of the time, Pallas kernels for 6%

profile of v6, /device:TPU:0, one launch (start us, length us, event | category | flops | bytes accessed | tf_op | source)
XLA Modules:
  0.0 73.9 jit_solution(10806126382781153613)
XLA Ops:
  0.7 6.2 %attention.1 = (bf16[2,64,256]{2,1,0:T(8,128)(2,1)S(1)}, bf16[2,64,256]{2,1,0:T(8,128)(2,1)S(1)}) custom-call(s32[2,128]{1,0:T(2,128)} %lengths.1, s32[1]{0:T(128)S(6)} %select_n.7.place, bf16[2,64,512]{2,1,0:T(8,128)(2,1)} %far_q.1, bf16[2,64,128]{2,1,0:T(8,128)(2,1)} %far_kv.1, bf16[2,64,128,128]{3,2,1,0:T(8,128)(2,1)} %far.1), custom_call_target="tpu_custom_call" | custom-call | flops 10000000000 | bytes 30000000 | tf_op jit(solution)/shard_map/attention/pallas_call | solution.py:297
  6.9 0.5 collective-permute-start
  7.4 0.9 %collective-permute-done.refs_1_ = bf16[2,64,256]{2,1,0:T(8,128)(2,1)S(1)} collective-permute-done((bf16[2,64,256]{2,1,0:T(8,128)(2,1)S(1)}, bf16[2,64,256]{2,1,0:T(8,128)(2,1)S(1)}, u32[]{:S(2)}, u32[]{:S(2)}) %collective-permute-start) | collective-permute-done | bytes 65568 | tf_op jit(solution)/shard_map/ppermute | solution.py:42
  8.3 0.6 project.1
  9.0 0.4 collective-permute-start.1
  9.4 0.2 collective-permute-start.6
  9.6 1.2 %collective-permute-done.1.refs_1_ = bf16[64,2944]{1,0:T(8,128)(2,1)S(1)} collective-permute-done((bf16[64,2944]{1,0:T(8,128)(2,1)S(1)}, bf16[64,2944]{1,0:T(8,128)(2,1)S(1)}, u32[]{:S(2)}, u32[]{:S(2)}) %collective-permute-start.1) | collective-permute-done | bytes 376864 | tf_op jit(solution)/shard_map/ppermute | solution.py:42
  10.8 0.1 add_split.6
  10.8 2.9 %collective-permute-start.2 = (bf16[16,2880]{1,0:T(8,128)(2,1)S(1)}, bf16[16,2880]{1,0:T(8,128)(2,1)S(1)}, u32[]{:S(2)}, u32[]{:S(2)}) collective-permute-start(bf16[16,2880]{1,0:T(8,128)(2,1)S(1)} %get-tuple-element.47), channel_id=1, source_target_pairs={{0,2},{1,3},{2,0},{3,1},{4,6},{5,7},{6,4},{7,5},{8,10},{9,11},{10,... | collective-permute-start | bytes 276488 | tf_op jit(solution)/shard_map/ppermute | solution.py:42
  13.8 1.6 %collective-permute-start.3 = (bf16[16,2880]{1,0:T(8,128)(2,1)S(1)}, bf16[16,2880]{1,0:T(8,128)(2,1)S(1)}, u32[]{:S(2)}, u32[]{:S(2)}) collective-permute-start(bf16[16,2880]{1,0:T(8,128)(2,1)S(1)} %get-tuple-element.48), channel_id=1, source_target_pairs={{0,4},{1,5},{2,6},{3,7},{4,0},{5,1},{6,2},{7,3},{8,12},{9,13},{10,... | collective-permute-start | bytes 276488 | tf_op jit(solution)/shard_map/ppermute | solution.py:42
  15.4 0.1 add_split.7
  15.5 2.0 %collective-permute-start.7 = (bf16[16,2880]{1,0:T(8,128)(2,1)S(1)}, bf16[16,2880]{1,0:T(8,128)(2,1)S(1)}, u32[]{:S(2)}, u32[]{:S(2)}) collective-permute-start(bf16[16,2880]{1,0:T(8,128)(2,1)S(1)} %get-tuple-element.56), channel_id=1, source_target_pairs={{0,2},{1,3},{2,0},{3,1},{4,6},{5,7},{6,4},{7,5},{8,10},{9,11},{10,... | collective-permute-start | bytes 276488 | tf_op jit(solution)/shard_map/ppermute | solution.py:42
  17.4 1.6 %collective-permute-start.8 = (bf16[16,2880]{1,0:T(8,128)(2,1)S(1)}, bf16[16,2880]{1,0:T(8,128)(2,1)S(1)}, u32[]{:S(2)}, u32[]{:S(2)}) collective-permute-start(bf16[16,2880]{1,0:T(8,128)(2,1)S(1)} %get-tuple-element.57), channel_id=1, source_target_pairs={{0,4},{1,5},{2,6},{3,7},{4,0},{5,1},{6,2},{7,3},{8,12},{9,13},{10,... | collective-permute-start | bytes 276488 | tf_op jit(solution)/shard_map/ppermute | solution.py:42
  19.0 0.5 collective-permute-start.9
  19.6 2.2 %collective-permute-done.4.refs_3_ = bf16[16,2880]{1,0:T(8,128)(2,1)S(1)} collective-permute-done((bf16[16,2880]{1,0:T(8,128)(2,1)S(1)}, bf16[16,2880]{1,0:T(8,128)(2,1)S(1)}, u32[]{:S(2)}, u32[]{:S(2)}) %collective-permute-start.4) | collective-permute-done | bytes 92192 | tf_op jit(solution)/shard_map/ppermute | solution.py:42
  21.8 0.0 slice-start.3
  21.8 0.0 slice-start.4
  21.8 0.0 slice-start.6
  21.8 0.0 slice-start.7
  21.8 0.7 share.2
  22.5 2.7 %collective-permute-start.5 = (bf16[16,2944]{1,0:T(8,128)(2,1)S(1)}, bf16[16,2944]{1,0:T(8,128)(2,1)S(1)}, u32[]{:S(2)}, u32[]{:S(2)}) collective-permute-start(bf16[16,2944]{1,0:T(8,128)(2,1)S(1)} %get-tuple-element.51.mine), channel_id=1, source_target_pairs={{0,8},{1,9},{2,10},{3,11},{4,12},{5,13},{6,14},{7,15},{8,0},{9,1},... | collective-permute-start | bytes 282632 | tf_op jit(solution)/shard_map/ppermute | solution.py:42
  25.2 0.0 copy-start.1
  25.2 0.0 slice-start.2
  25.2 0.0 slice-start.5
  25.2 0.0 slice-start.8
  25.3 0.7 share.3
  26.0 3.0 %collective-permute-start.10 = (bf16[16,2944]{1,0:T(8,128)(2,1)S(1)}, bf16[16,2944]{1,0:T(8,128)(2,1)S(1)}, u32[]{:S(2)}, u32[]{:S(2)}) collective-permute-start(bf16[16,2944]{1,0:T(8,128)(2,1)S(1)} %get-tuple-element.60.mine), channel_id=1, source_target_pairs={{0,8},{1,9},{2,10},{3,11},{4,12},{5,13},{6,14},{7,15},{8,0},{9,1},... | collective-permute-start | bytes 282632 | tf_op jit(solution)/shard_map/ppermute | solution.py:42
  28.9 3.2 %collective-permute-done.5.theirs = bf16[16,2944]{1,0:T(8,128)(2,1)S(1)} collective-permute-done((bf16[16,2944]{1,0:T(8,128)(2,1)S(1)}, bf16[16,2944]{1,0:T(8,128)(2,1)S(1)}, u32[]{:S(2)}, u32[]{:S(2)}) %collective-permute-start.5) | collective-permute-done | bytes 94240 | tf_op jit(solution)/shard_map/ppermute | solution.py:42
  32.2 0.5 norm.2
  32.7 0.0 collective-permute-start.14
  32.7 0.1 collective-permute-start.13
  32.8 0.1 collective-permute-start.12
  32.9 3.4 %collective-permute-start.11 = (bf16[16,2944]{1,0:T(8,128)(2,1)S(1)}, bf16[16,2944]{1,0:T(8,128)(2,1)S(1)}, u32[]{:S(2)}, u32[]{:S(2)}) collective-permute-start(bf16[16,2944]{1,0:T(8,128)(2,1)S(1)} %get-tuple-element.62.refs_0_), channel_id=1, source_target_pairs={{0,2},{1,3},{2,0},{3,1},{4,6},{5,7},{6,4},{7,5},{8,10},{9,11},{10,... | collective-permute-start | bytes 282632 | tf_op jit(solution)/shard_map/ppermute | solution.py:42
  36.3 0.5 norm.3
  36.8 0.0 collective-permute-start.21
  36.8 0.1 collective-permute-start.20
  37.0 2.2 %collective-permute-done.13.refs_3_ = bf16[16,2944]{1,0:T(8,128)(2,1)S(1)} collective-permute-done((bf16[16,2944]{1,0:T(8,128)(2,1)S(1)}, bf16[16,2944]{1,0:T(8,128)(2,1)S(1)}, u32[]{:S(2)}, u32[]{:S(2)}) %collective-permute-start.13) | collective-permute-done | bytes 94240 | tf_op jit(solution)/shard_map/ppermute | solution.py:42
  39.2 2.2 %collective-permute-start.18 = (bf16[16,2944]{1,0:T(8,128)(2,1)S(1)}, bf16[16,2944]{1,0:T(8,128)(2,1)S(1)}, u32[]{:S(2)}, u32[]{:S(2)}) collective-permute-start(bf16[16,2944]{1,0:T(8,128)(2,1)S(1)} %get-tuple-element.63.refs_8_), channel_id=1, source_target_pairs={{0,2},{1,3},{2,0},{3,1},{4,6},{5,7},{6,4},{7,5},{8,10},{9,11},{10,... | collective-permute-start | bytes 282632 | tf_op jit(solution)/shard_map/ppermute | solution.py:42
  41.4 0.5 collective-permute-start.16
  41.9 1.5 %collective-permute-done.20.refs_11_ = bf16[16,2944]{1,0:T(8,128)(2,1)S(1)} collective-permute-done((bf16[16,2944]{1,0:T(8,128)(2,1)S(1)}, bf16[16,2944]{1,0:T(8,128)(2,1)S(1)}, u32[]{:S(2)}, u32[]{:S(2)}) %collective-permute-start.20) | collective-permute-done | bytes 94240 | tf_op jit(solution)/shard_map/ppermute | solution.py:42
  43.3 0.4 collective-permute-done.19.refs_10_
  43.7 0.1 collective-permute-start.24
  43.8 1.1 %collective-permute-done.18.refs_9_ = bf16[16,2944]{1,0:T(8,128)(2,1)S(1)} collective-permute-done((bf16[16,2944]{1,0:T(8,128)(2,1)S(1)}, bf16[16,2944]{1,0:T(8,128)(2,1)S(1)}, u32[]{:S(2)}, u32[]{:S(2)}) %collective-permute-start.18) | collective-permute-done | bytes 94240 | tf_op jit(solution)/shard_map/ppermute | solution.py:42
  44.9 0.5 collective-permute-start.22
  45.4 0.8 %collective-permute-done.23.refs_14_ = bf16[16,2944]{1,0:T(8,128)(2,1)S(1)} collective-permute-done((bf16[16,2944]{1,0:T(8,128)(2,1)S(1)}, bf16[16,2944]{1,0:T(8,128)(2,1)S(1)}, u32[]{:S(2)}, u32[]{:S(2)}) %collective-permute-start.23) | collective-permute-done | bytes 94240 | tf_op jit(solution)/shard_map/ppermute | solution.py:42
  46.2 0.2 collective-permute-done.22.refs_13_
  46.4 6.3 %experts.1 = (f32[128,1536]{1,0:T(8,128)S(1)}, bf16[128,1536]{1,0:T(8,128)(2,1)S(1)}, bf16[256,1440]{1,0:T(8,128)(2,1)S(1)}, f32[1,256,128]{2,1,0:T(8,128)S(1)}) custom-call(s32[1]{0:T(128)} %bitcast.1.me_ref, bf16[16,2944]{1,0:T(8,128)(2,1)S(1)} %get-tuple-element.62.refs_0_, bf16[16,2944]{1,0:T(8,128)(2,1)S(1)} %collective-permute-done.11.refs_1_, ...), custom_call_target="tpu_custom_call" | custom-call | tf_op jit(solution)/shard_map/experts/pallas_call | solution.py:50
  52.8 0.4 collective-permute-start.25
  53.2 1.4 %down.1 = (f32[128,1344]{1,0:T(8,128)S(1)}, bf16[128,1408]{1,0:T(8,128)(2,1)S(1)}) custom-call(bf16[256,1440]{1,0:T(8,128)(2,1)S(1)} %get-tuple-element.72.active, f32[1,256,128]{2,1,0:T(8,128)S(1)} %get-tuple-element.73.weights, bf16[1440,2880]{1,0:T(8,128)(2,1)S(1)} %bitcast.14), custom_call_target="tpu_custom_call" | custom-call | tf_op jit(solution)/shard_map/down/pallas_call | solution.py:50
  54.6 0.2 collective-permute-start.30
  54.8 0.1 add_split.8
  54.9 1.1 %collective-permute-start.26 = (bf16[32,1536]{1,0:T(8,128)(2,1)S(1)}, bf16[32,1536]{1,0:T(8,128)(2,1)S(1)}, u32[]{:S(2)}, u32[]{:S(2)}) collective-permute-start(bf16[32,1536]{1,0:T(8,128)(2,1)S(1)} %get-tuple-element.67), channel_id=1, source_target_pairs={{0,2},{1,3},{2,0},{3,1},{4,6},{5,7},{6,4},{7,5},{8,10},{9,11},{10,... | collective-permute-start | bytes 294920 | tf_op jit(solution)/shard_map/ppermute | solution.py:42
  56.0 2.5 %collective-permute-start.28 = (bf16[32,1536]{1,0:T(8,128)(2,1)S(1)}, bf16[32,1536]{1,0:T(8,128)(2,1)S(1)}, u32[]{:S(2)}, u32[]{:S(2)}) collective-permute-start(bf16[32,1536]{1,0:T(8,128)(2,1)S(1)} %get-tuple-element.69), channel_id=1, source_target_pairs={{0,6},{1,7},{2,4},{3,5},{4,2},{5,3},{6,0},{7,1},{8,14},{9,15},{10,... | collective-permute-start | bytes 294920 | tf_op jit(solution)/shard_map/ppermute | solution.py:42
  58.5 0.1 add_split.10
  58.5 1.1 %collective-permute-start.31 = (bf16[32,1344]{1,0:T(8,128)(2,1)S(1)}, bf16[32,1344]{1,0:T(8,128)(2,1)S(1)}, u32[]{:S(2)}, u32[]{:S(2)}) collective-permute-start(bf16[32,1344]{1,0:T(8,128)(2,1)S(1)} %get-tuple-element.77), channel_id=1, source_target_pairs={{0,2},{1,3},{2,0},{3,1},{4,6},{5,7},{6,4},{7,5},{8,10},{9,11},{10,... | collective-permute-start | bytes 258056 | tf_op jit(solution)/shard_map/ppermute | solution.py:42
  59.6 0.4 collective-permute-done.26.refs_1_
  60.0 2.1 %collective-permute-start.33 = (bf16[32,1344]{1,0:T(8,128)(2,1)S(1)}, bf16[32,1344]{1,0:T(8,128)(2,1)S(1)}, u32[]{:S(2)}, u32[]{:S(2)}) collective-permute-start(bf16[32,1344]{1,0:T(8,128)(2,1)S(1)} %get-tuple-element.79), channel_id=1, source_target_pairs={{0,6},{1,7},{2,4},{3,5},{4,2},{5,3},{6,0},{7,1},{8,14},{9,15},{10,... | collective-permute-start | bytes 258056 | tf_op jit(solution)/shard_map/ppermute | solution.py:42
  62.1 2.1 %collective-permute-done.28.refs_3_ = bf16[32,1536]{1,0:T(8,128)(2,1)S(1)} collective-permute-done((bf16[32,1536]{1,0:T(8,128)(2,1)S(1)}, bf16[32,1536]{1,0:T(8,128)(2,1)S(1)}, u32[]{:S(2)}, u32[]{:S(2)}) %collective-permute-start.28) | collective-permute-done | bytes 98336 | tf_op jit(solution)/shard_map/ppermute | solution.py:42
  64.3 1.3 %collective-permute-start.29 = (bf16[16,1536]{1,0:T(8,128)(2,1)S(1)}, bf16[16,1536]{1,0:T(8,128)(2,1)S(1)}, u32[]{:S(2)}, u32[]{:S(2)}) collective-permute-start(bf16[16,1536]{1,0:T(8,128)(2,1)S(1)} %get-tuple-element.71), channel_id=1, source_target_pairs={{0,8},{1,9},{2,10},{3,11},{4,12},{5,13},{6,14},{7,15},{8,0},{9,1},... | collective-permute-start | bytes 147464 | tf_op jit(solution)/shard_map/ppermute | solution.py:42
  65.6 0.1 collective-permute-done.32.refs_2_
  65.7 2.0 %collective-permute-done.33.refs_3_ = bf16[32,1344]{1,0:T(8,128)(2,1)S(1)} collective-permute-done((bf16[32,1344]{1,0:T(8,128)(2,1)S(1)}, bf16[32,1344]{1,0:T(8,128)(2,1)S(1)}, u32[]{:S(2)}, u32[]{:S(2)}) %collective-permute-start.33) | collective-permute-done | bytes 86048 | tf_op jit(solution)/shard_map/ppermute | solution.py:42
  67.8 1.2 %collective-permute-start.34 = (bf16[16,1344]{1,0:T(8,128)(2,1)S(1)}, bf16[16,1344]{1,0:T(8,128)(2,1)S(1)}, u32[]{:S(2)}, u32[]{:S(2)}) collective-permute-start(bf16[16,1344]{1,0:T(8,128)(2,1)S(1)} %get-tuple-element.81), channel_id=1, source_target_pairs={{0,8},{1,9},{2,10},{3,11},{4,12},{5,13},{6,14},{7,15},{8,0},{9,1},... | collective-permute-start | bytes 129032 | tf_op jit(solution)/shard_map/ppermute | solution.py:42
  69.0 4.3 %collective-permute-done.34.refs_5_ = bf16[16,1344]{1,0:T(8,128)(2,1)S(1)} collective-permute-done((bf16[16,1344]{1,0:T(8,128)(2,1)S(1)}, bf16[16,1344]{1,0:T(8,128)(2,1)S(1)}, u32[]{:S(2)}, u32[]{:S(2)}) %collective-permute-start.34) | collective-permute-done | bytes 43040 | tf_op jit(solution)/shard_map/ppermute | solution.py:42
  73.3 0.7 finish.1
  (50 shorter events, 0.2 us)
Async XLA Ops:
  0.6 7.7 %copy-start = (bf16[256,2880]{0,1:T(8,128)(2,1)S(1)}, bf16[256,2880]{0,1:T(8,128)(2,1)}, u32[]{:S(2)}) copy-start(bf16[256,2880]{0,1:T(8,128)(2,1)} %param.16) | copy-start | bytes 4423684
  0.7 21.1 %copy-start.2 = (bf16[2,8,2880]{2,1,0:T(8,128)(2,1)S(1)}, bf16[2,8,2880]{2,1,0:T(8,128)(2,1)}, u32[]{:S(2)}) copy-start(bf16[2,8,2880]{2,1,0:T(8,128)(2,1)} %refs_4_.3) | copy-start | bytes 276484
  0.7 21.1 %copy-start.3 = (s32[2,8,4]{1,2,0:T(4,128)S(1)}, s32[2,8,4]{1,2,0:T(4,128)}, u32[]{:S(2)}) copy-start(s32[2,8,4]{1,2,0:T(4,128)} %param.21) | copy-start | bytes 772
  6.9 1.4 %collective-permute-start = (bf16[2,64,256]{2,1,0:T(8,128)(2,1)S(1)}, bf16[2,64,256]{2,1,0:T(8,128)(2,1)S(1)}, u32[]{:S(2)}, u32[]{:S(2)}) collective-permute-start(bf16[2,64,256]{2,1,0:T(8,128)(2,1)S(1)} %get-tuple-element.43), channel_id=1, source_target_pairs={{0,1},{1,0},{2,3},{3,2},{4,5},{5,4},{6,7},{7,6},{8,9},{9,8},{10,11... | collective-permute-start | bytes 196616 | tf_op jit(solution)/shard_map/ppermute | solution.py:42
  9.0 1.8 %collective-permute-start.1 = (bf16[64,2944]{1,0:T(8,128)(2,1)S(1)}, bf16[64,2944]{1,0:T(8,128)(2,1)S(1)}, u32[]{:S(2)}, u32[]{:S(2)}) collective-permute-start(bf16[64,2944]{1,0:T(8,128)(2,1)S(1)} %get-tuple-element.45), channel_id=1, source_target_pairs={{0,1},{1,0},{2,3},{3,2},{4,5},{5,4},{6,7},{7,6},{8,9},{9,8},{10,11... | collective-permute-start | bytes 1130504 | tf_op jit(solution)/shard_map/ppermute | solution.py:42
  9.4 6.0 %collective-permute-start.6 = (bf16[64,2944]{1,0:T(8,128)(2,1)S(1)}, bf16[64,2944]{1,0:T(8,128)(2,1)S(1)}, u32[]{:S(2)}, u32[]{:S(2)}) collective-permute-start(bf16[64,2944]{1,0:T(8,128)(2,1)S(1)} %get-tuple-element.54), channel_id=1, source_target_pairs={{0,1},{1,0},{2,3},{3,2},{4,5},{5,4},{6,7},{7,6},{8,9},{9,8},{10,11... | collective-permute-start | bytes 1130504 | tf_op jit(solution)/shard_map/ppermute | solution.py:42
  10.8 8.2 %collective-permute-start.2 = (bf16[16,2880]{1,0:T(8,128)(2,1)S(1)}, bf16[16,2880]{1,0:T(8,128)(2,1)S(1)}, u32[]{:S(2)}, u32[]{:S(2)}) collective-permute-start(bf16[16,2880]{1,0:T(8,128)(2,1)S(1)} %get-tuple-element.47), channel_id=1, source_target_pairs={{0,2},{1,3},{2,0},{3,1},{4,6},{5,7},{6,4},{7,5},{8,10},{9,11},{10,... | collective-permute-start | bytes 276488 | tf_op jit(solution)/shard_map/ppermute | solution.py:42
  13.8 5.8 %collective-permute-start.3 = (bf16[16,2880]{1,0:T(8,128)(2,1)S(1)}, bf16[16,2880]{1,0:T(8,128)(2,1)S(1)}, u32[]{:S(2)}, u32[]{:S(2)}) collective-permute-start(bf16[16,2880]{1,0:T(8,128)(2,1)S(1)} %get-tuple-element.48), channel_id=1, source_target_pairs={{0,4},{1,5},{2,6},{3,7},{4,0},{5,1},{6,2},{7,3},{8,12},{9,13},{10,... | collective-permute-start | bytes 276488 | tf_op jit(solution)/shard_map/ppermute | solution.py:42
  15.4 6.4 %collective-permute-start.4 = (bf16[16,2880]{1,0:T(8,128)(2,1)S(1)}, bf16[16,2880]{1,0:T(8,128)(2,1)S(1)}, u32[]{:S(2)}, u32[]{:S(2)}) collective-permute-start(bf16[16,2880]{1,0:T(8,128)(2,1)S(1)} %get-tuple-element.49), channel_id=1, source_target_pairs={{0,6},{1,7},{2,4},{3,5},{4,2},{5,3},{6,0},{7,1},{8,14},{9,15},{10,... | collective-permute-start | bytes 276488 | tf_op jit(solution)/shard_map/ppermute | solution.py:42
  15.5 9.7 %collective-permute-start.7 = (bf16[16,2880]{1,0:T(8,128)(2,1)S(1)}, bf16[16,2880]{1,0:T(8,128)(2,1)S(1)}, u32[]{:S(2)}, u32[]{:S(2)}) collective-permute-start(bf16[16,2880]{1,0:T(8,128)(2,1)S(1)} %get-tuple-element.56), channel_id=1, source_target_pairs={{0,2},{1,3},{2,0},{3,1},{4,6},{5,7},{6,4},{7,5},{8,10},{9,11},{10,... | collective-permute-start | bytes 276488 | tf_op jit(solution)/shard_map/ppermute | solution.py:42
  17.4 7.8 %collective-permute-start.8 = (bf16[16,2880]{1,0:T(8,128)(2,1)S(1)}, bf16[16,2880]{1,0:T(8,128)(2,1)S(1)}, u32[]{:S(2)}, u32[]{:S(2)}) collective-permute-start(bf16[16,2880]{1,0:T(8,128)(2,1)S(1)} %get-tuple-element.57), channel_id=1, source_target_pairs={{0,4},{1,5},{2,6},{3,7},{4,0},{5,1},{6,2},{7,3},{8,12},{9,13},{10,... | collective-permute-start | bytes 276488 | tf_op jit(solution)/shard_map/ppermute | solution.py:42
  19.0 6.2 %collective-permute-start.9 = (bf16[16,2880]{1,0:T(8,128)(2,1)S(1)}, bf16[16,2880]{1,0:T(8,128)(2,1)S(1)}, u32[]{:S(2)}, u32[]{:S(2)}) collective-permute-start(bf16[16,2880]{1,0:T(8,128)(2,1)S(1)} %get-tuple-element.58), channel_id=1, source_target_pairs={{0,6},{1,7},{2,4},{3,5},{4,2},{5,3},{6,0},{7,1},{8,14},{9,15},{10,... | collective-permute-start | bytes 276488 | tf_op jit(solution)/shard_map/ppermute | solution.py:42
  21.8 24.6 %slice-start = ((s8[8478720]{0:T(1024)(128)(4,1)}), s8[4194304]{0:T(1024)(128)(4,1)S(1)}, s32[]{:S(2)}) async-start(s8[8478720]{0:T(1024)(128)(4,1)} %bitcast.11), calls=%async_computation | async-start | bytes 8388608
  21.8 24.6 %slice-start.1 = ((s8[8478720]{0:T(1024)(128)(4,1)}), s8[4194304]{0:T(1024)(128)(4,1)S(1)}, s32[]{:S(2)}) async-start(s8[8478720]{0:T(1024)(128)(4,1)} %bitcast.11), calls=%async_computation.1 | async-start | bytes 8388608
  21.8 24.6 %slice-start.3 = ((s8[8478720]{0:T(1024)(128)(4,1)}), s8[4194304]{0:T(1024)(128)(4,1)S(1)}, s32[]{:S(2)}) async-start(s8[8478720]{0:T(1024)(128)(4,1)} %bitcast.15), calls=%async_computation.3 | async-start | bytes 8388608
  21.8 24.6 %slice-start.4 = ((s8[8478720]{0:T(1024)(128)(4,1)}), s8[4194304]{0:T(1024)(128)(4,1)S(1)}, s32[]{:S(2)}) async-start(s8[8478720]{0:T(1024)(128)(4,1)} %bitcast.15), calls=%async_computation.4 | async-start | bytes 8388608
  21.8 24.6 %slice-start.6 = ((s8[8478720]{0:T(1024)(128)(4,1)}), s8[4194304]{0:T(1024)(128)(4,1)S(1)}, s32[]{:S(2)}) async-start(s8[8478720]{0:T(1024)(128)(4,1)} %bitcast.18), calls=%async_computation.6 | async-start | bytes 8388608
  21.8 24.6 %slice-start.7 = ((s8[8478720]{0:T(1024)(128)(4,1)}), s8[4194304]{0:T(1024)(128)(4,1)S(1)}, s32[]{:S(2)}) async-start(s8[8478720]{0:T(1024)(128)(4,1)} %bitcast.18), calls=%async_computation.7 | async-start | bytes 8388608
  22.5 9.6 %collective-permute-start.5 = (bf16[16,2944]{1,0:T(8,128)(2,1)S(1)}, bf16[16,2944]{1,0:T(8,128)(2,1)S(1)}, u32[]{:S(2)}, u32[]{:S(2)}) collective-permute-start(bf16[16,2944]{1,0:T(8,128)(2,1)S(1)} %get-tuple-element.51.mine), channel_id=1, source_target_pairs={{0,8},{1,9},{2,10},{3,11},{4,12},{5,13},{6,14},{7,15},{8,0},{9,1},... | collective-permute-start | bytes 282632 | tf_op jit(solution)/shard_map/ppermute | solution.py:42
  25.2 7.0 %copy-start.1 = (bf16[2880,16]{0,1:T(8,128)(2,1)S(1)}, bf16[2880,16]{0,1:T(8,128)(2,1)}, u32[]{:S(2)}) copy-start(bf16[2880,16]{0,1:T(8,128)(2,1)} %param.17) | copy-start | bytes 276484
  25.2 21.2 %slice-start.2 = ((s8[8478720]{0:T(1024)(128)(4,1)}), s8[90112]{0:T(1024)(128)(4,1)S(1)}, s32[]{:S(2)}) async-start(s8[8478720]{0:T(1024)(128)(4,1)} %bitcast.11), calls=%async_computation.2 | async-start | bytes 180224
  25.2 21.2 %slice-start.5 = ((s8[8478720]{0:T(1024)(128)(4,1)}), s8[90112]{0:T(1024)(128)(4,1)S(1)}, s32[]{:S(2)}) async-start(s8[8478720]{0:T(1024)(128)(4,1)} %bitcast.15), calls=%async_computation.5 | async-start | bytes 180224
  25.2 21.2 %slice-start.8 = ((s8[8478720]{0:T(1024)(128)(4,1)}), s8[90112]{0:T(1024)(128)(4,1)S(1)}, s32[]{:S(2)}) async-start(s8[8478720]{0:T(1024)(128)(4,1)} %bitcast.18), calls=%async_computation.8 | async-start | bytes 180224
  26.0 10.3 %collective-permute-start.10 = (bf16[16,2944]{1,0:T(8,128)(2,1)S(1)}, bf16[16,2944]{1,0:T(8,128)(2,1)S(1)}, u32[]{:S(2)}, u32[]{:S(2)}) collective-permute-start(bf16[16,2944]{1,0:T(8,128)(2,1)S(1)} %get-tuple-element.60.mine), channel_id=1, source_target_pairs={{0,8},{1,9},{2,10},{3,11},{4,12},{5,13},{6,14},{7,15},{8,0},{9,1},... | collective-permute-start | bytes 282632 | tf_op jit(solution)/shard_map/ppermute | solution.py:42
  32.7 4.1 %collective-permute-start.14 = (bf16[16,2944]{1,0:T(8,128)(2,1)S(1)}, bf16[16,2944]{1,0:T(8,128)(2,1)S(1)}, u32[]{:S(2)}, u32[]{:S(2)}) collective-permute-start(bf16[16,2944]{1,0:T(8,128)(2,1)S(1)} %get-tuple-element.62.refs_0_), channel_id=1, source_target_pairs={{0,1},{1,0},{2,3},{3,2},{4,5},{5,4},{6,7},{7,6},{8,9},{9,8},{10,11... | collective-permute-start | bytes 282632 | tf_op jit(solution)/shard_map/ppermute | solution.py:42
  32.7 6.5 %collective-permute-start.13 = (bf16[16,2944]{1,0:T(8,128)(2,1)S(1)}, bf16[16,2944]{1,0:T(8,128)(2,1)S(1)}, u32[]{:S(2)}, u32[]{:S(2)}) collective-permute-start(bf16[16,2944]{1,0:T(8,128)(2,1)S(1)} %get-tuple-element.62.refs_0_), channel_id=1, source_target_pairs={{0,6},{1,7},{2,4},{3,5},{4,2},{5,3},{6,0},{7,1},{8,14},{9,15},{10,... | collective-permute-start | bytes 282632 | tf_op jit(solution)/shard_map/ppermute | solution.py:42
  32.8 6.4 %collective-permute-start.12 = (bf16[16,2944]{1,0:T(8,128)(2,1)S(1)}, bf16[16,2944]{1,0:T(8,128)(2,1)S(1)}, u32[]{:S(2)}, u32[]{:S(2)}) collective-permute-start(bf16[16,2944]{1,0:T(8,128)(2,1)S(1)} %get-tuple-element.62.refs_0_), channel_id=1, source_target_pairs={{0,4},{1,5},{2,6},{3,7},{4,0},{5,1},{6,2},{7,3},{8,12},{9,13},{10,... | collective-permute-start | bytes 282632 | tf_op jit(solution)/shard_map/ppermute | solution.py:42
  32.9 8.5 %collective-permute-start.11 = (bf16[16,2944]{1,0:T(8,128)(2,1)S(1)}, bf16[16,2944]{1,0:T(8,128)(2,1)S(1)}, u32[]{:S(2)}, u32[]{:S(2)}) collective-permute-start(bf16[16,2944]{1,0:T(8,128)(2,1)S(1)} %get-tuple-element.62.refs_0_), channel_id=1, source_target_pairs={{0,2},{1,3},{2,0},{3,1},{4,6},{5,7},{6,4},{7,5},{8,10},{9,11},{10,... | collective-permute-start | bytes 282632 | tf_op jit(solution)/shard_map/ppermute | solution.py:42
  36.8 4.6 %collective-permute-start.21 = (bf16[16,2944]{1,0:T(8,128)(2,1)S(1)}, bf16[16,2944]{1,0:T(8,128)(2,1)S(1)}, u32[]{:S(2)}, u32[]{:S(2)}) collective-permute-start(bf16[16,2944]{1,0:T(8,128)(2,1)S(1)} %get-tuple-element.63.refs_8_), channel_id=1, source_target_pairs={{0,1},{1,0},{2,3},{3,2},{4,5},{5,4},{6,7},{7,6},{8,9},{9,8},{10,11... | collective-permute-start | bytes 282632 | tf_op jit(solution)/shard_map/ppermute | solution.py:42
  36.8 6.5 %collective-permute-start.20 = (bf16[16,2944]{1,0:T(8,128)(2,1)S(1)}, bf16[16,2944]{1,0:T(8,128)(2,1)S(1)}, u32[]{:S(2)}, u32[]{:S(2)}) collective-permute-start(bf16[16,2944]{1,0:T(8,128)(2,1)S(1)} %get-tuple-element.63.refs_8_), channel_id=1, source_target_pairs={{0,6},{1,7},{2,4},{3,5},{4,2},{5,3},{6,0},{7,1},{8,14},{9,15},{10,... | collective-permute-start | bytes 282632 | tf_op jit(solution)/shard_map/ppermute | solution.py:42
  39.2 4.6 %collective-permute-start.19 = (bf16[16,2944]{1,0:T(8,128)(2,1)S(1)}, bf16[16,2944]{1,0:T(8,128)(2,1)S(1)}, u32[]{:S(2)}, u32[]{:S(2)}) collective-permute-start(bf16[16,2944]{1,0:T(8,128)(2,1)S(1)} %get-tuple-element.63.refs_8_), channel_id=1, source_target_pairs={{0,4},{1,5},{2,6},{3,7},{4,0},{5,1},{6,2},{7,3},{8,12},{9,13},{10,... | collective-permute-start | bytes 282632 | tf_op jit(solution)/shard_map/ppermute | solution.py:42
  39.2 5.7 %collective-permute-start.18 = (bf16[16,2944]{1,0:T(8,128)(2,1)S(1)}, bf16[16,2944]{1,0:T(8,128)(2,1)S(1)}, u32[]{:S(2)}, u32[]{:S(2)}) collective-permute-start(bf16[16,2944]{1,0:T(8,128)(2,1)S(1)} %get-tuple-element.63.refs_8_), channel_id=1, source_target_pairs={{0,2},{1,3},{2,0},{3,1},{4,6},{5,7},{6,4},{7,5},{8,10},{9,11},{10,... | collective-permute-start | bytes 282632 | tf_op jit(solution)/shard_map/ppermute | solution.py:42
  41.3 3.5 %collective-permute-start.17 = (bf16[16,2944]{1,0:T(8,128)(2,1)S(1)}, bf16[16,2944]{1,0:T(8,128)(2,1)S(1)}, u32[]{:S(2)}, u32[]{:S(2)}) collective-permute-start(bf16[16,2944]{1,0:T(8,128)(2,1)S(1)} %collective-permute-done.13.refs_3_), channel_id=1, source_target_pairs={{0,1},{1,0},{2,3},{3,2},{4,5},{5,4},{6,7},{7,6},{8,9},{9,8},{10,11... | collective-permute-start | bytes 282632 | tf_op jit(solution)/shard_map/ppermute | solution.py:42
  41.4 4.1 %collective-permute-start.16 = (bf16[16,2944]{1,0:T(8,128)(2,1)S(1)}, bf16[16,2944]{1,0:T(8,128)(2,1)S(1)}, u32[]{:S(2)}, u32[]{:S(2)}) collective-permute-start(bf16[16,2944]{1,0:T(8,128)(2,1)S(1)} %collective-permute-done.12.refs_2_), channel_id=1, source_target_pairs={{0,1},{1,0},{2,3},{3,2},{4,5},{5,4},{6,7},{7,6},{8,9},{9,8},{10,11... | collective-permute-start | bytes 282632 | tf_op jit(solution)/shard_map/ppermute | solution.py:42
  43.3 2.1 %collective-permute-start.15 = (bf16[16,2944]{1,0:T(8,128)(2,1)S(1)}, bf16[16,2944]{1,0:T(8,128)(2,1)S(1)}, u32[]{:S(2)}, u32[]{:S(2)}) collective-permute-start(bf16[16,2944]{1,0:T(8,128)(2,1)S(1)} %collective-permute-done.11.refs_1_), channel_id=1, source_target_pairs={{0,1},{1,0},{2,3},{3,2},{4,5},{5,4},{6,7},{7,6},{8,9},{9,8},{10,11... | collective-permute-start | bytes 282632 | tf_op jit(solution)/shard_map/ppermute | solution.py:42
  43.7 1.7 %collective-permute-start.24 = (bf16[16,2944]{1,0:T(8,128)(2,1)S(1)}, bf16[16,2944]{1,0:T(8,128)(2,1)S(1)}, u32[]{:S(2)}, u32[]{:S(2)}) collective-permute-start(bf16[16,2944]{1,0:T(8,128)(2,1)S(1)} %collective-permute-done.20.refs_11_), channel_id=1, source_target_pairs={{0,1},{1,0},{2,3},{3,2},{4,5},{5,4},{6,7},{7,6},{8,9},{9,8},{10,11... | collective-permute-start | bytes 282632 | tf_op jit(solution)/shard_map/ppermute | solution.py:42
  44.9 1.3 %collective-permute-start.23 = (bf16[16,2944]{1,0:T(8,128)(2,1)S(1)}, bf16[16,2944]{1,0:T(8,128)(2,1)S(1)}, u32[]{:S(2)}, u32[]{:S(2)}) collective-permute-start(bf16[16,2944]{1,0:T(8,128)(2,1)S(1)} %collective-permute-done.19.refs_10_), channel_id=1, source_target_pairs={{0,1},{1,0},{2,3},{3,2},{4,5},{5,4},{6,7},{7,6},{8,9},{9,8},{10,11... | collective-permute-start | bytes 282632 | tf_op jit(solution)/shard_map/ppermute | solution.py:42
  44.9 1.4 %collective-permute-start.22 = (bf16[16,2944]{1,0:T(8,128)(2,1)S(1)}, bf16[16,2944]{1,0:T(8,128)(2,1)S(1)}, u32[]{:S(2)}, u32[]{:S(2)}) collective-permute-start(bf16[16,2944]{1,0:T(8,128)(2,1)S(1)} %collective-permute-done.18.refs_9_), channel_id=1, source_target_pairs={{0,1},{1,0},{2,3},{3,2},{4,5},{5,4},{6,7},{7,6},{8,9},{9,8},{10,11... | collective-permute-start | bytes 282632 | tf_op jit(solution)/shard_map/ppermute | solution.py:42
  52.8 2.0 %collective-permute-start.25 = (bf16[128,1536]{1,0:T(8,128)(2,1)S(1)}, bf16[128,1536]{1,0:T(8,128)(2,1)S(1)}, u32[]{:S(2)}, u32[]{:S(2)}) collective-permute-start(bf16[128,1536]{1,0:T(8,128)(2,1)S(1)} %get-tuple-element.65), channel_id=1, source_target_pairs={{0,1},{1,0},{2,3},{3,2},{4,5},{5,4},{6,7},{7,6},{8,9},{9,8},{10,11... | collective-permute-start | bytes 1179656 | tf_op jit(solution)/shard_map/ppermute | solution.py:42
  54.6 3.9 %collective-permute-start.30 = (bf16[128,1408]{1,0:T(8,128)(2,1)S(1)}, bf16[128,1408]{1,0:T(8,128)(2,1)S(1)}, u32[]{:S(2)}, u32[]{:S(2)}) collective-permute-start(bf16[128,1408]{1,0:T(8,128)(2,1)S(1)} %get-tuple-element.75), channel_id=1, source_target_pairs={{0,1},{1,0},{2,3},{3,2},{4,5},{5,4},{6,7},{7,6},{8,9},{9,8},{10,11... | collective-permute-start | bytes 1081352 | tf_op jit(solution)/shard_map/ppermute | solution.py:42
  54.9 5.1 %collective-permute-start.26 = (bf16[32,1536]{1,0:T(8,128)(2,1)S(1)}, bf16[32,1536]{1,0:T(8,128)(2,1)S(1)}, u32[]{:S(2)}, u32[]{:S(2)}) collective-permute-start(bf16[32,1536]{1,0:T(8,128)(2,1)S(1)} %get-tuple-element.67), channel_id=1, source_target_pairs={{0,2},{1,3},{2,0},{3,1},{4,6},{5,7},{6,4},{7,5},{8,10},{9,11},{10,... | collective-permute-start | bytes 294920 | tf_op jit(solution)/shard_map/ppermute | solution.py:42
  56.0 6.1 %collective-permute-start.27 = (bf16[32,1536]{1,0:T(8,128)(2,1)S(1)}, bf16[32,1536]{1,0:T(8,128)(2,1)S(1)}, u32[]{:S(2)}, u32[]{:S(2)}) collective-permute-start(bf16[32,1536]{1,0:T(8,128)(2,1)S(1)} %get-tuple-element.68), channel_id=1, source_target_pairs={{0,4},{1,5},{2,6},{3,7},{4,0},{5,1},{6,2},{7,3},{8,12},{9,13},{10,... | collective-permute-start | bytes 294920 | tf_op jit(solution)/shard_map/ppermute | solution.py:42
  56.0 8.2 %collective-permute-start.28 = (bf16[32,1536]{1,0:T(8,128)(2,1)S(1)}, bf16[32,1536]{1,0:T(8,128)(2,1)S(1)}, u32[]{:S(2)}, u32[]{:S(2)}) collective-permute-start(bf16[32,1536]{1,0:T(8,128)(2,1)S(1)} %get-tuple-element.69), channel_id=1, source_target_pairs={{0,6},{1,7},{2,4},{3,5},{4,2},{5,3},{6,0},{7,1},{8,14},{9,15},{10,... | collective-permute-start | bytes 294920 | tf_op jit(solution)/shard_map/ppermute | solution.py:42
  58.5 7.0 %collective-permute-start.31 = (bf16[32,1344]{1,0:T(8,128)(2,1)S(1)}, bf16[32,1344]{1,0:T(8,128)(2,1)S(1)}, u32[]{:S(2)}, u32[]{:S(2)}) collective-permute-start(bf16[32,1344]{1,0:T(8,128)(2,1)S(1)} %get-tuple-element.77), channel_id=1, source_target_pairs={{0,2},{1,3},{2,0},{3,1},{4,6},{5,7},{6,4},{7,5},{8,10},{9,11},{10,... | collective-permute-start | bytes 258056 | tf_op jit(solution)/shard_map/ppermute | solution.py:42
  59.6 6.1 %collective-permute-start.32 = (bf16[32,1344]{1,0:T(8,128)(2,1)S(1)}, bf16[32,1344]{1,0:T(8,128)(2,1)S(1)}, u32[]{:S(2)}, u32[]{:S(2)}) collective-permute-start(bf16[32,1344]{1,0:T(8,128)(2,1)S(1)} %get-tuple-element.78), channel_id=1, source_target_pairs={{0,4},{1,5},{2,6},{3,7},{4,0},{5,1},{6,2},{7,3},{8,12},{9,13},{10,... | collective-permute-start | bytes 258056 | tf_op jit(solution)/shard_map/ppermute | solution.py:42
  60.0 7.7 %collective-permute-start.33 = (bf16[32,1344]{1,0:T(8,128)(2,1)S(1)}, bf16[32,1344]{1,0:T(8,128)(2,1)S(1)}, u32[]{:S(2)}, u32[]{:S(2)}) collective-permute-start(bf16[32,1344]{1,0:T(8,128)(2,1)S(1)} %get-tuple-element.79), channel_id=1, source_target_pairs={{0,6},{1,7},{2,4},{3,5},{4,2},{5,3},{6,0},{7,1},{8,14},{9,15},{10,... | collective-permute-start | bytes 258056 | tf_op jit(solution)/shard_map/ppermute | solution.py:42
  64.3 9.0 %collective-permute-start.29 = (bf16[16,1536]{1,0:T(8,128)(2,1)S(1)}, bf16[16,1536]{1,0:T(8,128)(2,1)S(1)}, u32[]{:S(2)}, u32[]{:S(2)}) collective-permute-start(bf16[16,1536]{1,0:T(8,128)(2,1)S(1)} %get-tuple-element.71), channel_id=1, source_target_pairs={{0,8},{1,9},{2,10},{3,11},{4,12},{5,13},{6,14},{7,15},{8,0},{9,1},... | collective-permute-start | bytes 147464 | tf_op jit(solution)/shard_map/ppermute | solution.py:42
  67.8 5.5 %collective-permute-start.34 = (bf16[16,1344]{1,0:T(8,128)(2,1)S(1)}, bf16[16,1344]{1,0:T(8,128)(2,1)S(1)}, u32[]{:S(2)}, u32[]{:S(2)}) collective-permute-start(bf16[16,1344]{1,0:T(8,128)(2,1)S(1)} %get-tuple-element.81), channel_id=1, source_target_pairs={{0,8},{1,9},{2,10},{3,11},{4,12},{5,13},{6,14},{7,15},{8,0},{9,1},... | collective-permute-start | bytes 129032 | tf_op jit(solution)/shard_map/ppermute | solution.py:42

commit v7 on v6

--- a/solution.py
+++ b/solution.py
@@ -91,13 +91,29 @@
     return pieces[0], received
 
 
-def gather_rows(pieces, stages):
+def join_kernel(*refs):
+    at = 0
+    for ref in refs[:-1]:
+        refs[-1][at : at + ref.shape[0], :] = ref[...]
+        at += ref.shape[0]
+
+
+def join(pieces):
+    if len(pieces) == 1:
+        return pieces[0]
+    shape = (sum(piece.shape[0] for piece in pieces), pieces[0].shape[1])
+    (joined,) = whole_call(
+        join_kernel, "join", [jax.ShapeDtypeStruct(shape, pieces[0].dtype)], pieces
+    )
+    return joined
+
+
+def gather_rows(rows, stages):
+    pieces = [rows]
     for bit, bits in reversed(stages):
-        if bit:
-            held = jnp.concatenate(pieces, axis=0) if len(pieces) > 1 else pieces[0]
-            pieces = [held] + [from_mask(held, r << bit) for r in range(1, 1 << bits)]
-        else:
-            pieces = pieces + [from_mask(piece, 1) for piece in pieces]
+        held = join(pieces)
+        received = [from_mask(held, r << bit) for r in range(1, 1 << bits)]
+        pieces = [held, *received] if bit else [*pieces, *received]
     return pieces
 
 
@@ -423,7 +439,7 @@
     units = w_down.shape[0] * hidden
     count = sum(piece.shape[0] for piece in pieces)
     parts = max(1, units // (SPLIT * hidden))
-    first = padded(pl.cdiv(width, 2))
+    first = padded(pl.cdiv(width * 10, 16))
 
     def halves(columns):
         return [
@@ -476,7 +492,7 @@
             m, total, received, residual, routes.swapaxes(1, 2), router.T, stages
         )
         attended.append(rows)
-        pieces += gather_rows([payload], stages[:-1])
+        pieces += gather_rows(payload, stages[:-1])
     sums = []
     for halves in expert_sums(me, batch, pieces, w_gate, w_up, w_down):
         total, (received,) = scatter_sum(halves, stages)

time: 74.1 us -> 71.8 us (0.969)
  waiting for transfers between devices: 22.5 us -> 19.7 us
    ppermute x35 -> x29, waiting for transfers between devices: 22.5 us -> 19.7 us  [from_mask(): return lax.ppermute(value, 'req', pairs)]
    ppermute x35 -> x29, starting transfers between devices: 32.2 us -> 32.7 us  [from_mask(): return lax.ppermute(value, 'req', pairs)]
    pallas_call x14 -> x16, Pallas kernels: 11.9 us -> 12 us  [whole_call(): pl.pallas_call(kernel, out_shape=outs, in_specs=[pl.BlockSpec(memory_spac...]
  transfers between devices with their start and end apart: 35 -> 29, of which waited for: 15 -> 14; matrix products, arithmetic and copies ran while one was open for 0% -> 0% of each run, Pallas kernels for 6% -> 5%
where the time goes in v7:
time: 71.8 us; the launch traced here: 71.7 us
  starting transfers between devices  32.7 us (46%)
  waiting for transfers between devices  19.7 us (27%)
  Pallas kernels  18.2 us (25%)
  between operations  0.93 us (1%)
    ppermute x29, starting transfers between devices, from_mask(): return lax.ppermute(value, 'req', pairs)  32.7 us
    ppermute x29, waiting for transfers between devices, from_mask(): return lax.ppermute(value, 'req', pairs)  19.7 us
    pallas_call x16, Pallas kernels, whole_call(): pl.pallas_call(kernel, out_shape=outs, in_specs=[pl.BlockSpec(memory_spac...  12 us
    pallas_call x1, Pallas kernels, attention(): pl.pallas_call(functools.partial(attention_kernel, group, block), out_sha...  6.24 us
  transfers between devices with their start and end apart: 29, of which 14 were waited for; matrix products, arithmetic and copies ran while one was open for 0% of the time, Pallas kernels for 5%

profile of v7, /device:TPU:0, one launch (start us, length us, event | category | flops | bytes accessed | tf_op | source)
XLA Modules:
  0.0 71.7 jit_solution(10208575218663764964)
XLA Ops:
  0.7 6.2 %attention.1 = (bf16[2,64,256]{2,1,0:T(8,128)(2,1)S(1)}, bf16[2,64,256]{2,1,0:T(8,128)(2,1)S(1)}) custom-call(s32[2,128]{1,0:T(2,128)} %lengths.1, s32[1]{0:T(128)S(6)} %select_n.7.place, bf16[2,64,512]{2,1,0:T(8,128)(2,1)} %far_q.1, bf16[2,64,128]{2,1,0:T(8,128)(2,1)} %far_kv.1, bf16[2,64,128,128]{3,2,1,0:T(8,128)(2,1)} %far.1), custom_call_target="tpu_custom_call" | custom-call | flops 10000000000 | bytes 30000000 | tf_op jit(solution)/shard_map/attention/pallas_call | solution.py:313
  6.9 0.5 collective-permute-start
  7.4 0.9 %collective-permute-done.refs_1_ = bf16[2,64,256]{2,1,0:T(8,128)(2,1)S(1)} collective-permute-done((bf16[2,64,256]{2,1,0:T(8,128)(2,1)S(1)}, bf16[2,64,256]{2,1,0:T(8,128)(2,1)S(1)}, u32[]{:S(2)}, u32[]{:S(2)}) %collective-permute-start) | collective-permute-done | bytes 65568 | tf_op jit(solution)/shard_map/ppermute | solution.py:42
  8.3 0.6 project.1
  9.0 0.4 collective-permute-start.1
  9.4 0.2 collective-permute-start.6
  9.6 1.2 %collective-permute-done.1.refs_1_ = bf16[64,2944]{1,0:T(8,128)(2,1)S(1)} collective-permute-done((bf16[64,2944]{1,0:T(8,128)(2,1)S(1)}, bf16[64,2944]{1,0:T(8,128)(2,1)S(1)}, u32[]{:S(2)}, u32[]{:S(2)}) %collective-permute-start.1) | collective-permute-done | bytes 376864 | tf_op jit(solution)/shard_map/ppermute | solution.py:42
  10.8 0.1 add_split.6
  10.8 2.9 %collective-permute-start.2 = (bf16[16,2880]{1,0:T(8,128)(2,1)S(1)}, bf16[16,2880]{1,0:T(8,128)(2,1)S(1)}, u32[]{:S(2)}, u32[]{:S(2)}) collective-permute-start(bf16[16,2880]{1,0:T(8,128)(2,1)S(1)} %get-tuple-element.47), channel_id=1, source_target_pairs={{0,2},{1,3},{2,0},{3,1},{4,6},{5,7},{6,4},{7,5},{8,10},{9,11},{10,... | collective-permute-start | bytes 276488 | tf_op jit(solution)/shard_map/ppermute | solution.py:42
  13.8 1.6 %collective-permute-start.3 = (bf16[16,2880]{1,0:T(8,128)(2,1)S(1)}, bf16[16,2880]{1,0:T(8,128)(2,1)S(1)}, u32[]{:S(2)}, u32[]{:S(2)}) collective-permute-start(bf16[16,2880]{1,0:T(8,128)(2,1)S(1)} %get-tuple-element.48), channel_id=1, source_target_pairs={{0,4},{1,5},{2,6},{3,7},{4,0},{5,1},{6,2},{7,3},{8,12},{9,13},{10,... | collective-permute-start | bytes 276488 | tf_op jit(solution)/shard_map/ppermute | solution.py:42
  15.4 0.0 collective-permute-start.4
  15.4 0.1 add_split.7
  15.5 2.0 %collective-permute-start.7 = (bf16[16,2880]{1,0:T(8,128)(2,1)S(1)}, bf16[16,2880]{1,0:T(8,128)(2,1)S(1)}, u32[]{:S(2)}, u32[]{:S(2)}) collective-permute-start(bf16[16,2880]{1,0:T(8,128)(2,1)S(1)} %get-tuple-element.56), channel_id=1, source_target_pairs={{0,2},{1,3},{2,0},{3,1},{4,6},{5,7},{6,4},{7,5},{8,10},{9,11},{10,... | collective-permute-start | bytes 276488 | tf_op jit(solution)/shard_map/ppermute | solution.py:42
  17.4 1.6 %collective-permute-start.8 = (bf16[16,2880]{1,0:T(8,128)(2,1)S(1)}, bf16[16,2880]{1,0:T(8,128)(2,1)S(1)}, u32[]{:S(2)}, u32[]{:S(2)}) collective-permute-start(bf16[16,2880]{1,0:T(8,128)(2,1)S(1)} %get-tuple-element.57), channel_id=1, source_target_pairs={{0,4},{1,5},{2,6},{3,7},{4,0},{5,1},{6,2},{7,3},{8,12},{9,13},{10,... | collective-permute-start | bytes 276488 | tf_op jit(solution)/shard_map/ppermute | solution.py:42
  19.0 0.5 collective-permute-start.9
  19.6 2.2 %collective-permute-done.4.refs_3_ = bf16[16,2880]{1,0:T(8,128)(2,1)S(1)} collective-permute-done((bf16[16,2880]{1,0:T(8,128)(2,1)S(1)}, bf16[16,2880]{1,0:T(8,128)(2,1)S(1)}, u32[]{:S(2)}, u32[]{:S(2)}) %collective-permute-start.4) | collective-permute-done | bytes 92192 | tf_op jit(solution)/shard_map/ppermute | solution.py:42
  21.8 0.0 slice-start.3
  21.8 0.0 slice-start.4
  21.8 0.0 slice-start.6
  21.8 0.0 slice-start.7
  21.8 0.7 share.2
  22.5 2.7 %collective-permute-start.5 = (bf16[16,2944]{1,0:T(8,128)(2,1)S(1)}, bf16[16,2944]{1,0:T(8,128)(2,1)S(1)}, u32[]{:S(2)}, u32[]{:S(2)}) collective-permute-start(bf16[16,2944]{1,0:T(8,128)(2,1)S(1)} %get-tuple-element.51.mine), channel_id=1, source_target_pairs={{0,8},{1,9},{2,10},{3,11},{4,12},{5,13},{6,14},{7,15},{8,0},{9,1},... | collective-permute-start | bytes 282632 | tf_op jit(solution)/shard_map/ppermute | solution.py:42
  25.2 0.0 copy-start.1
  25.2 0.0 slice-start.2
  25.2 0.0 slice-start.5
  25.2 0.0 slice-start.8
  25.3 0.7 share.3
  26.0 3.0 %collective-permute-start.10 = (bf16[16,2944]{1,0:T(8,128)(2,1)S(1)}, bf16[16,2944]{1,0:T(8,128)(2,1)S(1)}, u32[]{:S(2)}, u32[]{:S(2)}) collective-permute-start(bf16[16,2944]{1,0:T(8,128)(2,1)S(1)} %get-tuple-element.60.mine), channel_id=1, source_target_pairs={{0,8},{1,9},{2,10},{3,11},{4,12},{5,13},{6,14},{7,15},{8,0},{9,1},... | collective-permute-start | bytes 282632 | tf_op jit(solution)/shard_map/ppermute | solution.py:42
  28.9 2.7 %collective-permute-done.5.theirs = bf16[16,2944]{1,0:T(8,128)(2,1)S(1)} collective-permute-done((bf16[16,2944]{1,0:T(8,128)(2,1)S(1)}, bf16[16,2944]{1,0:T(8,128)(2,1)S(1)}, u32[]{:S(2)}, u32[]{:S(2)}) %collective-permute-start.5) | collective-permute-done | bytes 94240 | tf_op jit(solution)/shard_map/ppermute | solution.py:42
  31.6 0.5 norm.2
  32.1 0.6 collective-permute-start.13
  32.7 2.9 %collective-permute-start.11 = (bf16[16,2944]{1,0:T(8,128)(2,1)S(1)}, bf16[16,2944]{1,0:T(8,128)(2,1)S(1)}, u32[]{:S(2)}, u32[]{:S(2)}) collective-permute-start(bf16[16,2944]{1,0:T(8,128)(2,1)S(1)} %get-tuple-element.62.refs_0_), channel_id=1, source_target_pairs={{0,2},{1,3},{2,0},{3,1},{4,6},{5,7},{6,4},{7,5},{8,10},{9,11},{10,... | collective-permute-start | bytes 282632 | tf_op jit(solution)/shard_map/ppermute | solution.py:42
  35.7 0.5 norm.3
  36.2 0.6 collective-permute-start.17
  36.8 0.9 %collective-permute-start.16 = (bf16[16,2944]{1,0:T(8,128)(2,1)S(1)}, bf16[16,2944]{1,0:T(8,128)(2,1)S(1)}, u32[]{:S(2)}, u32[]{:S(2)}) collective-permute-start(bf16[16,2944]{1,0:T(8,128)(2,1)S(1)} %get-tuple-element.63.refs_0_.refs_5_), channel_id=1, source_target_pairs={{0,4},{1,5},{2,6},{3,7},{4,0},{5,1},{6,2},{7,3},{8,12},{9,13},{10,... | collective-permute-start | bytes 282632 | tf_op jit(solution)/shard_map/ppermute | solution.py:42
  37.7 1.0 %collective-permute-done.13.refs_3_ = bf16[16,2944]{1,0:T(8,128)(2,1)S(1)} collective-permute-done((bf16[16,2944]{1,0:T(8,128)(2,1)S(1)}, bf16[16,2944]{1,0:T(8,128)(2,1)S(1)}, u32[]{:S(2)}, u32[]{:S(2)}) %collective-permute-start.13) | collective-permute-done | bytes 94240 | tf_op jit(solution)/shard_map/ppermute | solution.py:42
  38.7 1.0 %collective-permute-start.15 = (bf16[16,2944]{1,0:T(8,128)(2,1)S(1)}, bf16[16,2944]{1,0:T(8,128)(2,1)S(1)}, u32[]{:S(2)}, u32[]{:S(2)}) collective-permute-start(bf16[16,2944]{1,0:T(8,128)(2,1)S(1)} %get-tuple-element.63.refs_0_.refs_5_), channel_id=1, source_target_pairs={{0,2},{1,3},{2,0},{3,1},{4,6},{5,7},{6,4},{7,5},{8,10},{9,11},{10,... | collective-permute-start | bytes 282632 | tf_op jit(solution)/shard_map/ppermute | solution.py:42
  39.7 0.9 %collective-permute-done.11.refs_1_ = bf16[16,2944]{1,0:T(8,128)(2,1)S(1)} collective-permute-done((bf16[16,2944]{1,0:T(8,128)(2,1)S(1)}, bf16[16,2944]{1,0:T(8,128)(2,1)S(1)}, u32[]{:S(2)}, u32[]{:S(2)}) %collective-permute-start.11) | collective-permute-done | bytes 94240 | tf_op jit(solution)/shard_map/ppermute | solution.py:42
  40.7 0.1 collective-permute-start.14
  40.8 0.9 %collective-permute-done.17.refs_3_.refs_8_ = bf16[16,2944]{1,0:T(8,128)(2,1)S(1)} collective-permute-done((bf16[16,2944]{1,0:T(8,128)(2,1)S(1)}, bf16[16,2944]{1,0:T(8,128)(2,1)S(1)}, u32[]{:S(2)}, u32[]{:S(2)}) %collective-permute-start.17) | collective-permute-done | bytes 94240 | tf_op jit(solution)/shard_map/ppermute | solution.py:42
  41.7 1.6 %collective-permute-done.15.refs_1_.refs_6_ = bf16[16,2944]{1,0:T(8,128)(2,1)S(1)} collective-permute-done((bf16[16,2944]{1,0:T(8,128)(2,1)S(1)}, bf16[16,2944]{1,0:T(8,128)(2,1)S(1)}, u32[]{:S(2)}, u32[]{:S(2)}) %collective-permute-start.15) | collective-permute-done | bytes 94240 | tf_op jit(solution)/shard_map/ppermute | solution.py:42
  43.3 0.1 collective-permute-start.18
  43.4 1.7 %collective-permute-done.18.refs_9_ = bf16[64,2944]{1,0:T(8,128)(2,1)S(1)} collective-permute-done((bf16[64,2944]{1,0:T(8,128)(2,1)S(1)}, bf16[64,2944]{1,0:T(8,128)(2,1)S(1)}, u32[]{:S(2)}, u32[]{:S(2)}) %collective-permute-start.18) | collective-permute-done | bytes 376864 | tf_op jit(solution)/shard_map/ppermute | solution.py:42
  45.2 6.8 %experts.1 = (f32[128,1920]{1,0:T(8,128)S(1)}, bf16[128,1920]{1,0:T(8,128)(2,1)S(1)}, bf16[256,1440]{1,0:T(8,128)(2,1)S(1)}, f32[1,256,128]{2,1,0:T(8,128)S(1)}) custom-call(s32[1]{0:T(128)} %bitcast.1.me_ref, bf16[16,2944]{1,0:T(8,128)(2,1)S(1)} %get-tuple-element.62.refs_0_, bf16[16,2944]{1,0:T(8,128)(2,1)S(1)} %collective-permute-done.11.refs_1_, ...), custom_call_target="tpu_custom_call" | custom-call | tf_op jit(solution)/shard_map/experts/pallas_call | solution.py:50
  52.0 0.2 collective-permute-start.19
  52.2 1.0 %down.1 = (f32[128,960]{1,0:T(8,128)S(1)}, bf16[128,1024]{1,0:T(8,128)(2,1)S(1)}) custom-call(bf16[256,1440]{1,0:T(8,128)(2,1)S(1)} %get-tuple-element.72.active, f32[1,256,128]{2,1,0:T(8,128)S(1)} %get-tuple-element.73.weights, bf16[1440,2880]{1,0:T(8,128)(2,1)S(1)} %bitcast.14), custom_call_target="tpu_custom_call" | custom-call | tf_op jit(solution)/shard_map/down/pallas_call | solution.py:50
  53.1 0.4 collective-permute-start.24
  53.6 0.3 collective-permute-done.19.refs_1_
  53.9 0.1 add_split.8
  54.0 1.1 %collective-permute-start.20 = (bf16[32,1920]{1,0:T(8,128)(2,1)S(1)}, bf16[32,1920]{1,0:T(8,128)(2,1)S(1)}, u32[]{:S(2)}, u32[]{:S(2)}) collective-permute-start(bf16[32,1920]{1,0:T(8,128)(2,1)S(1)} %get-tuple-element.67), channel_id=1, source_target_pairs={{0,2},{1,3},{2,0},{3,1},{4,6},{5,7},{6,4},{7,5},{8,10},{9,11},{10,... | collective-permute-start | bytes 368648 | tf_op jit(solution)/shard_map/ppermute | solution.py:42
  55.1 0.0 collective-permute-start.21
  55.1 2.5 %collective-permute-start.22 = (bf16[32,1920]{1,0:T(8,128)(2,1)S(1)}, bf16[32,1920]{1,0:T(8,128)(2,1)S(1)}, u32[]{:S(2)}, u32[]{:S(2)}) collective-permute-start(bf16[32,1920]{1,0:T(8,128)(2,1)S(1)} %get-tuple-element.69), channel_id=1, source_target_pairs={{0,6},{1,7},{2,4},{3,5},{4,2},{5,3},{6,0},{7,1},{8,14},{9,15},{10,... | collective-permute-start | bytes 368648 | tf_op jit(solution)/shard_map/ppermute | solution.py:42
  57.6 1.1 %collective-permute-start.25 = (bf16[32,960]{1,0:T(8,128)(2,1)S(1)}, bf16[32,960]{1,0:T(8,128)(2,1)S(1)}, u32[]{:S(2)}, u32[]{:S(2)}) collective-permute-start(bf16[32,960]{1,0:T(8,128)(2,1)S(1)} %get-tuple-element.77), channel_id=1, source_target_pairs={{0,2},{1,3},{2,0},{3,1},{4,6},{5,7},{6,4},{7,5},{8,10},{9,11},{10,... | collective-permute-start | bytes 184328 | tf_op jit(solution)/shard_map/ppermute | solution.py:42
  58.7 0.0 collective-permute-start.26
  58.7 0.7 %collective-permute-done.20.refs_1_ = bf16[32,1920]{1,0:T(8,128)(2,1)S(1)} collective-permute-done((bf16[32,1920]{1,0:T(8,128)(2,1)S(1)}, bf16[32,1920]{1,0:T(8,128)(2,1)S(1)}, u32[]{:S(2)}, u32[]{:S(2)}) %collective-permute-start.20) | collective-permute-done | bytes 122912 | tf_op jit(solution)/shard_map/ppermute | solution.py:42
  59.4 1.7 %collective-permute-start.27 = (bf16[32,960]{1,0:T(8,128)(2,1)S(1)}, bf16[32,960]{1,0:T(8,128)(2,1)S(1)}, u32[]{:S(2)}, u32[]{:S(2)}) collective-permute-start(bf16[32,960]{1,0:T(8,128)(2,1)S(1)} %get-tuple-element.79), channel_id=1, source_target_pairs={{0,6},{1,7},{2,4},{3,5},{4,2},{5,3},{6,0},{7,1},{8,14},{9,15},{10,... | collective-permute-start | bytes 184328 | tf_op jit(solution)/shard_map/ppermute | solution.py:42
  61.1 0.1 collective-permute-done.21.refs_2_
  61.3 3.1 %collective-permute-done.22.refs_3_ = bf16[32,1920]{1,0:T(8,128)(2,1)S(1)} collective-permute-done((bf16[32,1920]{1,0:T(8,128)(2,1)S(1)}, bf16[32,1920]{1,0:T(8,128)(2,1)S(1)}, u32[]{:S(2)}, u32[]{:S(2)}) %collective-permute-start.22) | collective-permute-done | bytes 122912 | tf_op jit(solution)/shard_map/ppermute | solution.py:42
  64.3 0.1 add_split.9
  64.4 1.6 %collective-permute-start.23 = (bf16[16,1920]{1,0:T(8,128)(2,1)S(1)}, bf16[16,1920]{1,0:T(8,128)(2,1)S(1)}, u32[]{:S(2)}, u32[]{:S(2)}) collective-permute-start(bf16[16,1920]{1,0:T(8,128)(2,1)S(1)} %get-tuple-element.71), channel_id=1, source_target_pairs={{0,8},{1,9},{2,10},{3,11},{4,12},{5,13},{6,14},{7,15},{8,0},{9,1},... | collective-permute-start | bytes 184328 | tf_op jit(solution)/shard_map/ppermute | solution.py:42
  66.0 0.0 collective-permute-done.27.refs_3_
  66.1 2.6 %collective-permute-start.28 = (bf16[16,960]{1,0:T(8,128)(2,1)S(1)}, bf16[16,960]{1,0:T(8,128)(2,1)S(1)}, u32[]{:S(2)}, u32[]{:S(2)}) collective-permute-start(bf16[16,960]{1,0:T(8,128)(2,1)S(1)} %get-tuple-element.81), channel_id=1, source_target_pairs={{0,8},{1,9},{2,10},{3,11},{4,12},{5,13},{6,14},{7,15},{8,0},{9,1},... | collective-permute-start | bytes 92168 | tf_op jit(solution)/shard_map/ppermute | solution.py:42
  68.6 2.3 %collective-permute-done.28.refs_5_ = bf16[16,960]{1,0:T(8,128)(2,1)S(1)} collective-permute-done((bf16[16,960]{1,0:T(8,128)(2,1)S(1)}, bf16[16,960]{1,0:T(8,128)(2,1)S(1)}, u32[]{:S(2)}, u32[]{:S(2)}) %collective-permute-start.28) | collective-permute-done | bytes 30752 | tf_op jit(solution)/shard_map/ppermute | solution.py:42
  71.0 0.7 finish.1
  (40 shorter events, 0.2 us)
Async XLA Ops:
  0.6 7.7 %copy-start = (bf16[256,2880]{0,1:T(8,128)(2,1)S(1)}, bf16[256,2880]{0,1:T(8,128)(2,1)}, u32[]{:S(2)}) copy-start(bf16[256,2880]{0,1:T(8,128)(2,1)} %param.16) | copy-start | bytes 4423684
  0.7 21.1 %copy-start.2 = (bf16[2,8,2880]{2,1,0:T(8,128)(2,1)S(1)}, bf16[2,8,2880]{2,1,0:T(8,128)(2,1)}, u32[]{:S(2)}) copy-start(bf16[2,8,2880]{2,1,0:T(8,128)(2,1)} %refs_4_.3) | copy-start | bytes 276484
  0.7 21.1 %copy-start.3 = (s32[2,8,4]{1,2,0:T(4,128)S(1)}, s32[2,8,4]{1,2,0:T(4,128)}, u32[]{:S(2)}) copy-start(s32[2,8,4]{1,2,0:T(4,128)} %param.21) | copy-start | bytes 772
  6.9 1.4 %collective-permute-start = (bf16[2,64,256]{2,1,0:T(8,128)(2,1)S(1)}, bf16[2,64,256]{2,1,0:T(8,128)(2,1)S(1)}, u32[]{:S(2)}, u32[]{:S(2)}) collective-permute-start(bf16[2,64,256]{2,1,0:T(8,128)(2,1)S(1)} %get-tuple-element.43), channel_id=1, source_target_pairs={{0,1},{1,0},{2,3},{3,2},{4,5},{5,4},{6,7},{7,6},{8,9},{9,8},{10,11... | collective-permute-start | bytes 196616 | tf_op jit(solution)/shard_map/ppermute | solution.py:42
  9.0 1.8 %collective-permute-start.1 = (bf16[64,2944]{1,0:T(8,128)(2,1)S(1)}, bf16[64,2944]{1,0:T(8,128)(2,1)S(1)}, u32[]{:S(2)}, u32[]{:S(2)}) collective-permute-start(bf16[64,2944]{1,0:T(8,128)(2,1)S(1)} %get-tuple-element.45), channel_id=1, source_target_pairs={{0,1},{1,0},{2,3},{3,2},{4,5},{5,4},{6,7},{7,6},{8,9},{9,8},{10,11... | collective-permute-start | bytes 1130504 | tf_op jit(solution)/shard_map/ppermute | solution.py:42
  9.4 6.0 %collective-permute-start.6 = (bf16[64,2944]{1,0:T(8,128)(2,1)S(1)}, bf16[64,2944]{1,0:T(8,128)(2,1)S(1)}, u32[]{:S(2)}, u32[]{:S(2)}) collective-permute-start(bf16[64,2944]{1,0:T(8,128)(2,1)S(1)} %get-tuple-element.54), channel_id=1, source_target_pairs={{0,1},{1,0},{2,3},{3,2},{4,5},{5,4},{6,7},{7,6},{8,9},{9,8},{10,11... | collective-permute-start | bytes 1130504 | tf_op jit(solution)/shard_map/ppermute | solution.py:42
  10.8 8.2 %collective-permute-start.2 = (bf16[16,2880]{1,0:T(8,128)(2,1)S(1)}, bf16[16,2880]{1,0:T(8,128)(2,1)S(1)}, u32[]{:S(2)}, u32[]{:S(2)}) collective-permute-start(bf16[16,2880]{1,0:T(8,128)(2,1)S(1)} %get-tuple-element.47), channel_id=1, source_target_pairs={{0,2},{1,3},{2,0},{3,1},{4,6},{5,7},{6,4},{7,5},{8,10},{9,11},{10,... | collective-permute-start | bytes 276488 | tf_op jit(solution)/shard_map/ppermute | solution.py:42
  13.8 5.8 %collective-permute-start.3 = (bf16[16,2880]{1,0:T(8,128)(2,1)S(1)}, bf16[16,2880]{1,0:T(8,128)(2,1)S(1)}, u32[]{:S(2)}, u32[]{:S(2)}) collective-permute-start(bf16[16,2880]{1,0:T(8,128)(2,1)S(1)} %get-tuple-element.48), channel_id=1, source_target_pairs={{0,4},{1,5},{2,6},{3,7},{4,0},{5,1},{6,2},{7,3},{8,12},{9,13},{10,... | collective-permute-start | bytes 276488 | tf_op jit(solution)/shard_map/ppermute | solution.py:42
  15.4 6.4 %collective-permute-start.4 = (bf16[16,2880]{1,0:T(8,128)(2,1)S(1)}, bf16[16,2880]{1,0:T(8,128)(2,1)S(1)}, u32[]{:S(2)}, u32[]{:S(2)}) collective-permute-start(bf16[16,2880]{1,0:T(8,128)(2,1)S(1)} %get-tuple-element.49), channel_id=1, source_target_pairs={{0,6},{1,7},{2,4},{3,5},{4,2},{5,3},{6,0},{7,1},{8,14},{9,15},{10,... | collective-permute-start | bytes 276488 | tf_op jit(solution)/shard_map/ppermute | solution.py:42
  15.5 9.7 %collective-permute-start.7 = (bf16[16,2880]{1,0:T(8,128)(2,1)S(1)}, bf16[16,2880]{1,0:T(8,128)(2,1)S(1)}, u32[]{:S(2)}, u32[]{:S(2)}) collective-permute-start(bf16[16,2880]{1,0:T(8,128)(2,1)S(1)} %get-tuple-element.56), channel_id=1, source_target_pairs={{0,2},{1,3},{2,0},{3,1},{4,6},{5,7},{6,4},{7,5},{8,10},{9,11},{10,... | collective-permute-start | bytes 276488 | tf_op jit(solution)/shard_map/ppermute | solution.py:42
  17.4 7.8 %collective-permute-start.8 = (bf16[16,2880]{1,0:T(8,128)(2,1)S(1)}, bf16[16,2880]{1,0:T(8,128)(2,1)S(1)}, u32[]{:S(2)}, u32[]{:S(2)}) collective-permute-start(bf16[16,2880]{1,0:T(8,128)(2,1)S(1)} %get-tuple-element.57), channel_id=1, source_target_pairs={{0,4},{1,5},{2,6},{3,7},{4,0},{5,1},{6,2},{7,3},{8,12},{9,13},{10,... | collective-permute-start | bytes 276488 | tf_op jit(solution)/shard_map/ppermute | solution.py:42
  19.0 6.2 %collective-permute-start.9 = (bf16[16,2880]{1,0:T(8,128)(2,1)S(1)}, bf16[16,2880]{1,0:T(8,128)(2,1)S(1)}, u32[]{:S(2)}, u32[]{:S(2)}) collective-permute-start(bf16[16,2880]{1,0:T(8,128)(2,1)S(1)} %get-tuple-element.58), channel_id=1, source_target_pairs={{0,6},{1,7},{2,4},{3,5},{4,2},{5,3},{6,0},{7,1},{8,14},{9,15},{10,... | collective-permute-start | bytes 276488 | tf_op jit(solution)/shard_map/ppermute | solution.py:42
  21.8 23.3 %slice-start = ((s8[8478720]{0:T(1024)(128)(4,1)}), s8[4194304]{0:T(1024)(128)(4,1)S(1)}, s32[]{:S(2)}) async-start(s8[8478720]{0:T(1024)(128)(4,1)} %bitcast.11), calls=%async_computation | async-start | bytes 8388608
  21.8 23.3 %slice-start.1 = ((s8[8478720]{0:T(1024)(128)(4,1)}), s8[4194304]{0:T(1024)(128)(4,1)S(1)}, s32[]{:S(2)}) async-start(s8[8478720]{0:T(1024)(128)(4,1)} %bitcast.11), calls=%async_computation.1 | async-start | bytes 8388608
  21.8 23.3 %slice-start.3 = ((s8[8478720]{0:T(1024)(128)(4,1)}), s8[4194304]{0:T(1024)(128)(4,1)S(1)}, s32[]{:S(2)}) async-start(s8[8478720]{0:T(1024)(128)(4,1)} %bitcast.15), calls=%async_computation.3 | async-start | bytes 8388608
  21.8 23.3 %slice-start.4 = ((s8[8478720]{0:T(1024)(128)(4,1)}), s8[4194304]{0:T(1024)(128)(4,1)S(1)}, s32[]{:S(2)}) async-start(s8[8478720]{0:T(1024)(128)(4,1)} %bitcast.15), calls=%async_computation.4 | async-start | bytes 8388608
  21.8 23.3 %slice-start.6 = ((s8[8478720]{0:T(1024)(128)(4,1)}), s8[4194304]{0:T(1024)(128)(4,1)S(1)}, s32[]{:S(2)}) async-start(s8[8478720]{0:T(1024)(128)(4,1)} %bitcast.18), calls=%async_computation.6 | async-start | bytes 8388608
  21.8 23.3 %slice-start.7 = ((s8[8478720]{0:T(1024)(128)(4,1)}), s8[4194304]{0:T(1024)(128)(4,1)S(1)}, s32[]{:S(2)}) async-start(s8[8478720]{0:T(1024)(128)(4,1)} %bitcast.18), calls=%async_computation.7 | async-start | bytes 8388608
  22.5 9.1 %collective-permute-start.5 = (bf16[16,2944]{1,0:T(8,128)(2,1)S(1)}, bf16[16,2944]{1,0:T(8,128)(2,1)S(1)}, u32[]{:S(2)}, u32[]{:S(2)}) collective-permute-start(bf16[16,2944]{1,0:T(8,128)(2,1)S(1)} %get-tuple-element.51.mine), channel_id=1, source_target_pairs={{0,8},{1,9},{2,10},{3,11},{4,12},{5,13},{6,14},{7,15},{8,0},{9,1},... | collective-permute-start | bytes 282632 | tf_op jit(solution)/shard_map/ppermute | solution.py:42
  25.2 6.4 %copy-start.1 = (bf16[2880,16]{0,1:T(8,128)(2,1)S(1)}, bf16[2880,16]{0,1:T(8,128)(2,1)}, u32[]{:S(2)}) copy-start(bf16[2880,16]{0,1:T(8,128)(2,1)} %param.17) | copy-start | bytes 276484
  25.2 19.9 %slice-start.2 = ((s8[8478720]{0:T(1024)(128)(4,1)}), s8[90112]{0:T(1024)(128)(4,1)S(1)}, s32[]{:S(2)}) async-start(s8[8478720]{0:T(1024)(128)(4,1)} %bitcast.11), calls=%async_computation.2 | async-start | bytes 180224
  25.2 19.9 %slice-start.5 = ((s8[8478720]{0:T(1024)(128)(4,1)}), s8[90112]{0:T(1024)(128)(4,1)S(1)}, s32[]{:S(2)}) async-start(s8[8478720]{0:T(1024)(128)(4,1)} %bitcast.15), calls=%async_computation.5 | async-start | bytes 180224
  25.2 19.9 %slice-start.8 = ((s8[8478720]{0:T(1024)(128)(4,1)}), s8[90112]{0:T(1024)(128)(4,1)S(1)}, s32[]{:S(2)}) async-start(s8[8478720]{0:T(1024)(128)(4,1)} %bitcast.18), calls=%async_computation.8 | async-start | bytes 180224
  26.0 9.7 %collective-permute-start.10 = (bf16[16,2944]{1,0:T(8,128)(2,1)S(1)}, bf16[16,2944]{1,0:T(8,128)(2,1)S(1)}, u32[]{:S(2)}, u32[]{:S(2)}) collective-permute-start(bf16[16,2944]{1,0:T(8,128)(2,1)S(1)} %get-tuple-element.60.mine), channel_id=1, source_target_pairs={{0,8},{1,9},{2,10},{3,11},{4,12},{5,13},{6,14},{7,15},{8,0},{9,1},... | collective-permute-start | bytes 282632 | tf_op jit(solution)/shard_map/ppermute | solution.py:42
  32.1 6.6 %collective-permute-start.13 = (bf16[16,2944]{1,0:T(8,128)(2,1)S(1)}, bf16[16,2944]{1,0:T(8,128)(2,1)S(1)}, u32[]{:S(2)}, u32[]{:S(2)}) collective-permute-start(bf16[16,2944]{1,0:T(8,128)(2,1)S(1)} %get-tuple-element.62.refs_0_), channel_id=1, source_target_pairs={{0,6},{1,7},{2,4},{3,5},{4,2},{5,3},{6,0},{7,1},{8,14},{9,15},{10,... | collective-permute-start | bytes 282632 | tf_op jit(solution)/shard_map/ppermute | solution.py:42
  32.7 7.0 %collective-permute-start.12 = (bf16[16,2944]{1,0:T(8,128)(2,1)S(1)}, bf16[16,2944]{1,0:T(8,128)(2,1)S(1)}, u32[]{:S(2)}, u32[]{:S(2)}) collective-permute-start(bf16[16,2944]{1,0:T(8,128)(2,1)S(1)} %get-tuple-element.62.refs_0_), channel_id=1, source_target_pairs={{0,4},{1,5},{2,6},{3,7},{4,0},{5,1},{6,2},{7,3},{8,12},{9,13},{10,... | collective-permute-start | bytes 282632 | tf_op jit(solution)/shard_map/ppermute | solution.py:42
  32.7 7.9 %collective-permute-start.11 = (bf16[16,2944]{1,0:T(8,128)(2,1)S(1)}, bf16[16,2944]{1,0:T(8,128)(2,1)S(1)}, u32[]{:S(2)}, u32[]{:S(2)}) collective-permute-start(bf16[16,2944]{1,0:T(8,128)(2,1)S(1)} %get-tuple-element.62.refs_0_), channel_id=1, source_target_pairs={{0,2},{1,3},{2,0},{3,1},{4,6},{5,7},{6,4},{7,5},{8,10},{9,11},{10,... | collective-permute-start | bytes 282632 | tf_op jit(solution)/shard_map/ppermute | solution.py:42
  36.2 5.5 %collective-permute-start.17 = (bf16[16,2944]{1,0:T(8,128)(2,1)S(1)}, bf16[16,2944]{1,0:T(8,128)(2,1)S(1)}, u32[]{:S(2)}, u32[]{:S(2)}) collective-permute-start(bf16[16,2944]{1,0:T(8,128)(2,1)S(1)} %get-tuple-element.63.refs_0_.refs_5_), channel_id=1, source_target_pairs={{0,6},{1,7},{2,4},{3,5},{4,2},{5,3},{6,0},{7,1},{8,14},{9,15},{10,... | collective-permute-start | bytes 282632 | tf_op jit(solution)/shard_map/ppermute | solution.py:42
  36.8 4.9 %collective-permute-start.16 = (bf16[16,2944]{1,0:T(8,128)(2,1)S(1)}, bf16[16,2944]{1,0:T(8,128)(2,1)S(1)}, u32[]{:S(2)}, u32[]{:S(2)}) collective-permute-start(bf16[16,2944]{1,0:T(8,128)(2,1)S(1)} %get-tuple-element.63.refs_0_.refs_5_), channel_id=1, source_target_pairs={{0,4},{1,5},{2,6},{3,7},{4,0},{5,1},{6,2},{7,3},{8,12},{9,13},{10,... | collective-permute-start | bytes 282632 | tf_op jit(solution)/shard_map/ppermute | solution.py:42
  38.7 4.6 %collective-permute-start.15 = (bf16[16,2944]{1,0:T(8,128)(2,1)S(1)}, bf16[16,2944]{1,0:T(8,128)(2,1)S(1)}, u32[]{:S(2)}, u32[]{:S(2)}) collective-permute-start(bf16[16,2944]{1,0:T(8,128)(2,1)S(1)} %get-tuple-element.63.refs_0_.refs_5_), channel_id=1, source_target_pairs={{0,2},{1,3},{2,0},{3,1},{4,6},{5,7},{6,4},{7,5},{8,10},{9,11},{10,... | collective-permute-start | bytes 282632 | tf_op jit(solution)/shard_map/ppermute | solution.py:42
  40.7 2.7 %collective-permute-start.14 = (bf16[64,2944]{1,0:T(8,128)(2,1)S(1)}, bf16[64,2944]{1,0:T(8,128)(2,1)S(1)}, u32[]{:S(2)}, u32[]{:S(2)}) collective-permute-start(bf16[64,2944]{1,0:T(8,128)(2,1)S(1)} %join.2), channel_id=1, source_target_pairs={{0,1},{1,0},{2,3},{3,2},{4,5},{5,4},{6,7},{7,6},{8,9},{9,8},{10,11... | collective-permute-start | bytes 1130504 | tf_op jit(solution)/shard_map/ppermute | solution.py:42
  43.3 1.8 %collective-permute-start.18 = (bf16[64,2944]{1,0:T(8,128)(2,1)S(1)}, bf16[64,2944]{1,0:T(8,128)(2,1)S(1)}, u32[]{:S(2)}, u32[]{:S(2)}) collective-permute-start(bf16[64,2944]{1,0:T(8,128)(2,1)S(1)} %join.3), channel_id=1, source_target_pairs={{0,1},{1,0},{2,3},{3,2},{4,5},{5,4},{6,7},{7,6},{8,9},{9,8},{10,11... | collective-permute-start | bytes 1130504 | tf_op jit(solution)/shard_map/ppermute | solution.py:42
  52.0 1.9 %collective-permute-start.19 = (bf16[128,1920]{1,0:T(8,128)(2,1)S(1)}, bf16[128,1920]{1,0:T(8,128)(2,1)S(1)}, u32[]{:S(2)}, u32[]{:S(2)}) collective-permute-start(bf16[128,1920]{1,0:T(8,128)(2,1)S(1)} %get-tuple-element.65), channel_id=1, source_target_pairs={{0,1},{1,0},{2,3},{3,2},{4,5},{5,4},{6,7},{7,6},{8,9},{9,8},{10,11... | collective-permute-start | bytes 1474568 | tf_op jit(solution)/shard_map/ppermute | solution.py:42
  53.1 4.4 %collective-permute-start.24 = (bf16[128,1024]{1,0:T(8,128)(2,1)S(1)}, bf16[128,1024]{1,0:T(8,128)(2,1)S(1)}, u32[]{:S(2)}, u32[]{:S(2)}) collective-permute-start(bf16[128,1024]{1,0:T(8,128)(2,1)S(1)} %get-tuple-element.75), channel_id=1, source_target_pairs={{0,1},{1,0},{2,3},{3,2},{4,5},{5,4},{6,7},{7,6},{8,9},{9,8},{10,11... | collective-permute-start | bytes 786440 | tf_op jit(solution)/shard_map/ppermute | solution.py:42
  54.0 5.4 %collective-permute-start.20 = (bf16[32,1920]{1,0:T(8,128)(2,1)S(1)}, bf16[32,1920]{1,0:T(8,128)(2,1)S(1)}, u32[]{:S(2)}, u32[]{:S(2)}) collective-permute-start(bf16[32,1920]{1,0:T(8,128)(2,1)S(1)} %get-tuple-element.67), channel_id=1, source_target_pairs={{0,2},{1,3},{2,0},{3,1},{4,6},{5,7},{6,4},{7,5},{8,10},{9,11},{10,... | collective-permute-start | bytes 368648 | tf_op jit(solution)/shard_map/ppermute | solution.py:42
  55.1 6.2 %collective-permute-start.21 = (bf16[32,1920]{1,0:T(8,128)(2,1)S(1)}, bf16[32,1920]{1,0:T(8,128)(2,1)S(1)}, u32[]{:S(2)}, u32[]{:S(2)}) collective-permute-start(bf16[32,1920]{1,0:T(8,128)(2,1)S(1)} %get-tuple-element.68), channel_id=1, source_target_pairs={{0,4},{1,5},{2,6},{3,7},{4,0},{5,1},{6,2},{7,3},{8,12},{9,13},{10,... | collective-permute-start | bytes 368648 | tf_op jit(solution)/shard_map/ppermute | solution.py:42
  55.1 9.3 %collective-permute-start.22 = (bf16[32,1920]{1,0:T(8,128)(2,1)S(1)}, bf16[32,1920]{1,0:T(8,128)(2,1)S(1)}, u32[]{:S(2)}, u32[]{:S(2)}) collective-permute-start(bf16[32,1920]{1,0:T(8,128)(2,1)S(1)} %get-tuple-element.69), channel_id=1, source_target_pairs={{0,6},{1,7},{2,4},{3,5},{4,2},{5,3},{6,0},{7,1},{8,14},{9,15},{10,... | collective-permute-start | bytes 368648 | tf_op jit(solution)/shard_map/ppermute | solution.py:42
  57.6 8.4 %collective-permute-start.25 = (bf16[32,960]{1,0:T(8,128)(2,1)S(1)}, bf16[32,960]{1,0:T(8,128)(2,1)S(1)}, u32[]{:S(2)}, u32[]{:S(2)}) collective-permute-start(bf16[32,960]{1,0:T(8,128)(2,1)S(1)} %get-tuple-element.77), channel_id=1, source_target_pairs={{0,2},{1,3},{2,0},{3,1},{4,6},{5,7},{6,4},{7,5},{8,10},{9,11},{10,... | collective-permute-start | bytes 184328 | tf_op jit(solution)/shard_map/ppermute | solution.py:42
  58.7 7.3 %collective-permute-start.26 = (bf16[32,960]{1,0:T(8,128)(2,1)S(1)}, bf16[32,960]{1,0:T(8,128)(2,1)S(1)}, u32[]{:S(2)}, u32[]{:S(2)}) collective-permute-start(bf16[32,960]{1,0:T(8,128)(2,1)S(1)} %get-tuple-element.78), channel_id=1, source_target_pairs={{0,4},{1,5},{2,6},{3,7},{4,0},{5,1},{6,2},{7,3},{8,12},{9,13},{10,... | collective-permute-start | bytes 184328 | tf_op jit(solution)/shard_map/ppermute | solution.py:42
  59.4 6.6 %collective-permute-start.27 = (bf16[32,960]{1,0:T(8,128)(2,1)S(1)}, bf16[32,960]{1,0:T(8,128)(2,1)S(1)}, u32[]{:S(2)}, u32[]{:S(2)}) collective-permute-start(bf16[32,960]{1,0:T(8,128)(2,1)S(1)} %get-tuple-element.79), channel_id=1, source_target_pairs={{0,6},{1,7},{2,4},{3,5},{4,2},{5,3},{6,0},{7,1},{8,14},{9,15},{10,... | collective-permute-start | bytes 184328 | tf_op jit(solution)/shard_map/ppermute | solution.py:42
  64.4 6.5 %collective-permute-start.23 = (bf16[16,1920]{1,0:T(8,128)(2,1)S(1)}, bf16[16,1920]{1,0:T(8,128)(2,1)S(1)}, u32[]{:S(2)}, u32[]{:S(2)}) collective-permute-start(bf16[16,1920]{1,0:T(8,128)(2,1)S(1)} %get-tuple-element.71), channel_id=1, source_target_pairs={{0,8},{1,9},{2,10},{3,11},{4,12},{5,13},{6,14},{7,15},{8,0},{9,1},... | collective-permute-start | bytes 184328 | tf_op jit(solution)/shard_map/ppermute | solution.py:42
  66.1 4.9 %collective-permute-start.28 = (bf16[16,960]{1,0:T(8,128)(2,1)S(1)}, bf16[16,960]{1,0:T(8,128)(2,1)S(1)}, u32[]{:S(2)}, u32[]{:S(2)}) collective-permute-start(bf16[16,960]{1,0:T(8,128)(2,1)S(1)} %get-tuple-element.81), channel_id=1, source_target_pairs={{0,8},{1,9},{2,10},{3,11},{4,12},{5,13},{6,14},{7,15},{8,0},{9,1},... | collective-permute-start | bytes 92168 | tf_op jit(solution)/shard_map/ppermute | solution.py:42

commit v8 on v7

--- a/solution.py
+++ b/solution.py
@@ -242,6 +242,7 @@
     started = finished = 0
     low = lax.broadcasted_iota(jnp.int32, (block, pair), 1) < HD
     position = lax.broadcasted_iota(jnp.int32, (QPK, window), 1)
+    upper = lax.broadcasted_iota(jnp.int32, (2 * QPK, window), 0) < QPK
     heads = QPK // group
     for m, i in steps:
         while started < min(finished + COPIES_AHEAD, len(copies)):
@@ -268,26 +269,34 @@
             if started < len(copies):
                 copies[started].start()
                 started += 1
-        for r in range(block):
-            part = slice(r * QPK, (r + 1) * QPK)
+        for r in range(0, block, 2):
+            part = slice(r * QPK, (r + 2) * QPK)
             found = lax.dot_general(
                 query[part, :].astype(jnp.bfloat16),
-                near[m, i + r],
+                near[m, i + r : i + r + 2].reshape(2 * window, pair),
                 ROWS_LAST,
                 preferred_element_type=jnp.float32,
             )
-            scores[part, :] = jnp.where(position < lengths[m, first + r], found, -jnp.inf)
+            for k in (0, 1):
+                own_part = found[k * QPK : (k + 1) * QPK, k * window : (k + 1) * window]
+                scores[(r + k) * QPK : (r + k + 1) * QPK, :] = jnp.where(
+                    position < lengths[m, first + r + k], own_part, -jnp.inf
+                )
         top = jnp.maximum(jnp.max(scores[...], axis=1, keepdims=True), own)
         weight = jnp.exp(scores[...] - top)
         weight_own = jnp.exp(own - top)
         total = jnp.sum(weight, axis=1, keepdims=True) + weight_own
         scores[...] = weight / total
         prob_own = (weight_own / total).astype(jnp.bfloat16).astype(jnp.float32)
-        for r in range(block):
-            part = slice(r * QPK, (r + 1) * QPK)
+        for r in range(0, block, 2):
+            part = slice(r * QPK, (r + 2) * QPK)
+            prob = scores[part, :]
+            prob = jnp.concatenate(
+                [jnp.where(upper, prob, 0.0), jnp.where(upper, 0.0, prob)], axis=1
+            )
             mixed[part, :] = jnp.dot(
-                scores[part, :].astype(jnp.bfloat16),
-                near[m, i + r],
+                prob.astype(jnp.bfloat16),
+                near[m, i + r : i + r + 2].reshape(2 * window, pair),
                 preferred_element_type=jnp.float32,
             )
         mixed[...] = mixed[...] + prob_own * fresh

time: 71.8 us -> 70.3 us (0.979)
  Pallas kernels: 18.2 us -> 16.6 us
    pallas_call x1, Pallas kernels: 6.24 us -> 4.64 us  [attention(): pl.pallas_call(functools.partial(attention_kernel, group, block), out_sha...]
  transfers between devices with their start and end apart: 29 -> 29, of which waited for: 14 -> 15; matrix products, arithmetic and copies ran while one was open for 0% -> 0% of each run, Pallas kernels for 5% -> 6%
where the time goes in v8:
time: 70.3 us; the launch traced here: 70.1 us
  starting transfers between devices  32.7 us (47%)
  waiting for transfers between devices  19.8 us (28%)
  Pallas kernels  16.6 us (24%)
  between operations  0.93 us (1%)
    ppermute x29, starting transfers between devices, from_mask(): return lax.ppermute(value, 'req', pairs)  32.7 us
    ppermute x29, waiting for transfers between devices, from_mask(): return lax.ppermute(value, 'req', pairs)  19.8 us
    pallas_call x16, Pallas kernels, whole_call(): pl.pallas_call(kernel, out_shape=outs, in_specs=[pl.BlockSpec(memory_spac...  12 us
    pallas_call x1, Pallas kernels, attention(): pl.pallas_call(functools.partial(attention_kernel, group, block), out_sha...  4.64 us
  transfers between devices with their start and end apart: 29, of which 15 were waited for; matrix products, arithmetic and copies ran while one was open for 0% of the time, Pallas kernels for 6%

profile of v8, /device:TPU:0, one launch (start us, length us, event | category | flops | bytes accessed | tf_op | source)
XLA Modules:
  0.0 70.1 jit_solution(11190237665956248016)
XLA Ops:
  0.7 4.6 %attention.1 = (bf16[2,64,256]{2,1,0:T(8,128)(2,1)S(1)}, bf16[2,64,256]{2,1,0:T(8,128)(2,1)S(1)}) custom-call(s32[2,128]{1,0:T(2,128)} %lengths.1, s32[1]{0:T(128)S(6)} %select_n.7.place, bf16[2,64,512]{2,1,0:T(8,128)(2,1)} %far_q.1, bf16[2,64,128]{2,1,0:T(8,128)(2,1)} %far_kv.1, bf16[2,64,128,128]{3,2,1,0:T(8,128)(2,1)} %far.1), custom_call_target="tpu_custom_call" | custom-call | flops 10000000000 | bytes 30000000 | tf_op jit(solution)/shard_map/attention/pallas_call | solution.py:322
  5.3 0.5 collective-permute-start
  5.8 0.9 %collective-permute-done.refs_1_ = bf16[2,64,256]{2,1,0:T(8,128)(2,1)S(1)} collective-permute-done((bf16[2,64,256]{2,1,0:T(8,128)(2,1)S(1)}, bf16[2,64,256]{2,1,0:T(8,128)(2,1)S(1)}, u32[]{:S(2)}, u32[]{:S(2)}) %collective-permute-start) | collective-permute-done | bytes 65568 | tf_op jit(solution)/shard_map/ppermute | solution.py:42
  6.7 0.6 project.1
  7.4 0.4 collective-permute-start.1
  7.8 0.2 collective-permute-start.6
  8.0 1.2 %collective-permute-done.1.refs_1_ = bf16[64,2944]{1,0:T(8,128)(2,1)S(1)} collective-permute-done((bf16[64,2944]{1,0:T(8,128)(2,1)S(1)}, bf16[64,2944]{1,0:T(8,128)(2,1)S(1)}, u32[]{:S(2)}, u32[]{:S(2)}) %collective-permute-start.1) | collective-permute-done | bytes 376864 | tf_op jit(solution)/shard_map/ppermute | solution.py:42
  9.2 0.1 add_split.6
  9.2 2.9 %collective-permute-start.2 = (bf16[16,2880]{1,0:T(8,128)(2,1)S(1)}, bf16[16,2880]{1,0:T(8,128)(2,1)S(1)}, u32[]{:S(2)}, u32[]{:S(2)}) collective-permute-start(bf16[16,2880]{1,0:T(8,128)(2,1)S(1)} %get-tuple-element.47), channel_id=1, source_target_pairs={{0,2},{1,3},{2,0},{3,1},{4,6},{5,7},{6,4},{7,5},{8,10},{9,11},{10,... | collective-permute-start | bytes 276488 | tf_op jit(solution)/shard_map/ppermute | solution.py:42
  12.2 1.6 %collective-permute-start.3 = (bf16[16,2880]{1,0:T(8,128)(2,1)S(1)}, bf16[16,2880]{1,0:T(8,128)(2,1)S(1)}, u32[]{:S(2)}, u32[]{:S(2)}) collective-permute-start(bf16[16,2880]{1,0:T(8,128)(2,1)S(1)} %get-tuple-element.48), channel_id=1, source_target_pairs={{0,4},{1,5},{2,6},{3,7},{4,0},{5,1},{6,2},{7,3},{8,12},{9,13},{10,... | collective-permute-start | bytes 276488 | tf_op jit(solution)/shard_map/ppermute | solution.py:42
  13.8 0.0 collective-permute-start.4
  13.8 0.1 add_split.7
  13.9 2.0 %collective-permute-start.7 = (bf16[16,2880]{1,0:T(8,128)(2,1)S(1)}, bf16[16,2880]{1,0:T(8,128)(2,1)S(1)}, u32[]{:S(2)}, u32[]{:S(2)}) collective-permute-start(bf16[16,2880]{1,0:T(8,128)(2,1)S(1)} %get-tuple-element.56), channel_id=1, source_target_pairs={{0,2},{1,3},{2,0},{3,1},{4,6},{5,7},{6,4},{7,5},{8,10},{9,11},{10,... | collective-permute-start | bytes 276488 | tf_op jit(solution)/shard_map/ppermute | solution.py:42
  15.8 1.6 %collective-permute-start.8 = (bf16[16,2880]{1,0:T(8,128)(2,1)S(1)}, bf16[16,2880]{1,0:T(8,128)(2,1)S(1)}, u32[]{:S(2)}, u32[]{:S(2)}) collective-permute-start(bf16[16,2880]{1,0:T(8,128)(2,1)S(1)} %get-tuple-element.57), channel_id=1, source_target_pairs={{0,4},{1,5},{2,6},{3,7},{4,0},{5,1},{6,2},{7,3},{8,12},{9,13},{10,... | collective-permute-start | bytes 276488 | tf_op jit(solution)/shard_map/ppermute | solution.py:42
  17.4 0.5 collective-permute-start.9
  18.0 0.0 collective-permute-done.3.refs_2_
  18.0 2.2 %collective-permute-done.4.refs_3_ = bf16[16,2880]{1,0:T(8,128)(2,1)S(1)} collective-permute-done((bf16[16,2880]{1,0:T(8,128)(2,1)S(1)}, bf16[16,2880]{1,0:T(8,128)(2,1)S(1)}, u32[]{:S(2)}, u32[]{:S(2)}) %collective-permute-start.4) | collective-permute-done | bytes 92192 | tf_op jit(solution)/shard_map/ppermute | solution.py:42
  20.2 0.0 slice-start.3
  20.2 0.0 slice-start.4
  20.2 0.0 slice-start.6
  20.2 0.0 slice-start.7
  20.2 0.7 %share.2 = (f32[16,2944]{1,0:T(8,128)S(1)}, bf16[16,2944]{1,0:T(8,128)(2,1)S(1)}) custom-call(s32[2,4,8]{2,1,0:T(4,128)S(1)} %bitcast.24, f32[16,2880]{1,0:T(8,128)S(1)} %get-tuple-element.46.refs_0_, bf16[16,2880]{1,0:T(8,128)(2,1)S(1)} %collective-permute-done.2.refs_1_, bf16[16,2880]{1,0:T(8,128)(2,1)S(1)} %collective-permute-done.3.refs_2_, ...), custom_call_target="tpu_custom_call" | custom-call | flops 60000002048 | bytes 180000000 | tf_op jit(solution)/shard_map/share/pallas_call | solution.py:50
  20.9 2.7 %collective-permute-start.5 = (bf16[16,2944]{1,0:T(8,128)(2,1)S(1)}, bf16[16,2944]{1,0:T(8,128)(2,1)S(1)}, u32[]{:S(2)}, u32[]{:S(2)}) collective-permute-start(bf16[16,2944]{1,0:T(8,128)(2,1)S(1)} %get-tuple-element.51.mine), channel_id=1, source_target_pairs={{0,8},{1,9},{2,10},{3,11},{4,12},{5,13},{6,14},{7,15},{8,0},{9,1},... | collective-permute-start | bytes 282632 | tf_op jit(solution)/shard_map/ppermute | solution.py:42
  23.6 0.0 collective-permute-done.9.refs_3_
  23.6 0.0 copy-start.1
  23.6 0.0 slice-start.2
  23.6 0.0 slice-start.5
  23.6 0.0 slice-start.8
  23.7 0.7 %share.3 = (f32[16,2944]{1,0:T(8,128)S(1)}, bf16[16,2944]{1,0:T(8,128)(2,1)S(1)}) custom-call(s32[2,4,8]{2,1,0:T(4,128)S(1)} %bitcast.25, f32[16,2880]{1,0:T(8,128)S(1)} %get-tuple-element.55.refs_0_, bf16[16,2880]{1,0:T(8,128)(2,1)S(1)} %collective-permute-done.7.refs_1_, bf16[16,2880]{1,0:T(8,128)(2,1)S(1)} %collective-permute-done.8.refs_2_, ...), custom_call_target="tpu_custom_call" | custom-call | flops 60000002048 | bytes 180000000 | tf_op jit(solution)/shard_map/share/pallas_call | solution.py:50
  24.4 3.0 %collective-permute-start.10 = (bf16[16,2944]{1,0:T(8,128)(2,1)S(1)}, bf16[16,2944]{1,0:T(8,128)(2,1)S(1)}, u32[]{:S(2)}, u32[]{:S(2)}) collective-permute-start(bf16[16,2944]{1,0:T(8,128)(2,1)S(1)} %get-tuple-element.60.mine), channel_id=1, source_target_pairs={{0,8},{1,9},{2,10},{3,11},{4,12},{5,13},{6,14},{7,15},{8,0},{9,1},... | collective-permute-start | bytes 282632 | tf_op jit(solution)/shard_map/ppermute | solution.py:42
  27.3 2.7 %collective-permute-done.5.theirs = bf16[16,2944]{1,0:T(8,128)(2,1)S(1)} collective-permute-done((bf16[16,2944]{1,0:T(8,128)(2,1)S(1)}, bf16[16,2944]{1,0:T(8,128)(2,1)S(1)}, u32[]{:S(2)}, u32[]{:S(2)}) %collective-permute-start.5) | collective-permute-done | bytes 94240 | tf_op jit(solution)/shard_map/ppermute | solution.py:42
  30.0 0.5 norm.2
  30.5 0.6 collective-permute-start.13
  31.1 3.0 %collective-permute-start.11 = (bf16[16,2944]{1,0:T(8,128)(2,1)S(1)}, bf16[16,2944]{1,0:T(8,128)(2,1)S(1)}, u32[]{:S(2)}, u32[]{:S(2)}) collective-permute-start(bf16[16,2944]{1,0:T(8,128)(2,1)S(1)} %get-tuple-element.62.refs_0_), channel_id=1, source_target_pairs={{0,2},{1,3},{2,0},{3,1},{4,6},{5,7},{6,4},{7,5},{8,10},{9,11},{10,... | collective-permute-start | bytes 282632 | tf_op jit(solution)/shard_map/ppermute | solution.py:42
  34.1 0.5 norm.3
  34.6 0.6 collective-permute-start.17
  35.2 0.9 %collective-permute-start.16 = (bf16[16,2944]{1,0:T(8,128)(2,1)S(1)}, bf16[16,2944]{1,0:T(8,128)(2,1)S(1)}, u32[]{:S(2)}, u32[]{:S(2)}) collective-permute-start(bf16[16,2944]{1,0:T(8,128)(2,1)S(1)} %get-tuple-element.63.refs_0_.refs_5_), channel_id=1, source_target_pairs={{0,4},{1,5},{2,6},{3,7},{4,0},{5,1},{6,2},{7,3},{8,12},{9,13},{10,... | collective-permute-start | bytes 282632 | tf_op jit(solution)/shard_map/ppermute | solution.py:42
  36.2 1.0 %collective-permute-done.13.refs_3_ = bf16[16,2944]{1,0:T(8,128)(2,1)S(1)} collective-permute-done((bf16[16,2944]{1,0:T(8,128)(2,1)S(1)}, bf16[16,2944]{1,0:T(8,128)(2,1)S(1)}, u32[]{:S(2)}, u32[]{:S(2)}) %collective-permute-start.13) | collective-permute-done | bytes 94240 | tf_op jit(solution)/shard_map/ppermute | solution.py:42
  37.2 1.0 %collective-permute-start.15 = (bf16[16,2944]{1,0:T(8,128)(2,1)S(1)}, bf16[16,2944]{1,0:T(8,128)(2,1)S(1)}, u32[]{:S(2)}, u32[]{:S(2)}) collective-permute-start(bf16[16,2944]{1,0:T(8,128)(2,1)S(1)} %get-tuple-element.63.refs_0_.refs_5_), channel_id=1, source_target_pairs={{0,2},{1,3},{2,0},{3,1},{4,6},{5,7},{6,4},{7,5},{8,10},{9,11},{10,... | collective-permute-start | bytes 282632 | tf_op jit(solution)/shard_map/ppermute | solution.py:42
  38.2 0.9 %collective-permute-done.11.refs_1_ = bf16[16,2944]{1,0:T(8,128)(2,1)S(1)} collective-permute-done((bf16[16,2944]{1,0:T(8,128)(2,1)S(1)}, bf16[16,2944]{1,0:T(8,128)(2,1)S(1)}, u32[]{:S(2)}, u32[]{:S(2)}) %collective-permute-start.11) | collective-permute-done | bytes 94240 | tf_op jit(solution)/shard_map/ppermute | solution.py:42
  39.1 0.1 collective-permute-start.14
  39.2 0.9 %collective-permute-done.17.refs_3_.refs_8_ = bf16[16,2944]{1,0:T(8,128)(2,1)S(1)} collective-permute-done((bf16[16,2944]{1,0:T(8,128)(2,1)S(1)}, bf16[16,2944]{1,0:T(8,128)(2,1)S(1)}, u32[]{:S(2)}, u32[]{:S(2)}) %collective-permute-start.17) | collective-permute-done | bytes 94240 | tf_op jit(solution)/shard_map/ppermute | solution.py:42
  40.2 1.6 %collective-permute-done.15.refs_1_.refs_6_ = bf16[16,2944]{1,0:T(8,128)(2,1)S(1)} collective-permute-done((bf16[16,2944]{1,0:T(8,128)(2,1)S(1)}, bf16[16,2944]{1,0:T(8,128)(2,1)S(1)}, u32[]{:S(2)}, u32[]{:S(2)}) %collective-permute-start.15) | collective-permute-done | bytes 94240 | tf_op jit(solution)/shard_map/ppermute | solution.py:42
  41.8 0.1 collective-permute-start.18
  41.9 1.7 %collective-permute-done.18.refs_9_ = bf16[64,2944]{1,0:T(8,128)(2,1)S(1)} collective-permute-done((bf16[64,2944]{1,0:T(8,128)(2,1)S(1)}, bf16[64,2944]{1,0:T(8,128)(2,1)S(1)}, u32[]{:S(2)}, u32[]{:S(2)}) %collective-permute-start.18) | collective-permute-done | bytes 376864 | tf_op jit(solution)/shard_map/ppermute | solution.py:42
  43.6 6.8 %experts.1 = (f32[128,1920]{1,0:T(8,128)S(1)}, bf16[128,1920]{1,0:T(8,128)(2,1)S(1)}, bf16[256,1440]{1,0:T(8,128)(2,1)S(1)}, f32[1,256,128]{2,1,0:T(8,128)S(1)}) custom-call(s32[1]{0:T(128)} %bitcast.1.me_ref, bf16[16,2944]{1,0:T(8,128)(2,1)S(1)} %get-tuple-element.62.refs_0_, bf16[16,2944]{1,0:T(8,128)(2,1)S(1)} %collective-permute-done.11.refs_1_, ...), custom_call_target="tpu_custom_call" | custom-call | tf_op jit(solution)/shard_map/experts/pallas_call | solution.py:50
  50.4 0.2 collective-permute-start.19
  50.6 1.0 %down.1 = (f32[128,960]{1,0:T(8,128)S(1)}, bf16[128,1024]{1,0:T(8,128)(2,1)S(1)}) custom-call(bf16[256,1440]{1,0:T(8,128)(2,1)S(1)} %get-tuple-element.72.active, f32[1,256,128]{2,1,0:T(8,128)S(1)} %get-tuple-element.73.weights, bf16[1440,2880]{1,0:T(8,128)(2,1)S(1)} %bitcast.14), custom_call_target="tpu_custom_call" | custom-call | tf_op jit(solution)/shard_map/down/pallas_call | solution.py:50
  51.6 0.5 collective-permute-start.24
  52.0 0.3 collective-permute-done.19.refs_1_
  52.3 0.1 add_split.8
  52.4 1.1 %collective-permute-start.20 = (bf16[32,1920]{1,0:T(8,128)(2,1)S(1)}, bf16[32,1920]{1,0:T(8,128)(2,1)S(1)}, u32[]{:S(2)}, u32[]{:S(2)}) collective-permute-start(bf16[32,1920]{1,0:T(8,128)(2,1)S(1)} %get-tuple-element.67), channel_id=1, source_target_pairs={{0,2},{1,3},{2,0},{3,1},{4,6},{5,7},{6,4},{7,5},{8,10},{9,11},{10,... | collective-permute-start | bytes 368648 | tf_op jit(solution)/shard_map/ppermute | solution.py:42
  53.5 2.5 %collective-permute-start.22 = (bf16[32,1920]{1,0:T(8,128)(2,1)S(1)}, bf16[32,1920]{1,0:T(8,128)(2,1)S(1)}, u32[]{:S(2)}, u32[]{:S(2)}) collective-permute-start(bf16[32,1920]{1,0:T(8,128)(2,1)S(1)} %get-tuple-element.69), channel_id=1, source_target_pairs={{0,6},{1,7},{2,4},{3,5},{4,2},{5,3},{6,0},{7,1},{8,14},{9,15},{10,... | collective-permute-start | bytes 368648 | tf_op jit(solution)/shard_map/ppermute | solution.py:42
  56.0 1.1 %collective-permute-start.25 = (bf16[32,960]{1,0:T(8,128)(2,1)S(1)}, bf16[32,960]{1,0:T(8,128)(2,1)S(1)}, u32[]{:S(2)}, u32[]{:S(2)}) collective-permute-start(bf16[32,960]{1,0:T(8,128)(2,1)S(1)} %get-tuple-element.77), channel_id=1, source_target_pairs={{0,2},{1,3},{2,0},{3,1},{4,6},{5,7},{6,4},{7,5},{8,10},{9,11},{10,... | collective-permute-start | bytes 184328 | tf_op jit(solution)/shard_map/ppermute | solution.py:42
  57.1 0.7 %collective-permute-done.20.refs_1_ = bf16[32,1920]{1,0:T(8,128)(2,1)S(1)} collective-permute-done((bf16[32,1920]{1,0:T(8,128)(2,1)S(1)}, bf16[32,1920]{1,0:T(8,128)(2,1)S(1)}, u32[]{:S(2)}, u32[]{:S(2)}) %collective-permute-start.20) | collective-permute-done | bytes 122912 | tf_op jit(solution)/shard_map/ppermute | solution.py:42
  57.8 1.7 %collective-permute-start.27 = (bf16[32,960]{1,0:T(8,128)(2,1)S(1)}, bf16[32,960]{1,0:T(8,128)(2,1)S(1)}, u32[]{:S(2)}, u32[]{:S(2)}) collective-permute-start(bf16[32,960]{1,0:T(8,128)(2,1)S(1)} %get-tuple-element.79), channel_id=1, source_target_pairs={{0,6},{1,7},{2,4},{3,5},{4,2},{5,3},{6,0},{7,1},{8,14},{9,15},{10,... | collective-permute-start | bytes 184328 | tf_op jit(solution)/shard_map/ppermute | solution.py:42
  59.6 0.1 collective-permute-done.21.refs_2_
  59.7 3.1 %collective-permute-done.22.refs_3_ = bf16[32,1920]{1,0:T(8,128)(2,1)S(1)} collective-permute-done((bf16[32,1920]{1,0:T(8,128)(2,1)S(1)}, bf16[32,1920]{1,0:T(8,128)(2,1)S(1)}, u32[]{:S(2)}, u32[]{:S(2)}) %collective-permute-start.22) | collective-permute-done | bytes 122912 | tf_op jit(solution)/shard_map/ppermute | solution.py:42
  62.8 0.1 add_split.9
  62.9 1.5 %collective-permute-start.23 = (bf16[16,1920]{1,0:T(8,128)(2,1)S(1)}, bf16[16,1920]{1,0:T(8,128)(2,1)S(1)}, u32[]{:S(2)}, u32[]{:S(2)}) collective-permute-start(bf16[16,1920]{1,0:T(8,128)(2,1)S(1)} %get-tuple-element.71), channel_id=1, source_target_pairs={{0,8},{1,9},{2,10},{3,11},{4,12},{5,13},{6,14},{7,15},{8,0},{9,1},... | collective-permute-start | bytes 184328 | tf_op jit(solution)/shard_map/ppermute | solution.py:42
  64.4 0.1 collective-permute-done.27.refs_3_
  64.5 2.5 %collective-permute-start.28 = (bf16[16,960]{1,0:T(8,128)(2,1)S(1)}, bf16[16,960]{1,0:T(8,128)(2,1)S(1)}, u32[]{:S(2)}, u32[]{:S(2)}) collective-permute-start(bf16[16,960]{1,0:T(8,128)(2,1)S(1)} %get-tuple-element.81), channel_id=1, source_target_pairs={{0,8},{1,9},{2,10},{3,11},{4,12},{5,13},{6,14},{7,15},{8,0},{9,1},... | collective-permute-start | bytes 92168 | tf_op jit(solution)/shard_map/ppermute | solution.py:42
  67.0 2.3 %collective-permute-done.28.refs_5_ = bf16[16,960]{1,0:T(8,128)(2,1)S(1)} collective-permute-done((bf16[16,960]{1,0:T(8,128)(2,1)S(1)}, bf16[16,960]{1,0:T(8,128)(2,1)S(1)}, u32[]{:S(2)}, u32[]{:S(2)}) %collective-permute-start.28) | collective-permute-done | bytes 30752 | tf_op jit(solution)/shard_map/ppermute | solution.py:42
  69.4 0.7 finish.1
  (40 shorter events, 0.2 us)
Async XLA Ops:
  0.6 6.1 %copy-start = (bf16[256,2880]{0,1:T(8,128)(2,1)S(1)}, bf16[256,2880]{0,1:T(8,128)(2,1)}, u32[]{:S(2)}) copy-start(bf16[256,2880]{0,1:T(8,128)(2,1)} %param.16) | copy-start | bytes 4423684
  0.7 19.5 %copy-start.2 = (bf16[2,8,2880]{2,1,0:T(8,128)(2,1)S(1)}, bf16[2,8,2880]{2,1,0:T(8,128)(2,1)}, u32[]{:S(2)}) copy-start(bf16[2,8,2880]{2,1,0:T(8,128)(2,1)} %refs_4_.3) | copy-start | bytes 276484
  0.7 19.5 %copy-start.3 = (s32[2,8,4]{1,2,0:T(4,128)S(1)}, s32[2,8,4]{1,2,0:T(4,128)}, u32[]{:S(2)}) copy-start(s32[2,8,4]{1,2,0:T(4,128)} %param.21) | copy-start | bytes 772
  5.3 1.4 %collective-permute-start = (bf16[2,64,256]{2,1,0:T(8,128)(2,1)S(1)}, bf16[2,64,256]{2,1,0:T(8,128)(2,1)S(1)}, u32[]{:S(2)}, u32[]{:S(2)}) collective-permute-start(bf16[2,64,256]{2,1,0:T(8,128)(2,1)S(1)} %get-tuple-element.43), channel_id=1, source_target_pairs={{0,1},{1,0},{2,3},{3,2},{4,5},{5,4},{6,7},{7,6},{8,9},{9,8},{10,11... | collective-permute-start | bytes 196616 | tf_op jit(solution)/shard_map/ppermute | solution.py:42
  7.4 1.8 %collective-permute-start.1 = (bf16[64,2944]{1,0:T(8,128)(2,1)S(1)}, bf16[64,2944]{1,0:T(8,128)(2,1)S(1)}, u32[]{:S(2)}, u32[]{:S(2)}) collective-permute-start(bf16[64,2944]{1,0:T(8,128)(2,1)S(1)} %get-tuple-element.45), channel_id=1, source_target_pairs={{0,1},{1,0},{2,3},{3,2},{4,5},{5,4},{6,7},{7,6},{8,9},{9,8},{10,11... | collective-permute-start | bytes 1130504 | tf_op jit(solution)/shard_map/ppermute | solution.py:42
  7.8 6.0 %collective-permute-start.6 = (bf16[64,2944]{1,0:T(8,128)(2,1)S(1)}, bf16[64,2944]{1,0:T(8,128)(2,1)S(1)}, u32[]{:S(2)}, u32[]{:S(2)}) collective-permute-start(bf16[64,2944]{1,0:T(8,128)(2,1)S(1)} %get-tuple-element.54), channel_id=1, source_target_pairs={{0,1},{1,0},{2,3},{3,2},{4,5},{5,4},{6,7},{7,6},{8,9},{9,8},{10,11... | collective-permute-start | bytes 1130504 | tf_op jit(solution)/shard_map/ppermute | solution.py:42
  9.2 8.2 %collective-permute-start.2 = (bf16[16,2880]{1,0:T(8,128)(2,1)S(1)}, bf16[16,2880]{1,0:T(8,128)(2,1)S(1)}, u32[]{:S(2)}, u32[]{:S(2)}) collective-permute-start(bf16[16,2880]{1,0:T(8,128)(2,1)S(1)} %get-tuple-element.47), channel_id=1, source_target_pairs={{0,2},{1,3},{2,0},{3,1},{4,6},{5,7},{6,4},{7,5},{8,10},{9,11},{10,... | collective-permute-start | bytes 276488 | tf_op jit(solution)/shard_map/ppermute | solution.py:42
  12.2 5.8 %collective-permute-start.3 = (bf16[16,2880]{1,0:T(8,128)(2,1)S(1)}, bf16[16,2880]{1,0:T(8,128)(2,1)S(1)}, u32[]{:S(2)}, u32[]{:S(2)}) collective-permute-start(bf16[16,2880]{1,0:T(8,128)(2,1)S(1)} %get-tuple-element.48), channel_id=1, source_target_pairs={{0,4},{1,5},{2,6},{3,7},{4,0},{5,1},{6,2},{7,3},{8,12},{9,13},{10,... | collective-permute-start | bytes 276488 | tf_op jit(solution)/shard_map/ppermute | solution.py:42
  13.8 6.4 %collective-permute-start.4 = (bf16[16,2880]{1,0:T(8,128)(2,1)S(1)}, bf16[16,2880]{1,0:T(8,128)(2,1)S(1)}, u32[]{:S(2)}, u32[]{:S(2)}) collective-permute-start(bf16[16,2880]{1,0:T(8,128)(2,1)S(1)} %get-tuple-element.49), channel_id=1, source_target_pairs={{0,6},{1,7},{2,4},{3,5},{4,2},{5,3},{6,0},{7,1},{8,14},{9,15},{10,... | collective-permute-start | bytes 276488 | tf_op jit(solution)/shard_map/ppermute | solution.py:42
  13.9 9.7 %collective-permute-start.7 = (bf16[16,2880]{1,0:T(8,128)(2,1)S(1)}, bf16[16,2880]{1,0:T(8,128)(2,1)S(1)}, u32[]{:S(2)}, u32[]{:S(2)}) collective-permute-start(bf16[16,2880]{1,0:T(8,128)(2,1)S(1)} %get-tuple-element.56), channel_id=1, source_target_pairs={{0,2},{1,3},{2,0},{3,1},{4,6},{5,7},{6,4},{7,5},{8,10},{9,11},{10,... | collective-permute-start | bytes 276488 | tf_op jit(solution)/shard_map/ppermute | solution.py:42
  15.8 7.8 %collective-permute-start.8 = (bf16[16,2880]{1,0:T(8,128)(2,1)S(1)}, bf16[16,2880]{1,0:T(8,128)(2,1)S(1)}, u32[]{:S(2)}, u32[]{:S(2)}) collective-permute-start(bf16[16,2880]{1,0:T(8,128)(2,1)S(1)} %get-tuple-element.57), channel_id=1, source_target_pairs={{0,4},{1,5},{2,6},{3,7},{4,0},{5,1},{6,2},{7,3},{8,12},{9,13},{10,... | collective-permute-start | bytes 276488 | tf_op jit(solution)/shard_map/ppermute | solution.py:42
  17.4 6.2 %collective-permute-start.9 = (bf16[16,2880]{1,0:T(8,128)(2,1)S(1)}, bf16[16,2880]{1,0:T(8,128)(2,1)S(1)}, u32[]{:S(2)}, u32[]{:S(2)}) collective-permute-start(bf16[16,2880]{1,0:T(8,128)(2,1)S(1)} %get-tuple-element.58), channel_id=1, source_target_pairs={{0,6},{1,7},{2,4},{3,5},{4,2},{5,3},{6,0},{7,1},{8,14},{9,15},{10,... | collective-permute-start | bytes 276488 | tf_op jit(solution)/shard_map/ppermute | solution.py:42
  20.2 23.4 %slice-start = ((s8[8478720]{0:T(1024)(128)(4,1)}), s8[4194304]{0:T(1024)(128)(4,1)S(1)}, s32[]{:S(2)}) async-start(s8[8478720]{0:T(1024)(128)(4,1)} %bitcast.11), calls=%async_computation | async-start | bytes 8388608
  20.2 23.4 %slice-start.1 = ((s8[8478720]{0:T(1024)(128)(4,1)}), s8[4194304]{0:T(1024)(128)(4,1)S(1)}, s32[]{:S(2)}) async-start(s8[8478720]{0:T(1024)(128)(4,1)} %bitcast.11), calls=%async_computation.1 | async-start | bytes 8388608
  20.2 23.4 %slice-start.3 = ((s8[8478720]{0:T(1024)(128)(4,1)}), s8[4194304]{0:T(1024)(128)(4,1)S(1)}, s32[]{:S(2)}) async-start(s8[8478720]{0:T(1024)(128)(4,1)} %bitcast.15), calls=%async_computation.3 | async-start | bytes 8388608
  20.2 23.4 %slice-start.4 = ((s8[8478720]{0:T(1024)(128)(4,1)}), s8[4194304]{0:T(1024)(128)(4,1)S(1)}, s32[]{:S(2)}) async-start(s8[8478720]{0:T(1024)(128)(4,1)} %bitcast.15), calls=%async_computation.4 | async-start | bytes 8388608
  20.2 23.4 %slice-start.6 = ((s8[8478720]{0:T(1024)(128)(4,1)}), s8[4194304]{0:T(1024)(128)(4,1)S(1)}, s32[]{:S(2)}) async-start(s8[8478720]{0:T(1024)(128)(4,1)} %bitcast.18), calls=%async_computation.6 | async-start | bytes 8388608
  20.2 23.4 %slice-start.7 = ((s8[8478720]{0:T(1024)(128)(4,1)}), s8[4194304]{0:T(1024)(128)(4,1)S(1)}, s32[]{:S(2)}) async-start(s8[8478720]{0:T(1024)(128)(4,1)} %bitcast.18), calls=%async_computation.7 | async-start | bytes 8388608
  20.9 9.1 %collective-permute-start.5 = (bf16[16,2944]{1,0:T(8,128)(2,1)S(1)}, bf16[16,2944]{1,0:T(8,128)(2,1)S(1)}, u32[]{:S(2)}, u32[]{:S(2)}) collective-permute-start(bf16[16,2944]{1,0:T(8,128)(2,1)S(1)} %get-tuple-element.51.mine), channel_id=1, source_target_pairs={{0,8},{1,9},{2,10},{3,11},{4,12},{5,13},{6,14},{7,15},{8,0},{9,1},... | collective-permute-start | bytes 282632 | tf_op jit(solution)/shard_map/ppermute | solution.py:42
  23.6 6.4 %copy-start.1 = (bf16[2880,16]{0,1:T(8,128)(2,1)S(1)}, bf16[2880,16]{0,1:T(8,128)(2,1)}, u32[]{:S(2)}) copy-start(bf16[2880,16]{0,1:T(8,128)(2,1)} %param.17) | copy-start | bytes 276484
  23.6 20.0 %slice-start.2 = ((s8[8478720]{0:T(1024)(128)(4,1)}), s8[90112]{0:T(1024)(128)(4,1)S(1)}, s32[]{:S(2)}) async-start(s8[8478720]{0:T(1024)(128)(4,1)} %bitcast.11), calls=%async_computation.2 | async-start | bytes 180224
  23.6 20.0 %slice-start.5 = ((s8[8478720]{0:T(1024)(128)(4,1)}), s8[90112]{0:T(1024)(128)(4,1)S(1)}, s32[]{:S(2)}) async-start(s8[8478720]{0:T(1024)(128)(4,1)} %bitcast.15), calls=%async_computation.5 | async-start | bytes 180224
  23.6 20.0 %slice-start.8 = ((s8[8478720]{0:T(1024)(128)(4,1)}), s8[90112]{0:T(1024)(128)(4,1)S(1)}, s32[]{:S(2)}) async-start(s8[8478720]{0:T(1024)(128)(4,1)} %bitcast.18), calls=%async_computation.8 | async-start | bytes 180224
  24.4 9.7 %collective-permute-start.10 = (bf16[16,2944]{1,0:T(8,128)(2,1)S(1)}, bf16[16,2944]{1,0:T(8,128)(2,1)S(1)}, u32[]{:S(2)}, u32[]{:S(2)}) collective-permute-start(bf16[16,2944]{1,0:T(8,128)(2,1)S(1)} %get-tuple-element.60.mine), channel_id=1, source_target_pairs={{0,8},{1,9},{2,10},{3,11},{4,12},{5,13},{6,14},{7,15},{8,0},{9,1},... | collective-permute-start | bytes 282632 | tf_op jit(solution)/shard_map/ppermute | solution.py:42
  30.5 6.6 %collective-permute-start.13 = (bf16[16,2944]{1,0:T(8,128)(2,1)S(1)}, bf16[16,2944]{1,0:T(8,128)(2,1)S(1)}, u32[]{:S(2)}, u32[]{:S(2)}) collective-permute-start(bf16[16,2944]{1,0:T(8,128)(2,1)S(1)} %get-tuple-element.62.refs_0_), channel_id=1, source_target_pairs={{0,6},{1,7},{2,4},{3,5},{4,2},{5,3},{6,0},{7,1},{8,14},{9,15},{10,... | collective-permute-start | bytes 282632 | tf_op jit(solution)/shard_map/ppermute | solution.py:42
  31.1 7.1 %collective-permute-start.12 = (bf16[16,2944]{1,0:T(8,128)(2,1)S(1)}, bf16[16,2944]{1,0:T(8,128)(2,1)S(1)}, u32[]{:S(2)}, u32[]{:S(2)}) collective-permute-start(bf16[16,2944]{1,0:T(8,128)(2,1)S(1)} %get-tuple-element.62.refs_0_), channel_id=1, source_target_pairs={{0,4},{1,5},{2,6},{3,7},{4,0},{5,1},{6,2},{7,3},{8,12},{9,13},{10,... | collective-permute-start | bytes 282632 | tf_op jit(solution)/shard_map/ppermute | solution.py:42
  31.1 8.0 %collective-permute-start.11 = (bf16[16,2944]{1,0:T(8,128)(2,1)S(1)}, bf16[16,2944]{1,0:T(8,128)(2,1)S(1)}, u32[]{:S(2)}, u32[]{:S(2)}) collective-permute-start(bf16[16,2944]{1,0:T(8,128)(2,1)S(1)} %get-tuple-element.62.refs_0_), channel_id=1, source_target_pairs={{0,2},{1,3},{2,0},{3,1},{4,6},{5,7},{6,4},{7,5},{8,10},{9,11},{10,... | collective-permute-start | bytes 282632 | tf_op jit(solution)/shard_map/ppermute | solution.py:42
  34.6 5.5 %collective-permute-start.17 = (bf16[16,2944]{1,0:T(8,128)(2,1)S(1)}, bf16[16,2944]{1,0:T(8,128)(2,1)S(1)}, u32[]{:S(2)}, u32[]{:S(2)}) collective-permute-start(bf16[16,2944]{1,0:T(8,128)(2,1)S(1)} %get-tuple-element.63.refs_0_.refs_5_), channel_id=1, source_target_pairs={{0,6},{1,7},{2,4},{3,5},{4,2},{5,3},{6,0},{7,1},{8,14},{9,15},{10,... | collective-permute-start | bytes 282632 | tf_op jit(solution)/shard_map/ppermute | solution.py:42
  35.2 5.0 %collective-permute-start.16 = (bf16[16,2944]{1,0:T(8,128)(2,1)S(1)}, bf16[16,2944]{1,0:T(8,128)(2,1)S(1)}, u32[]{:S(2)}, u32[]{:S(2)}) collective-permute-start(bf16[16,2944]{1,0:T(8,128)(2,1)S(1)} %get-tuple-element.63.refs_0_.refs_5_), channel_id=1, source_target_pairs={{0,4},{1,5},{2,6},{3,7},{4,0},{5,1},{6,2},{7,3},{8,12},{9,13},{10,... | collective-permute-start | bytes 282632 | tf_op jit(solution)/shard_map/ppermute | solution.py:42
  37.2 4.6 %collective-permute-start.15 = (bf16[16,2944]{1,0:T(8,128)(2,1)S(1)}, bf16[16,2944]{1,0:T(8,128)(2,1)S(1)}, u32[]{:S(2)}, u32[]{:S(2)}) collective-permute-start(bf16[16,2944]{1,0:T(8,128)(2,1)S(1)} %get-tuple-element.63.refs_0_.refs_5_), channel_id=1, source_target_pairs={{0,2},{1,3},{2,0},{3,1},{4,6},{5,7},{6,4},{7,5},{8,10},{9,11},{10,... | collective-permute-start | bytes 282632 | tf_op jit(solution)/shard_map/ppermute | solution.py:42
  39.1 2.7 %collective-permute-start.14 = (bf16[64,2944]{1,0:T(8,128)(2,1)S(1)}, bf16[64,2944]{1,0:T(8,128)(2,1)S(1)}, u32[]{:S(2)}, u32[]{:S(2)}) collective-permute-start(bf16[64,2944]{1,0:T(8,128)(2,1)S(1)} %join.2), channel_id=1, source_target_pairs={{0,1},{1,0},{2,3},{3,2},{4,5},{5,4},{6,7},{7,6},{8,9},{9,8},{10,11... | collective-permute-start | bytes 1130504 | tf_op jit(solution)/shard_map/ppermute | solution.py:42
  41.8 1.8 %collective-permute-start.18 = (bf16[64,2944]{1,0:T(8,128)(2,1)S(1)}, bf16[64,2944]{1,0:T(8,128)(2,1)S(1)}, u32[]{:S(2)}, u32[]{:S(2)}) collective-permute-start(bf16[64,2944]{1,0:T(8,128)(2,1)S(1)} %join.3), channel_id=1, source_target_pairs={{0,1},{1,0},{2,3},{3,2},{4,5},{5,4},{6,7},{7,6},{8,9},{9,8},{10,11... | collective-permute-start | bytes 1130504 | tf_op jit(solution)/shard_map/ppermute | solution.py:42
  50.4 1.9 %collective-permute-start.19 = (bf16[128,1920]{1,0:T(8,128)(2,1)S(1)}, bf16[128,1920]{1,0:T(8,128)(2,1)S(1)}, u32[]{:S(2)}, u32[]{:S(2)}) collective-permute-start(bf16[128,1920]{1,0:T(8,128)(2,1)S(1)} %get-tuple-element.65), channel_id=1, source_target_pairs={{0,1},{1,0},{2,3},{3,2},{4,5},{5,4},{6,7},{7,6},{8,9},{9,8},{10,11... | collective-permute-start | bytes 1474568 | tf_op jit(solution)/shard_map/ppermute | solution.py:42
  51.6 4.4 %collective-permute-start.24 = (bf16[128,1024]{1,0:T(8,128)(2,1)S(1)}, bf16[128,1024]{1,0:T(8,128)(2,1)S(1)}, u32[]{:S(2)}, u32[]{:S(2)}) collective-permute-start(bf16[128,1024]{1,0:T(8,128)(2,1)S(1)} %get-tuple-element.75), channel_id=1, source_target_pairs={{0,1},{1,0},{2,3},{3,2},{4,5},{5,4},{6,7},{7,6},{8,9},{9,8},{10,11... | collective-permute-start | bytes 786440 | tf_op jit(solution)/shard_map/ppermute | solution.py:42
  52.4 5.4 %collective-permute-start.20 = (bf16[32,1920]{1,0:T(8,128)(2,1)S(1)}, bf16[32,1920]{1,0:T(8,128)(2,1)S(1)}, u32[]{:S(2)}, u32[]{:S(2)}) collective-permute-start(bf16[32,1920]{1,0:T(8,128)(2,1)S(1)} %get-tuple-element.67), channel_id=1, source_target_pairs={{0,2},{1,3},{2,0},{3,1},{4,6},{5,7},{6,4},{7,5},{8,10},{9,11},{10,... | collective-permute-start | bytes 368648 | tf_op jit(solution)/shard_map/ppermute | solution.py:42
  53.5 6.2 %collective-permute-start.21 = (bf16[32,1920]{1,0:T(8,128)(2,1)S(1)}, bf16[32,1920]{1,0:T(8,128)(2,1)S(1)}, u32[]{:S(2)}, u32[]{:S(2)}) collective-permute-start(bf16[32,1920]{1,0:T(8,128)(2,1)S(1)} %get-tuple-element.68), channel_id=1, source_target_pairs={{0,4},{1,5},{2,6},{3,7},{4,0},{5,1},{6,2},{7,3},{8,12},{9,13},{10,... | collective-permute-start | bytes 368648 | tf_op jit(solution)/shard_map/ppermute | solution.py:42
  53.5 9.3 %collective-permute-start.22 = (bf16[32,1920]{1,0:T(8,128)(2,1)S(1)}, bf16[32,1920]{1,0:T(8,128)(2,1)S(1)}, u32[]{:S(2)}, u32[]{:S(2)}) collective-permute-start(bf16[32,1920]{1,0:T(8,128)(2,1)S(1)} %get-tuple-element.69), channel_id=1, source_target_pairs={{0,6},{1,7},{2,4},{3,5},{4,2},{5,3},{6,0},{7,1},{8,14},{9,15},{10,... | collective-permute-start | bytes 368648 | tf_op jit(solution)/shard_map/ppermute | solution.py:42
  56.0 8.4 %collective-permute-start.25 = (bf16[32,960]{1,0:T(8,128)(2,1)S(1)}, bf16[32,960]{1,0:T(8,128)(2,1)S(1)}, u32[]{:S(2)}, u32[]{:S(2)}) collective-permute-start(bf16[32,960]{1,0:T(8,128)(2,1)S(1)} %get-tuple-element.77), channel_id=1, source_target_pairs={{0,2},{1,3},{2,0},{3,1},{4,6},{5,7},{6,4},{7,5},{8,10},{9,11},{10,... | collective-permute-start | bytes 184328 | tf_op jit(solution)/shard_map/ppermute | solution.py:42
  57.1 7.3 %collective-permute-start.26 = (bf16[32,960]{1,0:T(8,128)(2,1)S(1)}, bf16[32,960]{1,0:T(8,128)(2,1)S(1)}, u32[]{:S(2)}, u32[]{:S(2)}) collective-permute-start(bf16[32,960]{1,0:T(8,128)(2,1)S(1)} %get-tuple-element.78), channel_id=1, source_target_pairs={{0,4},{1,5},{2,6},{3,7},{4,0},{5,1},{6,2},{7,3},{8,12},{9,13},{10,... | collective-permute-start | bytes 184328 | tf_op jit(solution)/shard_map/ppermute | solution.py:42
  57.8 6.6 %collective-permute-start.27 = (bf16[32,960]{1,0:T(8,128)(2,1)S(1)}, bf16[32,960]{1,0:T(8,128)(2,1)S(1)}, u32[]{:S(2)}, u32[]{:S(2)}) collective-permute-start(bf16[32,960]{1,0:T(8,128)(2,1)S(1)} %get-tuple-element.79), channel_id=1, source_target_pairs={{0,6},{1,7},{2,4},{3,5},{4,2},{5,3},{6,0},{7,1},{8,14},{9,15},{10,... | collective-permute-start | bytes 184328 | tf_op jit(solution)/shard_map/ppermute | solution.py:42
  62.9 6.5 %collective-permute-start.23 = (bf16[16,1920]{1,0:T(8,128)(2,1)S(1)}, bf16[16,1920]{1,0:T(8,128)(2,1)S(1)}, u32[]{:S(2)}, u32[]{:S(2)}) collective-permute-start(bf16[16,1920]{1,0:T(8,128)(2,1)S(1)} %get-tuple-element.71), channel_id=1, source_target_pairs={{0,8},{1,9},{2,10},{3,11},{4,12},{5,13},{6,14},{7,15},{8,0},{9,1},... | collective-permute-start | bytes 184328 | tf_op jit(solution)/shard_map/ppermute | solution.py:42
  64.5 4.9 %collective-permute-start.28 = (bf16[16,960]{1,0:T(8,128)(2,1)S(1)}, bf16[16,960]{1,0:T(8,128)(2,1)S(1)}, u32[]{:S(2)}, u32[]{:S(2)}) collective-permute-start(bf16[16,960]{1,0:T(8,128)(2,1)S(1)} %get-tuple-element.81), channel_id=1, source_target_pairs={{0,8},{1,9},{2,10},{3,11},{4,12},{5,13},{6,14},{7,15},{8,0},{9,1},... | collective-permute-start | bytes 92168 | tf_op jit(solution)/shard_map/ppermute | solution.py:42

commit v9 on v8

--- a/solution.py
+++ b/solution.py
@@ -356,7 +356,7 @@
         for m in range(batch):
             at = (m * len(masks) + p) * REQ_DEV
             rows[at : at + REQ_DEV, :] = wide[member, m, pl.ds(start, REQ_DEV), :]
-    half, width = outs[0].shape
+    half, width = outs[0].shape[0], weight.shape[0]
     found = lax.dot_general(
         rows[...].astype(jnp.bfloat16),
         weight[...],
@@ -367,26 +367,24 @@
         out[:, :width] = found[index * half : (index + 1) * half].astype(out.dtype)
 
 
-def project(me, held, weight, masks):
+def project(me, held, weight, masks, columns, dtype):
     batch, members, width = held[0].shape
     group = len(held)
-    half = len(masks) * REQ_DEV // 2
-    found = whole_call(
+    half = len(masks) * REQ_DEV
+    return whole_call(
         functools.partial(project_kernel, group, masks),
         "project",
-        [
-            jax.ShapeDtypeStruct((half, weight.shape[0]), jnp.float32),
-            jax.ShapeDtypeStruct((half, padded(weight.shape[0])), jnp.bfloat16),
-        ]
-        * batch,
+        [jax.ShapeDtypeStruct((half, columns), dtype)] * batch,
         [*held, weight],
         scratch=[
             pltpu.VMEM((group,) + held[0].shape, jnp.float32),
-            pltpu.VMEM((2 * batch * half, width), jnp.float32),
+            pltpu.VMEM((batch * half, width), jnp.float32),
         ],
         scalars=[me],
-    )
-    return [found[2 * m : 2 * m + 2] for m in range(batch)]
+        cost_estimate=pl.CostEstimate(
+            flops=600_000_000, bytes_accessed=2_000_000, transcendentals=0
+        ),
+    )
 
 
 def expert_kernel(batch, count, hidden, me_ref, *refs):
@@ -493,7 +491,10 @@
 
     held = attention(lengths, me % group_size, queries, new_kv, cache, group_size)
     held = [held[0]] + [from_mask(held[r], r) for r in range(1, group_size)]
-    halves = project(me, held, o_proj.T, masks)
+    width, middle = o_proj.shape[1], len(masks) // 2
+    sent = project(me, held, o_proj.T, masks[middle:], padded(width), jnp.bfloat16)
+    kept = project(me, held, o_proj.T, masks[:middle], width, jnp.float32)
+    halves = list(zip(kept, sent))
     attended, pieces = [], []
     for m in range(batch):
         total, received = scatter_sum(halves[m], stages[:-1])

time: 70.3 us -> 70.2 us (level)
    ppermute x29, waiting for transfers between devices: 19.8 us -> 19.1 us  [from_mask(): return lax.ppermute(value, 'req', pairs)]
    pallas_call x16 -> x17, Pallas kernels: 12 us -> 12.6 us  [whole_call(): pl.pallas_call(kernel, out_shape=outs, in_specs=[pl.BlockSpec(memory_spac...]
where the time goes in v9:
time: 70.2 us; the launch traced here: 70.1 us
  starting transfers between devices  32.8 us (47%)
  waiting for transfers between devices  19.1 us (27%)
  Pallas kernels  17.2 us (25%)
  between operations  0.94 us (1%)
    ppermute x29, starting transfers between devices, from_mask(): return lax.ppermute(value, 'req', pairs)  32.8 us
    ppermute x29, waiting for transfers between devices, from_mask(): return lax.ppermute(value, 'req', pairs)  19.1 us
    pallas_call x17, Pallas kernels, whole_call(): pl.pallas_call(kernel, out_shape=outs, in_specs=[pl.BlockSpec(memory_spac...  12.6 us
    pallas_call x1, Pallas kernels, attention(): pl.pallas_call(functools.partial(attention_kernel, group, block), out_sha...  4.64 us
  transfers between devices with their start and end apart: 29, of which 15 were waited for; matrix products, arithmetic and copies ran while one was open for 0% of the time, Pallas kernels for 6%

profile of v9, /device:TPU:0, one launch (start us, length us, event | category | flops | bytes accessed | tf_op | source)
XLA Modules:
  0.0 70.1 jit_solution(4939954189732192277)
XLA Ops:
  0.7 4.6 %attention.1 = (bf16[2,64,256]{2,1,0:T(8,128)(2,1)S(1)}, bf16[2,64,256]{2,1,0:T(8,128)(2,1)S(1)}) custom-call(s32[2,128]{1,0:T(2,128)} %lengths.1, s32[1]{0:T(128)S(6)} %select_n.7.place, bf16[2,64,512]{2,1,0:T(8,128)(2,1)} %far_q.1, bf16[2,64,128]{2,1,0:T(8,128)(2,1)} %far_kv.1, bf16[2,64,128,128]{3,2,1,0:T(8,128)(2,1)} %far.1), custom_call_target="tpu_custom_call" | custom-call | flops 10000000000 | bytes 30000000 | tf_op jit(solution)/shard_map/attention/pallas_call | solution.py:322
  5.3 0.5 collective-permute-start
  5.8 0.9 %collective-permute-done.refs_1_ = bf16[2,64,256]{2,1,0:T(8,128)(2,1)S(1)} collective-permute-done((bf16[2,64,256]{2,1,0:T(8,128)(2,1)S(1)}, bf16[2,64,256]{2,1,0:T(8,128)(2,1)S(1)}, u32[]{:S(2)}, u32[]{:S(2)}) %collective-permute-start) | collective-permute-done | bytes 65568 | tf_op jit(solution)/shard_map/ppermute | solution.py:42
  6.7 0.6 project.3
  7.4 0.4 collective-permute-start.6
  7.8 0.2 collective-permute-start.1
  8.0 0.6 project.2
  8.6 0.6 collective-permute-done.6.refs_1_
  9.2 0.1 add_split.7
  9.2 2.9 %collective-permute-start.7 = (bf16[16,2880]{1,0:T(8,128)(2,1)S(1)}, bf16[16,2880]{1,0:T(8,128)(2,1)S(1)}, u32[]{:S(2)}, u32[]{:S(2)}) collective-permute-start(bf16[16,2880]{1,0:T(8,128)(2,1)S(1)} %get-tuple-element.56), channel_id=1, source_target_pairs={{0,2},{1,3},{2,0},{3,1},{4,6},{5,7},{6,4},{7,5},{8,10},{9,11},{10,... | collective-permute-start | bytes 276488 | tf_op jit(solution)/shard_map/ppermute | solution.py:42
  12.2 1.6 %collective-permute-start.8 = (bf16[16,2880]{1,0:T(8,128)(2,1)S(1)}, bf16[16,2880]{1,0:T(8,128)(2,1)S(1)}, u32[]{:S(2)}, u32[]{:S(2)}) collective-permute-start(bf16[16,2880]{1,0:T(8,128)(2,1)S(1)} %get-tuple-element.57), channel_id=1, source_target_pairs={{0,4},{1,5},{2,6},{3,7},{4,0},{5,1},{6,2},{7,3},{8,12},{9,13},{10,... | collective-permute-start | bytes 276488 | tf_op jit(solution)/shard_map/ppermute | solution.py:42
  13.7 0.1 add_split.6
  13.8 2.0 %collective-permute-start.2 = (bf16[16,2880]{1,0:T(8,128)(2,1)S(1)}, bf16[16,2880]{1,0:T(8,128)(2,1)S(1)}, u32[]{:S(2)}, u32[]{:S(2)}) collective-permute-start(bf16[16,2880]{1,0:T(8,128)(2,1)S(1)} %get-tuple-element.47), channel_id=1, source_target_pairs={{0,2},{1,3},{2,0},{3,1},{4,6},{5,7},{6,4},{7,5},{8,10},{9,11},{10,... | collective-permute-start | bytes 276488 | tf_op jit(solution)/shard_map/ppermute | solution.py:42
  15.8 1.6 %collective-permute-start.3 = (bf16[16,2880]{1,0:T(8,128)(2,1)S(1)}, bf16[16,2880]{1,0:T(8,128)(2,1)S(1)}, u32[]{:S(2)}, u32[]{:S(2)}) collective-permute-start(bf16[16,2880]{1,0:T(8,128)(2,1)S(1)} %get-tuple-element.48), channel_id=1, source_target_pairs={{0,4},{1,5},{2,6},{3,7},{4,0},{5,1},{6,2},{7,3},{8,12},{9,13},{10,... | collective-permute-start | bytes 276488 | tf_op jit(solution)/shard_map/ppermute | solution.py:42
  17.4 0.6 collective-permute-start.4
  17.9 2.2 %collective-permute-done.9.refs_3_ = bf16[16,2880]{1,0:T(8,128)(2,1)S(1)} collective-permute-done((bf16[16,2880]{1,0:T(8,128)(2,1)S(1)}, bf16[16,2880]{1,0:T(8,128)(2,1)S(1)}, u32[]{:S(2)}, u32[]{:S(2)}) %collective-permute-start.9) | collective-permute-done | bytes 92192 | tf_op jit(solution)/shard_map/ppermute | solution.py:42
  20.2 0.0 slice-start.3
  20.2 0.0 slice-start.4
  20.2 0.0 slice-start.6
  20.2 0.0 slice-start.7
  20.2 0.7 %share.3 = (f32[16,2944]{1,0:T(8,128)S(1)}, bf16[16,2944]{1,0:T(8,128)(2,1)S(1)}) custom-call(s32[2,4,8]{2,1,0:T(4,128)S(1)} %bitcast.25, f32[16,2880]{1,0:T(8,128)S(1)} %get-tuple-element.55.refs_0_, bf16[16,2880]{1,0:T(8,128)(2,1)S(1)} %collective-permute-done.7.refs_1_, bf16[16,2880]{1,0:T(8,128)(2,1)S(1)} %collective-permute-done.8.refs_2_, ...), custom_call_target="tpu_custom_call" | custom-call | flops 60000002048 | bytes 180000000 | tf_op jit(solution)/shard_map/share/pallas_call | solution.py:50
  20.9 2.7 %collective-permute-start.10 = (bf16[16,2944]{1,0:T(8,128)(2,1)S(1)}, bf16[16,2944]{1,0:T(8,128)(2,1)S(1)}, u32[]{:S(2)}, u32[]{:S(2)}) collective-permute-start(bf16[16,2944]{1,0:T(8,128)(2,1)S(1)} %get-tuple-element.60.mine), channel_id=1, source_target_pairs={{0,8},{1,9},{2,10},{3,11},{4,12},{5,13},{6,14},{7,15},{8,0},{9,1},... | collective-permute-start | bytes 282632 | tf_op jit(solution)/shard_map/ppermute | solution.py:42
  23.6 0.0 copy-start
  23.6 0.0 slice-start.2
  23.6 0.0 slice-start.5
  23.6 0.0 slice-start.8
  23.7 0.7 %share.2 = (f32[16,2944]{1,0:T(8,128)S(1)}, bf16[16,2944]{1,0:T(8,128)(2,1)S(1)}) custom-call(s32[2,4,8]{2,1,0:T(4,128)S(1)} %bitcast.26, f32[16,2880]{1,0:T(8,128)S(1)} %get-tuple-element.46.refs_0_, bf16[16,2880]{1,0:T(8,128)(2,1)S(1)} %collective-permute-done.2.refs_1_, bf16[16,2880]{1,0:T(8,128)(2,1)S(1)} %collective-permute-done.3.refs_2_, ...), custom_call_target="tpu_custom_call" | custom-call | flops 60000002048 | bytes 180000000 | tf_op jit(solution)/shard_map/share/pallas_call | solution.py:50
  24.4 2.9 %collective-permute-start.5 = (bf16[16,2944]{1,0:T(8,128)(2,1)S(1)}, bf16[16,2944]{1,0:T(8,128)(2,1)S(1)}, u32[]{:S(2)}, u32[]{:S(2)}) collective-permute-start(bf16[16,2944]{1,0:T(8,128)(2,1)S(1)} %get-tuple-element.51.mine), channel_id=1, source_target_pairs={{0,8},{1,9},{2,10},{3,11},{4,12},{5,13},{6,14},{7,15},{8,0},{9,1},... | collective-permute-start | bytes 282632 | tf_op jit(solution)/shard_map/ppermute | solution.py:42
  27.3 2.7 %collective-permute-done.10.theirs = bf16[16,2944]{1,0:T(8,128)(2,1)S(1)} collective-permute-done((bf16[16,2944]{1,0:T(8,128)(2,1)S(1)}, bf16[16,2944]{1,0:T(8,128)(2,1)S(1)}, u32[]{:S(2)}, u32[]{:S(2)}) %collective-permute-start.10) | collective-permute-done | bytes 94240 | tf_op jit(solution)/shard_map/ppermute | solution.py:42
  30.0 0.5 norm.3
  30.5 0.6 collective-permute-start.17
  31.1 3.0 %collective-permute-start.15 = (bf16[16,2944]{1,0:T(8,128)(2,1)S(1)}, bf16[16,2944]{1,0:T(8,128)(2,1)S(1)}, u32[]{:S(2)}, u32[]{:S(2)}) collective-permute-start(bf16[16,2944]{1,0:T(8,128)(2,1)S(1)} %get-tuple-element.63.refs_0_.refs_5_), channel_id=1, source_target_pairs={{0,2},{1,3},{2,0},{3,1},{4,6},{5,7},{6,4},{7,5},{8,10},{9,11},{10,... | collective-permute-start | bytes 282632 | tf_op jit(solution)/shard_map/ppermute | solution.py:42
  34.1 0.5 norm.2
  34.6 0.6 collective-permute-start.13
  35.2 1.0 %collective-permute-start.12 = (bf16[16,2944]{1,0:T(8,128)(2,1)S(1)}, bf16[16,2944]{1,0:T(8,128)(2,1)S(1)}, u32[]{:S(2)}, u32[]{:S(2)}) collective-permute-start(bf16[16,2944]{1,0:T(8,128)(2,1)S(1)} %get-tuple-element.62.refs_0_), channel_id=1, source_target_pairs={{0,4},{1,5},{2,6},{3,7},{4,0},{5,1},{6,2},{7,3},{8,12},{9,13},{10,... | collective-permute-start | bytes 282632 | tf_op jit(solution)/shard_map/ppermute | solution.py:42
  36.2 1.0 %collective-permute-done.17.refs_3_.refs_8_ = bf16[16,2944]{1,0:T(8,128)(2,1)S(1)} collective-permute-done((bf16[16,2944]{1,0:T(8,128)(2,1)S(1)}, bf16[16,2944]{1,0:T(8,128)(2,1)S(1)}, u32[]{:S(2)}, u32[]{:S(2)}) %collective-permute-start.17) | collective-permute-done | bytes 94240 | tf_op jit(solution)/shard_map/ppermute | solution.py:42
  37.1 1.1 %collective-permute-start.11 = (bf16[16,2944]{1,0:T(8,128)(2,1)S(1)}, bf16[16,2944]{1,0:T(8,128)(2,1)S(1)}, u32[]{:S(2)}, u32[]{:S(2)}) collective-permute-start(bf16[16,2944]{1,0:T(8,128)(2,1)S(1)} %get-tuple-element.62.refs_0_), channel_id=1, source_target_pairs={{0,2},{1,3},{2,0},{3,1},{4,6},{5,7},{6,4},{7,5},{8,10},{9,11},{10,... | collective-permute-start | bytes 282632 | tf_op jit(solution)/shard_map/ppermute | solution.py:42
  38.2 0.8 %collective-permute-done.15.refs_1_.refs_6_ = bf16[16,2944]{1,0:T(8,128)(2,1)S(1)} collective-permute-done((bf16[16,2944]{1,0:T(8,128)(2,1)S(1)}, bf16[16,2944]{1,0:T(8,128)(2,1)S(1)}, u32[]{:S(2)}, u32[]{:S(2)}) %collective-permute-start.15) | collective-permute-done | bytes 94240 | tf_op jit(solution)/shard_map/ppermute | solution.py:42
  39.1 0.1 collective-permute-start.18
  39.2 1.0 %collective-permute-done.13.refs_3_ = bf16[16,2944]{1,0:T(8,128)(2,1)S(1)} collective-permute-done((bf16[16,2944]{1,0:T(8,128)(2,1)S(1)}, bf16[16,2944]{1,0:T(8,128)(2,1)S(1)}, u32[]{:S(2)}, u32[]{:S(2)}) %collective-permute-start.13) | collective-permute-done | bytes 94240 | tf_op jit(solution)/shard_map/ppermute | solution.py:42
  40.2 1.5 %collective-permute-done.11.refs_1_ = bf16[16,2944]{1,0:T(8,128)(2,1)S(1)} collective-permute-done((bf16[16,2944]{1,0:T(8,128)(2,1)S(1)}, bf16[16,2944]{1,0:T(8,128)(2,1)S(1)}, u32[]{:S(2)}, u32[]{:S(2)}) %collective-permute-start.11) | collective-permute-done | bytes 94240 | tf_op jit(solution)/shard_map/ppermute | solution.py:42
  41.7 0.1 collective-permute-start.14
  41.8 1.7 %collective-permute-done.14.refs_4_ = bf16[64,2944]{1,0:T(8,128)(2,1)S(1)} collective-permute-done((bf16[64,2944]{1,0:T(8,128)(2,1)S(1)}, bf16[64,2944]{1,0:T(8,128)(2,1)S(1)}, u32[]{:S(2)}, u32[]{:S(2)}) %collective-permute-start.14) | collective-permute-done | bytes 376864 | tf_op jit(solution)/shard_map/ppermute | solution.py:42
  43.6 6.8 %experts.1 = (f32[128,1920]{1,0:T(8,128)S(1)}, bf16[128,1920]{1,0:T(8,128)(2,1)S(1)}, bf16[256,1440]{1,0:T(8,128)(2,1)S(1)}, f32[1,256,128]{2,1,0:T(8,128)S(1)}) custom-call(s32[1]{0:T(128)} %bitcast.1.me_ref, bf16[16,2944]{1,0:T(8,128)(2,1)S(1)} %get-tuple-element.62.refs_0_, bf16[16,2944]{1,0:T(8,128)(2,1)S(1)} %collective-permute-done.11.refs_1_, ...), custom_call_target="tpu_custom_call" | custom-call | tf_op jit(solution)/shard_map/experts/pallas_call | solution.py:50
  50.4 0.2 collective-permute-start.19
  50.6 1.0 %down.1 = (f32[128,960]{1,0:T(8,128)S(1)}, bf16[128,1024]{1,0:T(8,128)(2,1)S(1)}) custom-call(bf16[256,1440]{1,0:T(8,128)(2,1)S(1)} %get-tuple-element.72.active, f32[1,256,128]{2,1,0:T(8,128)S(1)} %get-tuple-element.73.weights, bf16[1440,2880]{1,0:T(8,128)(2,1)S(1)} %bitcast.14), custom_call_target="tpu_custom_call" | custom-call | tf_op jit(solution)/shard_map/down/pallas_call | solution.py:50
  51.5 0.5 collective-permute-start.24
  52.0 0.3 collective-permute-done.19.refs_1_
  52.3 0.1 add_split.8
  52.4 1.1 %collective-permute-start.20 = (bf16[32,1920]{1,0:T(8,128)(2,1)S(1)}, bf16[32,1920]{1,0:T(8,128)(2,1)S(1)}, u32[]{:S(2)}, u32[]{:S(2)}) collective-permute-start(bf16[32,1920]{1,0:T(8,128)(2,1)S(1)} %get-tuple-element.67), channel_id=1, source_target_pairs={{0,2},{1,3},{2,0},{3,1},{4,6},{5,7},{6,4},{7,5},{8,10},{9,11},{10,... | collective-permute-start | bytes 368648 | tf_op jit(solution)/shard_map/ppermute | solution.py:42
  53.5 0.0 collective-permute-start.21
  53.5 2.4 %collective-permute-start.22 = (bf16[32,1920]{1,0:T(8,128)(2,1)S(1)}, bf16[32,1920]{1,0:T(8,128)(2,1)S(1)}, u32[]{:S(2)}, u32[]{:S(2)}) collective-permute-start(bf16[32,1920]{1,0:T(8,128)(2,1)S(1)} %get-tuple-element.69), channel_id=1, source_target_pairs={{0,6},{1,7},{2,4},{3,5},{4,2},{5,3},{6,0},{7,1},{8,14},{9,15},{10,... | collective-permute-start | bytes 368648 | tf_op jit(solution)/shard_map/ppermute | solution.py:42
  56.0 1.1 %collective-permute-start.25 = (bf16[32,960]{1,0:T(8,128)(2,1)S(1)}, bf16[32,960]{1,0:T(8,128)(2,1)S(1)}, u32[]{:S(2)}, u32[]{:S(2)}) collective-permute-start(bf16[32,960]{1,0:T(8,128)(2,1)S(1)} %get-tuple-element.77), channel_id=1, source_target_pairs={{0,2},{1,3},{2,0},{3,1},{4,6},{5,7},{6,4},{7,5},{8,10},{9,11},{10,... | collective-permute-start | bytes 184328 | tf_op jit(solution)/shard_map/ppermute | solution.py:42
  57.1 0.0 collective-permute-start.26
  57.1 0.7 collective-permute-done.20.refs_1_
  57.8 1.7 %collective-permute-start.27 = (bf16[32,960]{1,0:T(8,128)(2,1)S(1)}, bf16[32,960]{1,0:T(8,128)(2,1)S(1)}, u32[]{:S(2)}, u32[]{:S(2)}) collective-permute-start(bf16[32,960]{1,0:T(8,128)(2,1)S(1)} %get-tuple-element.79), channel_id=1, source_target_pairs={{0,6},{1,7},{2,4},{3,5},{4,2},{5,3},{6,0},{7,1},{8,14},{9,15},{10,... | collective-permute-start | bytes 184328 | tf_op jit(solution)/shard_map/ppermute | solution.py:42
  59.6 0.2 collective-permute-done.21.refs_2_
  59.7 3.0 %collective-permute-done.22.refs_3_ = bf16[32,1920]{1,0:T(8,128)(2,1)S(1)} collective-permute-done((bf16[32,1920]{1,0:T(8,128)(2,1)S(1)}, bf16[32,1920]{1,0:T(8,128)(2,1)S(1)}, u32[]{:S(2)}, u32[]{:S(2)}) %collective-permute-start.22) | collective-permute-done | bytes 122912 | tf_op jit(solution)/shard_map/ppermute | solution.py:42
  62.8 0.1 add_split.9
  62.8 1.6 %collective-permute-start.23 = (bf16[16,1920]{1,0:T(8,128)(2,1)S(1)}, bf16[16,1920]{1,0:T(8,128)(2,1)S(1)}, u32[]{:S(2)}, u32[]{:S(2)}) collective-permute-start(bf16[16,1920]{1,0:T(8,128)(2,1)S(1)} %get-tuple-element.71), channel_id=1, source_target_pairs={{0,8},{1,9},{2,10},{3,11},{4,12},{5,13},{6,14},{7,15},{8,0},{9,1},... | collective-permute-start | bytes 184328 | tf_op jit(solution)/shard_map/ppermute | solution.py:42
  64.4 0.1 collective-permute-done.27.refs_3_
  64.5 2.5 %collective-permute-start.28 = (bf16[16,960]{1,0:T(8,128)(2,1)S(1)}, bf16[16,960]{1,0:T(8,128)(2,1)S(1)}, u32[]{:S(2)}, u32[]{:S(2)}) collective-permute-start(bf16[16,960]{1,0:T(8,128)(2,1)S(1)} %get-tuple-element.81), channel_id=1, source_target_pairs={{0,8},{1,9},{2,10},{3,11},{4,12},{5,13},{6,14},{7,15},{8,0},{9,1},... | collective-permute-start | bytes 92168 | tf_op jit(solution)/shard_map/ppermute | solution.py:42
  67.0 2.3 %collective-permute-done.28.refs_5_ = bf16[16,960]{1,0:T(8,128)(2,1)S(1)} collective-permute-done((bf16[16,960]{1,0:T(8,128)(2,1)S(1)}, bf16[16,960]{1,0:T(8,128)(2,1)S(1)}, u32[]{:S(2)}, u32[]{:S(2)}) %collective-permute-start.28) | collective-permute-done | bytes 30752 | tf_op jit(solution)/shard_map/ppermute | solution.py:42
  69.4 0.7 finish.1
  (41 shorter events, 0.2 us)
Async XLA Ops:
  0.6 6.1 %copy-start.1 = (bf16[256,2880]{0,1:T(8,128)(2,1)S(1)}, bf16[256,2880]{0,1:T(8,128)(2,1)}, u32[]{:S(2)}) copy-start(bf16[256,2880]{0,1:T(8,128)(2,1)} %param.16) | copy-start | bytes 4423684
  0.7 19.5 %copy-start.2 = (bf16[2,8,2880]{2,1,0:T(8,128)(2,1)S(1)}, bf16[2,8,2880]{2,1,0:T(8,128)(2,1)}, u32[]{:S(2)}) copy-start(bf16[2,8,2880]{2,1,0:T(8,128)(2,1)} %refs_4_.3) | copy-start | bytes 276484
  0.7 19.5 %copy-start.3 = (s32[2,8,4]{1,2,0:T(4,128)S(1)}, s32[2,8,4]{1,2,0:T(4,128)}, u32[]{:S(2)}) copy-start(s32[2,8,4]{1,2,0:T(4,128)} %param.21) | copy-start | bytes 772
  5.3 1.4 %collective-permute-start = (bf16[2,64,256]{2,1,0:T(8,128)(2,1)S(1)}, bf16[2,64,256]{2,1,0:T(8,128)(2,1)S(1)}, u32[]{:S(2)}, u32[]{:S(2)}) collective-permute-start(bf16[2,64,256]{2,1,0:T(8,128)(2,1)S(1)} %get-tuple-element.43), channel_id=1, source_target_pairs={{0,1},{1,0},{2,3},{3,2},{4,5},{5,4},{6,7},{7,6},{8,9},{9,8},{10,11... | collective-permute-start | bytes 196616 | tf_op jit(solution)/shard_map/ppermute | solution.py:42
  7.4 1.8 %collective-permute-start.6 = (bf16[64,2944]{1,0:T(8,128)(2,1)S(1)}, bf16[64,2944]{1,0:T(8,128)(2,1)S(1)}, u32[]{:S(2)}, u32[]{:S(2)}) collective-permute-start(bf16[64,2944]{1,0:T(8,128)(2,1)S(1)} %get-tuple-element.54), channel_id=1, source_target_pairs={{0,1},{1,0},{2,3},{3,2},{4,5},{5,4},{6,7},{7,6},{8,9},{9,8},{10,11... | collective-permute-start | bytes 1130504 | tf_op jit(solution)/shard_map/ppermute | solution.py:42
  7.8 5.9 %collective-permute-start.1 = (bf16[64,2944]{1,0:T(8,128)(2,1)S(1)}, bf16[64,2944]{1,0:T(8,128)(2,1)S(1)}, u32[]{:S(2)}, u32[]{:S(2)}) collective-permute-start(bf16[64,2944]{1,0:T(8,128)(2,1)S(1)} %get-tuple-element.45), channel_id=1, source_target_pairs={{0,1},{1,0},{2,3},{3,2},{4,5},{5,4},{6,7},{7,6},{8,9},{9,8},{10,11... | collective-permute-start | bytes 1130504 | tf_op jit(solution)/shard_map/ppermute | solution.py:42
  9.2 8.1 %collective-permute-start.7 = (bf16[16,2880]{1,0:T(8,128)(2,1)S(1)}, bf16[16,2880]{1,0:T(8,128)(2,1)S(1)}, u32[]{:S(2)}, u32[]{:S(2)}) collective-permute-start(bf16[16,2880]{1,0:T(8,128)(2,1)S(1)} %get-tuple-element.56), channel_id=1, source_target_pairs={{0,2},{1,3},{2,0},{3,1},{4,6},{5,7},{6,4},{7,5},{8,10},{9,11},{10,... | collective-permute-start | bytes 276488 | tf_op jit(solution)/shard_map/ppermute | solution.py:42
  12.2 5.8 %collective-permute-start.8 = (bf16[16,2880]{1,0:T(8,128)(2,1)S(1)}, bf16[16,2880]{1,0:T(8,128)(2,1)S(1)}, u32[]{:S(2)}, u32[]{:S(2)}) collective-permute-start(bf16[16,2880]{1,0:T(8,128)(2,1)S(1)} %get-tuple-element.57), channel_id=1, source_target_pairs={{0,4},{1,5},{2,6},{3,7},{4,0},{5,1},{6,2},{7,3},{8,12},{9,13},{10,... | collective-permute-start | bytes 276488 | tf_op jit(solution)/shard_map/ppermute | solution.py:42
  13.7 6.4 %collective-permute-start.9 = (bf16[16,2880]{1,0:T(8,128)(2,1)S(1)}, bf16[16,2880]{1,0:T(8,128)(2,1)S(1)}, u32[]{:S(2)}, u32[]{:S(2)}) collective-permute-start(bf16[16,2880]{1,0:T(8,128)(2,1)S(1)} %get-tuple-element.58), channel_id=1, source_target_pairs={{0,6},{1,7},{2,4},{3,5},{4,2},{5,3},{6,0},{7,1},{8,14},{9,15},{10,... | collective-permute-start | bytes 276488 | tf_op jit(solution)/shard_map/ppermute | solution.py:42
  13.8 9.8 %collective-permute-start.2 = (bf16[16,2880]{1,0:T(8,128)(2,1)S(1)}, bf16[16,2880]{1,0:T(8,128)(2,1)S(1)}, u32[]{:S(2)}, u32[]{:S(2)}) collective-permute-start(bf16[16,2880]{1,0:T(8,128)(2,1)S(1)} %get-tuple-element.47), channel_id=1, source_target_pairs={{0,2},{1,3},{2,0},{3,1},{4,6},{5,7},{6,4},{7,5},{8,10},{9,11},{10,... | collective-permute-start | bytes 276488 | tf_op jit(solution)/shard_map/ppermute | solution.py:42
  15.8 7.8 %collective-permute-start.3 = (bf16[16,2880]{1,0:T(8,128)(2,1)S(1)}, bf16[16,2880]{1,0:T(8,128)(2,1)S(1)}, u32[]{:S(2)}, u32[]{:S(2)}) collective-permute-start(bf16[16,2880]{1,0:T(8,128)(2,1)S(1)} %get-tuple-element.48), channel_id=1, source_target_pairs={{0,4},{1,5},{2,6},{3,7},{4,0},{5,1},{6,2},{7,3},{8,12},{9,13},{10,... | collective-permute-start | bytes 276488 | tf_op jit(solution)/shard_map/ppermute | solution.py:42
  17.4 6.2 %collective-permute-start.4 = (bf16[16,2880]{1,0:T(8,128)(2,1)S(1)}, bf16[16,2880]{1,0:T(8,128)(2,1)S(1)}, u32[]{:S(2)}, u32[]{:S(2)}) collective-permute-start(bf16[16,2880]{1,0:T(8,128)(2,1)S(1)} %get-tuple-element.49), channel_id=1, source_target_pairs={{0,6},{1,7},{2,4},{3,5},{4,2},{5,3},{6,0},{7,1},{8,14},{9,15},{10,... | collective-permute-start | bytes 276488 | tf_op jit(solution)/shard_map/ppermute | solution.py:42
  20.2 23.3 %slice-start = ((s8[8478720]{0:T(1024)(128)(4,1)}), s8[4194304]{0:T(1024)(128)(4,1)S(1)}, s32[]{:S(2)}) async-start(s8[8478720]{0:T(1024)(128)(4,1)} %bitcast.11), calls=%async_computation | async-start | bytes 8388608
  20.2 23.4 %slice-start.1 = ((s8[8478720]{0:T(1024)(128)(4,1)}), s8[4194304]{0:T(1024)(128)(4,1)S(1)}, s32[]{:S(2)}) async-start(s8[8478720]{0:T(1024)(128)(4,1)} %bitcast.11), calls=%async_computation.1 | async-start | bytes 8388608
  20.2 23.3 %slice-start.3 = ((s8[8478720]{0:T(1024)(128)(4,1)}), s8[4194304]{0:T(1024)(128)(4,1)S(1)}, s32[]{:S(2)}) async-start(s8[8478720]{0:T(1024)(128)(4,1)} %bitcast.15), calls=%async_computation.3 | async-start | bytes 8388608
  20.2 23.3 %slice-start.4 = ((s8[8478720]{0:T(1024)(128)(4,1)}), s8[4194304]{0:T(1024)(128)(4,1)S(1)}, s32[]{:S(2)}) async-start(s8[8478720]{0:T(1024)(128)(4,1)} %bitcast.15), calls=%async_computation.4 | async-start | bytes 8388608
  20.2 23.3 %slice-start.6 = ((s8[8478720]{0:T(1024)(128)(4,1)}), s8[4194304]{0:T(1024)(128)(4,1)S(1)}, s32[]{:S(2)}) async-start(s8[8478720]{0:T(1024)(128)(4,1)} %bitcast.18), calls=%async_computation.6 | async-start | bytes 8388608
  20.2 23.3 %slice-start.7 = ((s8[8478720]{0:T(1024)(128)(4,1)}), s8[4194304]{0:T(1024)(128)(4,1)S(1)}, s32[]{:S(2)}) async-start(s8[8478720]{0:T(1024)(128)(4,1)} %bitcast.18), calls=%async_computation.7 | async-start | bytes 8388608
  20.9 9.1 %collective-permute-start.10 = (bf16[16,2944]{1,0:T(8,128)(2,1)S(1)}, bf16[16,2944]{1,0:T(8,128)(2,1)S(1)}, u32[]{:S(2)}, u32[]{:S(2)}) collective-permute-start(bf16[16,2944]{1,0:T(8,128)(2,1)S(1)} %get-tuple-element.60.mine), channel_id=1, source_target_pairs={{0,8},{1,9},{2,10},{3,11},{4,12},{5,13},{6,14},{7,15},{8,0},{9,1},... | collective-permute-start | bytes 282632 | tf_op jit(solution)/shard_map/ppermute | solution.py:42
  23.6 6.4 %copy-start = (bf16[2880,16]{0,1:T(8,128)(2,1)S(1)}, bf16[2880,16]{0,1:T(8,128)(2,1)}, u32[]{:S(2)}) copy-start(bf16[2880,16]{0,1:T(8,128)(2,1)} %param.17) | copy-start | bytes 276484
  23.6 19.9 %slice-start.2 = ((s8[8478720]{0:T(1024)(128)(4,1)}), s8[90112]{0:T(1024)(128)(4,1)S(1)}, s32[]{:S(2)}) async-start(s8[8478720]{0:T(1024)(128)(4,1)} %bitcast.11), calls=%async_computation.2 | async-start | bytes 180224
  23.6 19.9 %slice-start.5 = ((s8[8478720]{0:T(1024)(128)(4,1)}), s8[90112]{0:T(1024)(128)(4,1)S(1)}, s32[]{:S(2)}) async-start(s8[8478720]{0:T(1024)(128)(4,1)} %bitcast.15), calls=%async_computation.5 | async-start | bytes 180224
  23.6 19.9 %slice-start.8 = ((s8[8478720]{0:T(1024)(128)(4,1)}), s8[90112]{0:T(1024)(128)(4,1)S(1)}, s32[]{:S(2)}) async-start(s8[8478720]{0:T(1024)(128)(4,1)} %bitcast.18), calls=%async_computation.8 | async-start | bytes 180224
  24.4 9.8 %collective-permute-start.5 = (bf16[16,2944]{1,0:T(8,128)(2,1)S(1)}, bf16[16,2944]{1,0:T(8,128)(2,1)S(1)}, u32[]{:S(2)}, u32[]{:S(2)}) collective-permute-start(bf16[16,2944]{1,0:T(8,128)(2,1)S(1)} %get-tuple-element.51.mine), channel_id=1, source_target_pairs={{0,8},{1,9},{2,10},{3,11},{4,12},{5,13},{6,14},{7,15},{8,0},{9,1},... | collective-permute-start | bytes 282632 | tf_op jit(solution)/shard_map/ppermute | solution.py:42
  30.5 6.6 %collective-permute-start.17 = (bf16[16,2944]{1,0:T(8,128)(2,1)S(1)}, bf16[16,2944]{1,0:T(8,128)(2,1)S(1)}, u32[]{:S(2)}, u32[]{:S(2)}) collective-permute-start(bf16[16,2944]{1,0:T(8,128)(2,1)S(1)} %get-tuple-element.63.refs_0_.refs_5_), channel_id=1, source_target_pairs={{0,6},{1,7},{2,4},{3,5},{4,2},{5,3},{6,0},{7,1},{8,14},{9,15},{10,... | collective-permute-start | bytes 282632 | tf_op jit(solution)/shard_map/ppermute | solution.py:42
  31.1 7.1 %collective-permute-start.16 = (bf16[16,2944]{1,0:T(8,128)(2,1)S(1)}, bf16[16,2944]{1,0:T(8,128)(2,1)S(1)}, u32[]{:S(2)}, u32[]{:S(2)}) collective-permute-start(bf16[16,2944]{1,0:T(8,128)(2,1)S(1)} %get-tuple-element.63.refs_0_.refs_5_), channel_id=1, source_target_pairs={{0,4},{1,5},{2,6},{3,7},{4,0},{5,1},{6,2},{7,3},{8,12},{9,13},{10,... | collective-permute-start | bytes 282632 | tf_op jit(solution)/shard_map/ppermute | solution.py:42
  31.1 7.9 %collective-permute-start.15 = (bf16[16,2944]{1,0:T(8,128)(2,1)S(1)}, bf16[16,2944]{1,0:T(8,128)(2,1)S(1)}, u32[]{:S(2)}, u32[]{:S(2)}) collective-permute-start(bf16[16,2944]{1,0:T(8,128)(2,1)S(1)} %get-tuple-element.63.refs_0_.refs_5_), channel_id=1, source_target_pairs={{0,2},{1,3},{2,0},{3,1},{4,6},{5,7},{6,4},{7,5},{8,10},{9,11},{10,... | collective-permute-start | bytes 282632 | tf_op jit(solution)/shard_map/ppermute | solution.py:42
  34.6 5.5 %collective-permute-start.13 = (bf16[16,2944]{1,0:T(8,128)(2,1)S(1)}, bf16[16,2944]{1,0:T(8,128)(2,1)S(1)}, u32[]{:S(2)}, u32[]{:S(2)}) collective-permute-start(bf16[16,2944]{1,0:T(8,128)(2,1)S(1)} %get-tuple-element.62.refs_0_), channel_id=1, source_target_pairs={{0,6},{1,7},{2,4},{3,5},{4,2},{5,3},{6,0},{7,1},{8,14},{9,15},{10,... | collective-permute-start | bytes 282632 | tf_op jit(solution)/shard_map/ppermute | solution.py:42
  35.2 5.0 %collective-permute-start.12 = (bf16[16,2944]{1,0:T(8,128)(2,1)S(1)}, bf16[16,2944]{1,0:T(8,128)(2,1)S(1)}, u32[]{:S(2)}, u32[]{:S(2)}) collective-permute-start(bf16[16,2944]{1,0:T(8,128)(2,1)S(1)} %get-tuple-element.62.refs_0_), channel_id=1, source_target_pairs={{0,4},{1,5},{2,6},{3,7},{4,0},{5,1},{6,2},{7,3},{8,12},{9,13},{10,... | collective-permute-start | bytes 282632 | tf_op jit(solution)/shard_map/ppermute | solution.py:42
  37.1 4.6 %collective-permute-start.11 = (bf16[16,2944]{1,0:T(8,128)(2,1)S(1)}, bf16[16,2944]{1,0:T(8,128)(2,1)S(1)}, u32[]{:S(2)}, u32[]{:S(2)}) collective-permute-start(bf16[16,2944]{1,0:T(8,128)(2,1)S(1)} %get-tuple-element.62.refs_0_), channel_id=1, source_target_pairs={{0,2},{1,3},{2,0},{3,1},{4,6},{5,7},{6,4},{7,5},{8,10},{9,11},{10,... | collective-permute-start | bytes 282632 | tf_op jit(solution)/shard_map/ppermute | solution.py:42
  39.1 2.7 %collective-permute-start.18 = (bf16[64,2944]{1,0:T(8,128)(2,1)S(1)}, bf16[64,2944]{1,0:T(8,128)(2,1)S(1)}, u32[]{:S(2)}, u32[]{:S(2)}) collective-permute-start(bf16[64,2944]{1,0:T(8,128)(2,1)S(1)} %join.3), channel_id=1, source_target_pairs={{0,1},{1,0},{2,3},{3,2},{4,5},{5,4},{6,7},{7,6},{8,9},{9,8},{10,11... | collective-permute-start | bytes 1130504 | tf_op jit(solution)/shard_map/ppermute | solution.py:42
  41.7 1.8 %collective-permute-start.14 = (bf16[64,2944]{1,0:T(8,128)(2,1)S(1)}, bf16[64,2944]{1,0:T(8,128)(2,1)S(1)}, u32[]{:S(2)}, u32[]{:S(2)}) collective-permute-start(bf16[64,2944]{1,0:T(8,128)(2,1)S(1)} %join.2), channel_id=1, source_target_pairs={{0,1},{1,0},{2,3},{3,2},{4,5},{5,4},{6,7},{7,6},{8,9},{9,8},{10,11... | collective-permute-start | bytes 1130504 | tf_op jit(solution)/shard_map/ppermute | solution.py:42
  50.4 1.9 %collective-permute-start.19 = (bf16[128,1920]{1,0:T(8,128)(2,1)S(1)}, bf16[128,1920]{1,0:T(8,128)(2,1)S(1)}, u32[]{:S(2)}, u32[]{:S(2)}) collective-permute-start(bf16[128,1920]{1,0:T(8,128)(2,1)S(1)} %get-tuple-element.65), channel_id=1, source_target_pairs={{0,1},{1,0},{2,3},{3,2},{4,5},{5,4},{6,7},{7,6},{8,9},{9,8},{10,11... | collective-permute-start | bytes 1474568 | tf_op jit(solution)/shard_map/ppermute | solution.py:42
  51.5 4.4 %collective-permute-start.24 = (bf16[128,1024]{1,0:T(8,128)(2,1)S(1)}, bf16[128,1024]{1,0:T(8,128)(2,1)S(1)}, u32[]{:S(2)}, u32[]{:S(2)}) collective-permute-start(bf16[128,1024]{1,0:T(8,128)(2,1)S(1)} %get-tuple-element.75), channel_id=1, source_target_pairs={{0,1},{1,0},{2,3},{3,2},{4,5},{5,4},{6,7},{7,6},{8,9},{9,8},{10,11... | collective-permute-start | bytes 786440 | tf_op jit(solution)/shard_map/ppermute | solution.py:42
  52.4 5.4 %collective-permute-start.20 = (bf16[32,1920]{1,0:T(8,128)(2,1)S(1)}, bf16[32,1920]{1,0:T(8,128)(2,1)S(1)}, u32[]{:S(2)}, u32[]{:S(2)}) collective-permute-start(bf16[32,1920]{1,0:T(8,128)(2,1)S(1)} %get-tuple-element.67), channel_id=1, source_target_pairs={{0,2},{1,3},{2,0},{3,1},{4,6},{5,7},{6,4},{7,5},{8,10},{9,11},{10,... | collective-permute-start | bytes 368648 | tf_op jit(solution)/shard_map/ppermute | solution.py:42
  53.5 6.2 %collective-permute-start.21 = (bf16[32,1920]{1,0:T(8,128)(2,1)S(1)}, bf16[32,1920]{1,0:T(8,128)(2,1)S(1)}, u32[]{:S(2)}, u32[]{:S(2)}) collective-permute-start(bf16[32,1920]{1,0:T(8,128)(2,1)S(1)} %get-tuple-element.68), channel_id=1, source_target_pairs={{0,4},{1,5},{2,6},{3,7},{4,0},{5,1},{6,2},{7,3},{8,12},{9,13},{10,... | collective-permute-start | bytes 368648 | tf_op jit(solution)/shard_map/ppermute | solution.py:42
  53.5 9.2 %collective-permute-start.22 = (bf16[32,1920]{1,0:T(8,128)(2,1)S(1)}, bf16[32,1920]{1,0:T(8,128)(2,1)S(1)}, u32[]{:S(2)}, u32[]{:S(2)}) collective-permute-start(bf16[32,1920]{1,0:T(8,128)(2,1)S(1)} %get-tuple-element.69), channel_id=1, source_target_pairs={{0,6},{1,7},{2,4},{3,5},{4,2},{5,3},{6,0},{7,1},{8,14},{9,15},{10,... | collective-permute-start | bytes 368648 | tf_op jit(solution)/shard_map/ppermute | solution.py:42
  56.0 8.4 %collective-permute-start.25 = (bf16[32,960]{1,0:T(8,128)(2,1)S(1)}, bf16[32,960]{1,0:T(8,128)(2,1)S(1)}, u32[]{:S(2)}, u32[]{:S(2)}) collective-permute-start(bf16[32,960]{1,0:T(8,128)(2,1)S(1)} %get-tuple-element.77), channel_id=1, source_target_pairs={{0,2},{1,3},{2,0},{3,1},{4,6},{5,7},{6,4},{7,5},{8,10},{9,11},{10,... | collective-permute-start | bytes 184328 | tf_op jit(solution)/shard_map/ppermute | solution.py:42
  57.1 7.3 %collective-permute-start.26 = (bf16[32,960]{1,0:T(8,128)(2,1)S(1)}, bf16[32,960]{1,0:T(8,128)(2,1)S(1)}, u32[]{:S(2)}, u32[]{:S(2)}) collective-permute-start(bf16[32,960]{1,0:T(8,128)(2,1)S(1)} %get-tuple-element.78), channel_id=1, source_target_pairs={{0,4},{1,5},{2,6},{3,7},{4,0},{5,1},{6,2},{7,3},{8,12},{9,13},{10,... | collective-permute-start | bytes 184328 | tf_op jit(solution)/shard_map/ppermute | solution.py:42
  57.8 6.6 %collective-permute-start.27 = (bf16[32,960]{1,0:T(8,128)(2,1)S(1)}, bf16[32,960]{1,0:T(8,128)(2,1)S(1)}, u32[]{:S(2)}, u32[]{:S(2)}) collective-permute-start(bf16[32,960]{1,0:T(8,128)(2,1)S(1)} %get-tuple-element.79), channel_id=1, source_target_pairs={{0,6},{1,7},{2,4},{3,5},{4,2},{5,3},{6,0},{7,1},{8,14},{9,15},{10,... | collective-permute-start | bytes 184328 | tf_op jit(solution)/shard_map/ppermute | solution.py:42
  62.8 6.5 %collective-permute-start.23 = (bf16[16,1920]{1,0:T(8,128)(2,1)S(1)}, bf16[16,1920]{1,0:T(8,128)(2,1)S(1)}, u32[]{:S(2)}, u32[]{:S(2)}) collective-permute-start(bf16[16,1920]{1,0:T(8,128)(2,1)S(1)} %get-tuple-element.71), channel_id=1, source_target_pairs={{0,8},{1,9},{2,10},{3,11},{4,12},{5,13},{6,14},{7,15},{8,0},{9,1},... | collective-permute-start | bytes 184328 | tf_op jit(solution)/shard_map/ppermute | solution.py:42
  64.5 4.9 %collective-permute-start.28 = (bf16[16,960]{1,0:T(8,128)(2,1)S(1)}, bf16[16,960]{1,0:T(8,128)(2,1)S(1)}, u32[]{:S(2)}, u32[]{:S(2)}) collective-permute-start(bf16[16,960]{1,0:T(8,128)(2,1)S(1)} %get-tuple-element.81), channel_id=1, source_target_pairs={{0,8},{1,9},{2,10},{3,11},{4,12},{5,13},{6,14},{7,15},{8,0},{9,1},... | collective-permute-start | bytes 92168 | tf_op jit(solution)/shard_map/ppermute | solution.py:42

commit v10 on v9

--- a/solution.py
+++ b/solution.py
@@ -17,7 +17,7 @@
 TILE = 256
 LANES = 128
 COPY_ROWS = 16
-COPIES_AHEAD = 8
+COPIES_AHEAD = 4
 LIMIT = 16 << 20
 AHEAD = pl.CostEstimate(flops=60_000_000_000, bytes_accessed=150_000_000, transcendentals=0)
 ROWS_LAST = (((1,), (1,)), ((), ()))

time: 70.2 us -> 70.3 us (level)
  no operation moved by 1% of the time
where the time goes in v10:
time: 70.3 us; the launch traced here: 70.1 us
  starting transfers between devices  32.7 us (47%)
  waiting for transfers between devices  19.1 us (27%)
  Pallas kernels  17.3 us (25%)
  between operations  0.94 us (1%)
    ppermute x29, starting transfers between devices, from_mask(): return lax.ppermute(value, 'req', pairs)  32.7 us
    ppermute x29, waiting for transfers between devices, from_mask(): return lax.ppermute(value, 'req', pairs)  19.1 us
    pallas_call x17, Pallas kernels, whole_call(): pl.pallas_call(kernel, out_shape=outs, in_specs=[pl.BlockSpec(memory_spac...  12.6 us
    pallas_call x1, Pallas kernels, attention(): pl.pallas_call(functools.partial(attention_kernel, group, block), out_sha...  4.72 us
  transfers between devices with their start and end apart: 29, of which 15 were waited for; matrix products, arithmetic and copies ran while one was open for 0% of the time, Pallas kernels for 6%

profile of v10, /device:TPU:0, one launch (start us, length us, event | category | flops | bytes accessed | tf_op | source)
XLA Modules:
  0.0 70.1 jit_solution(4541864594161763124)
XLA Ops:
  0.7 4.7 %attention.1 = (bf16[2,64,256]{2,1,0:T(8,128)(2,1)S(1)}, bf16[2,64,256]{2,1,0:T(8,128)(2,1)S(1)}) custom-call(s32[2,128]{1,0:T(2,128)} %lengths.1, s32[1]{0:T(128)S(6)} %select_n.7.place, bf16[2,64,512]{2,1,0:T(8,128)(2,1)} %far_q.1, bf16[2,64,128]{2,1,0:T(8,128)(2,1)} %far_kv.1, bf16[2,64,128,128]{3,2,1,0:T(8,128)(2,1)} %far.1), custom_call_target="tpu_custom_call" | custom-call | flops 10000000000 | bytes 30000000 | tf_op jit(solution)/shard_map/attention/pallas_call | solution.py:322
  5.4 0.5 collective-permute-start
  5.9 0.9 %collective-permute-done.refs_1_ = bf16[2,64,256]{2,1,0:T(8,128)(2,1)S(1)} collective-permute-done((bf16[2,64,256]{2,1,0:T(8,128)(2,1)S(1)}, bf16[2,64,256]{2,1,0:T(8,128)(2,1)S(1)}, u32[]{:S(2)}, u32[]{:S(2)}) %collective-permute-start) | collective-permute-done | bytes 65568 | tf_op jit(solution)/shard_map/ppermute | solution.py:42
  6.8 0.6 project.3
  7.5 0.4 collective-permute-start.6
  7.9 0.2 collective-permute-start.1
  8.0 0.6 project.2
  8.7 0.6 collective-permute-done.6.refs_1_
  9.2 0.1 add_split.7
  9.3 2.9 %collective-permute-start.7 = (bf16[16,2880]{1,0:T(8,128)(2,1)S(1)}, bf16[16,2880]{1,0:T(8,128)(2,1)S(1)}, u32[]{:S(2)}, u32[]{:S(2)}) collective-permute-start(bf16[16,2880]{1,0:T(8,128)(2,1)S(1)} %get-tuple-element.56), channel_id=1, source_target_pairs={{0,2},{1,3},{2,0},{3,1},{4,6},{5,7},{6,4},{7,5},{8,10},{9,11},{10,... | collective-permute-start | bytes 276488 | tf_op jit(solution)/shard_map/ppermute | solution.py:42
  12.2 1.6 %collective-permute-start.8 = (bf16[16,2880]{1,0:T(8,128)(2,1)S(1)}, bf16[16,2880]{1,0:T(8,128)(2,1)S(1)}, u32[]{:S(2)}, u32[]{:S(2)}) collective-permute-start(bf16[16,2880]{1,0:T(8,128)(2,1)S(1)} %get-tuple-element.57), channel_id=1, source_target_pairs={{0,4},{1,5},{2,6},{3,7},{4,0},{5,1},{6,2},{7,3},{8,12},{9,13},{10,... | collective-permute-start | bytes 276488 | tf_op jit(solution)/shard_map/ppermute | solution.py:42
  13.8 0.0 collective-permute-done.1.refs_1_
  13.8 0.1 add_split.6
  13.9 2.0 %collective-permute-start.2 = (bf16[16,2880]{1,0:T(8,128)(2,1)S(1)}, bf16[16,2880]{1,0:T(8,128)(2,1)S(1)}, u32[]{:S(2)}, u32[]{:S(2)}) collective-permute-start(bf16[16,2880]{1,0:T(8,128)(2,1)S(1)} %get-tuple-element.47), channel_id=1, source_target_pairs={{0,2},{1,3},{2,0},{3,1},{4,6},{5,7},{6,4},{7,5},{8,10},{9,11},{10,... | collective-permute-start | bytes 276488 | tf_op jit(solution)/shard_map/ppermute | solution.py:42
  15.9 1.6 %collective-permute-start.3 = (bf16[16,2880]{1,0:T(8,128)(2,1)S(1)}, bf16[16,2880]{1,0:T(8,128)(2,1)S(1)}, u32[]{:S(2)}, u32[]{:S(2)}) collective-permute-start(bf16[16,2880]{1,0:T(8,128)(2,1)S(1)} %get-tuple-element.48), channel_id=1, source_target_pairs={{0,4},{1,5},{2,6},{3,7},{4,0},{5,1},{6,2},{7,3},{8,12},{9,13},{10,... | collective-permute-start | bytes 276488 | tf_op jit(solution)/shard_map/ppermute | solution.py:42
  17.4 0.6 collective-permute-start.4
  18.0 0.0 collective-permute-done.8.refs_2_
  18.0 2.2 %collective-permute-done.9.refs_3_ = bf16[16,2880]{1,0:T(8,128)(2,1)S(1)} collective-permute-done((bf16[16,2880]{1,0:T(8,128)(2,1)S(1)}, bf16[16,2880]{1,0:T(8,128)(2,1)S(1)}, u32[]{:S(2)}, u32[]{:S(2)}) %collective-permute-start.9) | collective-permute-done | bytes 92192 | tf_op jit(solution)/shard_map/ppermute | solution.py:42
  20.2 0.0 slice-start.3
  20.3 0.0 slice-start.4
  20.3 0.0 slice-start.6
  20.3 0.0 slice-start.7
  20.3 0.7 %share.3 = (f32[16,2944]{1,0:T(8,128)S(1)}, bf16[16,2944]{1,0:T(8,128)(2,1)S(1)}) custom-call(s32[2,4,8]{2,1,0:T(4,128)S(1)} %bitcast.25, f32[16,2880]{1,0:T(8,128)S(1)} %get-tuple-element.55.refs_0_, bf16[16,2880]{1,0:T(8,128)(2,1)S(1)} %collective-permute-done.7.refs_1_, bf16[16,2880]{1,0:T(8,128)(2,1)S(1)} %collective-permute-done.8.refs_2_, ...), custom_call_target="tpu_custom_call" | custom-call | flops 60000002048 | bytes 180000000 | tf_op jit(solution)/shard_map/share/pallas_call | solution.py:50
  21.0 2.7 %collective-permute-start.10 = (bf16[16,2944]{1,0:T(8,128)(2,1)S(1)}, bf16[16,2944]{1,0:T(8,128)(2,1)S(1)}, u32[]{:S(2)}, u32[]{:S(2)}) collective-permute-start(bf16[16,2944]{1,0:T(8,128)(2,1)S(1)} %get-tuple-element.60.mine), channel_id=1, source_target_pairs={{0,8},{1,9},{2,10},{3,11},{4,12},{5,13},{6,14},{7,15},{8,0},{9,1},... | collective-permute-start | bytes 282632 | tf_op jit(solution)/shard_map/ppermute | solution.py:42
  23.7 0.0 copy-start
  23.7 0.0 slice-start.2
  23.7 0.0 slice-start.5
  23.7 0.0 slice-start.8
  23.7 0.7 %share.2 = (f32[16,2944]{1,0:T(8,128)S(1)}, bf16[16,2944]{1,0:T(8,128)(2,1)S(1)}) custom-call(s32[2,4,8]{2,1,0:T(4,128)S(1)} %bitcast.26, f32[16,2880]{1,0:T(8,128)S(1)} %get-tuple-element.46.refs_0_, bf16[16,2880]{1,0:T(8,128)(2,1)S(1)} %collective-permute-done.2.refs_1_, bf16[16,2880]{1,0:T(8,128)(2,1)S(1)} %collective-permute-done.3.refs_2_, ...), custom_call_target="tpu_custom_call" | custom-call | flops 60000002048 | bytes 180000000 | tf_op jit(solution)/shard_map/share/pallas_call | solution.py:50
  24.4 2.9 %collective-permute-start.5 = (bf16[16,2944]{1,0:T(8,128)(2,1)S(1)}, bf16[16,2944]{1,0:T(8,128)(2,1)S(1)}, u32[]{:S(2)}, u32[]{:S(2)}) collective-permute-start(bf16[16,2944]{1,0:T(8,128)(2,1)S(1)} %get-tuple-element.51.mine), channel_id=1, source_target_pairs={{0,8},{1,9},{2,10},{3,11},{4,12},{5,13},{6,14},{7,15},{8,0},{9,1},... | collective-permute-start | bytes 282632 | tf_op jit(solution)/shard_map/ppermute | solution.py:42
  27.4 2.7 %collective-permute-done.10.theirs = bf16[16,2944]{1,0:T(8,128)(2,1)S(1)} collective-permute-done((bf16[16,2944]{1,0:T(8,128)(2,1)S(1)}, bf16[16,2944]{1,0:T(8,128)(2,1)S(1)}, u32[]{:S(2)}, u32[]{:S(2)}) %collective-permute-start.10) | collective-permute-done | bytes 94240 | tf_op jit(solution)/shard_map/ppermute | solution.py:42
  30.1 0.5 norm.3
  30.6 0.5 collective-permute-start.17
  31.2 3.0 %collective-permute-start.15 = (bf16[16,2944]{1,0:T(8,128)(2,1)S(1)}, bf16[16,2944]{1,0:T(8,128)(2,1)S(1)}, u32[]{:S(2)}, u32[]{:S(2)}) collective-permute-start(bf16[16,2944]{1,0:T(8,128)(2,1)S(1)} %get-tuple-element.63.refs_0_.refs_5_), channel_id=1, source_target_pairs={{0,2},{1,3},{2,0},{3,1},{4,6},{5,7},{6,4},{7,5},{8,10},{9,11},{10,... | collective-permute-start | bytes 282632 | tf_op jit(solution)/shard_map/ppermute | solution.py:42
  34.2 0.5 norm.2
  34.7 0.5 collective-permute-start.13
  35.2 1.0 %collective-permute-start.12 = (bf16[16,2944]{1,0:T(8,128)(2,1)S(1)}, bf16[16,2944]{1,0:T(8,128)(2,1)S(1)}, u32[]{:S(2)}, u32[]{:S(2)}) collective-permute-start(bf16[16,2944]{1,0:T(8,128)(2,1)S(1)} %get-tuple-element.62.refs_0_), channel_id=1, source_target_pairs={{0,4},{1,5},{2,6},{3,7},{4,0},{5,1},{6,2},{7,3},{8,12},{9,13},{10,... | collective-permute-start | bytes 282632 | tf_op jit(solution)/shard_map/ppermute | solution.py:42
  36.2 1.0 %collective-permute-done.17.refs_3_.refs_8_ = bf16[16,2944]{1,0:T(8,128)(2,1)S(1)} collective-permute-done((bf16[16,2944]{1,0:T(8,128)(2,1)S(1)}, bf16[16,2944]{1,0:T(8,128)(2,1)S(1)}, u32[]{:S(2)}, u32[]{:S(2)}) %collective-permute-start.17) | collective-permute-done | bytes 94240 | tf_op jit(solution)/shard_map/ppermute | solution.py:42
  37.2 1.1 %collective-permute-start.11 = (bf16[16,2944]{1,0:T(8,128)(2,1)S(1)}, bf16[16,2944]{1,0:T(8,128)(2,1)S(1)}, u32[]{:S(2)}, u32[]{:S(2)}) collective-permute-start(bf16[16,2944]{1,0:T(8,128)(2,1)S(1)} %get-tuple-element.62.refs_0_), channel_id=1, source_target_pairs={{0,2},{1,3},{2,0},{3,1},{4,6},{5,7},{6,4},{7,5},{8,10},{9,11},{10,... | collective-permute-start | bytes 282632 | tf_op jit(solution)/shard_map/ppermute | solution.py:42
  38.3 0.8 %collective-permute-done.15.refs_1_.refs_6_ = bf16[16,2944]{1,0:T(8,128)(2,1)S(1)} collective-permute-done((bf16[16,2944]{1,0:T(8,128)(2,1)S(1)}, bf16[16,2944]{1,0:T(8,128)(2,1)S(1)}, u32[]{:S(2)}, u32[]{:S(2)}) %collective-permute-start.15) | collective-permute-done | bytes 94240 | tf_op jit(solution)/shard_map/ppermute | solution.py:42
  39.2 0.1 collective-permute-start.18
  39.2 1.0 %collective-permute-done.13.refs_3_ = bf16[16,2944]{1,0:T(8,128)(2,1)S(1)} collective-permute-done((bf16[16,2944]{1,0:T(8,128)(2,1)S(1)}, bf16[16,2944]{1,0:T(8,128)(2,1)S(1)}, u32[]{:S(2)}, u32[]{:S(2)}) %collective-permute-start.13) | collective-permute-done | bytes 94240 | tf_op jit(solution)/shard_map/ppermute | solution.py:42
  40.3 1.5 %collective-permute-done.11.refs_1_ = bf16[16,2944]{1,0:T(8,128)(2,1)S(1)} collective-permute-done((bf16[16,2944]{1,0:T(8,128)(2,1)S(1)}, bf16[16,2944]{1,0:T(8,128)(2,1)S(1)}, u32[]{:S(2)}, u32[]{:S(2)}) %collective-permute-start.11) | collective-permute-done | bytes 94240 | tf_op jit(solution)/shard_map/ppermute | solution.py:42
  41.8 0.1 collective-permute-start.14
  41.9 1.7 %collective-permute-done.14.refs_4_ = bf16[64,2944]{1,0:T(8,128)(2,1)S(1)} collective-permute-done((bf16[64,2944]{1,0:T(8,128)(2,1)S(1)}, bf16[64,2944]{1,0:T(8,128)(2,1)S(1)}, u32[]{:S(2)}, u32[]{:S(2)}) %collective-permute-start.14) | collective-permute-done | bytes 376864 | tf_op jit(solution)/shard_map/ppermute | solution.py:42
  43.7 6.8 %experts.1 = (f32[128,1920]{1,0:T(8,128)S(1)}, bf16[128,1920]{1,0:T(8,128)(2,1)S(1)}, bf16[256,1440]{1,0:T(8,128)(2,1)S(1)}, f32[1,256,128]{2,1,0:T(8,128)S(1)}) custom-call(s32[1]{0:T(128)} %bitcast.1.me_ref, bf16[16,2944]{1,0:T(8,128)(2,1)S(1)} %get-tuple-element.62.refs_0_, bf16[16,2944]{1,0:T(8,128)(2,1)S(1)} %collective-permute-done.11.refs_1_, ...), custom_call_target="tpu_custom_call" | custom-call | tf_op jit(solution)/shard_map/experts/pallas_call | solution.py:50
  50.4 0.2 collective-permute-start.19
  50.6 1.0 %down.1 = (f32[128,960]{1,0:T(8,128)S(1)}, bf16[128,1024]{1,0:T(8,128)(2,1)S(1)}) custom-call(bf16[256,1440]{1,0:T(8,128)(2,1)S(1)} %get-tuple-element.72.active, f32[1,256,128]{2,1,0:T(8,128)S(1)} %get-tuple-element.73.weights, bf16[1440,2880]{1,0:T(8,128)(2,1)S(1)} %bitcast.14), custom_call_target="tpu_custom_call" | custom-call | tf_op jit(solution)/shard_map/down/pallas_call | solution.py:50
  51.6 0.5 collective-permute-start.24
  52.1 0.3 collective-permute-done.19.refs_1_
  52.4 0.1 add_split.8
  52.5 1.1 %collective-permute-start.20 = (bf16[32,1920]{1,0:T(8,128)(2,1)S(1)}, bf16[32,1920]{1,0:T(8,128)(2,1)S(1)}, u32[]{:S(2)}, u32[]{:S(2)}) collective-permute-start(bf16[32,1920]{1,0:T(8,128)(2,1)S(1)} %get-tuple-element.67), channel_id=1, source_target_pairs={{0,2},{1,3},{2,0},{3,1},{4,6},{5,7},{6,4},{7,5},{8,10},{9,11},{10,... | collective-permute-start | bytes 368648 | tf_op jit(solution)/shard_map/ppermute | solution.py:42
  53.6 2.4 %collective-permute-start.22 = (bf16[32,1920]{1,0:T(8,128)(2,1)S(1)}, bf16[32,1920]{1,0:T(8,128)(2,1)S(1)}, u32[]{:S(2)}, u32[]{:S(2)}) collective-permute-start(bf16[32,1920]{1,0:T(8,128)(2,1)S(1)} %get-tuple-element.69), channel_id=1, source_target_pairs={{0,6},{1,7},{2,4},{3,5},{4,2},{5,3},{6,0},{7,1},{8,14},{9,15},{10,... | collective-permute-start | bytes 368648 | tf_op jit(solution)/shard_map/ppermute | solution.py:42
  56.1 1.1 %collective-permute-start.25 = (bf16[32,960]{1,0:T(8,128)(2,1)S(1)}, bf16[32,960]{1,0:T(8,128)(2,1)S(1)}, u32[]{:S(2)}, u32[]{:S(2)}) collective-permute-start(bf16[32,960]{1,0:T(8,128)(2,1)S(1)} %get-tuple-element.77), channel_id=1, source_target_pairs={{0,2},{1,3},{2,0},{3,1},{4,6},{5,7},{6,4},{7,5},{8,10},{9,11},{10,... | collective-permute-start | bytes 184328 | tf_op jit(solution)/shard_map/ppermute | solution.py:42
  57.2 0.7 collective-permute-done.20.refs_1_
  57.9 1.7 %collective-permute-start.27 = (bf16[32,960]{1,0:T(8,128)(2,1)S(1)}, bf16[32,960]{1,0:T(8,128)(2,1)S(1)}, u32[]{:S(2)}, u32[]{:S(2)}) collective-permute-start(bf16[32,960]{1,0:T(8,128)(2,1)S(1)} %get-tuple-element.79), channel_id=1, source_target_pairs={{0,6},{1,7},{2,4},{3,5},{4,2},{5,3},{6,0},{7,1},{8,14},{9,15},{10,... | collective-permute-start | bytes 184328 | tf_op jit(solution)/shard_map/ppermute | solution.py:42
  59.6 0.2 collective-permute-done.21.refs_2_
  59.8 3.0 %collective-permute-done.22.refs_3_ = bf16[32,1920]{1,0:T(8,128)(2,1)S(1)} collective-permute-done((bf16[32,1920]{1,0:T(8,128)(2,1)S(1)}, bf16[32,1920]{1,0:T(8,128)(2,1)S(1)}, u32[]{:S(2)}, u32[]{:S(2)}) %collective-permute-start.22) | collective-permute-done | bytes 122912 | tf_op jit(solution)/shard_map/ppermute | solution.py:42
  62.8 0.1 add_split.9
  62.9 1.5 %collective-permute-start.23 = (bf16[16,1920]{1,0:T(8,128)(2,1)S(1)}, bf16[16,1920]{1,0:T(8,128)(2,1)S(1)}, u32[]{:S(2)}, u32[]{:S(2)}) collective-permute-start(bf16[16,1920]{1,0:T(8,128)(2,1)S(1)} %get-tuple-element.71), channel_id=1, source_target_pairs={{0,8},{1,9},{2,10},{3,11},{4,12},{5,13},{6,14},{7,15},{8,0},{9,1},... | collective-permute-start | bytes 184328 | tf_op jit(solution)/shard_map/ppermute | solution.py:42
  64.4 0.1 collective-permute-done.27.refs_3_
  64.6 2.5 %collective-permute-start.28 = (bf16[16,960]{1,0:T(8,128)(2,1)S(1)}, bf16[16,960]{1,0:T(8,128)(2,1)S(1)}, u32[]{:S(2)}, u32[]{:S(2)}) collective-permute-start(bf16[16,960]{1,0:T(8,128)(2,1)S(1)} %get-tuple-element.81), channel_id=1, source_target_pairs={{0,8},{1,9},{2,10},{3,11},{4,12},{5,13},{6,14},{7,15},{8,0},{9,1},... | collective-permute-start | bytes 92168 | tf_op jit(solution)/shard_map/ppermute | solution.py:42
  67.1 2.4 %collective-permute-done.28.refs_5_ = bf16[16,960]{1,0:T(8,128)(2,1)S(1)} collective-permute-done((bf16[16,960]{1,0:T(8,128)(2,1)S(1)}, bf16[16,960]{1,0:T(8,128)(2,1)S(1)}, u32[]{:S(2)}, u32[]{:S(2)}) %collective-permute-start.28) | collective-permute-done | bytes 30752 | tf_op jit(solution)/shard_map/ppermute | solution.py:42
  69.4 0.7 finish.1
  (41 shorter events, 0.2 us)
Async XLA Ops:
  0.6 6.2 %copy-start.1 = (bf16[256,2880]{0,1:T(8,128)(2,1)S(1)}, bf16[256,2880]{0,1:T(8,128)(2,1)}, u32[]{:S(2)}) copy-start(bf16[256,2880]{0,1:T(8,128)(2,1)} %param.16) | copy-start | bytes 4423684
  0.7 19.6 %copy-start.2 = (bf16[2,8,2880]{2,1,0:T(8,128)(2,1)S(1)}, bf16[2,8,2880]{2,1,0:T(8,128)(2,1)}, u32[]{:S(2)}) copy-start(bf16[2,8,2880]{2,1,0:T(8,128)(2,1)} %refs_4_.3) | copy-start | bytes 276484
  0.7 19.6 %copy-start.3 = (s32[2,8,4]{1,2,0:T(4,128)S(1)}, s32[2,8,4]{1,2,0:T(4,128)}, u32[]{:S(2)}) copy-start(s32[2,8,4]{1,2,0:T(4,128)} %param.21) | copy-start | bytes 772
  5.4 1.4 %collective-permute-start = (bf16[2,64,256]{2,1,0:T(8,128)(2,1)S(1)}, bf16[2,64,256]{2,1,0:T(8,128)(2,1)S(1)}, u32[]{:S(2)}, u32[]{:S(2)}) collective-permute-start(bf16[2,64,256]{2,1,0:T(8,128)(2,1)S(1)} %get-tuple-element.43), channel_id=1, source_target_pairs={{0,1},{1,0},{2,3},{3,2},{4,5},{5,4},{6,7},{7,6},{8,9},{9,8},{10,11... | collective-permute-start | bytes 196616 | tf_op jit(solution)/shard_map/ppermute | solution.py:42
  7.5 1.8 %collective-permute-start.6 = (bf16[64,2944]{1,0:T(8,128)(2,1)S(1)}, bf16[64,2944]{1,0:T(8,128)(2,1)S(1)}, u32[]{:S(2)}, u32[]{:S(2)}) collective-permute-start(bf16[64,2944]{1,0:T(8,128)(2,1)S(1)} %get-tuple-element.54), channel_id=1, source_target_pairs={{0,1},{1,0},{2,3},{3,2},{4,5},{5,4},{6,7},{7,6},{8,9},{9,8},{10,11... | collective-permute-start | bytes 1130504 | tf_op jit(solution)/shard_map/ppermute | solution.py:42
  7.9 5.9 %collective-permute-start.1 = (bf16[64,2944]{1,0:T(8,128)(2,1)S(1)}, bf16[64,2944]{1,0:T(8,128)(2,1)S(1)}, u32[]{:S(2)}, u32[]{:S(2)}) collective-permute-start(bf16[64,2944]{1,0:T(8,128)(2,1)S(1)} %get-tuple-element.45), channel_id=1, source_target_pairs={{0,1},{1,0},{2,3},{3,2},{4,5},{5,4},{6,7},{7,6},{8,9},{9,8},{10,11... | collective-permute-start | bytes 1130504 | tf_op jit(solution)/shard_map/ppermute | solution.py:42
  9.3 8.1 %collective-permute-start.7 = (bf16[16,2880]{1,0:T(8,128)(2,1)S(1)}, bf16[16,2880]{1,0:T(8,128)(2,1)S(1)}, u32[]{:S(2)}, u32[]{:S(2)}) collective-permute-start(bf16[16,2880]{1,0:T(8,128)(2,1)S(1)} %get-tuple-element.56), channel_id=1, source_target_pairs={{0,2},{1,3},{2,0},{3,1},{4,6},{5,7},{6,4},{7,5},{8,10},{9,11},{10,... | collective-permute-start | bytes 276488 | tf_op jit(solution)/shard_map/ppermute | solution.py:42
  12.2 5.8 %collective-permute-start.8 = (bf16[16,2880]{1,0:T(8,128)(2,1)S(1)}, bf16[16,2880]{1,0:T(8,128)(2,1)S(1)}, u32[]{:S(2)}, u32[]{:S(2)}) collective-permute-start(bf16[16,2880]{1,0:T(8,128)(2,1)S(1)} %get-tuple-element.57), channel_id=1, source_target_pairs={{0,4},{1,5},{2,6},{3,7},{4,0},{5,1},{6,2},{7,3},{8,12},{9,13},{10,... | collective-permute-start | bytes 276488 | tf_op jit(solution)/shard_map/ppermute | solution.py:42
  13.8 6.4 %collective-permute-start.9 = (bf16[16,2880]{1,0:T(8,128)(2,1)S(1)}, bf16[16,2880]{1,0:T(8,128)(2,1)S(1)}, u32[]{:S(2)}, u32[]{:S(2)}) collective-permute-start(bf16[16,2880]{1,0:T(8,128)(2,1)S(1)} %get-tuple-element.58), channel_id=1, source_target_pairs={{0,6},{1,7},{2,4},{3,5},{4,2},{5,3},{6,0},{7,1},{8,14},{9,15},{10,... | collective-permute-start | bytes 276488 | tf_op jit(solution)/shard_map/ppermute | solution.py:42
  13.9 9.8 %collective-permute-start.2 = (bf16[16,2880]{1,0:T(8,128)(2,1)S(1)}, bf16[16,2880]{1,0:T(8,128)(2,1)S(1)}, u32[]{:S(2)}, u32[]{:S(2)}) collective-permute-start(bf16[16,2880]{1,0:T(8,128)(2,1)S(1)} %get-tuple-element.47), channel_id=1, source_target_pairs={{0,2},{1,3},{2,0},{3,1},{4,6},{5,7},{6,4},{7,5},{8,10},{9,11},{10,... | collective-permute-start | bytes 276488 | tf_op jit(solution)/shard_map/ppermute | solution.py:42
  15.9 7.8 %collective-permute-start.3 = (bf16[16,2880]{1,0:T(8,128)(2,1)S(1)}, bf16[16,2880]{1,0:T(8,128)(2,1)S(1)}, u32[]{:S(2)}, u32[]{:S(2)}) collective-permute-start(bf16[16,2880]{1,0:T(8,128)(2,1)S(1)} %get-tuple-element.48), channel_id=1, source_target_pairs={{0,4},{1,5},{2,6},{3,7},{4,0},{5,1},{6,2},{7,3},{8,12},{9,13},{10,... | collective-permute-start | bytes 276488 | tf_op jit(solution)/shard_map/ppermute | solution.py:42
  17.4 6.2 %collective-permute-start.4 = (bf16[16,2880]{1,0:T(8,128)(2,1)S(1)}, bf16[16,2880]{1,0:T(8,128)(2,1)S(1)}, u32[]{:S(2)}, u32[]{:S(2)}) collective-permute-start(bf16[16,2880]{1,0:T(8,128)(2,1)S(1)} %get-tuple-element.49), channel_id=1, source_target_pairs={{0,6},{1,7},{2,4},{3,5},{4,2},{5,3},{6,0},{7,1},{8,14},{9,15},{10,... | collective-permute-start | bytes 276488 | tf_op jit(solution)/shard_map/ppermute | solution.py:42
  20.2 23.3 %slice-start = ((s8[8478720]{0:T(1024)(128)(4,1)}), s8[4194304]{0:T(1024)(128)(4,1)S(1)}, s32[]{:S(2)}) async-start(s8[8478720]{0:T(1024)(128)(4,1)} %bitcast.11), calls=%async_computation | async-start | bytes 8388608
  20.2 23.3 %slice-start.1 = ((s8[8478720]{0:T(1024)(128)(4,1)}), s8[4194304]{0:T(1024)(128)(4,1)S(1)}, s32[]{:S(2)}) async-start(s8[8478720]{0:T(1024)(128)(4,1)} %bitcast.11), calls=%async_computation.1 | async-start | bytes 8388608
  20.2 23.3 %slice-start.3 = ((s8[8478720]{0:T(1024)(128)(4,1)}), s8[4194304]{0:T(1024)(128)(4,1)S(1)}, s32[]{:S(2)}) async-start(s8[8478720]{0:T(1024)(128)(4,1)} %bitcast.15), calls=%async_computation.3 | async-start | bytes 8388608
  20.3 23.3 %slice-start.4 = ((s8[8478720]{0:T(1024)(128)(4,1)}), s8[4194304]{0:T(1024)(128)(4,1)S(1)}, s32[]{:S(2)}) async-start(s8[8478720]{0:T(1024)(128)(4,1)} %bitcast.15), calls=%async_computation.4 | async-start | bytes 8388608
  20.3 23.3 %slice-start.6 = ((s8[8478720]{0:T(1024)(128)(4,1)}), s8[4194304]{0:T(1024)(128)(4,1)S(1)}, s32[]{:S(2)}) async-start(s8[8478720]{0:T(1024)(128)(4,1)} %bitcast.18), calls=%async_computation.6 | async-start | bytes 8388608
  20.3 23.3 %slice-start.7 = ((s8[8478720]{0:T(1024)(128)(4,1)}), s8[4194304]{0:T(1024)(128)(4,1)S(1)}, s32[]{:S(2)}) async-start(s8[8478720]{0:T(1024)(128)(4,1)} %bitcast.18), calls=%async_computation.7 | async-start | bytes 8388608
  21.0 9.1 %collective-permute-start.10 = (bf16[16,2944]{1,0:T(8,128)(2,1)S(1)}, bf16[16,2944]{1,0:T(8,128)(2,1)S(1)}, u32[]{:S(2)}, u32[]{:S(2)}) collective-permute-start(bf16[16,2944]{1,0:T(8,128)(2,1)S(1)} %get-tuple-element.60.mine), channel_id=1, source_target_pairs={{0,8},{1,9},{2,10},{3,11},{4,12},{5,13},{6,14},{7,15},{8,0},{9,1},... | collective-permute-start | bytes 282632 | tf_op jit(solution)/shard_map/ppermute | solution.py:42
  23.7 6.4 %copy-start = (bf16[2880,16]{0,1:T(8,128)(2,1)S(1)}, bf16[2880,16]{0,1:T(8,128)(2,1)}, u32[]{:S(2)}) copy-start(bf16[2880,16]{0,1:T(8,128)(2,1)} %param.17) | copy-start | bytes 276484
  23.7 19.9 %slice-start.2 = ((s8[8478720]{0:T(1024)(128)(4,1)}), s8[90112]{0:T(1024)(128)(4,1)S(1)}, s32[]{:S(2)}) async-start(s8[8478720]{0:T(1024)(128)(4,1)} %bitcast.11), calls=%async_computation.2 | async-start | bytes 180224
  23.7 19.9 %slice-start.5 = ((s8[8478720]{0:T(1024)(128)(4,1)}), s8[90112]{0:T(1024)(128)(4,1)S(1)}, s32[]{:S(2)}) async-start(s8[8478720]{0:T(1024)(128)(4,1)} %bitcast.15), calls=%async_computation.5 | async-start | bytes 180224
  23.7 19.9 %slice-start.8 = ((s8[8478720]{0:T(1024)(128)(4,1)}), s8[90112]{0:T(1024)(128)(4,1)S(1)}, s32[]{:S(2)}) async-start(s8[8478720]{0:T(1024)(128)(4,1)} %bitcast.18), calls=%async_computation.8 | async-start | bytes 180224
  24.4 9.8 %collective-permute-start.5 = (bf16[16,2944]{1,0:T(8,128)(2,1)S(1)}, bf16[16,2944]{1,0:T(8,128)(2,1)S(1)}, u32[]{:S(2)}, u32[]{:S(2)}) collective-permute-start(bf16[16,2944]{1,0:T(8,128)(2,1)S(1)} %get-tuple-element.51.mine), channel_id=1, source_target_pairs={{0,8},{1,9},{2,10},{3,11},{4,12},{5,13},{6,14},{7,15},{8,0},{9,1},... | collective-permute-start | bytes 282632 | tf_op jit(solution)/shard_map/ppermute | solution.py:42
  30.6 6.6 %collective-permute-start.17 = (bf16[16,2944]{1,0:T(8,128)(2,1)S(1)}, bf16[16,2944]{1,0:T(8,128)(2,1)S(1)}, u32[]{:S(2)}, u32[]{:S(2)}) collective-permute-start(bf16[16,2944]{1,0:T(8,128)(2,1)S(1)} %get-tuple-element.63.refs_0_.refs_5_), channel_id=1, source_target_pairs={{0,6},{1,7},{2,4},{3,5},{4,2},{5,3},{6,0},{7,1},{8,14},{9,15},{10,... | collective-permute-start | bytes 282632 | tf_op jit(solution)/shard_map/ppermute | solution.py:42
  31.2 7.1 %collective-permute-start.16 = (bf16[16,2944]{1,0:T(8,128)(2,1)S(1)}, bf16[16,2944]{1,0:T(8,128)(2,1)S(1)}, u32[]{:S(2)}, u32[]{:S(2)}) collective-permute-start(bf16[16,2944]{1,0:T(8,128)(2,1)S(1)} %get-tuple-element.63.refs_0_.refs_5_), channel_id=1, source_target_pairs={{0,4},{1,5},{2,6},{3,7},{4,0},{5,1},{6,2},{7,3},{8,12},{9,13},{10,... | collective-permute-start | bytes 282632 | tf_op jit(solution)/shard_map/ppermute | solution.py:42
  31.2 8.0 %collective-permute-start.15 = (bf16[16,2944]{1,0:T(8,128)(2,1)S(1)}, bf16[16,2944]{1,0:T(8,128)(2,1)S(1)}, u32[]{:S(2)}, u32[]{:S(2)}) collective-permute-start(bf16[16,2944]{1,0:T(8,128)(2,1)S(1)} %get-tuple-element.63.refs_0_.refs_5_), channel_id=1, source_target_pairs={{0,2},{1,3},{2,0},{3,1},{4,6},{5,7},{6,4},{7,5},{8,10},{9,11},{10,... | collective-permute-start | bytes 282632 | tf_op jit(solution)/shard_map/ppermute | solution.py:42
  34.7 5.5 %collective-permute-start.13 = (bf16[16,2944]{1,0:T(8,128)(2,1)S(1)}, bf16[16,2944]{1,0:T(8,128)(2,1)S(1)}, u32[]{:S(2)}, u32[]{:S(2)}) collective-permute-start(bf16[16,2944]{1,0:T(8,128)(2,1)S(1)} %get-tuple-element.62.refs_0_), channel_id=1, source_target_pairs={{0,6},{1,7},{2,4},{3,5},{4,2},{5,3},{6,0},{7,1},{8,14},{9,15},{10,... | collective-permute-start | bytes 282632 | tf_op jit(solution)/shard_map/ppermute | solution.py:42
  35.2 5.0 %collective-permute-start.12 = (bf16[16,2944]{1,0:T(8,128)(2,1)S(1)}, bf16[16,2944]{1,0:T(8,128)(2,1)S(1)}, u32[]{:S(2)}, u32[]{:S(2)}) collective-permute-start(bf16[16,2944]{1,0:T(8,128)(2,1)S(1)} %get-tuple-element.62.refs_0_), channel_id=1, source_target_pairs={{0,4},{1,5},{2,6},{3,7},{4,0},{5,1},{6,2},{7,3},{8,12},{9,13},{10,... | collective-permute-start | bytes 282632 | tf_op jit(solution)/shard_map/ppermute | solution.py:42
  37.2 4.6 %collective-permute-start.11 = (bf16[16,2944]{1,0:T(8,128)(2,1)S(1)}, bf16[16,2944]{1,0:T(8,128)(2,1)S(1)}, u32[]{:S(2)}, u32[]{:S(2)}) collective-permute-start(bf16[16,2944]{1,0:T(8,128)(2,1)S(1)} %get-tuple-element.62.refs_0_), channel_id=1, source_target_pairs={{0,2},{1,3},{2,0},{3,1},{4,6},{5,7},{6,4},{7,5},{8,10},{9,11},{10,... | collective-permute-start | bytes 282632 | tf_op jit(solution)/shard_map/ppermute | solution.py:42
  39.2 2.7 %collective-permute-start.18 = (bf16[64,2944]{1,0:T(8,128)(2,1)S(1)}, bf16[64,2944]{1,0:T(8,128)(2,1)S(1)}, u32[]{:S(2)}, u32[]{:S(2)}) collective-permute-start(bf16[64,2944]{1,0:T(8,128)(2,1)S(1)} %join.3), channel_id=1, source_target_pairs={{0,1},{1,0},{2,3},{3,2},{4,5},{5,4},{6,7},{7,6},{8,9},{9,8},{10,11... | collective-permute-start | bytes 1130504 | tf_op jit(solution)/shard_map/ppermute | solution.py:42
  41.8 1.8 %collective-permute-start.14 = (bf16[64,2944]{1,0:T(8,128)(2,1)S(1)}, bf16[64,2944]{1,0:T(8,128)(2,1)S(1)}, u32[]{:S(2)}, u32[]{:S(2)}) collective-permute-start(bf16[64,2944]{1,0:T(8,128)(2,1)S(1)} %join.2), channel_id=1, source_target_pairs={{0,1},{1,0},{2,3},{3,2},{4,5},{5,4},{6,7},{7,6},{8,9},{9,8},{10,11... | collective-permute-start | bytes 1130504 | tf_op jit(solution)/shard_map/ppermute | solution.py:42
  50.4 1.9 %collective-permute-start.19 = (bf16[128,1920]{1,0:T(8,128)(2,1)S(1)}, bf16[128,1920]{1,0:T(8,128)(2,1)S(1)}, u32[]{:S(2)}, u32[]{:S(2)}) collective-permute-start(bf16[128,1920]{1,0:T(8,128)(2,1)S(1)} %get-tuple-element.65), channel_id=1, source_target_pairs={{0,1},{1,0},{2,3},{3,2},{4,5},{5,4},{6,7},{7,6},{8,9},{9,8},{10,11... | collective-permute-start | bytes 1474568 | tf_op jit(solution)/shard_map/ppermute | solution.py:42
  51.6 4.4 %collective-permute-start.24 = (bf16[128,1024]{1,0:T(8,128)(2,1)S(1)}, bf16[128,1024]{1,0:T(8,128)(2,1)S(1)}, u32[]{:S(2)}, u32[]{:S(2)}) collective-permute-start(bf16[128,1024]{1,0:T(8,128)(2,1)S(1)} %get-tuple-element.75), channel_id=1, source_target_pairs={{0,1},{1,0},{2,3},{3,2},{4,5},{5,4},{6,7},{7,6},{8,9},{9,8},{10,11... | collective-permute-start | bytes 786440 | tf_op jit(solution)/shard_map/ppermute | solution.py:42
  52.5 5.4 %collective-permute-start.20 = (bf16[32,1920]{1,0:T(8,128)(2,1)S(1)}, bf16[32,1920]{1,0:T(8,128)(2,1)S(1)}, u32[]{:S(2)}, u32[]{:S(2)}) collective-permute-start(bf16[32,1920]{1,0:T(8,128)(2,1)S(1)} %get-tuple-element.67), channel_id=1, source_target_pairs={{0,2},{1,3},{2,0},{3,1},{4,6},{5,7},{6,4},{7,5},{8,10},{9,11},{10,... | collective-permute-start | bytes 368648 | tf_op jit(solution)/shard_map/ppermute | solution.py:42
  53.6 6.2 %collective-permute-start.21 = (bf16[32,1920]{1,0:T(8,128)(2,1)S(1)}, bf16[32,1920]{1,0:T(8,128)(2,1)S(1)}, u32[]{:S(2)}, u32[]{:S(2)}) collective-permute-start(bf16[32,1920]{1,0:T(8,128)(2,1)S(1)} %get-tuple-element.68), channel_id=1, source_target_pairs={{0,4},{1,5},{2,6},{3,7},{4,0},{5,1},{6,2},{7,3},{8,12},{9,13},{10,... | collective-permute-start | bytes 368648 | tf_op jit(solution)/shard_map/ppermute | solution.py:42
  53.6 9.2 %collective-permute-start.22 = (bf16[32,1920]{1,0:T(8,128)(2,1)S(1)}, bf16[32,1920]{1,0:T(8,128)(2,1)S(1)}, u32[]{:S(2)}, u32[]{:S(2)}) collective-permute-start(bf16[32,1920]{1,0:T(8,128)(2,1)S(1)} %get-tuple-element.69), channel_id=1, source_target_pairs={{0,6},{1,7},{2,4},{3,5},{4,2},{5,3},{6,0},{7,1},{8,14},{9,15},{10,... | collective-permute-start | bytes 368648 | tf_op jit(solution)/shard_map/ppermute | solution.py:42
  56.1 8.4 %collective-permute-start.25 = (bf16[32,960]{1,0:T(8,128)(2,1)S(1)}, bf16[32,960]{1,0:T(8,128)(2,1)S(1)}, u32[]{:S(2)}, u32[]{:S(2)}) collective-permute-start(bf16[32,960]{1,0:T(8,128)(2,1)S(1)} %get-tuple-element.77), channel_id=1, source_target_pairs={{0,2},{1,3},{2,0},{3,1},{4,6},{5,7},{6,4},{7,5},{8,10},{9,11},{10,... | collective-permute-start | bytes 184328 | tf_op jit(solution)/shard_map/ppermute | solution.py:42
  57.2 7.2 %collective-permute-start.26 = (bf16[32,960]{1,0:T(8,128)(2,1)S(1)}, bf16[32,960]{1,0:T(8,128)(2,1)S(1)}, u32[]{:S(2)}, u32[]{:S(2)}) collective-permute-start(bf16[32,960]{1,0:T(8,128)(2,1)S(1)} %get-tuple-element.78), channel_id=1, source_target_pairs={{0,4},{1,5},{2,6},{3,7},{4,0},{5,1},{6,2},{7,3},{8,12},{9,13},{10,... | collective-permute-start | bytes 184328 | tf_op jit(solution)/shard_map/ppermute | solution.py:42
  57.9 6.6 %collective-permute-start.27 = (bf16[32,960]{1,0:T(8,128)(2,1)S(1)}, bf16[32,960]{1,0:T(8,128)(2,1)S(1)}, u32[]{:S(2)}, u32[]{:S(2)}) collective-permute-start(bf16[32,960]{1,0:T(8,128)(2,1)S(1)} %get-tuple-element.79), channel_id=1, source_target_pairs={{0,6},{1,7},{2,4},{3,5},{4,2},{5,3},{6,0},{7,1},{8,14},{9,15},{10,... | collective-permute-start | bytes 184328 | tf_op jit(solution)/shard_map/ppermute | solution.py:42
  62.9 6.5 %collective-permute-start.23 = (bf16[16,1920]{1,0:T(8,128)(2,1)S(1)}, bf16[16,1920]{1,0:T(8,128)(2,1)S(1)}, u32[]{:S(2)}, u32[]{:S(2)}) collective-permute-start(bf16[16,1920]{1,0:T(8,128)(2,1)S(1)} %get-tuple-element.71), channel_id=1, source_target_pairs={{0,8},{1,9},{2,10},{3,11},{4,12},{5,13},{6,14},{7,15},{8,0},{9,1},... | collective-permute-start | bytes 184328 | tf_op jit(solution)/shard_map/ppermute | solution.py:42
  64.6 4.9 %collective-permute-start.28 = (bf16[16,960]{1,0:T(8,128)(2,1)S(1)}, bf16[16,960]{1,0:T(8,128)(2,1)S(1)}, u32[]{:S(2)}, u32[]{:S(2)}) collective-permute-start(bf16[16,960]{1,0:T(8,128)(2,1)S(1)} %get-tuple-element.81), channel_id=1, source_target_pairs={{0,8},{1,9},{2,10},{3,11},{4,12},{5,13},{6,14},{7,15},{8,0},{9,1},... | collective-permute-start | bytes 92168 | tf_op jit(solution)/shard_map/ppermute | solution.py:42
